TPU v7x, 32 devices: a whole 2x2x4 slice. The times are simulated.
32 devices in a mesh: dp: 4 (over x, core), seq: 8 (over z, y).
Axes of the slice: x: 2, y: 2, z: 4, core: 2. Of those that a mesh axis runs over, the one named last changes fastest.
Arguments:
- tokens: bfloat16 [16384, 1024], P(('dp', 'seq')), may hold values from -6 to 6
- mixer_gain: bfloat16 [1024], P('seq'), may hold values from 0.099609375 to 1.8984375
- in_weight: bfloat16 [1024, 3072], P('seq', 'dp'), may hold values from -0.1875 to 0.1875
- conv_weight: bfloat16 [3, 1024], P(None, 'seq'), may hold values from -3.5 to 3.5
- out_weight: bfloat16 [1024, 1024], P('seq', 'dp'), may hold values from -0.1875 to 0.1875
- feed_gain: bfloat16 [1024], P('seq'), may hold values from 0.099609375 to 1.8984375
- gate_weight: bfloat16 [1024, 4608], P('seq', 'dp'), may hold values from -0.1875 to 0.1875
- up_weight: bfloat16 [1024, 4608], P('seq', 'dp'), may hold values from -0.1875 to 0.1875
- down_weight: bfloat16 [4608, 1024], P('seq', 'dp'), may hold values from -0.09375 to 0.09375
- lengths: int32 [4, 1], P('dp'), may hold values from 1024 to 4096, as said below
- cotangent: bfloat16 [16384, 1024], P(('dp', 'seq')), may hold values from -6 to 6
Outputs:
- output: bfloat16 [16384, 1024], P(('dp', 'seq'))
- grad_tokens: bfloat16 [16384, 1024], P(('dp', 'seq'))
- grad_mixer_gain: float32 [1024], P('seq')
- grad_in_weight: float32 [1024, 3072], P('seq', 'dp')
- grad_conv_weight: float32 [3, 1024], P(None, 'seq')
- grad_out_weight: float32 [1024, 1024], P('seq', 'dp')
- grad_feed_gain: float32 [1024], P('seq')
- grad_gate_weight: float32 [1024, 4608], P('seq', 'dp')
- grad_up_weight: float32 [1024, 4608], P('seq', 'dp')
- grad_down_weight: float32 [4608, 1024], P('seq', 'dp')
Inputs may be any that keep to these rules, and one draw needn't show every extreme that they name: `lengths`: each slot of 4096 rows holds one sequence from its first row on, padding after it; at least one slot of the batch is full.
All inputs are finite; a program needn't handle non-finite values.
Results may differ from a plain program's by a relative error of at most 0.0097.
Values may be sent and summed in bfloat16 or wider, within the bound.
No kernel may reach another device: no remote copies, remote signals or barrier semaphores. Data moves between devices by JAX's collectives and lax.ppermute only.
A program may use at most 256 MiB of HBM per device.

v0:
```python
import jax
import jax.numpy as jnp
from jax import lax
from jax.sharding import PartitionSpec as P

SLOT_MAX = 8192


norm_eps = 1e-05


def passed_along(shard, axis, by):
    count = lax.axis_size(axis)
    pairs = [(i, i + by) for i in range(count) if 0 <= i + by < count]
    return lax.ppermute(shard, axis, pairs)


def multiply(left_side, right_side):
    return jnp.dot(left_side, right_side, preferred_element_type=jnp.float32)


def against(left_side, right_side):
    return lax.dot_general(
        left_side, right_side, (((1,), (1,)), ((), ())), preferred_element_type=jnp.float32
    )


def outer_sum(left_side, right_side):
    return lax.dot_general(
        left_side, right_side, (((0,), (0,)), ((), ())), preferred_element_type=jnp.float32
    )


def rms_forward(values, gain_row):
    scales = lax.rsqrt(jnp.mean(values * values, axis=1, keepdims=True) + norm_eps)
    return (scales, values * scales * gain_row)


def rms_backward(values, scales, gain_row, grad_normed):
    weighted = grad_normed * gain_row
    grad_gain = jnp.sum(grad_normed * values * scales, axis=0)
    inner_mean = jnp.mean(weighted * values, axis=1, keepdims=True)
    return (scales * weighted - values * scales * scales * scales * inner_mean, grad_gain)


def per_device(
    tokens,
    mixer_gain,
    in_weight,
    conv_weight,
    out_weight,
    feed_gain,
    gate_weight,
    up_weight,
    down_weight,
    lengths,
    cotangent,
):
    tok_rows = tokens.shape[0]
    features = tokens.shape[1]
    group_rows = tok_rows * lax.axis_size("seq")
    slot_size = min(SLOT_MAX, group_rows)
    position = lax.axis_index("seq") * tok_rows + jnp.arange(tok_rows, dtype=jnp.int32)
    in_slot = position % slot_size
    slot_index = position // slot_size
    slot_ids = jnp.arange(lengths.shape[1], dtype=jnp.int32)
    slot_length = jnp.sum(
        jnp.where(slot_index[:, None] == slot_ids[None, :], lengths[0][None, :], 0), axis=1
    )
    live_mask = (in_slot < slot_length).astype(jnp.float32)[:, None]
    tap_masks = [(in_slot >= 2 - tap_index).astype(jnp.float32)[:, None] for tap_index in range(3)]
    wide = (
        lax.all_gather(in_weight, "dp", axis=1, tiled=True),
        lax.all_gather(out_weight, "dp", axis=1, tiled=True),
        lax.all_gather(gate_weight, "dp", axis=1, tiled=True),
        lax.all_gather(up_weight, "dp", axis=1, tiled=True),
        lax.all_gather(down_weight, "dp", axis=1, tiled=True),
    )
    whole = (
        lax.all_gather(wide[0], "seq", axis=0, tiled=True),
        lax.all_gather(wide[1], "seq", axis=0, tiled=True),
        lax.all_gather(wide[2], "seq", axis=0, tiled=True),
        lax.all_gather(wide[3], "seq", axis=0, tiled=True),
        lax.all_gather(wide[4], "seq", axis=0, tiled=True),
        lax.all_gather(mixer_gain, "seq", axis=0, tiled=True),
        lax.all_gather(feed_gain, "seq", axis=0, tiled=True),
        lax.all_gather(conv_weight, "seq", axis=1, tiled=True),
    )
    weight_in, weight_out, weight_gate, weight_up, weight_down = (
        whole[0],
        whole[1],
        whole[2],
        whole[3],
        whole[4],
    )
    gain_one = whole[5].astype(jnp.float32)
    gain_two = whole[6].astype(jnp.float32)
    conv_taps = whole[7].astype(jnp.float32)
    residual = tokens.astype(jnp.float32)
    scale_one, normed = rms_forward(residual, gain_one)
    normed_one = normed.astype(jnp.bfloat16)
    projected = multiply(normed_one, weight_in)
    b_part = projected[:, :features]
    c_part = projected[:, features : 2 * features]
    x_part = projected[:, 2 * features :]
    mixed_in = (b_part * x_part).astype(jnp.bfloat16)
    carried = passed_along(mixed_in[tok_rows - 2 :], "seq", 1)
    extended = jnp.concatenate([carried, mixed_in], axis=0).astype(jnp.float32)
    conv_out = sum(
        (
            tap_masks[tap_index] * conv_taps[tap_index] * extended[tap_index : tap_index + tok_rows]
            for tap_index in range(3)
        )
    )
    gated = (c_part * conv_out).astype(jnp.bfloat16)
    hidden = residual + multiply(gated, weight_out)
    scale_two, normed_mid = rms_forward(hidden, gain_two)
    normed_two = normed_mid.astype(jnp.bfloat16)
    gate_val = multiply(normed_two, weight_gate)
    up_val = multiply(normed_two, weight_up)
    sigmoid_gate = jax.nn.sigmoid(gate_val)
    silu_gate = gate_val * sigmoid_gate
    activated = (silu_gate * up_val).astype(jnp.bfloat16)
    output = (live_mask * (hidden + multiply(activated, weight_down))).astype(jnp.bfloat16)
    wide_again = (
        lax.all_gather(in_weight, "dp", axis=1, tiled=True),
        lax.all_gather(out_weight, "dp", axis=1, tiled=True),
        lax.all_gather(gate_weight, "dp", axis=1, tiled=True),
        lax.all_gather(up_weight, "dp", axis=1, tiled=True),
        lax.all_gather(down_weight, "dp", axis=1, tiled=True),
    )
    whole_again = (
        lax.all_gather(wide_again[0], "seq", axis=0, tiled=True),
        lax.all_gather(wide_again[1], "seq", axis=0, tiled=True),
        lax.all_gather(wide_again[2], "seq", axis=0, tiled=True),
        lax.all_gather(wide_again[3], "seq", axis=0, tiled=True),
        lax.all_gather(wide_again[4], "seq", axis=0, tiled=True),
        lax.all_gather(mixer_gain, "seq", axis=0, tiled=True),
        lax.all_gather(feed_gain, "seq", axis=0, tiled=True),
        lax.all_gather(conv_weight, "seq", axis=1, tiled=True),
    )
    weight_in, weight_out, weight_gate, weight_up, weight_down = (
        whole_again[0],
        whole_again[1],
        whole_again[2],
        whole_again[3],
        whole_again[4],
    )
    gain_one = whole_again[5].astype(jnp.float32)
    gain_two = whole_again[6].astype(jnp.float32)
    conv_taps = whole_again[7].astype(jnp.float32)
    grad_final = (live_mask * cotangent.astype(jnp.float32)).astype(jnp.bfloat16)
    grad_down = outer_sum(activated, grad_final)
    grad_act = against(grad_final, weight_down)
    grad_gate = (grad_act * up_val * sigmoid_gate * (1.0 + gate_val * (1.0 - sigmoid_gate))).astype(
        jnp.bfloat16
    )
    grad_up = (grad_act * silu_gate).astype(jnp.bfloat16)
    grad_gate_w = outer_sum(normed_two, grad_gate)
    grad_up_w = outer_sum(normed_two, grad_up)
    grad_norm_two = against(grad_gate, weight_gate) + against(grad_up, weight_up)
    grad_from_norm, grad_gain_two = rms_backward(hidden, scale_two, gain_two, grad_norm_two)
    grad_hidden = grad_final.astype(jnp.float32) + grad_from_norm
    grad_branch = grad_hidden.astype(jnp.bfloat16)
    grad_out_w = outer_sum(gated, grad_branch)
    grad_gated = against(grad_branch, weight_out)
    grad_conv = grad_gated * c_part
    grad_c = grad_gated * conv_out
    grad_taps = [tap_masks[tap_index] * grad_conv for tap_index in range(3)]
    grad_conv_w = jnp.stack(
        [
            jnp.sum(grad_taps[tap_index] * extended[tap_index : tap_index + tok_rows], axis=0)
            for tap_index in range(3)
        ]
    )
    grad_extended = sum(
        (
            jnp.pad(
                grad_taps[tap_index] * conv_taps[tap_index], ((tap_index, 2 - tap_index), (0, 0))
            )
            for tap_index in range(3)
        )
    )
    returned = passed_along(grad_extended[:2], "seq", -1)
    grad_mixed = grad_extended[2:] + jnp.pad(returned, ((tok_rows - 2, 0), (0, 0)))
    grad_proj = jnp.concatenate([grad_mixed * x_part, grad_c, grad_mixed * b_part], axis=1).astype(
        jnp.bfloat16
    )
    grad_in_w = outer_sum(normed_one, grad_proj)
    grad_norm_one = against(grad_proj, weight_in)
    grad_from_first, grad_gain_one = rms_backward(residual, scale_one, gain_one, grad_norm_one)
    grad_tokens = (grad_hidden + grad_from_first).astype(jnp.bfloat16)
    small_sums = lax.psum((grad_gain_one, grad_gain_two, grad_conv_w), "dp")
    by_rows = (
        lax.psum_scatter(grad_in_w, "seq", scatter_dimension=0, tiled=True),
        lax.psum_scatter(grad_out_w, "seq", scatter_dimension=0, tiled=True),
        lax.psum_scatter(grad_gate_w, "seq", scatter_dimension=0, tiled=True),
        lax.psum_scatter(grad_up_w, "seq", scatter_dimension=0, tiled=True),
        lax.psum_scatter(grad_down, "seq", scatter_dimension=0, tiled=True),
        lax.psum_scatter(small_sums[0], "seq", scatter_dimension=0, tiled=True),
        lax.psum_scatter(small_sums[1], "seq", scatter_dimension=0, tiled=True),
        lax.psum_scatter(small_sums[2], "seq", scatter_dimension=1, tiled=True),
    )
    by_cols = (
        lax.psum_scatter(by_rows[0], "dp", scatter_dimension=1, tiled=True),
        lax.psum_scatter(by_rows[1], "dp", scatter_dimension=1, tiled=True),
        lax.psum_scatter(by_rows[2], "dp", scatter_dimension=1, tiled=True),
        lax.psum_scatter(by_rows[3], "dp", scatter_dimension=1, tiled=True),
        lax.psum_scatter(by_rows[4], "dp", scatter_dimension=1, tiled=True),
    )
    owned = (
        by_cols[0],
        by_cols[1],
        by_cols[2],
        by_cols[3],
        by_cols[4],
        by_rows[5],
        by_rows[6],
        by_rows[7],
    )
    return (
        output,
        grad_tokens,
        owned[5],
        owned[0],
        owned[7],
        owned[1],
        owned[6],
        owned[2],
        owned[3],
        owned[4],
    )


def solution(mesh):
    in_specs = (
        P(("dp", "seq"), None),
        P("seq"),
        P("seq", "dp"),
        P(None, "seq"),
        P("seq", "dp"),
        P("seq"),
        P("seq", "dp"),
        P("seq", "dp"),
        P("seq", "dp"),
        P("dp", None),
        P(("dp", "seq"), None),
    )
    out_specs = (
        P(("dp", "seq"), None),
        P(("dp", "seq"), None),
        P("seq"),
        P("seq", "dp"),
        P(None, "seq"),
        P("seq", "dp"),
        P("seq"),
        P("seq", "dp"),
        P("seq", "dp"),
        P("seq", "dp"),
    )
    return jax.shard_map(
        per_device, mesh=mesh, in_specs=in_specs, out_specs=out_specs, check_vma=False
    )
```

profile of v0, /device:TPU:0, one launch (start us, length us, event | category | flops | bytes accessed | tf_op | source)
XLA Modules:
  0.0 2159.6 jit_solution(14255080628207878739)
XLA Ops:
  31.2 19.0 all-gather.19.cloned.1.call-done
  50.3 19.1 all-gather.23.cloned.1.call-done
  69.5 20.5 all-gather
  90.6 16.7 all_gather.55
  107.7 62.9 %all-gather.11.cloned.1.call-done = bf16[1024,3072]{1,0:T(8,128)(2,1)} async-done(((bf16[128,3072]{1,0:T(8,128)(2,1)}), bf16[1024,3072]{1,0:T(8,128)(2,1)}) %all-gather.11.cloned.1.call-update) | async-done | bytes 6291472 | tf_op jit(solution)/shard_map/all_gather | solution.py:80
  179.2 17.7 all-gather.1
  199.6 20.6 all-gather.13.cloned.1.call-done
  225.1 133.8 %all-gather.17.cloned.1.call-done = bf16[1024,4608]{1,0:T(8,128)(2,1)} async-done(((bf16[128,4608]{1,0:T(8,128)(2,1)}), bf16[1024,4608]{1,0:T(8,128)(2,1)}) %all-gather.17.cloned.1.call-update) | async-done | bytes 9437200 | tf_op jit(solution)/shard_map/all_gather | solution.py:82
  369.9 127.4 %all-gather.21.cloned.1.call-done = bf16[1024,4608]{1,0:T(8,128)(2,1)} async-done(((bf16[128,4608]{1,0:T(8,128)(2,1)}), bf16[1024,4608]{1,0:T(8,128)(2,1)}) %all-gather.21.cloned.1.call-update) | async-done | bytes 9437200 | tf_op jit(solution)/shard_map/all_gather | solution.py:83
  508.4 127.3 %all-gather.25.cloned.1.call-done = bf16[4608,1024]{1,0:T(8,128)(2,1)} async-done(((bf16[576,1024]{1,0:T(8,128)(2,1)}), bf16[4608,1024]{1,0:T(8,128)(2,1)}) %all-gather.25.cloned.1.call-update) | async-done | bytes 9437200 | tf_op jit(solution)/shard_map/all_gather | solution.py:84
  635.8 17.9 multiply_convert_fusion
  698.9 11.9 fusion.35
  736.5 26.7 %reduce-scatter.18.cloned.1.call-done = f32[128,1024]{1,0:T(8,128)} async-done(((f32[1024,1024]{1,0:T(8,128)}), f32[128,1024]{1,0:T(8,128)}) %reduce-scatter.18.cloned.1.call-update) | async-done | bytes 524304 | tf_op jit(solution)/shard_map/reduce_scatter | solution.py:196
  763.3 211.0 %reduce-scatter.14.cloned.1.call-done = f32[128,3072]{1,0:T(8,128)} async-done(((f32[1024,3072]{1,0:T(8,128)}), f32[128,3072]{1,0:T(8,128)}) %reduce-scatter.14.cloned.1.call-update) | async-done | bytes 1572880 | tf_op jit(solution)/shard_map/reduce_scatter | solution.py:195
  974.3 316.8 %reduce-scatter.22.cloned.1.call-done = f32[128,4608]{1,0:T(8,128)} async-done(((f32[1024,4608]{1,0:T(8,128)}), f32[128,4608]{1,0:T(8,128)}) %reduce-scatter.22.cloned.1.call-update) | async-done | bytes 2359312 | tf_op jit(solution)/shard_map/reduce_scatter | solution.py:197
  1291.1 316.6 %reduce-scatter.26.cloned.1.call-done = f32[128,4608]{1,0:T(8,128)} async-done(((f32[1024,4608]{1,0:T(8,128)}), f32[128,4608]{1,0:T(8,128)}) %reduce-scatter.26.cloned.1.call-update) | async-done | bytes 2359312 | tf_op jit(solution)/shard_map/reduce_scatter | solution.py:198
  1607.8 316.9 %reduce-scatter.30.cloned.1.call-done = f32[576,1024]{1,0:T(8,128)} async-done(((f32[4608,1024]{1,0:T(8,128)}), f32[576,1024]{1,0:T(8,128)}) %reduce-scatter.30.cloned.1.call-update) | async-done | bytes 2359312 | tf_op jit(solution)/shard_map/reduce_scatter | solution.py:199
  1944.2 19.8 all-reduce.6
  1967.4 21.9 %reduce-scatter.34.cloned.1.call-done = f32[128,3]{1,0:T(8,128)} async-done(((f32[1024,3]{1,0:T(8,128)}), f32[128,3]{1,0:T(8,128)}) %reduce-scatter.34.cloned.1.call-update) | async-done | bytes 1552
  1996.4 16.5 reduce-scatter.20.cloned.1.call-done
  2012.9 31.4 %reduce-scatter.16.cloned.1.call-done = f32[128,768]{1,0:T(8,128)} async-done(((f32[128,3072]{1,0:T(8,128)}), f32[128,768]{1,0:T(8,128)}) %reduce-scatter.16.cloned.1.call-update) | async-done | bytes 393232 | tf_op jit(solution)/shard_map/reduce_scatter | solution.py:205
  2044.3 36.1 %reduce-scatter.24.cloned.1.call-done = f32[128,1152]{1,0:T(8,128)} async-done(((f32[128,4608]{1,0:T(8,128)}), f32[128,1152]{1,0:T(8,128)}) %reduce-scatter.24.cloned.1.call-update) | async-done | bytes 589840 | tf_op jit(solution)/shard_map/reduce_scatter | solution.py:207
  2080.3 36.2 %reduce-scatter.28.cloned.1.call-done = f32[128,1152]{1,0:T(8,128)} async-done(((f32[128,4608]{1,0:T(8,128)}), f32[128,1152]{1,0:T(8,128)}) %reduce-scatter.28.cloned.1.call-update) | async-done | bytes 589840 | tf_op jit(solution)/shard_map/reduce_scatter | solution.py:208
  2116.5 36.2 %reduce-scatter.32.cloned.1.call-done = f32[576,256]{1,0:T(8,128)} async-done(((f32[576,1024]{1,0:T(8,128)}), f32[576,256]{1,0:T(8,128)}) %reduce-scatter.32.cloned.1.call-update) | async-done | bytes 589840 | tf_op jit(solution)/shard_map/reduce_scatter | solution.py:209
  (143 shorter events, 162.8 us)
Async XLA Ops:
  7.2 24.0 %all-gather.15.cloned.1.call-start = ((), (), s32[]{:S(2)}) async-start(), calls=%async_computation.13 | async-start | bytes 1474560 | tf_op jit(solution)/shard_map/all_gather | solution.py:75
  7.9 42.3 %all-gather.19.cloned.1.call-start = ((), (), s32[]{:S(2)}) async-start(), calls=%async_computation.15 | async-start | bytes 1474560 | tf_op jit(solution)/shard_map/all_gather | solution.py:76
  8.7 60.7 %all-gather.23.cloned.1.call-start = ((), (), s32[]{:S(2)}) async-start(), calls=%async_computation.17 | async-start | bytes 1474560 | tf_op jit(solution)/shard_map/all_gather | solution.py:77
  9.4 161.2 %all-gather.11.cloned.1.call-start = ((), (), s32[]{:S(2)}) async-start(), calls=%async_computation.11 | async-start | bytes 7077888 | tf_op jit(solution)/shard_map/all_gather | solution.py:80
  21.2 86.2 %copy-start.3 = (bf16[512,1024]{1,0:T(8,128)(2,1)S(1)}, bf16[512,1024]{1,0:T(8,128)(2,1)}, u32[]{:S(2)}) copy-start(bf16[512,1024]{1,0:T(8,128)(2,1)} %param.11) | copy-start | bytes 3145732
  21.2 199.0 %all-gather.13.cloned.1.call-start = ((), (), s32[]{:S(2)}) async-start(), calls=%async_computation.12 | async-start | bytes 2359296 | tf_op jit(solution)/shard_map/all_gather | solution.py:81
  29.5 329.3 %all-gather.17.cloned.1.call-start = ((), (), s32[]{:S(2)}) async-start(), calls=%async_computation.14 | async-start | bytes 10616832 | tf_op jit(solution)/shard_map/all_gather | solution.py:82
  31.2 466.1 %all-gather.21.cloned.1.call-start = ((), (), s32[]{:S(2)}) async-start(), calls=%async_computation.16 | async-start | bytes 10616832 | tf_op jit(solution)/shard_map/all_gather | solution.py:83
  50.2 585.5 %all-gather.25.cloned.1.call-start = ((), (), s32[]{:S(2)}) async-start(), calls=%async_computation.18 | async-start | bytes 10616832 | tf_op jit(solution)/shard_map/all_gather | solution.py:84
  69.4 693.7 %reduce-scatter.18.cloned.1.call-start = ((), (), s32[]{:S(2)}) async-start(), calls=%async_computation.21 | async-start | bytes 4718592 | tf_op jit(solution)/shard_map/reduce_scatter | solution.py:196
  176.7 20.2 collective-permute-start
  676.8 297.5 %reduce-scatter.14.cloned.1.call-start = ((), (), s32[]{:S(2)}) async-start(), calls=%async_computation.19 | async-start | bytes 14155776 | tf_op jit(solution)/shard_map/reduce_scatter | solution.py:195
  683.7 6.0 collective-permute-start.1
  698.8 592.2 %reduce-scatter.22.cloned.1.call-start = ((), (), s32[]{:S(2)}) async-start(), calls=%async_computation.23 | async-start | bytes 21233664 | tf_op jit(solution)/shard_map/reduce_scatter | solution.py:197
  710.8 896.9 %reduce-scatter.26.cloned.1.call-start = ((), (), s32[]{:S(2)}) async-start(), calls=%async_computation.25 | async-start | bytes 21233664 | tf_op jit(solution)/shard_map/reduce_scatter | solution.py:198
  722.5 1202.2 %reduce-scatter.30.cloned.1.call-start = ((), (), s32[]{:S(2)}) async-start(), calls=%async_computation.27 | async-start | bytes 21233664 | tf_op jit(solution)/shard_map/reduce_scatter | solution.py:199
  735.3 1254.0 %reduce-scatter.34.cloned.1.call-start = ((), (), s32[]{:S(2)}) async-start(), calls=%async_computation.29 | async-start | bytes 589824
  736.4 1276.5 %reduce-scatter.20.cloned.1.call-start = ((), (), s32[]{:S(2)}) async-start(), calls=%async_computation.22 | async-start | bytes 655360 | tf_op jit(solution)/shard_map/reduce_scatter | solution.py:206
  763.2 1281.1 %reduce-scatter.16.cloned.1.call-start = ((), (), s32[]{:S(2)}) async-start(), calls=%async_computation.20 | async-start | bytes 1966080 | tf_op jit(solution)/shard_map/reduce_scatter | solution.py:205
  974.2 1106.1 %reduce-scatter.24.cloned.1.call-start = ((), (), s32[]{:S(2)}) async-start(), calls=%async_computation.24 | async-start | bytes 2949120 | tf_op jit(solution)/shard_map/reduce_scatter | solution.py:207
  1291.1 825.5 %reduce-scatter.28.cloned.1.call-start = ((), (), s32[]{:S(2)}) async-start(), calls=%async_computation.26 | async-start | bytes 2949120 | tf_op jit(solution)/shard_map/reduce_scatter | solution.py:208
  1607.7 317.0 %copy-start.24 = (u32[32]{0:T(128)S(1)}, u32[32]{0:T(128)}, u32[]{:S(2)}) copy-start(u32[32]{0:T(128)} %constant.64) | copy-start | bytes 388
  1607.7 318.2 %copy-start.9 = (f32[512,1024]{1,0:T(8,128)S(1)}, f32[512,1024]{1,0:T(8,128)}, u32[]{:S(2)}) copy-start(f32[512,1024]{1,0:T(8,128)} %copy-done.7) | copy-start | bytes 6291460
  1607.7 545.0 %reduce-scatter.32.cloned.1.call-start = ((), (), s32[]{:S(2)}) async-start(), calls=%async_computation.28 | async-start | bytes 2949120 | tf_op jit(solution)/shard_map/reduce_scatter | solution.py:209
  (24 other events, 288.4 us)
Sparse Core Ops, SparseCore 0:
  9.6 21.5 all-gather.14
  32.7 17.4 all-gather.18
  51.8 17.5 all-gather.22
  71.4 99.1 all-gather.10
  172.6 47.6 all-gather.12
  222.3 136.5 all-gather.16
  361.0 136.2 all-gather.20
  499.5 136.2 all-gather.24
  676.9 86.2 reduce-scatter.17
  767.0 207.1 reduce-scatter.13
  978.6 312.4 reduce-scatter.21
  1295.3 312.3 reduce-scatter.25
  1612.1 312.5 reduce-scatter.29
  1928.2 61.0 reduce-scatter.33
  1992.2 20.6 reduce-scatter.19
  2016.0 28.1 reduce-scatter.15
  2047.2 33.0 reduce-scatter.23
  2083.5 33.0 reduce-scatter.27
  2119.6 33.0 reduce-scatter.31
where the time goes:
time: 2160 us
  waiting for transfers between devices  1880 us (87%)
  matrix products  134 us (6%)
  blocking collectives  101 us (5%)
    reduce_scatter x1, waiting for transfers between devices, per_device(): lax.psum_scatter(grad_down, 'seq', scatter_dimension=0, tiled=True)  317 us
    reduce_scatter x1, waiting for transfers between devices, per_device(): lax.psum_scatter(grad_gate_w, 'seq', scatter_dimension=0, tiled=True)  317 us
    reduce_scatter x1, waiting for transfers between devices, per_device(): lax.psum_scatter(grad_up_w, 'seq', scatter_dimension=0, tiled=True)  317 us
    reduce_scatter x1, waiting for transfers between devices, per_device(): lax.psum_scatter(grad_in_w, 'seq', scatter_dimension=0, tiled=True)  211 us
    all_gather x1, waiting for transfers between devices, per_device(): lax.all_gather(wide[2], 'seq', axis=0, tiled=True)  134 us
    all_gather x1, waiting for transfers between devices, per_device(): lax.all_gather(wide[3], 'seq', axis=0, tiled=True)  127 us
    all_gather x1, waiting for transfers between devices, per_device(): lax.all_gather(wide[4], 'seq', axis=0, tiled=True)  127 us
    all_gather x1, waiting for transfers between devices, per_device(): lax.all_gather(wide[0], 'seq', axis=0, tiled=True)  62.9 us
  transfers between devices with their start and end apart: 21, of which 20 were waited for; matrix products, arithmetic and copies ran while one was open for 5% of the time, Pallas kernels for 0%

commit v1 on v0

v1 whole, which is shorter than its diff:
```python
import functools

import jax
import jax.numpy as jnp
from jax import lax
from jax.experimental import pallas as pl
from jax.experimental.pallas import tpu as pltpu
from jax.sharding import PartitionSpec as P

SLOT_MAX = 8192
HALO = 16
SMALL_ROWS = 16

norm_eps = 1e-05


def multiply(left_side, right_side):
    return jnp.dot(left_side, right_side, preferred_element_type=jnp.float32)


def against(left_side, right_side):
    return lax.dot_general(
        left_side, right_side, (((1,), (1,)), ((), ())), preferred_element_type=jnp.float32
    )


def outer_sum(left_side, right_side):
    return lax.dot_general(
        left_side, right_side, (((0,), (0,)), ((), ())), preferred_element_type=jnp.float32
    )


def rms_forward(values, gain_row):
    scales = lax.rsqrt(jnp.mean(values * values, axis=1, keepdims=True) + norm_eps)
    return (scales, values * scales * gain_row)


def rms_backward(values, scales, gain_row, grad_normed):
    weighted = grad_normed * gain_row
    grad_gain = jnp.sum(grad_normed * values * scales, axis=0)
    inner_mean = jnp.mean(weighted * values, axis=1, keepdims=True)
    return (scales * weighted - values * scales * scales * scales * inner_mean, grad_gain)


def swap(shard, step):
    axis, bit = step
    count = lax.axis_size(axis)
    return lax.ppermute(shard, axis, [(i, i ^ bit) for i in range(count)])


def exchange_gather(block, steps):
    stack = block[None]
    for step in steps[:-1]:
        stack = jnp.concatenate([stack, swap(stack, step)], axis=0)
    return [stack, swap(stack, steps[-1])]


def exchange_scatter(keep, send, steps):
    for step in reversed(steps):
        total = keep.astype(jnp.float32) + swap(send, step).astype(jnp.float32)
        half = total.shape[0] // 2
        if half:
            keep = total[:half].astype(jnp.bfloat16)
            send = total[half:].astype(jnp.bfloat16)
    return total[0]


def masks_at(position, steps):
    masks = {"dp": 0, "seq": 0}
    for place, (axis, bit) in enumerate(steps):
        masks[axis] = masks[axis] + ((position >> place) & 1) * bit
    return masks["dp"], masks["seq"]


def move_blocks(ids, sources, out_shapes, moves):
    def kernel(ids_ref, *refs):
        ins, outs, sems = refs[: len(sources)], refs[len(sources) : -1], refs[-1]
        own_dp, own_seq = ids_ref[0], ids_ref[1]
        for source, target, first, count, steps, views in moves:

            def start(position, carry):
                mask_dp, mask_seq = masks_at(position + first, steps)
                for view in views:
                    a, b = view(
                        ins[source],
                        outs[target],
                        position,
                        own_dp ^ mask_dp,
                        own_seq ^ mask_seq,
                    )
                    pltpu.make_async_copy(a, b, sems.at[target]).start()
                return carry

            lax.fori_loop(0, count, start, 0)
        for place, out in enumerate(outs):
            pltpu.make_async_copy(out, out, sems.at[place]).wait()

    return pl.pallas_call(
        kernel,
        out_shape=out_shapes,
        grid_spec=pltpu.PrefetchScalarGridSpec(
            num_scalar_prefetch=1,
            in_specs=[pl.BlockSpec(memory_space=pl.ANY)] * len(sources),
            out_specs=[pl.BlockSpec(memory_space=pl.ANY)] * len(out_shapes),
            scratch_shapes=[pltpu.SemaphoreType.DMA((len(out_shapes),))],
            grid=(),
        ),
    )(ids, *sources)


def tile_of(ref, row, rows, col, cols):
    return ref.at[pl.ds(pl.multiple_of(row * rows, rows), rows), pl.ds(pl.multiple_of(col * cols, cols), cols)]


def assembled(ids, stacks, steps, shape, view):
    sources, moves = [], []
    for piece, parts in enumerate(stacks):
        first = 0
        for part in parts:
            moves.append(
                (
                    len(sources),
                    0,
                    first,
                    part.shape[0],
                    steps[piece],
                    [lambda a, b, at, dp, seq, piece=piece: (a.at[at], view(b, piece, dp, seq))],
                )
            )
            sources.append(part)
            first += part.shape[0]
    return move_blocks(ids, sources, [jax.ShapeDtypeStruct(shape, jnp.bfloat16)], moves)[0]


def blocks_of(ids, whole, steps, block, view):
    shapes, moves = [], []
    for piece, order in enumerate(steps):
        half = 2 ** (len(order) - 1)
        for first in (0, half):
            moves.append(
                (
                    0,
                    len(shapes),
                    first,
                    half,
                    order,
                    [lambda a, b, at, dp, seq, piece=piece: (view(a, piece, dp, seq), b.at[at])],
                )
            )
            shapes.append(jax.ShapeDtypeStruct((half, *block), jnp.bfloat16))
    parts = move_blocks(ids, [whole], shapes, moves)
    return [(parts[2 * i], parts[2 * i + 1]) for i in range(len(steps))]


def dp_gather(block, steps):
    blocks = [block]
    for step in steps:
        blocks = blocks + [swap(b, step) for b in blocks]
    return blocks


def dp_scatter(parts, steps):
    for step in reversed(steps):
        half = len(parts) // 2
        parts = [
            keep + swap(send.astype(jnp.bfloat16), step).astype(jnp.float32)
            for keep, send in zip(parts[:half], parts[half:])
        ]
    return parts[0]


def bits_below(count):
    return [1 << i for i in range(count.bit_length() - 1)]


def per_device(
    tokens,
    mixer_gain,
    in_weight,
    conv_weight,
    out_weight,
    feed_gain,
    gate_weight,
    up_weight,
    down_weight,
    lengths,
    cotangent,
):
    n_dp, n_seq = lax.axis_size("dp"), lax.axis_size("seq")
    tok_rows, features = tokens.shape
    slot_size = min(SLOT_MAX, tok_rows * n_seq)
    own_dp, own_seq = lax.axis_index("dp"), lax.axis_index("seq")
    ids = jnp.stack([own_dp, own_seq]).astype(jnp.int32)

    seq_bits = bits_below(n_seq)
    along_y = seq_bits[: len(seq_bits) // 2]
    ys = [("seq", b) for b in reversed(along_y)]
    zs = [("seq", b) for b in reversed(seq_bits[len(along_y) :])]
    core = [("dp", 1)]
    xs = [("dp", b) for b in reversed(bits_below(n_dp)[1:])]
    in_orders = [zs + xs + ys + core, zs + ys + xs + core, zs[:1] + ys + xs + zs[1:] + core]
    out_order = zs + ys + xs + core
    gate_order, up_order, down_order = zs + ys, zs + ys, zs[:1] + ys + zs[1:]
    token_order = xs + core

    position = own_seq * tok_rows + jnp.arange(tok_rows, dtype=jnp.int32)
    in_slot = position % slot_size
    slot_index = position // slot_size
    slot_ids = jnp.arange(lengths.shape[1], dtype=jnp.int32)
    slot_length = jnp.sum(
        jnp.where(slot_index[:, None] == slot_ids[None, :], lengths[0][None, :], 0), axis=1
    )
    live_mask = (in_slot < slot_length).astype(jnp.float32)[:, None]
    tap_masks = [(in_slot >= 2 - tap_index).astype(jnp.float32)[:, None] for tap_index in range(3)]

    in_rows, in_cols = in_weight.shape[0], in_weight.shape[1] // 3
    out_rows, out_cols = out_weight.shape
    small = jnp.concatenate([mixer_gain[None], feed_gain[None], conv_weight], axis=0)
    small = jnp.pad(small, ((0, SMALL_ROWS - small.shape[0]), (0, out_cols - small.shape[1])))
    out_block = jnp.concatenate([out_weight, small], axis=0)
    before = lax.ppermute(
        tokens[tok_rows - HALO :], "seq", [(i, i + 1) for i in range(n_seq - 1)]
    )
    in_stacks = []
    for piece, order in enumerate(in_orders):
        shard = in_weight[:, piece * in_cols : (piece + 1) * in_cols]
        in_stacks.append(exchange_gather(shard, order))
    out_stacks = exchange_gather(out_block, out_order)

    def in_view(ref, piece, dp, seq):
        return tile_of(ref, seq, in_rows, dp * 3 + piece, in_cols)

    weight_in = assembled(ids, in_stacks, in_orders, (features, 3 * features), in_view)
    out_moves, first = [], 0
    for source, part in enumerate(out_stacks):
        out_moves.append(
            (
                source,
                0,
                first,
                part.shape[0],
                out_order,
                [
                    lambda a, b, at, dp, seq: (
                        a.at[at, pl.ds(0, out_rows)],
                        tile_of(b, seq, out_rows, dp, out_cols),
                    )
                ],
            )
        )
        out_moves.append(
            (
                source,
                1,
                first,
                part.shape[0],
                out_order,
                [
                    lambda a, b, at, dp, seq: (
                        a.at[at, pl.ds(out_rows, SMALL_ROWS)],
                        b.at[dp, seq],
                    )
                ],
            )
        )
        first += part.shape[0]
    weight_out, smalls = move_blocks(
        ids,
        out_stacks,
        [
            jax.ShapeDtypeStruct((features, features), jnp.bfloat16),
            jax.ShapeDtypeStruct((n_dp, n_seq, SMALL_ROWS, out_cols), jnp.bfloat16),
        ],
        out_moves,
    )
    smalls = smalls[0, :, :5, : mixer_gain.shape[0]].astype(jnp.float32)
    smalls = smalls.transpose(1, 0, 2).reshape(5, features)
    gain_one, gain_two, conv_taps = smalls[0], smalls[1], smalls[2:]

    ratio = n_seq // n_dp
    home = [
        (e * n_seq + s, (s // ratio) * n_seq + e * ratio + s % ratio)
        for e in range(n_dp)
        for s in range(n_seq)
    ]
    down_shard = lax.ppermute(down_weight, ("dp", "seq"), home)
    hidden_units = gate_weight.shape[1]
    gate_rows = gate_weight.shape[0]
    down_rows, down_cols = down_weight.shape
    gate_stacks = exchange_gather(gate_weight, gate_order)
    up_stacks = exchange_gather(up_weight, up_order)
    down_stacks = exchange_gather(down_shard, down_order)

    def gate_view(ref, piece, dp, seq):
        return ref.at[pl.ds(pl.multiple_of(seq * gate_rows, gate_rows), gate_rows)]

    def down_view(ref, piece, dp, seq):
        return tile_of(ref, seq % ratio, down_rows, seq // ratio, down_cols)

    wide = (features, hidden_units)
    weight_gate = assembled(ids, [gate_stacks], [gate_order], wide, gate_view)
    weight_up = assembled(ids, [up_stacks], [up_order], wide, gate_view)
    weight_down = assembled(ids, [down_stacks], [down_order], (hidden_units, features), down_view)

    residual = tokens.astype(jnp.float32)
    extended_rows = jnp.concatenate([before, tokens], axis=0).astype(jnp.float32)
    scale_ext, normed_ext = rms_forward(extended_rows, gain_one)
    normed_ext = normed_ext.astype(jnp.bfloat16)
    scale_one, normed_one = scale_ext[HALO:], normed_ext[HALO:]
    projected = multiply(normed_ext, weight_in)
    mixed_ext = projected[:, :features] * projected[:, 2 * features :]
    b_part = projected[HALO:, :features]
    c_part = projected[HALO:, features : 2 * features]
    x_part = projected[HALO:, 2 * features :]
    extended = mixed_ext[HALO - 2 :].astype(jnp.bfloat16).astype(jnp.float32)
    conv_out = sum(
        (
            tap_masks[tap_index] * conv_taps[tap_index] * extended[tap_index : tap_index + tok_rows]
            for tap_index in range(3)
        )
    )
    gated = (c_part * conv_out).astype(jnp.bfloat16)
    hidden = residual + multiply(gated, weight_out)
    scale_two, normed_mid = rms_forward(hidden, gain_two)
    normed_two = normed_mid.astype(jnp.bfloat16)

    grad_final = (live_mask * cotangent.astype(jnp.float32)).astype(jnp.bfloat16)
    final_all = jnp.concatenate(dp_gather(grad_final, token_order), axis=0)
    normed_all = jnp.concatenate(dp_gather(normed_two, token_order), axis=0)

    def split_rows(v):
        return [v[i * tok_rows : (i + 1) * tok_rows] for i in range(n_dp)]

    gate_val = multiply(normed_all, weight_gate)
    up_val = multiply(normed_all, weight_up)
    sigmoid_gate = jax.nn.sigmoid(gate_val)
    silu_gate = gate_val * sigmoid_gate
    activated = (silu_gate * up_val).astype(jnp.bfloat16)
    feed_out = dp_scatter(split_rows(multiply(activated, weight_down)), token_order)
    output = (live_mask * (hidden + feed_out)).astype(jnp.bfloat16)
    grad_down = outer_sum(activated, final_all).astype(jnp.bfloat16)
    grad_act = against(final_all, weight_down)
    grad_gate = (grad_act * up_val * sigmoid_gate * (1.0 + gate_val * (1.0 - sigmoid_gate))).astype(
        jnp.bfloat16
    )
    grad_up = (grad_act * silu_gate).astype(jnp.bfloat16)
    grad_norm_parts = against(grad_gate, weight_gate) + against(grad_up, weight_up)
    grad_norm_two = dp_scatter(split_rows(grad_norm_parts), token_order)
    grad_gate_w = outer_sum(normed_all, grad_gate).astype(jnp.bfloat16)
    grad_up_w = outer_sum(normed_all, grad_up).astype(jnp.bfloat16)

    def scattered(whole, order, block, view):
        ((keep, send),) = blocks_of(ids, whole, [order], block, view)
        return exchange_scatter(keep, send, order)

    own_down = scattered(grad_down, down_order, down_weight.shape, down_view)
    own_down = lax.ppermute(
        own_down.astype(jnp.bfloat16), ("dp", "seq"), [(b, a) for a, b in home]
    ).astype(jnp.float32)
    own_gate = scattered(grad_gate_w, gate_order, gate_weight.shape, gate_view)
    own_up = scattered(grad_up_w, up_order, up_weight.shape, gate_view)

    grad_from_norm, grad_gain_two = rms_backward(hidden, scale_two, gain_two, grad_norm_two)
    grad_hidden = grad_final.astype(jnp.float32) + grad_from_norm
    grad_branch = grad_hidden.astype(jnp.bfloat16)
    grad_out_w = outer_sum(gated, grad_branch).astype(jnp.bfloat16)

    def out_view(ref, piece, dp, seq):
        return tile_of(ref, seq, out_rows, dp, out_cols)

    own_out = scattered(grad_out_w, out_order, out_weight.shape, out_view)
    grad_gated = against(grad_branch, weight_out)
    grad_conv = grad_gated * c_part
    grad_c = grad_gated * conv_out
    grad_taps = [tap_masks[tap_index] * grad_conv for tap_index in range(3)]
    grad_conv_w = jnp.stack(
        [
            jnp.sum(grad_taps[tap_index] * extended[tap_index : tap_index + tok_rows], axis=0)
            for tap_index in range(3)
        ]
    )
    grad_extended = sum(
        (
            jnp.pad(
                grad_taps[tap_index] * conv_taps[tap_index], ((tap_index, 2 - tap_index), (0, 0))
            )
            for tap_index in range(3)
        )
    )
    returned = lax.ppermute(grad_extended[:2], "seq", [(i + 1, i) for i in range(n_seq - 1)])
    grad_mixed = grad_extended[2:] + jnp.pad(returned, ((tok_rows - 2, 0), (0, 0)))
    grad_proj = jnp.concatenate([grad_mixed * x_part, grad_c, grad_mixed * b_part], axis=1).astype(
        jnp.bfloat16
    )
    grad_in_w = outer_sum(normed_one, grad_proj).astype(jnp.bfloat16)
    in_parts = blocks_of(ids, grad_in_w, in_orders, (in_rows, in_cols), in_view)
    own_in = jnp.concatenate(
        [exchange_scatter(keep, send, order) for (keep, send), order in zip(in_parts, in_orders)],
        axis=1,
    )
    grad_norm_one = against(grad_proj, weight_in)
    grad_from_first, grad_gain_one = rms_backward(residual, scale_one, gain_one, grad_norm_one)
    grad_tokens = (grad_hidden + grad_from_first).astype(jnp.bfloat16)

    sums = jnp.concatenate([grad_gain_one[None], grad_gain_two[None], grad_conv_w], axis=0)
    sums = jnp.pad(sums, ((0, 3), (0, 0)))
    for step in zs + ys + xs + core:
        sums = sums + swap(sums, step)
    columns = mixer_gain.shape[0]
    own_sums = lax.dynamic_slice(sums, (0, own_seq * columns), (8, columns))
    return (
        output,
        grad_tokens,
        own_sums[0],
        own_in,
        own_sums[2:5],
        own_out,
        own_sums[1],
        own_gate,
        own_up,
        own_down,
    )


def solution(mesh):
    in_specs = (
        P(("dp", "seq"), None),
        P("seq"),
        P("seq", "dp"),
        P(None, "seq"),
        P("seq", "dp"),
        P("seq"),
        P("seq", "dp"),
        P("seq", "dp"),
        P("seq", "dp"),
        P("dp", None),
        P(("dp", "seq"), None),
    )
    out_specs = (
        P(("dp", "seq"), None),
        P(("dp", "seq"), None),
        P("seq"),
        P("seq", "dp"),
        P(None, "seq"),
        P("seq", "dp"),
        P("seq"),
        P("seq", "dp"),
        P("seq", "dp"),
        P("seq", "dp"),
    )
    return jax.shard_map(
        per_device, mesh=mesh, in_specs=in_specs, out_specs=out_specs, check_vma=False
    )
```

time: 2160 us -> 1440 us (0.67)
  waiting for transfers between devices: 1880 us -> 196 us
  Pallas kernels: 0 us -> 963 us
  blocking collectives: 101 us -> 0 us
  starting transfers between devices: 4.75 us -> 79.4 us
  other arithmetic: 12.5 us -> 52.5 us
    reduce_scatter x10 -> x0, waiting for transfers between devices: 1340 us -> none  [the longest x1 317 us: per_device(): lax.psum_scatter(grad_down, 'seq', scatter_dimension=0, tiled=True)]
    pallas_call x0 -> x10, Pallas kernels: none -> 963 us  [move_blocks(): pl.pallas_call(kernel, out_shape=out_shapes, grid_spec=pltpu.PrefetchScal...]
    all_gather x8 -> x0, waiting for transfers between devices: 512 us -> none  [the longest x1 134 us: per_device(): lax.all_gather(wide[2], 'seq', axis=0, tiled=True)]
    ppermute x2 -> x79, waiting for transfers between devices: 3.61 us -> 196 us  [the longest x75 191 us: swap(): return lax.ppermute(shard, axis, [(i, i ^ bit) for i in range(count)])]
    ppermute x2 -> x79, starting transfers between devices: 4 us -> 79.4 us  [the longest x75 71.6 us: swap(): return lax.ppermute(shard, axis, [(i, i ^ bit) for i in range(count)])]
    all_gather x5 -> x0, blocking collectives: 74.8 us -> none  [the longest x1 20.5 us: per_device(): lax.all_gather(mixer_gain, 'seq', axis=0, tiled=True)]
    unnamed x20 -> x0, waiting for transfers between devices: 24.2 us -> none
  transfers between devices with their start and end apart: 21 -> 79, of which waited for: 20 -> 33; matrix products, arithmetic and copies ran while one was open for 5% -> 10% of each run, Pallas kernels for 0% -> 62%
where the time goes in v1:
time: 1440 us
  Pallas kernels  963 us (67%)
  waiting for transfers between devices  196 us (14%)
  matrix products  124 us (9%)
  starting transfers between devices  79.4 us (6%)
  other arithmetic  52.5 us (4%)
  local copies, waits for them, and re-layouts  21.6 us (2%)
    pallas_call x10, Pallas kernels, move_blocks(): pl.pallas_call(kernel, out_shape=out_shapes, grid_spec=pltpu.PrefetchScal...  963 us
    ppermute x75, waiting for transfers between devices, swap(): return lax.ppermute(shard, axis, [(i, i ^ bit) for i in range(count)])  191 us
    ppermute x75, starting transfers between devices, swap(): return lax.ppermute(shard, axis, [(i, i ^ bit) for i in range(count)])  71.6 us
    dot_general x5, matrix products, multiply(): return jnp.dot(left_side, right_side, preferred_element_type=jnp.float32)  47.5 us
    dot_general x5, matrix products, against(): lax.dot_general(left_side, right_side, (((1,), (1,)), ((), ())), preferre...  38.4 us
    dot_general x5, matrix products, outer_sum(): lax.dot_general(left_side, right_side, (((0,), (0,)), ((), ())), preferre...  38.2 us
  transfers between devices with their start and end apart: 79, of which 33 were waited for; matrix products, arithmetic and copies ran while one was open for 10% of the time, Pallas kernels for 62%

profile of v1, /device:TPU:0, one launch (start us, length us, event | category | flops | bytes accessed | tf_op | source)
XLA Modules:
  0.0 1439.7 jit_solution(9584069394177020903)
XLA Ops:
  36.4 14.7 %collective-permute-done.12 = bf16[2,128,256]{2,1,0:T(8,128)(2,1)S(1)} collective-permute-done((bf16[2,128,256]{2,1,0:T(8,128)(2,1)S(1)}, bf16[2,128,256]{2,1,0:T(8,128)(2,1)S(1)}, u32[]{:S(2)}, u32[]{:S(2)}) %collective-permute-start.12) | collective-permute-done | bytes 131104 | tf_op jit(solution)/shard_map/ppermute | solution.py:48
  117.1 10.4 collective-permute-done.32
  137.9 192.4 %shard_map.187 = bf16[1024,3072]{1,0:T(8,128)(2,1)} custom-call(s32[2]{0:T(128)} %pad_add_fusion.2.ids_ref, bf16[16,128,256]{2,1,0:T(8,128)(2,1)} %copy-done.15, bf16[16,128,256]{2,1,0:T(8,128)(2,1)} %copy-done.31, bf16[16,128,256]{2,1,0:T(8,128)(2,1)} %constant_dynamic-update-slice_fusion.10.refs_2_, bf16[16,128,256]{2,1,0:T(8,128)(2,1)} %copy-done.34, ...), custom_call_target="tpu_custom_call" | custom-call | tf_op jit(solution)/shard_map/pallas_call | solution.py:98
  330.3 73.3 %shard_map.186 = (bf16[1024,1024]{1,0:T(8,128)(2,1)}, bf16[4,8,16,256]{3,2,1,0:T(8,128)(2,1)}) custom-call(s32[2]{0:T(128)} %pad_add_fusion.2.ids_ref, bf16[16,144,256]{2,1,0:T(8,128)(2,1)} %copy-done.12, bf16[16,144,256]{2,1,0:T(8,128)(2,1)} %collective-permute-done.5.refs_1_), custom_call_target="tpu_custom_call" | custom-call | tf_op jit(solution)/shard_map/pallas_call | solution.py:98
  420.3 22.5 %collective-permute-done.21 = bf16[512,1024]{1,0:T(8,128)(2,1)} collective-permute-done((bf16[512,1024]{1,0:T(8,128)(2,1)S(1)}, bf16[512,1024]{1,0:T(8,128)(2,1)}, u32[]{:S(2)}, u32[]{:S(2)}) %collective-permute-start.21) | collective-permute-done | bytes 1048608 | tf_op jit(solution)/shard_map/ppermute | solution.py:48
  443.4 73.2 %shard_map.189 = bf16[1024,1152]{1,0:T(8,128)(2,1)} custom-call(s32[2]{0:T(128)} %pad_add_fusion.2.ids_ref, bf16[4,128,1152]{2,1,0:T(8,128)(2,1)} %pad_maximum_fusion.6.refs_0_, bf16[4,128,1152]{2,1,0:T(8,128)(2,1)} %collective-permute-done.29.refs_1_), custom_call_target="tpu_custom_call" | custom-call | tf_op jit(solution)/shard_map/pallas_call | solution.py:98
  516.7 73.2 %shard_map.188 = bf16[1024,1152]{1,0:T(8,128)(2,1)} custom-call(s32[2]{0:T(128)} %pad_add_fusion.2.ids_ref, bf16[4,128,1152]{2,1,0:T(8,128)(2,1)} %pad_maximum_fusion.5.refs_0_, bf16[4,128,1152]{2,1,0:T(8,128)(2,1)} %collective-permute-done.26.refs_1_), custom_call_target="tpu_custom_call" | custom-call | tf_op jit(solution)/shard_map/pallas_call | solution.py:98
  589.9 73.3 %shard_map.190 = bf16[1152,1024]{1,0:T(8,128)(2,1)} custom-call(s32[2]{0:T(128)} %pad_add_fusion.2.ids_ref, bf16[4,576,256]{2,1,0:T(8,128)(2,1)} %pad_maximum_fusion.7.refs_0_, bf16[4,576,256]{2,1,0:T(8,128)(2,1)} %collective-permute-done.33.refs_1_), custom_call_target="tpu_custom_call" | custom-call | tf_op jit(solution)/shard_map/pallas_call | solution.py:98
  663.2 12.4 fusion.26
  675.7 11.2 fusion.49
  686.9 18.3 %multiply_convert_fusion.1 = (bf16[2048,1152]{1,0:T(8,128)(2,1)}, bf16[2048,1152]{1,0:T(8,128)(2,1)}, bf16[2048,1152]{1,0:T(8,128)(2,1)}) fusion(f32[2048,1152]{1,0:T(8,128)} %fusion.26, f32[2048,1152]{1,0:T(8,128)} %fusion.49, bf16[1024,1152]{1,0:T(8,128)(2,1)} %shard_map.188, bf16[512,1024]{1,0:T(8,128)(2,1)} %collective-permute-done.23, ...), kind=kOutput, calls=%fused_computation.1 | convolution fusion | flops 4884004864 | bytes 39583744 | tf_op jit(solution)/shard_map/dot_general | solution.py:18
  705.2 11.0 fusion.56
  724.2 73.3 %shard_map.195 = (bf16[4,576,256]{2,1,0:T(8,128)(2,1)}, bf16[4,576,256]{2,1,0:T(8,128)(2,1)}) custom-call(s32[2]{0:T(128)} %pad_add_fusion.2.ids_ref, bf16[1152,1024]{1,0:T(8,128)(2,1)} %convolution_convert_fusion.1.refs_0_), custom_call_target="tpu_custom_call" | custom-call | tf_op jit(solution)/shard_map/pallas_call | solution.py:98
  797.8 9.9 convolution_convert_fusion.3.refs_0_
  807.7 73.3 %shard_map.193 = (bf16[4,128,1152]{2,1,0:T(8,128)(2,1)}, bf16[4,128,1152]{2,1,0:T(8,128)(2,1)}) custom-call(s32[2]{0:T(128)} %pad_add_fusion.2.ids_ref, bf16[1024,1152]{1,0:T(8,128)(2,1)} %convolution_convert_fusion.3.refs_0_), custom_call_target="tpu_custom_call" | custom-call | tf_op jit(solution)/shard_map/pallas_call | solution.py:98
  890.6 10.3 fusion.55
  913.6 73.3 %shard_map.194 = (bf16[4,128,1152]{2,1,0:T(8,128)(2,1)}, bf16[4,128,1152]{2,1,0:T(8,128)(2,1)}) custom-call(s32[2]{0:T(128)} %pad_add_fusion.2.ids_ref, bf16[1024,1152]{1,0:T(8,128)(2,1)} %convolution_convert_fusion.2.refs_0_), custom_call_target="tpu_custom_call" | custom-call | tf_op jit(solution)/shard_map/pallas_call | solution.py:98
  996.7 19.2 %collective-permute-done.72 = bf16[4,128,1152]{2,1,0:T(8,128)(2,1)S(1)} collective-permute-done((bf16[4,128,1152]{2,1,0:T(8,128)(2,1)}, bf16[4,128,1152]{2,1,0:T(8,128)(2,1)S(1)}, u32[]{:S(2)}, u32[]{:S(2)}) %collective-permute-start.72) | collective-permute-done | bytes 1179680 | tf_op jit(solution)/shard_map/ppermute | solution.py:48
  1018.0 10.1 collective-permute-done.76
  1033.7 15.8 %collective-permute-done.73 = bf16[2,128,1152]{2,1,0:T(8,128)(2,1)S(1)} collective-permute-done((bf16[2,128,1152]{2,1,0:T(8,128)(2,1)S(1)}, bf16[2,128,1152]{2,1,0:T(8,128)(2,1)S(1)}, u32[]{:S(2)}, u32[]{:S(2)}) %collective-permute-start.73) | collective-permute-done | bytes 589856 | tf_op jit(solution)/shard_map/ppermute | solution.py:48
  1053.0 11.5 collective-permute-done.71
  1106.5 65.6 %shard_map.192 = (bf16[16,128,256]{2,1,0:T(8,128)(2,1)}, bf16[16,128,256]{2,1,0:T(8,128)(2,1)}) custom-call(s32[2]{0:T(128)} %pad_add_fusion.2.ids_ref, bf16[1024,1024]{1,0:T(8,128)(2,1)} %convolution_convert_fusion.4.refs_0_), custom_call_target="tpu_custom_call" | custom-call | tf_op jit(solution)/shard_map/pallas_call | solution.py:98
  1183.2 192.4 %shard_map.191 = (bf16[16,128,256]{2,1,0:T(8,128)(2,1)}, bf16[16,128,256]{2,1,0:T(8,128)(2,1)}, bf16[16,128,256]{2,1,0:T(8,128)(2,1)}, bf16[16,128,256]{2,1,0:T(...) custom-call(s32[2]{0:T(128)} %pad_add_fusion.2.ids_ref, ...), custom_call_target="tpu_custom_call" | custom-call | tf_op jit(solution)/shard_map/pallas_call | solution.py:98
  1393.0 10.3 collective-permute-done.65
  (430 shorter events, 285.5 us)
Async XLA Ops:
  10.8 53.7 %collective-permute-start.24 = (bf16[1,128,1152]{2,1,0:T(8,128)(2,1)}, bf16[1,128,1152]{2,1,0:T(8,128)(2,1)}, u32[]{:S(2)}, u32[]{:S(2)}) collective-permute-start(bf16[1,128,1152]{2,1,0:T(8,128)(2,1)} %bitcast.83), channel_id=1, source_target_pairs={{0,4},{1,5},{2,6},{3,7},{4,0},{5,1},{6,2},{7,3},{8,12},{9,13},{10,... | collective-permute-start | bytes 884744 | tf_op jit(solution)/shard_map/ppermute | solution.py:48
  27.0 35.7 %collective-permute-start.27 = (bf16[1,128,1152]{2,1,0:T(8,128)(2,1)S(1)}, bf16[1,128,1152]{2,1,0:T(8,128)(2,1)S(1)}, u32[]{:S(2)}, u32[]{:S(2)}) collective-permute-start(bf16[1,128,1152]{2,1,0:T(8,128)(2,1)S(1)} %bitcast.86), channel_id=1, source_target_pairs={{0,4},{1,5},{2,6},{3,7},{4,0},{5,1},{6,2},{7,3},{8,12},{9,13},{10,... | collective-permute-start | bytes 884744 | tf_op jit(solution)/shard_map/ppermute | solution.py:48
  27.9 52.6 %collective-permute-start.30 = (bf16[576,256]{1,0:T(8,128)(2,1)S(1)}, bf16[576,256]{1,0:T(8,128)(2,1)S(1)}, u32[]{:S(2)}, u32[]{:S(2)}) collective-permute-start(bf16[576,256]{1,0:T(8,128)(2,1)S(1)} %copy-done.57), channel_id=1, source_target_pairs={{0,0},{1,1},{2,8},{3,9},{4,16},{5,17},{6,24},{7,25},{8,2},{9,3},{1... | collective-permute-start | bytes 884744 | tf_op jit(solution)/shard_map/ppermute | solution.py:286
  105.0 225.3 %collective-permute-start.5 = (bf16[16,144,256]{2,1,0:T(8,128)(2,1)S(1)}, bf16[16,144,256]{2,1,0:T(8,128)(2,1)}, u32[]{:S(2)}, u32[]{:S(2)}) collective-permute-start(bf16[16,144,256]{2,1,0:T(8,128)(2,1)S(1)} %constant_dynamic-update-slice_fusion.refs_0_), channel_id=1, source_target_pairs={{0,8},{8,0},{16,24},{24,16},{1,9},{9,1},{17,25},{25,17},{2,10},{10... | collective-permute-start | bytes 3538952 | tf_op jit(solution)/shard_map/ppermute | solution.py:48
  127.5 292.2 %collective-permute-start.37 = (bf16[512,1024]{1,0:T(8,128)(2,1)}, bf16[512,1024]{1,0:T(8,128)(2,1)}, u32[]{:S(2)}, u32[]{:S(2)}) collective-permute-start(bf16[512,1024]{1,0:T(8,128)(2,1)} %multiply_convert_fusion.4), channel_id=1, source_target_pairs={{0,16},{8,24},{16,0},{24,8},{1,17},{9,25},{17,1},{25,9},{2,18},{10... | collective-permute-start | bytes 3145736 | tf_op jit(solution)/shard_map/ppermute | solution.py:48
  129.4 290.3 %collective-permute-start.29 = (bf16[4,128,1152]{2,1,0:T(8,128)(2,1)}, bf16[4,128,1152]{2,1,0:T(8,128)(2,1)}, u32[]{:S(2)}, u32[]{:S(2)}) collective-permute-start(bf16[4,128,1152]{2,1,0:T(8,128)(2,1)} %pad_maximum_fusion.6.refs_0_), channel_id=1, source_target_pairs={{0,1},{1,0},{2,3},{3,2},{4,5},{5,4},{6,7},{7,6},{8,9},{9,8},{10,11... | collective-permute-start | bytes 3538952 | tf_op jit(solution)/shard_map/ppermute | solution.py:48
  131.2 289.0 %collective-permute-start.26 = (bf16[4,128,1152]{2,1,0:T(8,128)(2,1)}, bf16[4,128,1152]{2,1,0:T(8,128)(2,1)}, u32[]{:S(2)}, u32[]{:S(2)}) collective-permute-start(bf16[4,128,1152]{2,1,0:T(8,128)(2,1)} %pad_maximum_fusion.5.refs_0_), channel_id=1, source_target_pairs={{0,1},{1,0},{2,3},{3,2},{4,5},{5,4},{6,7},{7,6},{8,9},{9,8},{10,11... | collective-permute-start | bytes 3538952 | tf_op jit(solution)/shard_map/ppermute | solution.py:48
  133.1 456.8 %collective-permute-start.33 = (bf16[4,576,256]{2,1,0:T(8,128)(2,1)}, bf16[4,576,256]{2,1,0:T(8,128)(2,1)}, u32[]{:S(2)}, u32[]{:S(2)}) collective-permute-start(bf16[4,576,256]{2,1,0:T(8,128)(2,1)} %pad_maximum_fusion.7.refs_0_), channel_id=1, source_target_pairs={{0,2},{1,3},{2,0},{3,1},{4,6},{5,7},{6,4},{7,5},{8,10},{9,11},{10,... | collective-permute-start | bytes 3538952 | tf_op jit(solution)/shard_map/ppermute | solution.py:48
  419.7 243.5 %collective-permute-start.38 = (bf16[512,1024]{1,0:T(8,128)(2,1)}, bf16[512,1024]{1,0:T(8,128)(2,1)}, u32[]{:S(2)}, u32[]{:S(2)}) collective-permute-start(bf16[512,1024]{1,0:T(8,128)(2,1)} %multiply_convert_fusion.4), channel_id=1, source_target_pairs={{0,8},{8,0},{16,24},{24,16},{1,9},{9,1},{17,25},{25,17},{2,10},{10... | collective-permute-start | bytes 3145736 | tf_op jit(solution)/shard_map/ppermute | solution.py:48
  419.7 243.5 %collective-permute-start.39 = (bf16[512,1024]{1,0:T(8,128)(2,1)}, bf16[512,1024]{1,0:T(8,128)(2,1)}, u32[]{:S(2)}, u32[]{:S(2)}) collective-permute-start(bf16[512,1024]{1,0:T(8,128)(2,1)} %collective-permute-done.37), channel_id=1, source_target_pairs={{0,8},{8,0},{16,24},{24,16},{1,9},{9,1},{17,25},{25,17},{2,10},{10... | collective-permute-start | bytes 3145736 | tf_op jit(solution)/shard_map/ppermute | solution.py:48
  420.2 255.5 %collective-permute-start.22 = (bf16[512,1024]{1,0:T(8,128)(2,1)S(1)}, bf16[512,1024]{1,0:T(8,128)(2,1)}, u32[]{:S(2)}, u32[]{:S(2)}) collective-permute-start(bf16[512,1024]{1,0:T(8,128)(2,1)S(1)} %multiply_convert_fusion.5), channel_id=1, source_target_pairs={{0,8},{8,0},{16,24},{24,16},{1,9},{9,1},{17,25},{25,17},{2,10},{10... | collective-permute-start | bytes 3145736 | tf_op jit(solution)/shard_map/ppermute | solution.py:48
  442.8 232.9 %collective-permute-start.23 = (bf16[512,1024]{1,0:T(8,128)(2,1)}, bf16[512,1024]{1,0:T(8,128)(2,1)}, u32[]{:S(2)}, u32[]{:S(2)}) collective-permute-start(bf16[512,1024]{1,0:T(8,128)(2,1)} %collective-permute-done.21), channel_id=1, source_target_pairs={{0,8},{8,0},{16,24},{24,16},{1,9},{9,1},{17,25},{25,17},{2,10},{10... | collective-permute-start | bytes 3145736 | tf_op jit(solution)/shard_map/ppermute | solution.py:48
  797.4 195.5 %collective-permute-start.75 = (bf16[4,576,256]{2,1,0:T(8,128)(2,1)}, bf16[4,576,256]{2,1,0:T(8,128)(2,1)}, u32[]{:S(2)}, u32[]{:S(2)}) collective-permute-start(bf16[4,576,256]{2,1,0:T(8,128)(2,1)} %get-tuple-element.41), channel_id=1, source_target_pairs={{0,2},{1,3},{2,0},{3,1},{4,6},{5,7},{6,4},{7,5},{8,10},{9,11},{10,... | collective-permute-start | bytes 3538952 | tf_op jit(solution)/shard_map/ppermute | solution.py:48
  881.0 114.1 %collective-permute-start.69 = (bf16[4,128,1152]{2,1,0:T(8,128)(2,1)}, bf16[4,128,1152]{2,1,0:T(8,128)(2,1)S(1)}, u32[]{:S(2)}, u32[]{:S(2)}) collective-permute-start(bf16[4,128,1152]{2,1,0:T(8,128)(2,1)} %get-tuple-element.37), channel_id=1, source_target_pairs={{0,1},{1,0},{2,3},{3,2},{4,5},{5,4},{6,7},{7,6},{8,9},{9,8},{10,11... | collective-permute-start | bytes 3538952 | tf_op jit(solution)/shard_map/ppermute | solution.py:48
  902.4 85.4 %collective-permute-start.41 = (bf16[512,1024]{1,0:T(8,128)(2,1)}, bf16[512,1024]{1,0:T(8,128)(2,1)}, u32[]{:S(2)}, u32[]{:S(2)}) collective-permute-start(bf16[512,1024]{1,0:T(8,128)(2,1)} %get-tuple-element.60), channel_id=1, source_target_pairs={{0,8},{8,0},{16,24},{24,16},{1,9},{9,1},{17,25},{25,17},{2,10},{10... | collective-permute-start | bytes 3145736 | tf_op jit(solution)/shard_map/ppermute | solution.py:48
  905.3 84.9 %collective-permute-start.35 = (bf16[512,1024]{1,0:T(8,128)(2,1)}, bf16[512,1024]{1,0:T(8,128)(2,1)}, u32[]{:S(2)}, u32[]{:S(2)}) collective-permute-start(bf16[512,1024]{1,0:T(8,128)(2,1)} %get-tuple-element.62), channel_id=1, source_target_pairs={{0,8},{8,0},{16,24},{24,16},{1,9},{9,1},{17,25},{25,17},{2,10},{10... | collective-permute-start | bytes 3145736 | tf_op jit(solution)/shard_map/ppermute | solution.py:48
  987.8 77.6 %collective-permute-start.40 = (bf16[512,1024]{1,0:T(8,128)(2,1)}, bf16[512,1024]{1,0:T(8,128)(2,1)S(1)}, u32[]{:S(2)}, u32[]{:S(2)}) collective-permute-start(bf16[512,1024]{1,0:T(8,128)(2,1)} %get-tuple-element.59), channel_id=1, source_target_pairs={{0,8},{8,0},{16,24},{24,16},{1,9},{9,1},{17,25},{25,17},{2,10},{10... | collective-permute-start | bytes 3145736 | tf_op jit(solution)/shard_map/ppermute | solution.py:48
  990.3 77.6 %collective-permute-start.34 = (bf16[512,1024]{1,0:T(8,128)(2,1)S(1)}, bf16[512,1024]{1,0:T(8,128)(2,1)S(1)}, u32[]{:S(2)}, u32[]{:S(2)}) collective-permute-start(bf16[512,1024]{1,0:T(8,128)(2,1)S(1)} %copy-done.39), channel_id=1, source_target_pairs={{0,8},{8,0},{16,24},{24,16},{1,9},{9,1},{17,25},{25,17},{2,10},{10... | collective-permute-start | bytes 3145736 | tf_op jit(solution)/shard_map/ppermute | solution.py:48
  993.0 73.9 %collective-permute-start.42 = (bf16[512,1024]{1,0:T(8,128)(2,1)S(1)}, bf16[512,1024]{1,0:T(8,128)(2,1)S(1)}, u32[]{:S(2)}, u32[]{:S(2)}) collective-permute-start(bf16[512,1024]{1,0:T(8,128)(2,1)S(1)} %fusion.16), channel_id=1, source_target_pairs={{0,16},{8,24},{16,0},{24,8},{1,17},{9,25},{17,1},{25,9},{2,18},{10... | collective-permute-start | bytes 3145736 | tf_op jit(solution)/shard_map/ppermute | solution.py:48
  1064.5 33.5 %collective-permute-start.74 = (bf16[1,128,1152]{2,1,0:T(8,128)(2,1)}, bf16[1,128,1152]{2,1,0:T(8,128)(2,1)}, u32[]{:S(2)}, u32[]{:S(2)}) collective-permute-start(bf16[1,128,1152]{2,1,0:T(8,128)(2,1)} %slice.442), channel_id=1, source_target_pairs={{0,4},{1,5},{2,6},{3,7},{4,0},{5,1},{6,2},{7,3},{8,12},{9,13},{10,... | collective-permute-start | bytes 884744 | tf_op jit(solution)/shard_map/ppermute | solution.py:48
  1065.4 319.5 %collective-permute-start.78 = (bf16[576,256]{1,0:T(8,128)(2,1)S(1)}, bf16[576,256]{1,0:T(8,128)(2,1)}, u32[]{:S(2)}, u32[]{:S(2)}) collective-permute-start(bf16[576,256]{1,0:T(8,128)(2,1)S(1)} %fusion.30), channel_id=1, source_target_pairs={{0,0},{1,1},{8,2},{9,3},{16,4},{17,5},{24,6},{25,7},{2,8},{3,9},{1... | collective-permute-start | bytes 884744 | tf_op jit(solution)/shard_map/ppermute | solution.py:357
  1099.9 72.3 %collective-permute-start.45 = (f32[8,1024]{1,0:T(8,128)S(1)}, f32[8,1024]{1,0:T(8,128)S(1)}, u32[]{:S(2)}, u32[]{:S(2)}) collective-permute-start(f32[8,1024]{1,0:T(8,128)S(1)} %pad_add_fusion.3), channel_id=1, source_target_pairs={{0,2},{1,3},{2,0},{3,1},{4,6},{5,7},{6,4},{7,5},{8,10},{9,11},{10,... | collective-permute-start | bytes 98312 | tf_op jit(solution)/shard_map/ppermute | solution.py:48
  1172.1 214.6 %collective-permute-start.64 = (bf16[16,128,256]{2,1,0:T(8,128)(2,1)}, bf16[16,128,256]{2,1,0:T(8,128)(2,1)}, u32[]{:S(2)}, u32[]{:S(2)}) collective-permute-start(bf16[16,128,256]{2,1,0:T(8,128)(2,1)} %get-tuple-element.35), channel_id=1, source_target_pairs={{0,8},{8,0},{16,24},{24,16},{1,9},{9,1},{17,25},{25,17},{2,10},{10... | collective-permute-start | bytes 3145736 | tf_op jit(solution)/shard_map/ppermute | solution.py:48
  1172.2 203.6 %collective-permute-start.46 = (f32[8,1024]{1,0:T(8,128)S(1)}, f32[8,1024]{1,0:T(8,128)S(1)}, u32[]{:S(2)}, u32[]{:S(2)}) collective-permute-start(f32[8,1024]{1,0:T(8,128)S(1)} %add.272), channel_id=1, source_target_pairs={{0,1},{1,0},{2,3},{3,2},{4,5},{5,4},{6,7},{7,6},{8,9},{9,8},{10,11... | collective-permute-start | bytes 98312 | tf_op jit(solution)/shard_map/ppermute | solution.py:48
  (123 other events, 1921.1 us)

commit v2 on v1

--- a/solution.py
+++ b/solution.py
@@ -10,6 +10,7 @@
 SLOT_MAX = 8192
 HALO = 16
 SMALL_ROWS = 16
+VMEM_BYTES = 16 << 20
 
 norm_eps = 1e-05
 
@@ -72,7 +73,7 @@
     return masks["dp"], masks["seq"]
 
 
-def move_blocks(ids, sources, out_shapes, moves):
+def move_blocks(ids, sources, out_shapes, moves, into_vmem):
     def kernel(ids_ref, *refs):
         ins, outs, sems = refs[: len(sources)], refs[len(sources) : -1], refs[-1]
         own_dp, own_seq = ids_ref[0], ids_ref[1]
@@ -100,11 +101,12 @@
         out_shape=out_shapes,
         grid_spec=pltpu.PrefetchScalarGridSpec(
             num_scalar_prefetch=1,
-            in_specs=[pl.BlockSpec(memory_space=pl.ANY)] * len(sources),
-            out_specs=[pl.BlockSpec(memory_space=pl.ANY)] * len(out_shapes),
+            in_specs=[pl.BlockSpec(memory_space=pl.ANY if into_vmem else pltpu.VMEM)] * len(sources),
+            out_specs=[pl.BlockSpec(memory_space=pltpu.VMEM if into_vmem else pl.ANY)] * len(out_shapes),
             scratch_shapes=[pltpu.SemaphoreType.DMA((len(out_shapes),))],
             grid=(),
         ),
+        compiler_params=pltpu.CompilerParams(vmem_limit_bytes=VMEM_BYTES),
     )(ids, *sources)
 
 
@@ -129,7 +131,7 @@
             )
             sources.append(part)
             first += part.shape[0]
-    return move_blocks(ids, sources, [jax.ShapeDtypeStruct(shape, jnp.bfloat16)], moves)[0]
+    return move_blocks(ids, sources, [jax.ShapeDtypeStruct(shape, jnp.bfloat16)], moves, True)[0]
 
 
 def blocks_of(ids, whole, steps, block, view):
@@ -148,7 +150,7 @@
                 )
             )
             shapes.append(jax.ShapeDtypeStruct((half, *block), jnp.bfloat16))
-    parts = move_blocks(ids, [whole], shapes, moves)
+    parts = move_blocks(ids, [whole], shapes, moves, False)
     return [(parts[2 * i], parts[2 * i + 1]) for i in range(len(steps))]
 
 
@@ -272,6 +274,7 @@
             jax.ShapeDtypeStruct((n_dp, n_seq, SMALL_ROWS, out_cols), jnp.bfloat16),
         ],
         out_moves,
+        True,
     )
     smalls = smalls[0, :, :5, : mixer_gain.shape[0]].astype(jnp.float32)
     smalls = smalls.transpose(1, 0, 2).reshape(5, features)

time: 1440 us -> 505 us (0.35)
  Pallas kernels: 963 us -> 17.9 us
  other arithmetic: 52.5 us -> 32.5 us
  starting transfers between devices: 79.4 us -> 94.9 us
    pallas_call x10, Pallas kernels: 963 us -> 17.9 us  [move_blocks(): pl.pallas_call(kernel, out_shape=out_shapes, grid_spec=pltpu.PrefetchScal...]
    ppermute x75, starting transfers between devices: 71.6 us -> 88.6 us  [swap(): return lax.ppermute(shard, axis, [(i, i ^ bit) for i in range(count)])]
  transfers between devices with their start and end apart: 79 -> 79, of which waited for: 33 -> 33; matrix products, arithmetic and copies ran while one was open for 10% -> 24% of each run, Pallas kernels for 62% -> 3%
where the time goes in v2:
time: 505 us; the launch traced here: 496 us
  waiting for transfers between devices  200 us (40%)
  matrix products  119 us (24%)
  starting transfers between devices  94.9 us (19%)
  other arithmetic  32.5 us (6%)
  local copies, waits for them, and re-layouts  28 us (6%)
  Pallas kernels  17.9 us (4%)
    ppermute x75, waiting for transfers between devices, swap(): return lax.ppermute(shard, axis, [(i, i ^ bit) for i in range(count)])  197 us
    ppermute x75, starting transfers between devices, swap(): return lax.ppermute(shard, axis, [(i, i ^ bit) for i in range(count)])  88.6 us
    dot_general x5, matrix products, multiply(): return jnp.dot(left_side, right_side, preferred_element_type=jnp.float32)  45.7 us
    dot_general x5, matrix products, against(): lax.dot_general(left_side, right_side, (((1,), (1,)), ((), ())), preferre...  43 us
    dot_general x5, matrix products, outer_sum(): lax.dot_general(left_side, right_side, (((0,), (0,)), ((), ())), preferre...  30.2 us
    pallas_call x10, Pallas kernels, move_blocks(): pl.pallas_call(kernel, out_shape=out_shapes, grid_spec=pltpu.PrefetchScal...  17.9 us
    unnamed x141, local copies, waits for them, and re-layouts  17.5 us
  transfers between devices with their start and end apart: 79, of which 33 were waited for; matrix products, arithmetic and copies ran while one was open for 24% of the time, Pallas kernels for 3%

profile of v2, /device:TPU:0, one launch (start us, length us, event | category | flops | bytes accessed | tf_op | source)
XLA Modules:
  0.0 495.7 jit_solution(17318056611637376782)
XLA Ops:
  20.8 5.4 %collective-permute-done.11 = bf16[1,128,256]{2,1,0:T(8,128)(2,1)S(1)} collective-permute-done((bf16[1,128,256]{2,1,0:T(8,128)(2,1)S(1)}, bf16[1,128,256]{2,1,0:T(8,128)(2,1)S(1)}, u32[]{:S(2)}, u32[]{:S(2)}) %collective-permute-start.11) | collective-permute-done | bytes 65568 | tf_op jit(solution)/shard_map/ppermute | solution.py:49
  42.7 9.9 %collective-permute-done.7 = bf16[2,128,256]{2,1,0:T(8,128)(2,1)S(1)} collective-permute-done((bf16[2,128,256]{2,1,0:T(8,128)(2,1)S(1)}, bf16[2,128,256]{2,1,0:T(8,128)(2,1)S(1)}, u32[]{:S(2)}, u32[]{:S(2)}) %collective-permute-start.7) | collective-permute-done | bytes 131104 | tf_op jit(solution)/shard_map/ppermute | solution.py:49
  62.2 5.2 %collective-permute-done.8 = bf16[4,128,256]{2,1,0:T(8,128)(2,1)S(1)} collective-permute-done((bf16[4,128,256]{2,1,0:T(8,128)(2,1)S(1)}, bf16[4,128,256]{2,1,0:T(8,128)(2,1)S(1)}, u32[]{:S(2)}, u32[]{:S(2)}) %collective-permute-start.8) | collective-permute-done | bytes 262176 | tf_op jit(solution)/shard_map/ppermute | solution.py:49
  90.1 7.4 %collective-permute-done.4 = bf16[8,144,256]{2,1,0:T(8,128)(2,1)S(1)} collective-permute-done((bf16[8,144,256]{2,1,0:T(8,128)(2,1)S(1)}, bf16[8,144,256]{2,1,0:T(8,128)(2,1)S(1)}, u32[]{:S(2)}, u32[]{:S(2)}) %collective-permute-start.4) | collective-permute-done | bytes 589856 | tf_op jit(solution)/shard_map/ppermute | solution.py:49
  102.1 8.8 %collective-permute-done.31 = bf16[1,576,256]{2,1,0:T(8,128)(2,1)S(1)} collective-permute-done((bf16[1,576,256]{2,1,0:T(8,128)(2,1)S(1)}, bf16[1,576,256]{2,1,0:T(8,128)(2,1)S(1)}, u32[]{:S(2)}, u32[]{:S(2)}) %collective-permute-start.31) | collective-permute-done | bytes 294944 | tf_op jit(solution)/shard_map/ppermute | solution.py:49
  113.6 13.8 %collective-permute-done.32 = bf16[2,576,256]{2,1,0:T(8,128)(2,1)S(1)} collective-permute-done((bf16[2,576,256]{2,1,0:T(8,128)(2,1)S(1)}, bf16[2,576,256]{2,1,0:T(8,128)(2,1)S(1)}, u32[]{:S(2)}, u32[]{:S(2)}) %collective-permute-start.32) | collective-permute-done | bytes 589856 | tf_op jit(solution)/shard_map/ppermute | solution.py:49
  159.2 22.7 %collective-permute-done.26.refs_1_ = bf16[4,128,1152]{2,1,0:T(8,128)(2,1)S(1)} collective-permute-done((bf16[4,128,1152]{2,1,0:T(8,128)(2,1)S(1)}, bf16[4,128,1152]{2,1,0:T(8,128)(2,1)S(1)}, u32[]{:S(2)}, u32[]{:S(2)}) %collective-permute-start.26) | collective-permute-done | bytes 1179680 | tf_op jit(solution)/shard_map/ppermute | solution.py:49
  191.2 12.4 %fusion.26 = f32[2048,1152]{1,0:T(8,128)} fusion(bf16[1152,1024]{1,0:T(8,128)(2,1)S(1)} %shard_map.190, bf16[512,1024]{1,0:T(8,128)(2,1)} %collective-permute-done.39, bf16[512,1024]{1,0:T(8,128)(2,1)} %collective-permute-done.38, bf16[512,1024]{1,0:T(8,128)(2,1)} %collective-permute-done.37, bf16[512,1024]{1,0:T(8,128)(2,1)} %multiply_convert_fusion.4), kind=kOutput, calls=%fused_computation.88 | convolution fusion | flops 4848615424 | bytes 15990784 | tf_op jit(solution)/shard_map/dot_general | solution.py:23
  203.6 11.4 %fusion.49 = f32[2048,1152]{1,0:T(8,128)} fusion(bf16[1024,1152]{1,0:T(8,128)(2,1)S(1)} %shard_map.189, bf16[512,1024]{1,0:T(8,128)(2,1)} %collective-permute-done.23, bf16[512,1024]{1,0:T(8,128)(2,1)} %collective-permute-done.22, bf16[512,1024]{1,0:T(8,128)(2,1)} %collective-permute-done.21, bf16[512,1024]{1,0:T(8,128)(2,1)} %multiply_convert_fusion.5), kind=kOutput, calls=%fused_computation.190 | convolution fusion | flops 4848615424 | bytes 15990784 | tf_op jit(solution)/shard_map/dot_general | solution.py:19
  215.0 18.3 %multiply_convert_fusion.1 = (bf16[2048,1152]{1,0:T(8,128)(2,1)}, bf16[2048,1152]{1,0:T(8,128)(2,1)}, bf16[2048,1152]{1,0:T(8,128)(2,1)}) fusion(f32[2048,1152]{1,0:T(8,128)} %fusion.26, f32[2048,1152]{1,0:T(8,128)} %fusion.49, bf16[1024,1152]{1,0:T(8,128)(2,1)S(1)} %copy-done.2, bf16[512,1024]{1,0:T(8,128)(2,1)} %collective-permute-done.23, ...), kind=kOutput, calls=%fused_computation.1 | convolution fusion | flops 4884004864 | bytes 39583744 | tf_op jit(solution)/shard_map/dot_general | solution.py:19
  233.4 11.0 %fusion.56 = (bf16[2048,1024]{1,0:T(8,128)(2,1)}, f32[2048,1024]{1,0:T(8,128)}) fusion(bf16[2048,1152]{1,0:T(8,128)(2,1)} %get-tuple-element.54, bf16[1152,1024]{1,0:T(8,128)(2,1)} %copy-done.5), kind=kOutput, calls=%fused_computation.197 | convolution fusion | flops 4833935360 | bytes 19660800 | tf_op jit(solution)/shard_map/dot_general | solution.py:19
  244.3 6.9 %convolution_convert_fusion.1.refs_0_ = bf16[1152,1024]{1,0:T(8,128)(2,1)S(1)} fusion(bf16[2048,1152]{1,0:T(8,128)(2,1)S(1)} %copy-done.55, bf16[512,1024]{1,0:T(8,128)(2,1)} %collective-permute-done.39, bf16[512,1024]{1,0:T(8,128)(2,1)} %collective-permute-done.38, bf16[512,1024]{1,0:T(8,128)(2,1)} %collective-permute-done.37, ...), kind=kOutput, calls=%fused_computation.9 | convolution fusion | flops 4849795072 | bytes 11272192 | tf_op jit(solution)/shard_map/dot_general | solution.py:29
  256.3 7.6 %convolution_convert_fusion.3.refs_0_ = bf16[1024,1152]{1,0:T(8,128)(2,1)S(1)} fusion(bf16[2048,1152]{1,0:T(8,128)(2,1)S(1)} %bitcast.110, bf16[512,1024]{1,0:T(8,128)(2,1)} %collective-permute-done.23, bf16[512,1024]{1,0:T(8,128)(2,1)} %collective-permute-done.22, bf16[512,1024]{1,0:T(8,128)(2,1)} %collective-permute-done.21, ...), kind=kOutput, calls=%fused_computation.11 | convolution fusion | flops 4849795072 | bytes 11272192 | tf_op jit(solution)/shard_map/dot_general | solution.py:29
  266.5 8.4 %fusion.58 = f32[2048,1024]{1,0:T(8,128)} fusion(bf16[2048,1152]{1,0:T(8,128)(2,1)S(1)} %bitcast.112, bf16[1024,1152]{1,0:T(8,128)(2,1)S(1)} %copy-done.4), kind=kOutput, calls=%fused_computation.199 | convolution fusion | flops 4831838208 | bytes 15466496 | tf_op jit(solution)/shard_map/dot_general | solution.py:23
  274.9 13.8 %fusion.55 = (bf16[2048,1024]{1,0:T(8,128)(2,1)}, f32[2048,1024]{1,0:T(8,128)S(1)}) fusion(f32[2048,1024]{1,0:T(8,128)} %fusion.58, bf16[2048,1152]{1,0:T(8,128)(2,1)} %get-tuple-element.52, bf16[1024,1152]{1,0:T(8,128)(2,1)S(1)} %copy-done.2), kind=kOutput, calls=%fused_computation.196 | convolution fusion | flops 4836032512 | bytes 28049408 | tf_op jit(solution)/shard_map/dot_general | solution.py:23
  291.7 8.9 %convolution_convert_fusion.2.refs_0_ = bf16[1024,1152]{1,0:T(8,128)(2,1)S(1)} fusion(bf16[2048,1152]{1,0:T(8,128)(2,1)} %get-tuple-element.53, bf16[512,1024]{1,0:T(8,128)(2,1)} %collective-permute-done.23, bf16[512,1024]{1,0:T(8,128)(2,1)} %collective-permute-done.22, bf16[512,1024]{1,0:T(8,128)(2,1)} %collective-permute-done.21, ...), kind=kOutput, calls=%fused_computation.10 | convolution fusion | flops 4849795072 | bytes 11272192 | tf_op jit(solution)/shard_map/dot_general | solution.py:29
  309.3 21.5 %collective-permute-done.72 = bf16[4,128,1152]{2,1,0:T(8,128)(2,1)S(1)} collective-permute-done((bf16[4,128,1152]{2,1,0:T(8,128)(2,1)S(1)}, bf16[4,128,1152]{2,1,0:T(8,128)(2,1)S(1)}, u32[]{:S(2)}, u32[]{:S(2)}) %collective-permute-start.72) | collective-permute-done | bytes 1179680 | tf_op jit(solution)/shard_map/ppermute | solution.py:49
  331.3 11.8 %collective-permute-done.76 = bf16[2,576,256]{2,1,0:T(8,128)(2,1)S(1)} collective-permute-done((bf16[2,576,256]{2,1,0:T(8,128)(2,1)S(1)}, bf16[2,576,256]{2,1,0:T(8,128)(2,1)S(1)}, u32[]{:S(2)}, u32[]{:S(2)}) %collective-permute-start.76) | collective-permute-done | bytes 589856 | tf_op jit(solution)/shard_map/ppermute | solution.py:49
  348.7 15.6 %collective-permute-done.73 = bf16[2,128,1152]{2,1,0:T(8,128)(2,1)S(1)} collective-permute-done((bf16[2,128,1152]{2,1,0:T(8,128)(2,1)S(1)}, bf16[2,128,1152]{2,1,0:T(8,128)(2,1)S(1)}, u32[]{:S(2)}, u32[]{:S(2)}) %collective-permute-start.73) | collective-permute-done | bytes 589856 | tf_op jit(solution)/shard_map/ppermute | solution.py:49
  368.1 11.5 %collective-permute-done.71 = bf16[1,128,1152]{2,1,0:T(8,128)(2,1)S(1)} collective-permute-done((bf16[1,128,1152]{2,1,0:T(8,128)(2,1)S(1)}, bf16[1,128,1152]{2,1,0:T(8,128)(2,1)S(1)}, u32[]{:S(2)}, u32[]{:S(2)}) %collective-permute-start.71) | collective-permute-done | bytes 294944 | tf_op jit(solution)/shard_map/ppermute | solution.py:49
  382.8 7.7 %collective-permute-done.36 = bf16[512,1024]{1,0:T(8,128)(2,1)S(1)} collective-permute-done((bf16[512,1024]{1,0:T(8,128)(2,1)S(1)}, bf16[512,1024]{1,0:T(8,128)(2,1)S(1)}, u32[]{:S(2)}, u32[]{:S(2)}) %collective-permute-start.36) | collective-permute-done | bytes 1048608 | tf_op jit(solution)/shard_map/ppermute | solution.py:49
  405.1 5.1 %fusion.13 = (f32[1024]{0:T(1024)S(1)}, f32[512]{0:T(512)S(1)}, f32[512,1024]{1,0:T(8,128)}) fusion(bf16[512,1024]{1,0:T(8,128)(2,1)S(1)} %copy-done.18, f32[512]{0:T(512)S(1)} %copy-done.51, f32[1024]{0:T(1024)S(1)} %bitcast.94, bf16[1024,3072]{1,0:T(8,128)(2,1)S(1)} %bitcast.78, bf16[512,1024]{1,0:T(8,128)(2,1)S(1)} %get-tuple-element.56, ...), kind=kOutput, calls=%fused_computation.36 | convolution fusion | flops 3234331136 | bytes 12595200 | tf_op jit(solution)/shard_map/dot_general | solution.py:23
  447.5 11.0 %collective-permute-done.65 = bf16[8,128,256]{2,1,0:T(8,128)(2,1)S(1)} collective-permute-done((bf16[8,128,256]{2,1,0:T(8,128)(2,1)S(1)}, bf16[8,128,256]{2,1,0:T(8,128)(2,1)S(1)}, u32[]{:S(2)}, u32[]{:S(2)}) %collective-permute-start.65) | collective-permute-done | bytes 524320 | tf_op jit(solution)/shard_map/ppermute | solution.py:49
  461.4 8.4 %collective-permute-done.55 = bf16[8,128,256]{2,1,0:T(8,128)(2,1)S(1)} collective-permute-done((bf16[8,128,256]{2,1,0:T(8,128)(2,1)S(1)}, bf16[8,128,256]{2,1,0:T(8,128)(2,1)S(1)}, u32[]{:S(2)}, u32[]{:S(2)}) %collective-permute-start.55) | collective-permute-done | bytes 524320 | tf_op jit(solution)/shard_map/ppermute | solution.py:49
  (422 shorter events, 227.9 us)
Async XLA Ops:
  2.3 28.2 %collective-permute-start.1 = (bf16[1,144,256]{2,1,0:T(8,128)(2,1)S(1)}, bf16[1,144,256]{2,1,0:T(8,128)(2,1)S(1)}, u32[]{:S(2)}, u32[]{:S(2)}) collective-permute-start(bf16[1,144,256]{2,1,0:T(8,128)(2,1)S(1)} %maximum_bitcast_fusion), channel_id=1, source_target_pairs={{0,4},{1,5},{2,6},{3,7},{4,0},{5,1},{6,2},{7,3},{8,12},{9,13},{10,... | collective-permute-start | bytes 221192 | tf_op jit(solution)/shard_map/ppermute | solution.py:49
  10.3 51.6 %collective-permute-start.24 = (bf16[1,128,1152]{2,1,0:T(8,128)(2,1)}, bf16[1,128,1152]{2,1,0:T(8,128)(2,1)S(1)}, u32[]{:S(2)}, u32[]{:S(2)}) collective-permute-start(bf16[1,128,1152]{2,1,0:T(8,128)(2,1)} %bitcast.81), channel_id=1, source_target_pairs={{0,4},{1,5},{2,6},{3,7},{4,0},{5,1},{6,2},{7,3},{8,12},{9,13},{10,... | collective-permute-start | bytes 884744 | tf_op jit(solution)/shard_map/ppermute | solution.py:49
  26.3 32.7 %collective-permute-start.27 = (bf16[1,128,1152]{2,1,0:T(8,128)(2,1)S(1)}, bf16[1,128,1152]{2,1,0:T(8,128)(2,1)S(1)}, u32[]{:S(2)}, u32[]{:S(2)}) collective-permute-start(bf16[1,128,1152]{2,1,0:T(8,128)(2,1)S(1)} %bitcast.84), channel_id=1, source_target_pairs={{0,4},{1,5},{2,6},{3,7},{4,0},{5,1},{6,2},{7,3},{8,12},{9,13},{10,... | collective-permute-start | bytes 884744 | tf_op jit(solution)/shard_map/ppermute | solution.py:49
  26.3 52.6 %collective-permute-start.30 = (bf16[576,256]{1,0:T(8,128)(2,1)S(1)}, bf16[576,256]{1,0:T(8,128)(2,1)S(1)}, u32[]{:S(2)}, u32[]{:S(2)}) collective-permute-start(bf16[576,256]{1,0:T(8,128)(2,1)S(1)} %copy-done.52), channel_id=1, source_target_pairs={{0,0},{1,1},{2,8},{3,9},{4,16},{5,17},{6,24},{7,25},{8,2},{9,3},{1... | collective-permute-start | bytes 884744 | tf_op jit(solution)/shard_map/ppermute | solution.py:289
  67.5 33.3 %collective-permute-start.9 = (bf16[8,128,256]{2,1,0:T(8,128)(2,1)S(1)}, bf16[8,128,256]{2,1,0:T(8,128)(2,1)S(1)}, u32[]{:S(2)}, u32[]{:S(2)}) collective-permute-start(bf16[8,128,256]{2,1,0:T(8,128)(2,1)S(1)} %pad_maximum_fusion.15), channel_id=1, source_target_pairs={{0,1},{1,0},{2,3},{3,2},{4,5},{5,4},{6,7},{7,6},{8,9},{9,8},{10,11... | collective-permute-start | bytes 1572872 | tf_op jit(solution)/shard_map/ppermute | solution.py:49
  78.9 32.0 %collective-permute-start.25 = (bf16[2,128,1152]{2,1,0:T(8,128)(2,1)S(1)}, bf16[2,128,1152]{2,1,0:T(8,128)(2,1)S(1)}, u32[]{:S(2)}, u32[]{:S(2)}) collective-permute-start(bf16[2,128,1152]{2,1,0:T(8,128)(2,1)S(1)} %pad_maximum_fusion.12), channel_id=1, source_target_pairs={{0,2},{1,3},{2,0},{3,1},{4,6},{5,7},{6,4},{7,5},{8,10},{9,11},{10,... | collective-permute-start | bytes 1769480 | tf_op jit(solution)/shard_map/ppermute | solution.py:49
  79.6 33.4 %collective-permute-start.28 = (bf16[2,128,1152]{2,1,0:T(8,128)(2,1)S(1)}, bf16[2,128,1152]{2,1,0:T(8,128)(2,1)S(1)}, u32[]{:S(2)}, u32[]{:S(2)}) collective-permute-start(bf16[2,128,1152]{2,1,0:T(8,128)(2,1)S(1)} %pad_maximum_fusion.13), channel_id=1, source_target_pairs={{0,2},{1,3},{2,0},{3,1},{4,6},{5,7},{6,4},{7,5},{8,10},{9,11},{10,... | collective-permute-start | bytes 1769480 | tf_op jit(solution)/shard_map/ppermute | solution.py:49
  100.7 37.6 %collective-permute-start.5 = (bf16[16,144,256]{2,1,0:T(8,128)(2,1)}, bf16[16,144,256]{2,1,0:T(8,128)(2,1)S(1)}, u32[]{:S(2)}, u32[]{:S(2)}) collective-permute-start(bf16[16,144,256]{2,1,0:T(8,128)(2,1)} %constant_dynamic-update-slice_fusion.refs_0_), channel_id=1, source_target_pairs={{0,8},{8,0},{16,24},{24,16},{1,9},{9,1},{17,25},{25,17},{2,10},{10... | collective-permute-start | bytes 3538952 | tf_op jit(solution)/shard_map/ppermute | solution.py:49
  101.6 27.6 %collective-permute-start.10 = (bf16[16,128,256]{2,1,0:T(8,128)(2,1)}, bf16[16,128,256]{2,1,0:T(8,128)(2,1)S(1)}, u32[]{:S(2)}, u32[]{:S(2)}) collective-permute-start(bf16[16,128,256]{2,1,0:T(8,128)(2,1)} %constant_dynamic-update-slice_fusion.5.refs_0_), channel_id=1, source_target_pairs={{0,8},{8,0},{16,24},{24,16},{1,9},{9,1},{17,25},{25,17},{2,10},{10... | collective-permute-start | bytes 3145736 | tf_op jit(solution)/shard_map/ppermute | solution.py:49
  129.2 29.0 %collective-permute-start.29 = (bf16[4,128,1152]{2,1,0:T(8,128)(2,1)S(1)}, bf16[4,128,1152]{2,1,0:T(8,128)(2,1)S(1)}, u32[]{:S(2)}, u32[]{:S(2)}) collective-permute-start(bf16[4,128,1152]{2,1,0:T(8,128)(2,1)S(1)} %pad_maximum_fusion.6.refs_0_), channel_id=1, source_target_pairs={{0,1},{1,0},{2,3},{3,2},{4,5},{5,4},{6,7},{7,6},{8,9},{9,8},{10,11... | collective-permute-start | bytes 3538952 | tf_op jit(solution)/shard_map/ppermute | solution.py:49
  130.4 51.5 %collective-permute-start.26 = (bf16[4,128,1152]{2,1,0:T(8,128)(2,1)S(1)}, bf16[4,128,1152]{2,1,0:T(8,128)(2,1)S(1)}, u32[]{:S(2)}, u32[]{:S(2)}) collective-permute-start(bf16[4,128,1152]{2,1,0:T(8,128)(2,1)S(1)} %pad_maximum_fusion.5.refs_0_), channel_id=1, source_target_pairs={{0,1},{1,0},{2,3},{3,2},{4,5},{5,4},{6,7},{7,6},{8,9},{9,8},{10,11... | collective-permute-start | bytes 3538952 | tf_op jit(solution)/shard_map/ppermute | solution.py:49
  131.3 57.8 %collective-permute-start.33 = (bf16[4,576,256]{2,1,0:T(8,128)(2,1)S(1)}, bf16[4,576,256]{2,1,0:T(8,128)(2,1)}, u32[]{:S(2)}, u32[]{:S(2)}) collective-permute-start(bf16[4,576,256]{2,1,0:T(8,128)(2,1)S(1)} %pad_maximum_fusion.7.refs_0_), channel_id=1, source_target_pairs={{0,2},{1,3},{2,0},{3,1},{4,6},{5,7},{6,4},{7,5},{8,10},{9,11},{10,... | collective-permute-start | bytes 3538952 | tf_op jit(solution)/shard_map/ppermute | solution.py:49
  153.1 29.8 %collective-permute-start.21 = (bf16[512,1024]{1,0:T(8,128)(2,1)}, bf16[512,1024]{1,0:T(8,128)(2,1)}, u32[]{:S(2)}, u32[]{:S(2)}) collective-permute-start(bf16[512,1024]{1,0:T(8,128)(2,1)} %multiply_convert_fusion.5), channel_id=1, source_target_pairs={{0,16},{8,24},{16,0},{24,8},{1,17},{9,25},{17,1},{25,9},{2,18},{10... | collective-permute-start | bytes 3145736 | tf_op jit(solution)/shard_map/ppermute | solution.py:49
  154.5 36.6 %collective-permute-start.38 = (bf16[512,1024]{1,0:T(8,128)(2,1)}, bf16[512,1024]{1,0:T(8,128)(2,1)}, u32[]{:S(2)}, u32[]{:S(2)}) collective-permute-start(bf16[512,1024]{1,0:T(8,128)(2,1)} %multiply_convert_fusion.4), channel_id=1, source_target_pairs={{0,8},{8,0},{16,24},{24,16},{1,9},{9,1},{17,25},{25,17},{2,10},{10... | collective-permute-start | bytes 3145736 | tf_op jit(solution)/shard_map/ppermute | solution.py:49
  159.2 31.9 %collective-permute-start.39 = (bf16[512,1024]{1,0:T(8,128)(2,1)}, bf16[512,1024]{1,0:T(8,128)(2,1)}, u32[]{:S(2)}, u32[]{:S(2)}) collective-permute-start(bf16[512,1024]{1,0:T(8,128)(2,1)} %collective-permute-done.37), channel_id=1, source_target_pairs={{0,8},{8,0},{16,24},{24,16},{1,9},{9,1},{17,25},{25,17},{2,10},{10... | collective-permute-start | bytes 3145736 | tf_op jit(solution)/shard_map/ppermute | solution.py:49
  252.3 53.2 %collective-permute-start.75 = (bf16[4,576,256]{2,1,0:T(8,128)(2,1)S(1)}, bf16[4,576,256]{2,1,0:T(8,128)(2,1)S(1)}, u32[]{:S(2)}, u32[]{:S(2)}) collective-permute-start(bf16[4,576,256]{2,1,0:T(8,128)(2,1)S(1)} %get-tuple-element.41), channel_id=1, source_target_pairs={{0,2},{1,3},{2,0},{3,1},{4,6},{5,7},{6,4},{7,5},{8,10},{9,11},{10,... | collective-permute-start | bytes 3538952 | tf_op jit(solution)/shard_map/ppermute | solution.py:49
  265.0 42.3 %collective-permute-start.69 = (bf16[4,128,1152]{2,1,0:T(8,128)(2,1)S(1)}, bf16[4,128,1152]{2,1,0:T(8,128)(2,1)S(1)}, u32[]{:S(2)}, u32[]{:S(2)}) collective-permute-start(bf16[4,128,1152]{2,1,0:T(8,128)(2,1)S(1)} %get-tuple-element.37), channel_id=1, source_target_pairs={{0,1},{1,0},{2,3},{3,2},{4,5},{5,4},{6,7},{7,6},{8,9},{9,8},{10,11... | collective-permute-start | bytes 3538952 | tf_op jit(solution)/shard_map/ppermute | solution.py:49
  302.0 28.8 %collective-permute-start.72 = (bf16[4,128,1152]{2,1,0:T(8,128)(2,1)S(1)}, bf16[4,128,1152]{2,1,0:T(8,128)(2,1)S(1)}, u32[]{:S(2)}, u32[]{:S(2)}) collective-permute-start(bf16[4,128,1152]{2,1,0:T(8,128)(2,1)S(1)} %get-tuple-element.39), channel_id=1, source_target_pairs={{0,1},{1,0},{2,3},{3,2},{4,5},{5,4},{6,7},{7,6},{8,9},{9,8},{10,11... | collective-permute-start | bytes 3538952 | tf_op jit(solution)/shard_map/ppermute | solution.py:49
  302.6 77.8 %collective-permute-start.40 = (bf16[512,1024]{1,0:T(8,128)(2,1)S(1)}, bf16[512,1024]{1,0:T(8,128)(2,1)S(1)}, u32[]{:S(2)}, u32[]{:S(2)}) collective-permute-start(bf16[512,1024]{1,0:T(8,128)(2,1)S(1)} %get-tuple-element.59), channel_id=1, source_target_pairs={{0,8},{8,0},{16,24},{24,16},{1,9},{9,1},{17,25},{25,17},{2,10},{10... | collective-permute-start | bytes 3145736 | tf_op jit(solution)/shard_map/ppermute | solution.py:49
  303.2 79.6 %collective-permute-start.34 = (bf16[512,1024]{1,0:T(8,128)(2,1)S(1)}, bf16[512,1024]{1,0:T(8,128)(2,1)S(1)}, u32[]{:S(2)}, u32[]{:S(2)}) collective-permute-start(bf16[512,1024]{1,0:T(8,128)(2,1)S(1)} %get-tuple-element.61), channel_id=1, source_target_pairs={{0,8},{8,0},{16,24},{24,16},{1,9},{9,1},{17,25},{25,17},{2,10},{10... | collective-permute-start | bytes 3145736 | tf_op jit(solution)/shard_map/ppermute | solution.py:49
  305.6 76.4 %collective-permute-start.42 = (bf16[512,1024]{1,0:T(8,128)(2,1)S(1)}, bf16[512,1024]{1,0:T(8,128)(2,1)S(1)}, u32[]{:S(2)}, u32[]{:S(2)}) collective-permute-start(bf16[512,1024]{1,0:T(8,128)(2,1)S(1)} %fusion.16), channel_id=1, source_target_pairs={{0,16},{8,24},{16,0},{24,8},{1,17},{9,25},{17,1},{25,9},{2,18},{10... | collective-permute-start | bytes 3145736 | tf_op jit(solution)/shard_map/ppermute | solution.py:49
  307.3 35.7 %collective-permute-start.76 = (bf16[2,576,256]{2,1,0:T(8,128)(2,1)S(1)}, bf16[2,576,256]{2,1,0:T(8,128)(2,1)S(1)}, u32[]{:S(2)}, u32[]{:S(2)}) collective-permute-start(bf16[2,576,256]{2,1,0:T(8,128)(2,1)S(1)} %slice.444), channel_id=1, source_target_pairs={{0,1},{1,0},{2,3},{3,2},{4,5},{5,4},{6,7},{7,6},{8,9},{9,8},{10,11... | collective-permute-start | bytes 1769480 | tf_op jit(solution)/shard_map/ppermute | solution.py:49
  379.5 35.7 %collective-permute-start.74 = (bf16[1,128,1152]{2,1,0:T(8,128)(2,1)}, bf16[1,128,1152]{2,1,0:T(8,128)(2,1)}, u32[]{:S(2)}, u32[]{:S(2)}) collective-permute-start(bf16[1,128,1152]{2,1,0:T(8,128)(2,1)} %slice.442), channel_id=1, source_target_pairs={{0,4},{1,5},{2,6},{3,7},{4,0},{5,1},{6,2},{7,3},{8,12},{9,13},{10,... | collective-permute-start | bytes 884744 | tf_op jit(solution)/shard_map/ppermute | solution.py:49
  380.4 61.1 %collective-permute-start.78 = (bf16[576,256]{1,0:T(8,128)(2,1)S(1)}, bf16[576,256]{1,0:T(8,128)(2,1)}, u32[]{:S(2)}, u32[]{:S(2)}) collective-permute-start(bf16[576,256]{1,0:T(8,128)(2,1)S(1)} %fusion.30), channel_id=1, source_target_pairs={{0,0},{1,1},{8,2},{9,3},{16,4},{17,5},{24,6},{25,7},{2,8},{3,9},{1... | collective-permute-start | bytes 884744 | tf_op jit(solution)/shard_map/ppermute | solution.py:360
  (119 other events, 1477.4 us)

commit v3 on v0

v3 whole, which is shorter than its diff:
```python
from typing import NamedTuple

import jax
import jax.numpy as jnp
from jax import lax
from jax.experimental import pallas as pl
from jax.experimental.pallas import tpu as pltpu
from jax.sharding import PartitionSpec as P

SLOT_MAX = 8192
HALO = 16
SMALL_ROWS = 16
VMEM_BYTES = 56 << 20
TILE = 256
KERNEL_COST = pl.CostEstimate(flops=1 << 36, bytes_accessed=1 << 20, transcendentals=0)

norm_eps = 1e-05


def multiply(left_side, right_side):
    return jnp.dot(left_side, right_side, preferred_element_type=jnp.float32)


def against(left_side, right_side):
    return lax.dot_general(
        left_side, right_side, (((1,), (1,)), ((), ())), preferred_element_type=jnp.float32
    )


def outer_sum(left_side, right_side):
    return lax.dot_general(
        left_side, right_side, (((0,), (0,)), ((), ())), preferred_element_type=jnp.float32
    )


def tie(*values):
    return lax.optimization_barrier(values)


def swap(shard, step):
    axis, bit = step
    count = lax.axis_size(axis)
    return lax.ppermute(shard, axis, [(i, i ^ bit) for i in range(count)])


def gather_steps(stack, steps):
    for step in steps:
        stack = jnp.concatenate([stack, swap(stack, step)], axis=0)
    return stack


def last_step(stack, step):
    return [stack, swap(stack, step)]


def scatter_step(parts, step):
    keep, send = parts
    total = keep.astype(jnp.float32) + swap(send, step).astype(jnp.float32)
    half = total.shape[0] // 2
    if not half:
        return total[0]
    return total[:half].astype(jnp.bfloat16), total[half:].astype(jnp.bfloat16)


def scatter_steps(parts, steps):
    for step in reversed(steps):
        parts = scatter_step(parts, step)
    return parts


def masks_at(position, steps):
    masks = {"dp": 0, "seq": 0}
    for place, (axis, bit) in enumerate(steps):
        masks[axis] = masks[axis] + ((position >> place) & 1) * bit
    return masks["dp"], masks["seq"]


def tile_of(ref, row, rows, col, cols):
    return ref.at[pl.ds(pl.multiple_of(row * rows, rows), rows), pl.ds(pl.multiple_of(col * cols, cols), cols)]


def dp_gather(block, steps):
    blocks = [block]
    for step in steps:
        blocks = blocks + [swap(b, step) for b in blocks]
    return blocks


def dp_scatter(parts, steps):
    for step in reversed(steps):
        half = len(parts) // 2
        moved = [swap(send.astype(jnp.bfloat16), step) for send in parts[half:]]
        parts = [
            new if keep is None else keep.astype(jnp.float32) + new.astype(jnp.float32)
            for keep, new in zip(parts[:half], moved)
        ]
    return parts


class Piece(NamedTuple):
    steps: list
    block: tuple
    view: object


def start_loads(ids_ref, refs, pieces, into, sem):
    for place, piece in enumerate(pieces):
        first = 0
        for part in refs[2 * place : 2 * place + 2]:

            def start(position, carry, part=part, first=first, piece=piece):
                mask_dp, mask_seq = masks_at(position + first, piece.steps)
                pltpu.make_async_copy(
                    part.at[position],
                    piece.view(into, ids_ref[0] ^ mask_dp, ids_ref[1] ^ mask_seq),
                    sem,
                ).start()
                return carry

            lax.fori_loop(0, part.shape[0], start, 0)
            first += part.shape[0]


def start_stores(ids_ref, whole, pieces, outs, sem):
    for place, piece in enumerate(pieces):
        half = 2 ** (len(piece.steps) - 1)
        for first, out in ((0, outs[2 * place]), (half, outs[2 * place + 1])):

            def start(position, carry, first=first, out=out, piece=piece):
                mask_dp, mask_seq = masks_at(position + first, piece.steps)
                source = piece.view(whole, ids_ref[0] ^ mask_dp, ids_ref[1] ^ mask_seq)
                pltpu.make_async_copy(source, out.at[position], sem).start()
                return carry

            lax.fori_loop(0, half, start, 0)


def wait_whole(ref, sem):
    pltpu.make_async_copy(ref, ref, sem).wait()


def fetch_block(blocks, buffers, sems):
    i = pl.program_id(0)

    rows = buffers.shape[1]

    def copy(place):
        slot = place % 2
        source = blocks[place // 2].at[pl.ds(place % 2 * rows, rows)]
        return pltpu.make_async_copy(source, buffers.at[slot], sems.at[slot])

    for place in range(2 * len(blocks)):

        @pl.when(i == place)
        def _(place=place):
            if place == 0:
                copy(0).start()
            if place + 1 < 2 * len(blocks):
                copy(place + 1).start()
            copy(place).wait()

    return buffers[i % 2]


def token_call(kernel, ids, blocks, tiled, stacks, outs, scratch):
    rows, width = blocks[0].shape
    rows, count, steps = rows // 2, len(blocks), 2 * len(blocks)
    return pl.pallas_call(
        kernel,
        out_shape=[jax.ShapeDtypeStruct((rows * steps, n), t) for n, t in outs],
        grid_spec=pltpu.PrefetchScalarGridSpec(
            num_scalar_prefetch=1,
            grid=(steps,),
            in_specs=[pl.BlockSpec(memory_space=pl.ANY)] * count
            + [pl.BlockSpec((rows, v.shape[1]), lambda i, ids: (i, 0)) for v in tiled]
            + [pl.BlockSpec(memory_space=pl.ANY)] * len(stacks),
            out_specs=[pl.BlockSpec((rows, n), lambda i, ids: (i, 0)) for n, _ in outs],
            scratch_shapes=[
                pltpu.VMEM((2, rows, width), jnp.bfloat16),
                pltpu.SemaphoreType.DMA((2,)),
                *scratch,
            ],
        ),
        compiler_params=pltpu.CompilerParams(vmem_limit_bytes=VMEM_BYTES),
        cost_estimate=KERNEL_COST,
    )(ids, *blocks, *tiled, *stacks)


def feed_up(ids, normed, gate, gate_stacks, up, up_stacks, shape):
    count = len(normed)

    def kernel(ids_ref, *refs):
        blocks, stacks, refs = refs[:count], refs[count:-8], refs[-8:]
        act, slope, silu, buffers, block_sems, gate_v, up_v, sems = refs

        @pl.when(pl.program_id(0) == 0)
        def _():
            start_loads(ids_ref, stacks[: 2 * len(gate)], gate, gate_v, sems.at[0])
            start_loads(ids_ref, stacks[2 * len(gate) :], up, up_v, sems.at[1])

        x = fetch_block(blocks, buffers, block_sems)

        @pl.when(pl.program_id(0) == 0)
        def _():
            wait_whole(gate_v, sems.at[0])
            wait_whole(up_v, sems.at[1])

        gate_val = multiply(x, gate_v[...])
        up_val = multiply(x, up_v[...])
        sigmoid = jax.nn.sigmoid(gate_val)
        silu_gate = gate_val * sigmoid
        act[...] = (silu_gate * up_val).astype(jnp.bfloat16)
        slope[...] = (up_val * sigmoid * (1.0 + gate_val * (1.0 - sigmoid))).astype(jnp.bfloat16)
        silu[...] = silu_gate.astype(jnp.bfloat16)

    n = shape[1]
    return token_call(
        kernel,
        ids,
        normed,
        [],
        [*gate_stacks, *up_stacks],
        [(n, jnp.bfloat16)] * 3,
        [pltpu.VMEM(shape, jnp.bfloat16)] * 2 + [pltpu.SemaphoreType.DMA((2,))],
    )


def feed_back(ids, final, activated, slope, silu, gate, gate_stacks, up, up_stacks, down, down_stacks, shape):
    count = len(final)
    ends = [2 * len(gate), 2 * len(gate) + 2 * len(up)]

    def kernel(ids_ref, *refs):
        blocks, (act_ref, slope_ref, silu_ref) = refs[:count], refs[count : count + 3]
        stacks, refs = refs[count + 3 : -10], refs[-10:]
        grad_gate, grad_up, grad_norm, out, buffers, block_sems, gate_v, up_v, down_v, sems = refs

        @pl.when(pl.program_id(0) == 0)
        def _():
            start_loads(ids_ref, stacks[ends[1] :], down, down_v, sems.at[2])
            start_loads(ids_ref, stacks[: ends[0]], gate, gate_v, sems.at[0])
            start_loads(ids_ref, stacks[ends[0] : ends[1]], up, up_v, sems.at[1])

        f = fetch_block(blocks, buffers, block_sems)

        @pl.when(pl.program_id(0) == 0)
        def _():
            wait_whole(down_v, sems.at[2])
            wait_whole(gate_v, sems.at[0])
            wait_whole(up_v, sems.at[1])

        grad_act = against(f, down_v[...])
        gg = (grad_act * slope_ref[...].astype(jnp.float32)).astype(jnp.bfloat16)
        gu = (grad_act * silu_ref[...].astype(jnp.float32)).astype(jnp.bfloat16)
        grad_gate[...] = gg
        grad_up[...] = gu
        out[...] = multiply(act_ref[...], down_v[...]).astype(jnp.bfloat16)
        grad_norm[...] = (against(gg, gate_v[...]) + against(gu, up_v[...])).astype(jnp.bfloat16)

    features, n = shape
    return token_call(
        kernel,
        ids,
        final,
        [activated, slope, silu],
        [*gate_stacks, *up_stacks, *down_stacks],
        [(n, jnp.bfloat16), (n, jnp.bfloat16), (features, jnp.bfloat16), (features, jnp.bfloat16)],
        [
            pltpu.VMEM(shape, jnp.bfloat16),
            pltpu.VMEM(shape, jnp.bfloat16),
            pltpu.VMEM((n, features), jnp.bfloat16),
            pltpu.SemaphoreType.DMA((3,)),
        ],
    )


def stack_shapes(pieces):
    shapes = []
    for piece in pieces:
        half = 2 ** (len(piece.steps) - 1)
        shapes += [jax.ShapeDtypeStruct((half, *piece.block), jnp.bfloat16)] * 2
    return shapes


def paired(parts):
    return [(parts[i], parts[i + 1]) for i in range(0, len(parts), 2)]


def weight_gradient(ids, lefts, rights, pieces):
    rows, columns = lefts[0].shape[1], rights[0].shape[1]
    step = min(v.shape[0] for v in (*lefts, *rights))
    tile = next((t for t in (512, 384, 256, 128) if rows % t == 0), rows)
    count = rows // tile
    shapes = stack_shapes(pieces)

    def kernel(ids_ref, *refs):
        sides, refs = refs[: len(lefts) + len(rights)], refs[len(lefts) + len(rights) :]
        outs, (whole, sems) = refs[:-2], refs[-2:]
        i = pl.program_id(0)
        left_rows, right_rows = [
            [v[at : at + step] for v in side for at in range(0, v.shape[0], step)]
            for side in (sides[: len(lefts)], sides[len(lefts) :])
        ]
        total = sum(outer_sum(a, b) for a, b in zip(left_rows, right_rows))
        whole[pl.ds(pl.multiple_of(i * tile, tile), tile)] = total.astype(jnp.bfloat16)

        @pl.when(i == count - 1)
        def _():
            start_stores(ids_ref, whole, pieces, outs, sems.at[0])
            wait_whole(whole, sems.at[0])

    parts = pl.pallas_call(
        kernel,
        out_shape=shapes,
        grid_spec=pltpu.PrefetchScalarGridSpec(
            num_scalar_prefetch=1,
            grid=(count,),
            in_specs=[
                *(pl.BlockSpec((v.shape[0], tile), lambda i, ids: (0, i)) for v in lefts),
                *(pl.BlockSpec((v.shape[0], columns), lambda i, ids: (0, 0)) for v in rights),
            ],
            out_specs=[pl.BlockSpec(memory_space=pl.ANY)] * len(shapes),
            scratch_shapes=[
                pltpu.VMEM((rows, columns), jnp.bfloat16),
                pltpu.SemaphoreType.DMA((1,)),
            ],
        ),
        compiler_params=pltpu.CompilerParams(vmem_limit_bytes=VMEM_BYTES),
        cost_estimate=KERNEL_COST,
    )(ids, *lefts, *rights)
    return paired(parts)


def mixer_forward(ids, extended, consts, in_pieces, in_stacks, out_pieces, out_stacks, slot_size):
    rows, features = extended.shape
    rows = rows - HALO
    tile = rows // 2
    count = len(in_stacks)
    wide = 3 * features

    def kernel(ids_ref, ext_ref, const_ref, *refs):
        stacks, refs = refs[: count + len(out_stacks)], refs[count + len(out_stacks) :]
        normed_one, b_out, c_out, x_out, mixed_out, conv_out, gated_out, hidden_out, normed_two = refs[:9]
        in_v, out_v, mixed_s, sems = refs[9:]
        i = pl.program_id(0)

        @pl.when(i == 0)
        def _():
            start_loads(ids_ref, stacks[:count], in_pieces, in_v, sems.at[0])
            start_loads(ids_ref, stacks[count:], out_pieces, out_v, sems.at[1])

        at = pl.multiple_of(i * tile, HALO)
        x = ext_ref[pl.ds(at, HALO + tile)].astype(jnp.float32)
        scale = lax.rsqrt(jnp.mean(x * x, axis=1, keepdims=True) + norm_eps)
        normed = (x * scale * const_ref[0:1]).astype(jnp.bfloat16)
        normed_one[...] = normed[HALO:]

        @pl.when(i == 0)
        def _():
            wait_whole(in_v, sems.at[0])
            wait_whole(out_v, sems.at[1])

        b_part = multiply(normed, in_v[:, :features])
        x_part = multiply(normed, in_v[:, 2 * features :])
        b_out[...] = b_part[HALO:]
        x_out[...] = x_part[HALO:]
        mixed = (b_part * x_part).astype(jnp.bfloat16)
        mixed_s[...] = mixed.astype(jnp.float32)
        base = lax.rem(ids_ref[1] * rows, slot_size)

        @pl.when(jnp.logical_and(i == 0, base == 0))
        def _():
            mixed_s[0:HALO] = jnp.zeros((HALO, features), jnp.float32)

        mixed_out[pl.ds(at, HALO)] = mixed_s[0:HALO].astype(jnp.bfloat16)
        mixed_out[pl.ds(pl.multiple_of(at + HALO, HALO), tile)] = mixed[HALO:]
        conv = sum(
            const_ref[2 + k : 3 + k] * mixed_s[HALO - 2 + k : HALO - 2 + k + tile] for k in range(3)
        )
        conv_out[...] = conv
        c_part = multiply(normed[HALO:], in_v[:, features : 2 * features])
        c_out[...] = c_part
        gated = (c_part * conv).astype(jnp.bfloat16)
        gated_out[...] = gated
        hidden = x[HALO:] + multiply(gated, out_v[...])
        hidden_out[...] = hidden
        scale = lax.rsqrt(jnp.mean(hidden * hidden, axis=1, keepdims=True) + norm_eps)
        normed_two[...] = (hidden * scale * const_ref[1:2]).astype(jnp.bfloat16)

    f32, bf16 = jnp.float32, jnp.bfloat16
    kinds = [bf16, f32, f32, f32, bf16, f32, bf16, f32, bf16]
    shapes = [(rows + (HALO if i == 4 else 0), features) for i in range(9)]
    whole = pl.BlockSpec((rows + HALO, features), lambda i, ids: (0, 0))
    part = pl.BlockSpec((tile, features), lambda i, ids: (i, 0))
    return pl.pallas_call(
        kernel,
        out_shape=[jax.ShapeDtypeStruct(s, t) for s, t in zip(shapes, kinds)],
        grid_spec=pltpu.PrefetchScalarGridSpec(
            num_scalar_prefetch=1,
            grid=(2,),
            in_specs=[whole, pl.BlockSpec(consts.shape, lambda i, ids: (0, 0))]
            + [pl.BlockSpec(memory_space=pl.ANY)] * (count + len(out_stacks)),
            out_specs=[whole if i == 4 else part for i in range(9)],
            scratch_shapes=[
                pltpu.VMEM((features, wide), bf16),
                pltpu.VMEM((features, features), bf16),
                pltpu.VMEM((tile + HALO, features), f32),
                pltpu.SemaphoreType.DMA((2,)),
            ],
        ),
        compiler_params=pltpu.CompilerParams(vmem_limit_bytes=VMEM_BYTES),
        cost_estimate=KERNEL_COST,
    )(ids, extended, consts, *in_stacks, *out_stacks)


def mixer_back(
    ids, near, more, far, final, hidden, c_part, conv, gated, mixed, consts, out_pieces, out_stacks, slot_size
):
    rows, features = hidden.shape
    tile = rows // 2
    shapes = stack_shapes(out_pieces)

    def kernel(
        ids_ref, near_ref, more_ref, far_ref, final_ref, hidden_ref, c_ref, conv_ref, gated_ref, mixed_ref, const_ref, *refs
    ):
        stacks, refs = refs[: len(out_stacks)], refs[len(out_stacks) :]
        grad_hidden, grad_c, grad_mixed, head, sums = refs[:5]
        outs, (out_v, whole, mixed_s, conv_s, sems) = refs[5:-5], refs[-5:]
        i = pl.program_id(0)

        @pl.when(i == 0)
        def _():
            start_loads(ids_ref, stacks, out_pieces, out_v, sems.at[0])
            sums[...] = jnp.zeros(sums.shape, jnp.float32)
            conv_s[tile:] = jnp.zeros((8, features), jnp.float32)

        @pl.when(i > 0)
        def _():
            conv_s[tile:] = conv_s[0:8]

        normed_grad = near_ref[...].astype(jnp.float32) + more_ref[...].astype(jnp.float32)
        normed_grad += far_ref[...].astype(jnp.float32)
        h = hidden_ref[...]
        scale = lax.rsqrt(jnp.mean(h * h, axis=1, keepdims=True) + norm_eps)
        weighted = normed_grad * const_ref[1:2]
        inner = jnp.mean(weighted * h, axis=1, keepdims=True)
        sums[1:2] += jnp.sum(normed_grad * h * scale, axis=0, keepdims=True)
        total = final_ref[...].astype(jnp.float32) + scale * weighted - h * (scale * scale * scale * inner)
        grad_hidden[...] = total
        branch = total.astype(jnp.bfloat16)
        outer = outer_sum(gated_ref[...], branch)

        @pl.when(i == 0)
        def _():
            wait_whole(out_v, sems.at[0])

        grad_gated = against(branch, out_v[...])
        grad_c[...] = (grad_gated * conv_ref[...]).astype(jnp.bfloat16)
        grad_conv = grad_gated * c_ref[...]
        conv_s[0:tile] = grad_conv
        at = pl.multiple_of((1 - i) * tile, HALO)
        mixed_s[...] = mixed_ref[pl.ds(at, HALO + tile)].astype(jnp.float32)
        for k in range(3):
            sums[2 + k : 3 + k] += jnp.sum(
                grad_conv * mixed_s[HALO - 2 + k : HALO - 2 + k + tile], axis=0, keepdims=True
            )
        grad_mixed[...] = sum(const_ref[2 + k : 3 + k] * conv_s[2 - k : 2 - k + tile] for k in range(3))

        @pl.when(i == 1)
        def _():
            live = jnp.where(lax.rem(ids_ref[1] * rows, slot_size) > 0, 1.0, 0.0)
            head[...] = jnp.zeros(head.shape, jnp.float32)
            head[0:1] = live * const_ref[2:3] * conv_s[0:1]
            head[1:2] = live * (const_ref[2:3] * conv_s[1:2] + const_ref[3:4] * conv_s[0:1])
            out_v[...] = (whole[...] + outer).astype(jnp.bfloat16)
            start_stores(ids_ref, out_v, out_pieces, outs, sems.at[0])
            wait_whole(out_v, sems.at[0])

        @pl.when(i == 0)
        def _():
            whole[...] = outer

    f32, bf16 = jnp.float32, jnp.bfloat16
    part = pl.BlockSpec((tile, features), lambda i, ids: (1 - i, 0))
    once = pl.BlockSpec((8, features), lambda i, ids: (0, 0))
    parts = pl.pallas_call(
        kernel,
        out_shape=[jax.ShapeDtypeStruct((rows, features), t) for t in (f32, bf16, f32)]
        + [jax.ShapeDtypeStruct((8, features), f32)] * 2
        + shapes,
        grid_spec=pltpu.PrefetchScalarGridSpec(
            num_scalar_prefetch=1,
            grid=(2,),
            in_specs=[part] * 8
            + [pl.BlockSpec((rows + HALO, features), lambda i, ids: (0, 0)), once]
            + [pl.BlockSpec(memory_space=pl.ANY)] * len(out_stacks),
            out_specs=[part] * 3 + [once] * 2 + [pl.BlockSpec(memory_space=pl.ANY)] * len(shapes),
            scratch_shapes=[
                pltpu.VMEM((features, features), bf16),
                pltpu.VMEM((features, features), f32),
                pltpu.VMEM((tile + HALO, features), f32),
                pltpu.VMEM((tile + 8, features), f32),
                pltpu.SemaphoreType.DMA((1,)),
            ],
        ),
        compiler_params=pltpu.CompilerParams(vmem_limit_bytes=VMEM_BYTES),
        cost_estimate=KERNEL_COST,
    )(ids, near, more, far, final, hidden, c_part, conv, gated, mixed, consts, *out_stacks)
    return [*parts[:5], paired(parts[5:])]


def projection_gradient(ids, normed, grad_mixed, returned, grad_c, b_part, x_part, pieces):
    rows, features = normed.shape
    tile = features // 4
    shapes = stack_shapes(pieces)

    def kernel(ids_ref, normed_ref, mixed_ref, back_ref, c_ref, b_ref, x_ref, proj, *refs):
        outs, (whole, mixed_s, sems) = refs[:-3], refs[-3:]
        i = pl.program_id(0)

        @pl.when(i == 0)
        def _():
            mixed_s[...] = mixed_ref[...]
            mixed_s[rows - 2 :] += back_ref[0:2]
            grad = mixed_s[...]
            proj[:, :features] = (grad * x_ref[...]).astype(jnp.bfloat16)
            proj[:, features : 2 * features] = c_ref[...]
            proj[:, 2 * features :] = (grad * b_ref[...]).astype(jnp.bfloat16)

        whole[pl.ds(pl.multiple_of(i * tile, tile), tile)] = outer_sum(
            normed_ref[...], proj[...]
        ).astype(jnp.bfloat16)

        @pl.when(i == 3)
        def _():
            start_stores(ids_ref, whole, pieces, outs, sems.at[0])
            wait_whole(whole, sems.at[0])

    def same(n, width):
        return pl.BlockSpec((n, width), lambda i, ids: (0, 0))

    parts = pl.pallas_call(
        kernel,
        out_shape=[jax.ShapeDtypeStruct((rows, 3 * features), jnp.bfloat16), *shapes],
        grid_spec=pltpu.PrefetchScalarGridSpec(
            num_scalar_prefetch=1,
            grid=(4,),
            in_specs=[
                pl.BlockSpec((rows, tile), lambda i, ids: (0, i)),
                same(rows, features),
                same(8, features),
                same(rows, features),
                same(rows, features),
                same(rows, features),
            ],
            out_specs=[same(rows, 3 * features)] + [pl.BlockSpec(memory_space=pl.ANY)] * len(shapes),
            scratch_shapes=[
                pltpu.VMEM((features, 3 * features), jnp.bfloat16),
                pltpu.VMEM((rows, features), jnp.float32),
                pltpu.SemaphoreType.DMA((1,)),
            ],
        ),
        compiler_params=pltpu.CompilerParams(vmem_limit_bytes=VMEM_BYTES),
        cost_estimate=KERNEL_COST,
    )(ids, normed, grad_mixed, returned, grad_c, b_part, x_part)
    return parts[0], paired(parts[1:])


def mixer_first(ids, proj, tokens, grad_hidden, sums, consts, in_pieces, in_stacks):
    rows, features = tokens.shape
    tile = rows // 2

    def kernel(ids_ref, proj_ref, x_ref, hidden_ref, sums_ref, const_ref, *refs):
        stacks, (grad_tokens, sums_out, in_v, sems) = refs[:-4], refs[-4:]

        @pl.when(pl.program_id(0) == 0)
        def _():
            start_loads(ids_ref, stacks, in_pieces, in_v, sems.at[0])
            sums_out[...] = sums_ref[...]
            wait_whole(in_v, sems.at[0])

        normed_grad = against(proj_ref[...], in_v[...])
        x = x_ref[...].astype(jnp.float32)
        scale = lax.rsqrt(jnp.mean(x * x, axis=1, keepdims=True) + norm_eps)
        weighted = normed_grad * const_ref[0:1]
        inner = jnp.mean(weighted * x, axis=1, keepdims=True)
        sums_out[0:1] += jnp.sum(normed_grad * x * scale, axis=0, keepdims=True)
        grad_tokens[...] = (
            hidden_ref[...] + scale * weighted - x * (scale * scale * scale * inner)
        ).astype(jnp.bfloat16)

    part = pl.BlockSpec((tile, features), lambda i, ids: (i, 0))
    once = pl.BlockSpec((8, features), lambda i, ids: (0, 0))
    return pl.pallas_call(
        kernel,
        out_shape=[
            jax.ShapeDtypeStruct((rows, features), jnp.bfloat16),
            jax.ShapeDtypeStruct((8, features), jnp.float32),
        ],
        grid_spec=pltpu.PrefetchScalarGridSpec(
            num_scalar_prefetch=1,
            grid=(2,),
            in_specs=[pl.BlockSpec((tile, 3 * features), lambda i, ids: (i, 0)), part, part, once, once]
            + [pl.BlockSpec(memory_space=pl.ANY)] * len(in_stacks),
            out_specs=[part, once],
            scratch_shapes=[
                pltpu.VMEM((features, 3 * features), jnp.bfloat16),
                pltpu.SemaphoreType.DMA((1,)),
            ],
        ),
        compiler_params=pltpu.CompilerParams(vmem_limit_bytes=VMEM_BYTES),
        cost_estimate=KERNEL_COST,
    )(ids, proj, tokens, grad_hidden, sums, consts, *in_stacks)


def bits_below(count):
    return [1 << i for i in range(count.bit_length() - 1)]


def per_device(
    tokens,
    mixer_gain,
    in_weight,
    conv_weight,
    out_weight,
    feed_gain,
    gate_weight,
    up_weight,
    down_weight,
    lengths,
    cotangent,
):
    n_dp, n_seq = lax.axis_size("dp"), lax.axis_size("seq")
    tok_rows, features = tokens.shape
    slot_size = min(SLOT_MAX, tok_rows * n_seq)
    own_dp, own_seq = lax.axis_index("dp"), lax.axis_index("seq")
    ids = jnp.stack([own_dp, own_seq]).astype(jnp.int32)

    seq_bits = bits_below(n_seq)
    along_y = seq_bits[: len(seq_bits) // 2]
    ys = [("seq", b) for b in reversed(along_y)]
    zs = [("seq", b) for b in reversed(seq_bits[len(along_y) :])]
    core = [("dp", 1)]
    xs = [("dp", b) for b in reversed(bits_below(n_dp)[1:])]
    in_orders = [zs + xs + ys + core, ys + zs + xs + core]
    out_order = zs[:1] + xs + ys + zs[1:] + core
    far_order, near_order = zs[:1] + ys + zs[1:], zs + ys
    token_order = xs + core

    position = own_seq * tok_rows + jnp.arange(tok_rows, dtype=jnp.int32)
    in_slot = position % slot_size
    slot_index = position // slot_size
    slot_ids = jnp.arange(lengths.shape[1], dtype=jnp.int32)
    slot_length = jnp.sum(
        jnp.where(slot_index[:, None] == slot_ids[None, :], lengths[0][None, :], 0), axis=1
    )
    live_mask = (in_slot < slot_length).astype(jnp.float32)[:, None]

    in_rows, in_cols = in_weight.shape
    out_rows, out_cols = out_weight.shape
    in_cut = (in_cols // 128 + 1) // 2 * 128
    in_cuts = [0, in_cut, in_cols]
    small_cols = mixer_gain.shape[0]
    small = jnp.concatenate([mixer_gain[None], feed_gain[None], conv_weight], axis=0)
    small = jnp.pad(small, ((0, SMALL_ROWS - small.shape[0]), (0, -small_cols % 128)))
    small_order = zs + ys
    small = gather_steps(small[None], small_order)
    places = jnp.stack([jnp.int32(masks_at(p, small_order)[1]) for p in range(n_seq)])
    chosen = (own_seq ^ jnp.arange(n_seq))[:, None] == places[None]
    consts = jnp.einsum(
        "sp,pkc->ksc",
        chosen.astype(jnp.bfloat16),
        small[:, :8, :small_cols],
        preferred_element_type=jnp.float32,
    ).reshape(8, features)
    mixer = [in_weight[None, :, :in_cut], in_weight[None, :, in_cut:], out_weight[None]]
    orders = [*in_orders, out_order]
    before = lax.ppermute(
        tokens[tok_rows - HALO :], "seq", [(i, i + 1) for i in range(n_seq - 1)]
    )
    extended = jnp.concatenate([before, tokens], axis=0)
    hidden_units = gate_weight.shape[1]
    gate_rows = gate_weight.shape[0]
    down_rows, down_cols = down_weight.shape
    ratio = n_seq // n_dp
    home = [
        (e * n_seq + s, (s // ratio) * n_seq + e * ratio + s % ratio)
        for e in range(n_dp)
        for s in range(n_seq)
    ]
    cuts = [0, -(-down_rows // 32) * 16, down_rows]

    def gate_view(ref, dp, seq):
        return ref.at[pl.ds(pl.multiple_of(seq * gate_rows, gate_rows), gate_rows)]

    def down_view(cut):
        low, high = cuts[cut], cuts[cut + 1]

        def view(ref, dp, seq):
            row = pl.multiple_of((seq % ratio) * down_rows + low, 16)
            col = pl.multiple_of((seq // ratio) * down_cols, down_cols)
            return ref.at[pl.ds(row, high - low), pl.ds(col, down_cols)]

        return view

    gate = [Piece(near_order, gate_weight.shape, gate_view)]
    up = [Piece(far_order, up_weight.shape, gate_view)]
    down = [
        Piece(order, (cuts[i + 1] - cuts[i], down_cols), down_view(i))
        for i, order in enumerate((near_order, far_order))
    ]

    grad_final = (live_mask * cotangent.astype(jnp.float32)).astype(jnp.bfloat16)
    middle = len(orders[0]) // 2
    z_first, last = len(zs) // 2, len(zs) + len(ys) - 1
    mixer = [gather_steps(v, order[:middle]) for v, order in zip(mixer, orders)]
    mixer, gate_weight, up_weight = tie(mixer, gate_weight, up_weight)
    mixer = [gather_steps(v, order[middle:-1]) for v, order in zip(mixer, orders)]
    gate_up = [
        gather_steps(v[None], p.steps[:z_first])
        for v, p in zip((gate_weight, up_weight), (*gate, *up))
    ]
    mixer, gate_up, consts, extended, down_weight, grad_final = tie(
        mixer, gate_up, consts, extended, down_weight, grad_final
    )
    stacks = [last_step(v, order[-1]) for v, order in zip(mixer, orders)]
    stacks, gate_up, down_weight, grad_final = tie(stacks, gate_up, down_weight, grad_final)

    def in_view(cut):
        low, high = in_cuts[cut], in_cuts[cut + 1]

        def view(ref, dp, seq):
            row = pl.multiple_of(seq * in_rows, in_rows)
            col = pl.multiple_of(dp * in_cols + low, 128)
            return ref.at[pl.ds(row, in_rows), pl.ds(col, high - low)]

        return view

    def out_view(ref, dp, seq):
        return tile_of(ref, seq, out_rows, dp, out_cols)

    in_pieces = [
        Piece(order, (in_rows, in_cuts[i + 1] - in_cuts[i]), in_view(i))
        for i, order in enumerate(in_orders)
    ]
    out_pieces = [Piece(out_order, out_weight.shape, out_view)]
    in_stacks, out_stacks = stacks[0] + stacks[1], stacks[2]

    gate_up = [gather_steps(v, p.steps[z_first:last]) for v, p in zip(gate_up, (*gate, *up))]
    down_shard = lax.ppermute(down_weight, ("dp", "seq"), home)
    forward = mixer_forward(
        ids, extended, consts, in_pieces, in_stacks, out_pieces, out_stacks, slot_size
    )
    forward, gate_up, down_shard, grad_final = tie(forward, gate_up, down_shard, grad_final)
    normed_one, b_part, c_part, x_part, mixed, conv, gated, hidden, normed_two = forward

    def split_rows(v):
        return [v[i : i + tok_rows] for i in range(0, v.shape[0], tok_rows)]

    def with_core(blocks):
        return blocks + [swap(v, core[0]) for v in blocks]

    wide = (features, hidden_units)
    gate_stacks, up_stacks = [last_step(v, p.steps[-1]) for v, p in zip(gate_up, (*gate, *up))]
    downs = [
        gather_steps(down_shard[None, a:b], p.steps[:z_first])
        for a, b, p in zip(cuts, cuts[1:], down)
    ]
    normed_there = dp_gather(normed_two, xs)[1:]
    normed_two, normed_there, gate_stacks, up_stacks, downs, grad_final = tie(
        normed_two, normed_there, gate_stacks, up_stacks, downs, grad_final
    )
    normed_blocks = with_core([normed_two]) + with_core(normed_there)
    downs = [gather_steps(v, p.steps[z_first:last]) for v, p in zip(downs, down)]
    normed_blocks, downs, gate_stacks, up_stacks, grad_final = tie(
        normed_blocks, downs, gate_stacks, up_stacks, grad_final
    )
    down_stacks = [v for stack, p in zip(downs, down) for v in last_step(stack, p.steps[-1])]
    final_there = dp_gather(grad_final, xs)[1:]
    activated, slope, silu = feed_up(ids, normed_blocks, gate, gate_stacks, up, up_stacks, wide)
    activated, down_stacks, grad_final, final_there = tie(
        activated, down_stacks, grad_final, final_there
    )
    final_blocks = with_core([grad_final]) + with_core(final_there)
    down_parts = weight_gradient(ids, [activated], final_blocks, down)
    down_parts, down_stacks = tie(down_parts, down_stacks)

    def lower(parts):
        return tuple(v[: v.shape[0] // 2] for v in parts)

    def upper(parts):
        return tuple(v[v.shape[0] // 2 :] for v in parts)

    def one_step(parts, pieces, place):
        return [scatter_step(v, p.steps[place]) for v, p in zip(parts, pieces)]

    def exchanged(parts, step):
        return (parts[0], swap(parts[1], step))

    def added(low, high):
        return tuple(
            (v[0].astype(jnp.float32) + v[1].astype(jnp.float32)).astype(jnp.bfloat16)
            for v in (low, high)
        )

    def core_halves(v):
        blocks = split_rows(v)
        near, far = blocks[:2], blocks[2:]
        half = len(far) // 2
        return near[0], near[1], far[:half], far[half:]

    down_parts = one_step(down_parts, down, -1)
    grad_gate, grad_up, back, feed = feed_back(
        ids, final_blocks, activated, slope, silu, gate, gate_stacks, up, up_stacks, down, down_stacks, wide
    )
    back, feed, grad_gate, grad_up, down_parts = tie(back, feed, grad_gate, grad_up, down_parts)
    near, near_send, far, far_send = core_halves(back)
    far = dp_scatter(far + far_send, core)
    far, near, near_send, grad_gate, grad_up, feed = tie(far, near, near_send, grad_gate, grad_up, feed)
    far = [v.astype(jnp.bfloat16) for v in far]
    half_rows = tok_rows // 2
    far_low = dp_scatter([None] + [v[:half_rows] for v in far], xs)
    near_more = swap(near_send, core[0])
    feed_near, feed_send, feed_far, feed_far_send = core_halves(feed)
    down_parts = one_step(down_parts, down, -2)
    gate_parts = weight_gradient(ids, normed_blocks, [grad_gate], gate)
    gate_parts, far, far_low, grad_up, near, near_more, down_parts, feed_far, feed_far_send = tie(
        gate_parts, far, far_low, grad_up, near, near_more, down_parts, feed_far, feed_far_send
    )
    far_high = dp_scatter([None] + [v[half_rows:] for v in far], xs)
    gate_low = exchanged(lower(gate_parts[0]), gate[0].steps[-1])
    feed_far = [v.astype(jnp.bfloat16) for v in dp_scatter(feed_far + feed_far_send, core)]
    up_parts = weight_gradient(ids, normed_blocks, [grad_up], up)
    up_parts, far_low, far_high, gate_low, gate_parts, feed_far, down_parts = tie(
        up_parts, far_low, far_high, gate_low, gate_parts, feed_far, down_parts
    )

    gate_high = exchanged(upper(gate_parts[0]), gate[0].steps[-1])
    up_low = exchanged(lower(up_parts[0]), up[0].steps[-1])
    feed_low = dp_scatter([None] + [v[:half_rows] for v in feed_far], xs)
    far = jnp.concatenate(far_low + far_high, axis=0)
    grad_hidden, grad_c, grad_mixed, first_rows, sums, out_parts = mixer_back(
        ids,
        near,
        near_more,
        far,
        grad_final,
        hidden,
        c_part,
        conv,
        gated,
        mixed,
        consts,
        out_pieces,
        out_stacks,
        slot_size,
    )
    out_parts, grad_mixed, first_rows, gate_low, gate_high, up_low, up_parts, feed_far, feed_low = tie(
        out_parts, grad_mixed, first_rows, gate_low, gate_high, up_low, up_parts, feed_far, feed_low
    )
    returned = lax.ppermute(first_rows, "seq", [(i + 1, i) for i in range(n_seq - 1)])
    up_high = exchanged(upper(up_parts[0]), up[0].steps[-1])
    feed_high = dp_scatter([None] + [v[half_rows:] for v in feed_far], xs)
    own_down = [scatter_steps(v, p.steps[:-2]) for v, p in zip(down_parts, down)]
    own_down = jnp.concatenate(own_down, axis=0).astype(jnp.bfloat16)
    grad_proj, in_parts = projection_gradient(
        ids, normed_one, grad_mixed, returned, grad_c, b_part, x_part, in_pieces
    )
    in_parts, up_low, up_high, own_down, gate_low, gate_high, grad_proj, out_parts, feed_high = tie(
        in_parts, up_low, up_high, own_down, gate_low, gate_high, grad_proj, out_parts, feed_high
    )
    in_parts = one_step(in_parts, in_pieces, -1)
    out_parts = one_step(out_parts, out_pieces, -1)
    in_parts, out_parts, grad_proj, gate_low, gate_high, up_low, up_high = tie(
        in_parts, out_parts, grad_proj, gate_low, gate_high, up_low, up_high
    )
    in_parts = one_step(in_parts, in_pieces, -2)
    out_parts = one_step(out_parts, out_pieces, -2)
    gate_parts = scatter_step(added(gate_low, gate_high), gate[0].steps[-2])
    up_parts = added(up_low, up_high)
    grad_tokens, sums = mixer_first(ids, grad_proj, tokens, grad_hidden, sums, consts, in_pieces, in_stacks)
    in_parts, sums, out_parts, gate_parts, up_parts, own_down = tie(
        in_parts, sums, out_parts, gate_parts, up_parts, own_down
    )
    in_parts = one_step(in_parts, in_pieces, -3)
    out_parts = one_step(out_parts, out_pieces, -3)
    own_gate = scatter_steps(gate_parts, gate[0].steps[:-2])
    up_parts = scatter_step(up_parts, up[0].steps[-2])
    sum_steps = zs + ys + xs + core
    for step in sum_steps[:2]:
        sums = sums + swap(sums, step)
    in_parts, out_parts, own_gate, up_parts, sums, own_down = tie(
        in_parts, out_parts, own_gate, up_parts, sums, own_down
    )
    own_in = [scatter_step(v, p.steps[-4]) for v, p in zip(in_parts, in_pieces)]
    own_up = scatter_steps(up_parts, up[0].steps[:-2])
    out_parts = one_step(out_parts, out_pieces, -4)
    for step in sum_steps[2:4]:
        sums = sums + swap(sums, step)
    own_in, out_parts, own_up, sums, own_down = tie(own_in, out_parts, own_up, sums, own_down)
    own_in = [scatter_steps(v, p.steps[:-4]) for v, p in zip(own_in, in_pieces)]
    own_in = jnp.concatenate(own_in, axis=1)
    own_out = scatter_steps(out_parts[0], out_order[:-4])
    for step in sum_steps[4:]:
        sums = sums + swap(sums, step)
    own_down = lax.ppermute(own_down, ("dp", "seq"), [(b, a) for a, b in home]).astype(jnp.float32)
    own_sums = lax.dynamic_slice(sums, (0, own_seq * small_cols), (8, small_cols))
    feed_more = swap(feed_send, core[0])
    feed_out = jnp.concatenate(feed_low + feed_high, axis=0).astype(jnp.float32)
    feed_out = feed_out + feed_near.astype(jnp.float32) + feed_more.astype(jnp.float32)
    output = (live_mask * (hidden + feed_out)).astype(jnp.bfloat16)
    return (
        output,
        grad_tokens,
        own_sums[0],
        own_in,
        own_sums[2:5],
        own_out,
        own_sums[1],
        own_gate,
        own_up,
        own_down,
    )


def solution(mesh):
    in_specs = (
        P(("dp", "seq"), None),
        P("seq"),
        P("seq", "dp"),
        P(None, "seq"),
        P("seq", "dp"),
        P("seq"),
        P("seq", "dp"),
        P("seq", "dp"),
        P("seq", "dp"),
        P("dp", None),
        P(("dp", "seq"), None),
    )
    out_specs = (
        P(("dp", "seq"), None),
        P(("dp", "seq"), None),
        P("seq"),
        P("seq", "dp"),
        P(None, "seq"),
        P("seq", "dp"),
        P("seq"),
        P("seq", "dp"),
        P("seq", "dp"),
        P("seq", "dp"),
    )
    return jax.shard_map(
        per_device, mesh=mesh, in_specs=in_specs, out_specs=out_specs, check_vma=False
    )
```

time: 2160 us -> 436 us (0.20)
  waiting for transfers between devices: 1880 us -> 159 us
  Pallas kernels: 0 us -> 135 us
  matrix products: 134 us -> 0.19 us
  blocking collectives: 101 us -> 0 us
  starting transfers between devices: 4.75 us -> 86 us
    reduce_scatter x10 -> x0, waiting for transfers between devices: 1340 us -> none  [the longest x1 317 us: per_device(): lax.psum_scatter(grad_down, 'seq', scatter_dimension=0, tiled=True)]
    all_gather x8 -> x0, waiting for transfers between devices: 512 us -> none  [the longest x1 134 us: per_device(): lax.all_gather(wide[2], 'seq', axis=0, tiled=True)]
    ppermute x2 -> x82, waiting for transfers between devices: 3.61 us -> 159 us  [the longest x78 159 us: swap(): return lax.ppermute(shard, axis, [(i, i ^ bit) for i in range(count)])]
    pallas_call x0 -> x9, Pallas kernels: none -> 135 us  [the longest x2 49 us: token_call(): pl.pallas_call(kernel, out_shape=[jax.ShapeDtypeStruct((rows * steps, n),...]
    dot_general x15 -> x1, matrix products: 134 us -> 0.19 us  [per_device(): jnp.einsum('sp,pkc->ksc', chosen.astype(jnp.bfloat16), small[:, :8, :smal...]
    ppermute x2 -> x82, starting transfers between devices: 4 us -> 86 us  [the longest x78 80.8 us: swap(): return lax.ppermute(shard, axis, [(i, i ^ bit) for i in range(count)])]
    all_gather x5 -> x0, blocking collectives: 74.8 us -> none  [the longest x1 20.5 us: per_device(): lax.all_gather(mixer_gain, 'seq', axis=0, tiled=True)]
    unnamed x20 -> x0, waiting for transfers between devices: 24.2 us -> none
  transfers between devices with their start and end apart: 21 -> 82, of which waited for: 20 -> 34; matrix products, arithmetic and copies ran while one was open for 5% -> 8% of each run, Pallas kernels for 0% -> 29%
where the time goes in v3:
time: 436 us; the launch traced here: 428 us
  waiting for transfers between devices  159 us (36%)
  Pallas kernels  135 us (31%)
  starting transfers between devices  86 us (20%)
  other arithmetic  27.5 us (6%)
  local copies, waits for them, and re-layouts  17.8 us (4%)
    ppermute x78, waiting for transfers between devices, swap(): return lax.ppermute(shard, axis, [(i, i ^ bit) for i in range(count)])  159 us
    ppermute x78, starting transfers between devices, swap(): return lax.ppermute(shard, axis, [(i, i ^ bit) for i in range(count)])  80.8 us
    pallas_call x2, Pallas kernels, token_call(): pl.pallas_call(kernel, out_shape=[jax.ShapeDtypeStruct((rows * steps, n),...  49 us
    pallas_call x3, Pallas kernels, weight_gradient(): pl.pallas_call(kernel, out_shape=shapes, grid_spec=pltpu.PrefetchScalarGr...  33.2 us
    pallas_call x1, Pallas kernels, mixer_back(): pl.pallas_call(kernel, out_shape=[jax.ShapeDtypeStruct((rows, features),...  14.3 us
    pallas_call x1, Pallas kernels, mixer_forward(): pl.pallas_call(kernel, out_shape=[jax.ShapeDtypeStruct(s, t) for s, t in...  14 us
    pallas_call x1, Pallas kernels, projection_gradient(): pl.pallas_call(kernel, out_shape=[jax.ShapeDtypeStruct((rows, 3 * feature...  13.6 us
    pallas_call x1, Pallas kernels, mixer_first(): pl.pallas_call(kernel, out_shape=[jax.ShapeDtypeStruct((rows, features),...  10.5 us
  transfers between devices with their start and end apart: 82, of which 34 were waited for; matrix products, arithmetic and copies ran while one was open for 8% of the time, Pallas kernels for 29%

profile of v3, /device:TPU:0, one launch (start us, length us, event | category | flops | bytes accessed | tf_op | source)
XLA Modules:
  0.0 428.2 jit_solution(16105440160433760222)
XLA Ops:
  24.1 6.4 %collective-permute-done.3 = bf16[2,128,384]{2,1,0:T(8,128)(2,1)S(1)} collective-permute-done((bf16[2,128,384]{2,1,0:T(8,128)(2,1)S(1)}, bf16[2,128,384]{2,1,0:T(8,128)(2,1)S(1)}, u32[]{:S(2)}, u32[]{:S(2)}) %collective-permute-start.3) | collective-permute-done | bytes 196640 | tf_op jit(solution)/shard_map/ppermute | solution.py:43
  45.1 3.5 collective-permute-done.6
  50.5 9.1 %collective-permute-done.13 = bf16[1,128,1152]{2,1,0:T(8,128)(2,1)S(1)} collective-permute-done((bf16[1,128,1152]{2,1,0:T(8,128)(2,1)S(1)}, bf16[1,128,1152]{2,1,0:T(8,128)(2,1)S(1)}, u32[]{:S(2)}, u32[]{:S(2)}) %collective-permute-start.13) | collective-permute-done | bytes 294944 | tf_op jit(solution)/shard_map/ppermute | solution.py:43
  59.7 4.2 collective-permute-done.12
  68.5 5.3 %collective-permute-done.20.refs_5_.refs_1_ = bf16[16,128,256]{2,1,0:T(8,128)(2,1)} collective-permute-done((bf16[16,128,256]{2,1,0:T(8,128)(2,1)}, bf16[16,128,256]{2,1,0:T(8,128)(2,1)}, u32[]{:S(2)}, u32[]{:S(2)}) %collective-permute-start.20) | collective-permute-done | bytes 1048608 | tf_op jit(solution)/shard_map/ppermute | solution.py:43
  76.2 14.0 %shard_map.186 = (bf16[512,1024]{1,0:T(8,128)(2,1)}, f32[512,1024]{1,0:T(8,128)}, f32[512,1024]{1,0:T(8,128)}, f32[512,1024]{1,0:T(8,128)}, bf16[528,1024]{1,0:T...) custom-call(s32[2]{0:T(128)} %pad_add_fusion.ids_ref, ...), custom_call_target="tpu_custom_call" | custom-call | flops 68719476736 | bytes 1048576 | tf_op jit(solution)/shard_map/pallas_call | solution.py:394
  90.4 4.8 %collective-permute-done.21 = bf16[2,128,1152]{2,1,0:T(8,128)(2,1)S(1)} collective-permute-done((bf16[2,128,1152]{2,1,0:T(8,128)(2,1)S(1)}, bf16[2,128,1152]{2,1,0:T(8,128)(2,1)S(1)}, u32[]{:S(2)}, u32[]{:S(2)}) %collective-permute-start.21) | collective-permute-done | bytes 589856 | tf_op jit(solution)/shard_map/ppermute | solution.py:43
  97.1 3.5 collective-permute-start.26
  100.6 4.4 %collective-permute-start.28 = (bf16[1,288,256]{2,1,0:T(8,128)(2,1)S(1)}, bf16[1,288,256]{2,1,0:T(8,128)(2,1)S(1)}, u32[]{:S(2)}, u32[]{:S(2)}) collective-permute-start(bf16[1,288,256]{2,1,0:T(8,128)(2,1)S(1)} %get-tuple-element.500), channel_id=1, source_target_pairs={{0,4},{1,5},{2,6},{3,7},{4,0},{5,1},{6,2},{7,3},{8,12},{9,13},{10,... | collective-permute-start | bytes 442376 | tf_op jit(solution)/shard_map/ppermute | solution.py:43
  105.0 24.9 %collective-permute-done.28 = bf16[1,288,256]{2,1,0:T(8,128)(2,1)S(1)} collective-permute-done((bf16[1,288,256]{2,1,0:T(8,128)(2,1)S(1)}, bf16[1,288,256]{2,1,0:T(8,128)(2,1)S(1)}, u32[]{:S(2)}, u32[]{:S(2)}) %collective-permute-start.28) | collective-permute-done | bytes 147488 | tf_op jit(solution)/shard_map/ppermute | solution.py:43
  134.5 8.4 %collective-permute-done.32 = bf16[2,288,256]{2,1,0:T(8,128)(2,1)S(1)} collective-permute-done((bf16[2,288,256]{2,1,0:T(8,128)(2,1)S(1)}, bf16[2,288,256]{2,1,0:T(8,128)(2,1)S(1)}, u32[]{:S(2)}, u32[]{:S(2)}) %collective-permute-start.32) | collective-permute-done | bytes 294944 | tf_op jit(solution)/shard_map/ppermute | solution.py:43
  148.1 18.2 %shard_map.187 = (bf16[2048,1152]{1,0:T(8,128)(2,1)}, bf16[2048,1152]{1,0:T(8,128)(2,1)}, bf16[2048,1152]{1,0:T(8,128)(2,1)}) custom-call(s32[2]{0:T(128)} %pad_add_fusion.ids_ref, bf16[512,1024]{1,0:T(8,128)(2,1)} %get-tuple-element.286.refs_0_, bf16[512,1024]{1,0:T(8,128)(2,1)} %copy-done.40, bf16[512,1024]{1,0:T(8,128)(2,1)} %copy-done.39, ...), custom_call_target="tpu_custom_call" | custom-call | flops 68719476736 | bytes 1048576 | tf_op jit(solution)/shard_map/pallas_call | solution.py:168
  173.7 10.3 %shard_map.188 = (bf16[4,288,256]{2,1,0:T(8,128)(2,1)}, bf16[4,288,256]{2,1,0:T(8,128)(2,1)}, bf16[4,288,256]{2,1,0:T(8,128)(2,1)}, bf16[4,288,256]{2,1,0:T(8,128)(2,1)}) custom-call(s32[2]{0:T(128)} %pad_add_fusion.ids_ref, bf16[2048,1152]{1,0:T(8,128)(2,1)} %get-tuple-element.300.refs_0_.refs_4_, ...), custom_call_target="tpu_custom_call" | custom-call | flops 68719476736 | bytes 1048576 | tf_op jit(solution)/shard_map/pallas_call | solution.py:311
  186.2 30.8 %shard_map.189 = (bf16[2048,1152]{1,0:T(8,128)(2,1)}, bf16[2048,1152]{1,0:T(8,128)(2,1)}, bf16[2048,1024]{1,0:T(8,128)(2,1)}, bf16[2048,1024]{1,0:T(8,128)(2,1)}) custom-call(s32[2]{0:T(128)} %pad_add_fusion.ids_ref, bf16[512,1024]{1,0:T(8,128)(2,1)} %multiply_convert_fusion.1.refs_1_.refs_0_.final_ref, bf16[512,1024]{1,0:T(8,128)(2,1)} %copy-done.44, ...), custom_call_target="tpu_custom_call" | custom-call | flops 68719476736 | bytes 1048576 | tf_op jit(solution)/shard_map/pallas_call | solution.py:168
  222.0 4.8 %collective-permute-done.44 = bf16[2,288,256]{2,1,0:T(8,128)(2,1)S(1)} collective-permute-done((bf16[2,288,256]{2,1,0:T(8,128)(2,1)S(1)}, bf16[2,288,256]{2,1,0:T(8,128)(2,1)S(1)}, u32[]{:S(2)}, u32[]{:S(2)}) %collective-permute-start.44) | collective-permute-done | bytes 294944 | tf_op jit(solution)/shard_map/ppermute | solution.py:43
  233.9 11.6 %shard_map.190 = (bf16[4,128,1152]{2,1,0:T(8,128)(2,1)}, bf16[4,128,1152]{2,1,0:T(8,128)(2,1)}) custom-call(s32[2]{0:T(128)} %pad_add_fusion.ids_ref, bf16[512,1024]{1,0:T(8,128)(2,1)} %get-tuple-element.286.refs_0_, bf16[512,1024]{1,0:T(8,128)(2,1)} %copy-done.40, bf16[512,1024]{1,0:T(8,128)(2,1)} %copy-done.39, bf16[512,1024]{1,0:T(8,128)(2,1)} %copy-done.41, ...), custom_call_target="tpu_custom_call" | custom-call | flops 68719476736 | bytes 1048576 | tf_op jit(solution)/shard_map/pallas_call | solution.py:311
  250.0 11.3 %shard_map.191 = (bf16[4,128,1152]{2,1,0:T(8,128)(2,1)}, bf16[4,128,1152]{2,1,0:T(8,128)(2,1)}) custom-call(s32[2]{0:T(128)} %pad_add_fusion.ids_ref, bf16[512,1024]{1,0:T(8,128)(2,1)} %get-tuple-element.286.refs_0_, bf16[512,1024]{1,0:T(8,128)(2,1)} %copy-done.40, bf16[512,1024]{1,0:T(8,128)(2,1)} %copy-done.39, bf16[512,1024]{1,0:T(8,128)(2,1)} %copy-done.41, ...), custom_call_target="tpu_custom_call" | custom-call | flops 68719476736 | bytes 1048576 | tf_op jit(solution)/shard_map/pallas_call | solution.py:311
  272.1 14.3 %shard_map.192 = (f32[512,1024]{1,0:T(8,128)}, bf16[512,1024]{1,0:T(8,128)(2,1)}, f32[512,1024]{1,0:T(8,128)}, f32[8,1024]{1,0:T(8,128)}, f32[8,1024]{1,0:T(8,12...) custom-call(s32[2]{0:T(128)} %pad_add_fusion.ids_ref, bf16[512,1024]{1,0:T(8,128)(2,1)} %get-tuple-element.339.near_ref, ...), custom_call_target="tpu_custom_call" | custom-call | flops 68719476736 | bytes 1048576 | tf_op jit(solution)/shard_map/pallas_call | solution.py:485
  297.2 13.6 %shard_map.193 = (bf16[512,3072]{1,0:T(8,128)(2,1)}, bf16[16,128,384]{2,1,0:T(8,128)(2,1)}, bf16[16,128,384]{2,1,0:T(8,128)(2,1)}, bf16[16,128,384]{2,1,0:T(8,128)(2,1)}, bf16[16,128,384]{2,1,0:T(8,128)(2,1)}) custom-call(s32[2]{0:T(128)} %pad_add_fusion.ids_ref, bf16[512,1024]{1,0:T(8,128)(2,1)} %get-tuple-element.372.normed_ref, ...), custom_call_target="tpu_custom_call" | custom-call | flops 68719476736 | bytes 1048576 | tf_op jit(solution)/shard_map/pallas_call | solution.py:541
  324.7 10.5 %shard_map.194 = (bf16[512,1024]{1,0:T(8,128)(2,1)}, f32[8,1024]{1,0:T(8,128)}) custom-call(s32[2]{0:T(128)} %pad_add_fusion.ids_ref, bf16[512,3072]{1,0:T(8,128)(2,1)} %get-tuple-element.414.proj_ref, bf16[512,1024]{1,0:T(8,128)(2,1)} %x_ref.1, f32[512,1024]{1,0:T(8,128)} %get-tuple-element.415.hidden_ref, f32[8,1024]{1,0:T(8,128)} %get-tuple-element.416.sums_ref, ...), custom_call_target="tpu_custom_call" | custom-call | flops 68719476736 | bytes 1048576 | tf_op jit(solution)/shard_map/pallas_call | solution.py:593
  335.5 11.4 %collective-permute-done.62 = bf16[8,128,256]{2,1,0:T(8,128)(2,1)} collective-permute-done((bf16[8,128,256]{2,1,0:T(8,128)(2,1)}, bf16[8,128,256]{2,1,0:T(8,128)(2,1)}, u32[]{:S(2)}, u32[]{:S(2)}) %collective-permute-start.62) | collective-permute-done | bytes 524320 | tf_op jit(solution)/shard_map/ppermute | solution.py:43
  362.1 9.4 %collective-permute-done.67 = bf16[1,128,1152]{2,1,0:T(8,128)(2,1)S(1)} collective-permute-done((bf16[1,128,1152]{2,1,0:T(8,128)(2,1)S(1)}, bf16[1,128,1152]{2,1,0:T(8,128)(2,1)S(1)}, u32[]{:S(2)}, u32[]{:S(2)}) %collective-permute-start.67) | collective-permute-done | bytes 294944 | tf_op jit(solution)/shard_map/ppermute | solution.py:43
  384.5 21.1 %collective-permute-done.72 = bf16[2,128,384]{2,1,0:T(8,128)(2,1)S(1)} collective-permute-done((bf16[2,128,384]{2,1,0:T(8,128)(2,1)S(1)}, bf16[2,128,384]{2,1,0:T(8,128)(2,1)S(1)}, u32[]{:S(2)}, u32[]{:S(2)}) %collective-permute-start.72) | collective-permute-done | bytes 196640 | tf_op jit(solution)/shard_map/ppermute | solution.py:43
  418.3 7.8 %collective-permute-done.78 = bf16[1,128,384]{2,1,0:T(8,128)(2,1)S(1)} collective-permute-done((bf16[1,128,384]{2,1,0:T(8,128)(2,1)S(1)}, bf16[1,128,384]{2,1,0:T(8,128)(2,1)S(1)}, u32[]{:S(2)}, u32[]{:S(2)}) %collective-permute-start.78) | collective-permute-done | bytes 98336 | tf_op jit(solution)/shard_map/ppermute | solution.py:43
  (360 shorter events, 161.6 us)
Async XLA Ops:
  11.7 25.6 %collective-permute-start.17 = (bf16[16,1024]{1,0:T(8,128)(2,1)S(1)}, bf16[16,1024]{1,0:T(8,128)(2,1)S(1)}, u32[]{:S(2)}, u32[]{:S(2)}) collective-permute-start(bf16[16,1024]{1,0:T(8,128)(2,1)S(1)} %slice.234), channel_id=1, source_target_pairs={{0,1},{1,2},{2,3},{3,4},{4,5},{5,6},{6,7},{8,9},{9,10},{10,11},{11... | collective-permute-start | bytes 98312 | tf_op jit(solution)/shard_map/ppermute | solution.py:677
  38.5 21.1 %collective-permute-start.13 = (bf16[1,128,1152]{2,1,0:T(8,128)(2,1)S(1)}, bf16[1,128,1152]{2,1,0:T(8,128)(2,1)S(1)}, u32[]{:S(2)}, u32[]{:S(2)}) collective-permute-start(bf16[1,128,1152]{2,1,0:T(8,128)(2,1)S(1)} %bitcast.46), channel_id=1, source_target_pairs={{0,4},{1,5},{2,6},{3,7},{4,0},{5,1},{6,2},{7,3},{8,12},{9,13},{10,... | collective-permute-start | bytes 884744 | tf_op jit(solution)/shard_map/ppermute | solution.py:43
  41.3 22.5 %collective-permute-start.12 = (bf16[1,128,1152]{2,1,0:T(8,128)(2,1)S(1)}, bf16[1,128,1152]{2,1,0:T(8,128)(2,1)S(1)}, u32[]{:S(2)}, u32[]{:S(2)}) collective-permute-start(bf16[1,128,1152]{2,1,0:T(8,128)(2,1)S(1)} %bitcast.48), channel_id=1, source_target_pairs={{0,4},{1,5},{2,6},{3,7},{4,0},{5,1},{6,2},{7,3},{8,12},{9,13},{10,... | collective-permute-start | bytes 884744 | tf_op jit(solution)/shard_map/ppermute | solution.py:43
  43.6 21.9 %collective-permute-start.9 = (bf16[8,128,384]{2,1,0:T(8,128)(2,1)S(1)}, bf16[8,128,384]{2,1,0:T(8,128)(2,1)S(1)}, u32[]{:S(2)}, u32[]{:S(2)}) collective-permute-start(bf16[8,128,384]{2,1,0:T(8,128)(2,1)S(1)} %pad_maximum_fusion.8), channel_id=1, source_target_pairs={{0,16},{8,24},{16,0},{24,8},{1,17},{9,25},{17,1},{25,9},{2,18},{10... | collective-permute-start | bytes 2359304 | tf_op jit(solution)/shard_map/ppermute | solution.py:43
  95.4 37.5 %collective-permute-start.25 = (bf16[4,128,1152]{2,1,0:T(8,128)(2,1)S(1)}, bf16[4,128,1152]{2,1,0:T(8,128)(2,1)S(1)}, u32[]{:S(2)}, u32[]{:S(2)}) collective-permute-start(bf16[4,128,1152]{2,1,0:T(8,128)(2,1)S(1)} %pad_maximum_fusion.2.refs_4_.refs_7_), channel_id=1, source_target_pairs={{0,1},{1,0},{2,3},{3,2},{4,5},{5,4},{6,7},{7,6},{8,9},{9,8},{10,11... | collective-permute-start | bytes 3538952 | tf_op jit(solution)/shard_map/ppermute | solution.py:43
  97.1 35.8 %collective-permute-start.26 = (bf16[4,128,1152]{2,1,0:T(8,128)(2,1)S(1)}, bf16[4,128,1152]{2,1,0:T(8,128)(2,1)S(1)}, u32[]{:S(2)}, u32[]{:S(2)}) collective-permute-start(bf16[4,128,1152]{2,1,0:T(8,128)(2,1)S(1)} %pad_maximum_fusion.3.refs_6_.refs_9_), channel_id=1, source_target_pairs={{0,2},{1,3},{2,0},{3,1},{4,6},{5,7},{6,4},{7,5},{8,10},{9,11},{10,... | collective-permute-start | bytes 3538952 | tf_op jit(solution)/shard_map/ppermute | solution.py:43
  100.5 32.3 %collective-permute-start.24 = (bf16[512,1024]{1,0:T(8,128)(2,1)S(1)}, bf16[512,1024]{1,0:T(8,128)(2,1)S(1)}, u32[]{:S(2)}, u32[]{:S(2)}) collective-permute-start(bf16[512,1024]{1,0:T(8,128)(2,1)S(1)} %copy-done.38), channel_id=1, source_target_pairs={{0,16},{8,24},{16,0},{24,8},{1,17},{9,25},{17,1},{25,9},{2,18},{10... | collective-permute-start | bytes 3145736 | tf_op jit(solution)/shard_map/ppermute | solution.py:43
  100.6 29.4 %collective-permute-start.28 = (bf16[1,288,256]{2,1,0:T(8,128)(2,1)S(1)}, bf16[1,288,256]{2,1,0:T(8,128)(2,1)S(1)}, u32[]{:S(2)}, u32[]{:S(2)}) collective-permute-start(bf16[1,288,256]{2,1,0:T(8,128)(2,1)S(1)} %get-tuple-element.500), channel_id=1, source_target_pairs={{0,4},{1,5},{2,6},{3,7},{4,0},{5,1},{6,2},{7,3},{8,12},{9,13},{10,... | collective-permute-start | bytes 442376 | tf_op jit(solution)/shard_map/ppermute | solution.py:43
  105.0 27.9 %collective-permute-start.27 = (bf16[1,288,256]{2,1,0:T(8,128)(2,1)S(1)}, bf16[1,288,256]{2,1,0:T(8,128)(2,1)S(1)}, u32[]{:S(2)}, u32[]{:S(2)}) collective-permute-start(bf16[1,288,256]{2,1,0:T(8,128)(2,1)S(1)} %get-tuple-element.501), channel_id=1, source_target_pairs={{0,4},{1,5},{2,6},{3,7},{4,0},{5,1},{6,2},{7,3},{8,12},{9,13},{10,... | collective-permute-start | bytes 442376 | tf_op jit(solution)/shard_map/ppermute | solution.py:43
  143.8 24.8 %collective-permute-start.35 = (bf16[512,1024]{1,0:T(8,128)(2,1)S(1)}, bf16[512,1024]{1,0:T(8,128)(2,1)S(1)}, u32[]{:S(2)}, u32[]{:S(2)}) collective-permute-start(bf16[512,1024]{1,0:T(8,128)(2,1)S(1)} %copy-done.15), channel_id=1, source_target_pairs={{0,16},{8,24},{16,0},{24,8},{1,17},{9,25},{17,1},{25,9},{2,18},{10... | collective-permute-start | bytes 3145736 | tf_op jit(solution)/shard_map/ppermute | solution.py:43
  184.0 33.0 %collective-permute-start.39 = (bf16[4,288,256]{2,1,0:T(8,128)(2,1)}, bf16[4,288,256]{2,1,0:T(8,128)(2,1)S(1)}, u32[]{:S(2)}, u32[]{:S(2)}) collective-permute-start(bf16[4,288,256]{2,1,0:T(8,128)(2,1)} %get-tuple-element.322), channel_id=1, source_target_pairs={{0,2},{1,3},{2,0},{3,1},{4,6},{5,7},{6,4},{7,5},{8,10},{9,11},{10,... | collective-permute-start | bytes 1769480 | tf_op jit(solution)/shard_map/ppermute | solution.py:43
  185.5 31.7 %collective-permute-start.38 = (bf16[4,288,256]{2,1,0:T(8,128)(2,1)}, bf16[4,288,256]{2,1,0:T(8,128)(2,1)S(1)}, u32[]{:S(2)}, u32[]{:S(2)}) collective-permute-start(bf16[4,288,256]{2,1,0:T(8,128)(2,1)} %get-tuple-element.320), channel_id=1, source_target_pairs={{0,1},{1,0},{2,3},{3,2},{4,5},{5,4},{6,7},{7,6},{8,9},{9,8},{10,11... | collective-permute-start | bytes 1769480 | tf_op jit(solution)/shard_map/ppermute | solution.py:43
  263.6 24.1 %collective-permute-start.53 = (bf16[1,288,256]{2,1,0:T(8,128)(2,1)}, bf16[1,288,256]{2,1,0:T(8,128)(2,1)}, u32[]{:S(2)}, u32[]{:S(2)}) collective-permute-start(bf16[1,288,256]{2,1,0:T(8,128)(2,1)} %get-tuple-element.387), channel_id=1, source_target_pairs={{0,4},{1,5},{2,6},{3,7},{4,0},{5,1},{6,2},{7,3},{8,12},{9,13},{10,... | collective-permute-start | bytes 442376 | tf_op jit(solution)/shard_map/ppermute | solution.py:43
  264.4 24.3 %collective-permute-start.54 = (bf16[1,288,256]{2,1,0:T(8,128)(2,1)}, bf16[1,288,256]{2,1,0:T(8,128)(2,1)}, u32[]{:S(2)}, u32[]{:S(2)}) collective-permute-start(bf16[1,288,256]{2,1,0:T(8,128)(2,1)} %get-tuple-element.389), channel_id=1, source_target_pairs={{0,4},{1,5},{2,6},{3,7},{4,0},{5,1},{6,2},{7,3},{8,12},{9,13},{10,... | collective-permute-start | bytes 442376 | tf_op jit(solution)/shard_map/ppermute | solution.py:43
  266.6 23.1 %collective-permute-start.48 = (bf16[2,128,1152]{2,1,0:T(8,128)(2,1)S(1)}, bf16[2,128,1152]{2,1,0:T(8,128)(2,1)S(1)}, u32[]{:S(2)}, u32[]{:S(2)}) collective-permute-start(bf16[2,128,1152]{2,1,0:T(8,128)(2,1)S(1)} %slice.256), channel_id=1, source_target_pairs={{0,1},{1,0},{2,3},{3,2},{4,5},{5,4},{6,7},{7,6},{8,9},{9,8},{10,11... | collective-permute-start | bytes 1769480 | tf_op jit(solution)/shard_map/ppermute | solution.py:43
  267.7 22.1 %collective-permute-start.49 = (bf16[2,128,1152]{2,1,0:T(8,128)(2,1)S(1)}, bf16[2,128,1152]{2,1,0:T(8,128)(2,1)S(1)}, u32[]{:S(2)}, u32[]{:S(2)}) collective-permute-start(bf16[2,128,1152]{2,1,0:T(8,128)(2,1)S(1)} %slice.258), channel_id=1, source_target_pairs={{0,2},{1,3},{2,0},{3,1},{4,6},{5,7},{6,4},{7,5},{8,10},{9,11},{10,... | collective-permute-start | bytes 1769480 | tf_op jit(solution)/shard_map/ppermute | solution.py:43
  319.9 28.1 %collective-permute-start.63 = (bf16[2,128,1152]{2,1,0:T(8,128)(2,1)}, bf16[2,128,1152]{2,1,0:T(8,128)(2,1)}, u32[]{:S(2)}, u32[]{:S(2)}) collective-permute-start(bf16[2,128,1152]{2,1,0:T(8,128)(2,1)} %add_convert_fusion.10), channel_id=1, source_target_pairs={{0,2},{1,3},{2,0},{3,1},{4,6},{5,7},{6,4},{7,5},{8,10},{9,11},{10,... | collective-permute-start | bytes 1769480 | tf_op jit(solution)/shard_map/ppermute | solution.py:43
  320.3 26.5 %collective-permute-start.62 = (bf16[8,128,256]{2,1,0:T(8,128)(2,1)}, bf16[8,128,256]{2,1,0:T(8,128)(2,1)}, u32[]{:S(2)}, u32[]{:S(2)}) collective-permute-start(bf16[8,128,256]{2,1,0:T(8,128)(2,1)} %get-tuple-element.424), channel_id=1, source_target_pairs={{0,2},{1,3},{2,0},{3,1},{4,6},{5,7},{6,4},{7,5},{8,10},{9,11},{10,... | collective-permute-start | bytes 1572872 | tf_op jit(solution)/shard_map/ppermute | solution.py:43
  322.0 27.5 %collective-permute-start.61 = (bf16[8,128,384]{2,1,0:T(8,128)(2,1)S(1)}, bf16[8,128,384]{2,1,0:T(8,128)(2,1)S(1)}, u32[]{:S(2)}, u32[]{:S(2)}) collective-permute-start(bf16[8,128,384]{2,1,0:T(8,128)(2,1)S(1)} %get-tuple-element.421), channel_id=1, source_target_pairs={{0,16},{8,24},{16,0},{24,8},{1,17},{9,25},{17,1},{25,9},{2,18},{10... | collective-permute-start | bytes 2359304 | tf_op jit(solution)/shard_map/ppermute | solution.py:43
  322.6 27.1 %collective-permute-start.60 = (bf16[8,128,384]{2,1,0:T(8,128)(2,1)S(1)}, bf16[8,128,384]{2,1,0:T(8,128)(2,1)S(1)}, u32[]{:S(2)}, u32[]{:S(2)}) collective-permute-start(bf16[8,128,384]{2,1,0:T(8,128)(2,1)S(1)} %get-tuple-element.419), channel_id=1, source_target_pairs={{0,1},{1,0},{2,3},{3,2},{4,5},{5,4},{6,7},{7,6},{8,9},{9,8},{10,11... | collective-permute-start | bytes 2359304 | tf_op jit(solution)/shard_map/ppermute | solution.py:43
  380.6 26.2 %collective-permute-start.56 = (bf16[512,1024]{1,0:T(8,128)(2,1)S(1)}, bf16[512,1024]{1,0:T(8,128)(2,1)S(1)}, u32[]{:S(2)}, u32[]{:S(2)}) collective-permute-start(bf16[512,1024]{1,0:T(8,128)(2,1)S(1)} %copy-done.16), channel_id=1, source_target_pairs={{0,8},{8,0},{16,24},{24,16},{1,9},{9,1},{17,25},{25,17},{2,10},{10... | collective-permute-start | bytes 3145736 | tf_op jit(solution)/shard_map/ppermute | solution.py:43
  380.6 25.3 %collective-permute-start.74 = (bf16[1,128,1152]{2,1,0:T(8,128)(2,1)S(1)}, bf16[1,128,1152]{2,1,0:T(8,128)(2,1)S(1)}, u32[]{:S(2)}, u32[]{:S(2)}) collective-permute-start(bf16[1,128,1152]{2,1,0:T(8,128)(2,1)S(1)} %get-tuple-element.453), channel_id=1, source_target_pairs={{0,4},{1,5},{2,6},{3,7},{4,0},{5,1},{6,2},{7,3},{8,12},{9,13},{10,... | collective-permute-start | bytes 884744 | tf_op jit(solution)/shard_map/ppermute | solution.py:43
  381.6 24.1 %collective-permute-start.72 = (bf16[2,128,384]{2,1,0:T(8,128)(2,1)S(1)}, bf16[2,128,384]{2,1,0:T(8,128)(2,1)S(1)}, u32[]{:S(2)}, u32[]{:S(2)}) collective-permute-start(bf16[2,128,384]{2,1,0:T(8,128)(2,1)S(1)} %get-tuple-element.449), channel_id=1, source_target_pairs={{0,4},{1,5},{2,6},{3,7},{4,0},{5,1},{6,2},{7,3},{8,12},{9,13},{10,... | collective-permute-start | bytes 589832 | tf_op jit(solution)/shard_map/ppermute | solution.py:43
  383.7 22.0 %collective-permute-start.71 = (bf16[2,128,384]{2,1,0:T(8,128)(2,1)S(1)}, bf16[2,128,384]{2,1,0:T(8,128)(2,1)S(1)}, u32[]{:S(2)}, u32[]{:S(2)}) collective-permute-start(bf16[2,128,384]{2,1,0:T(8,128)(2,1)S(1)} %get-tuple-element.447), channel_id=1, source_target_pairs={{0,2},{1,3},{2,0},{3,1},{4,6},{5,7},{6,4},{7,5},{8,10},{9,11},{10,... | collective-permute-start | bytes 589832 | tf_op jit(solution)/shard_map/ppermute | solution.py:43
  (110 other events, 1255.6 us)

commit v4 on v3

--- a/solution.py
+++ b/solution.py
@@ -53,19 +53,18 @@
     return [stack, swap(stack, step)]
 
 
-def scatter_step(parts, step):
+def exchanged(parts, step):
     keep, send = parts
-    total = keep.astype(jnp.float32) + swap(send, step).astype(jnp.float32)
+    return keep, swap(send, step)
+
+
+def folded(parts):
+    keep, come = parts
+    total = keep.astype(jnp.float32) + come.astype(jnp.float32)
     half = total.shape[0] // 2
     if not half:
         return total[0]
     return total[:half].astype(jnp.bfloat16), total[half:].astype(jnp.bfloat16)
-
-
-def scatter_steps(parts, steps):
-    for step in reversed(steps):
-        parts = scatter_step(parts, step)
-    return parts
 
 
 def masks_at(position, steps):
@@ -162,19 +161,25 @@
     return buffers[i % 2]
 
 
-def token_call(kernel, ids, blocks, tiled, stacks, outs, scratch):
+def token_call(kernel, ids, blocks, tiled, stacks, outs, apart, scratch):
     rows, width = blocks[0].shape
     rows, count, steps = rows // 2, len(blocks), 2 * len(blocks)
     return pl.pallas_call(
         kernel,
-        out_shape=[jax.ShapeDtypeStruct((rows * steps, n), t) for n, t in outs],
+        out_shape=[jax.ShapeDtypeStruct((rows * steps, n), t) for n, t in outs]
+        + [jax.ShapeDtypeStruct((rows * 2, n), t) for n, t in apart for _ in range(count)],
         grid_spec=pltpu.PrefetchScalarGridSpec(
             num_scalar_prefetch=1,
             grid=(steps,),
             in_specs=[pl.BlockSpec(memory_space=pl.ANY)] * count
             + [pl.BlockSpec((rows, v.shape[1]), lambda i, ids: (i, 0)) for v in tiled]
             + [pl.BlockSpec(memory_space=pl.ANY)] * len(stacks),
-            out_specs=[pl.BlockSpec((rows, n), lambda i, ids: (i, 0)) for n, _ in outs],
+            out_specs=[pl.BlockSpec((rows, n), lambda i, ids: (i, 0)) for n, _ in outs]
+            + [
+                pl.BlockSpec((rows, n), lambda i, ids, b=b: (jnp.clip(i - 2 * b, 0, 1), 0))
+                for n, _ in apart
+                for b in range(count)
+            ],
             scratch_shapes=[
                 pltpu.VMEM((2, rows, width), jnp.bfloat16),
                 pltpu.SemaphoreType.DMA((2,)),
@@ -221,6 +226,7 @@
         [],
         [*gate_stacks, *up_stacks],
         [(n, jnp.bfloat16)] * 3,
+        [],
         [pltpu.VMEM(shape, jnp.bfloat16)] * 2 + [pltpu.SemaphoreType.DMA((2,))],
     )
 
@@ -231,8 +237,10 @@
 
     def kernel(ids_ref, *refs):
         blocks, (act_ref, slope_ref, silu_ref) = refs[:count], refs[count : count + 3]
-        stacks, refs = refs[count + 3 : -10], refs[-10:]
-        grad_gate, grad_up, grad_norm, out, buffers, block_sems, gate_v, up_v, down_v, sems = refs
+        parts = 2 * count
+        stacks, refs = refs[count + 3 : -8 - parts], refs[-8 - parts :]
+        grad_gate, grad_up, buffers, block_sems, gate_v, up_v, down_v, sems = refs[:2] + refs[2 + parts :]
+        norm_parts, out_parts = refs[2 : 2 + count], refs[2 + count : 2 + parts]
 
         @pl.when(pl.program_id(0) == 0)
         def _():
@@ -253,8 +261,14 @@
         gu = (grad_act * silu_ref[...].astype(jnp.float32)).astype(jnp.bfloat16)
         grad_gate[...] = gg
         grad_up[...] = gu
-        out[...] = multiply(act_ref[...], down_v[...]).astype(jnp.bfloat16)
-        grad_norm[...] = (against(gg, gate_v[...]) + against(gu, up_v[...])).astype(jnp.bfloat16)
+        out = multiply(act_ref[...], down_v[...]).astype(jnp.bfloat16)
+        grad_norm = (against(gg, gate_v[...]) + against(gu, up_v[...])).astype(jnp.bfloat16)
+        for place in range(count):
+
+            @pl.when(pl.program_id(0) // 2 == place)
+            def _(place=place):
+                norm_parts[place][...] = grad_norm
+                out_parts[place][...] = out
 
     features, n = shape
     return token_call(
@@ -263,7 +277,8 @@
         final,
         [activated, slope, silu],
         [*gate_stacks, *up_stacks, *down_stacks],
-        [(n, jnp.bfloat16), (n, jnp.bfloat16), (features, jnp.bfloat16), (features, jnp.bfloat16)],
+        [(n, jnp.bfloat16)] * 2,
+        [(features, jnp.bfloat16)] * 2,
         [
             pltpu.VMEM(shape, jnp.bfloat16),
             pltpu.VMEM(shape, jnp.bfloat16),
@@ -412,16 +427,15 @@
     )(ids, extended, consts, *in_stacks, *out_stacks)
 
 
-def mixer_back(
-    ids, near, more, far, final, hidden, c_part, conv, gated, mixed, consts, out_pieces, out_stacks, slot_size
-):
-    rows, features = hidden.shape
+def mixer_back(ids, tiled, far, mixed, consts, out_pieces, out_stacks, out_grads, slot_size):
+    rows, features = tiled[0].shape
     tile = rows // 2
-    shapes = stack_shapes(out_pieces)
-
-    def kernel(
-        ids_ref, near_ref, more_ref, far_ref, final_ref, hidden_ref, c_ref, conv_ref, gated_ref, mixed_ref, const_ref, *refs
-    ):
+    shapes = stack_shapes(out_grads)
+
+    def kernel(ids_ref, *refs):
+        near_ref, more_ref, final_ref, hidden_ref, c_ref, conv_ref, gated_ref = refs[:7]
+        low_ref, high_ref, mixed_ref, const_ref = refs[7:11]
+        refs = refs[11:]
         stacks, refs = refs[: len(out_stacks)], refs[len(out_stacks) :]
         grad_hidden, grad_c, grad_mixed, head, sums = refs[:5]
         outs, (out_v, whole, mixed_s, conv_s, sems) = refs[5:-5], refs[-5:]
@@ -438,7 +452,7 @@
             conv_s[tile:] = conv_s[0:8]
 
         normed_grad = near_ref[...].astype(jnp.float32) + more_ref[...].astype(jnp.float32)
-        normed_grad += far_ref[...].astype(jnp.float32)
+        normed_grad += jnp.where(i == 0, high_ref[...].astype(jnp.float32), low_ref[...].astype(jnp.float32))
         h = hidden_ref[...]
         scale = lax.rsqrt(jnp.mean(h * h, axis=1, keepdims=True) + norm_eps)
         weighted = normed_grad * const_ref[1:2]
@@ -472,7 +486,7 @@
             head[0:1] = live * const_ref[2:3] * conv_s[0:1]
             head[1:2] = live * (const_ref[2:3] * conv_s[1:2] + const_ref[3:4] * conv_s[0:1])
             out_v[...] = (whole[...] + outer).astype(jnp.bfloat16)
-            start_stores(ids_ref, out_v, out_pieces, outs, sems.at[0])
+            start_stores(ids_ref, out_v, out_grads, outs, sems.at[0])
             wait_whole(out_v, sems.at[0])
 
         @pl.when(i == 0)
@@ -490,7 +504,8 @@
         grid_spec=pltpu.PrefetchScalarGridSpec(
             num_scalar_prefetch=1,
             grid=(2,),
-            in_specs=[part] * 8
+            in_specs=[part] * 7
+            + [pl.BlockSpec((tile, features), lambda i, ids: (0, 0))] * 2
             + [pl.BlockSpec((rows + HALO, features), lambda i, ids: (0, 0)), once]
             + [pl.BlockSpec(memory_space=pl.ANY)] * len(out_stacks),
             out_specs=[part] * 3 + [once] * 2 + [pl.BlockSpec(memory_space=pl.ANY)] * len(shapes),
@@ -504,7 +519,7 @@
         ),
         compiler_params=pltpu.CompilerParams(vmem_limit_bytes=VMEM_BYTES),
         cost_estimate=KERNEL_COST,
-    )(ids, near, more, far, final, hidden, c_part, conv, gated, mixed, consts, *out_stacks)
+    )(ids, *tiled, *far, mixed, consts, *out_stacks)
     return [*parts[:5], paired(parts[5:])]
 
 
@@ -659,11 +674,67 @@
     out_rows, out_cols = out_weight.shape
     in_cut = (in_cols // 128 + 1) // 2 * 128
     in_cuts = [0, in_cut, in_cols]
+    third = in_cols // 3
     small_cols = mixer_gain.shape[0]
     small = jnp.concatenate([mixer_gain[None], feed_gain[None], conv_weight], axis=0)
     small = jnp.pad(small, ((0, SMALL_ROWS - small.shape[0]), (0, -small_cols % 128)))
     small_order = zs + ys
+    mixer = [in_weight[None, :, :in_cut], in_weight[None, :, in_cut:], out_weight[None]]
+    orders = [*in_orders, out_order]
+    hidden_units = gate_weight.shape[1]
+    gate_rows = gate_weight.shape[0]
+    down_rows, down_cols = down_weight.shape
+    ratio = n_seq // n_dp
+    turned = [(e % 2) * (n_dp // 2) + e // 2 for e in range(n_dp)]
+    home = [
+        (e * n_seq + s, (s // ratio) * n_seq + turned[e] * ratio + s % ratio)
+        for e in range(n_dp)
+        for s in range(n_seq)
+    ]
+    cuts = [0, -(-down_rows // 32) * 16, down_rows]
+
+    def gate_view(ref, dp, seq):
+        return ref.at[pl.ds(pl.multiple_of(seq * gate_rows, gate_rows), gate_rows)]
+
+    def down_view(cut):
+        low, high = cuts[cut], cuts[cut + 1]
+
+        def view(ref, dp, seq):
+            row = pl.multiple_of((seq % ratio) * down_rows + low, 16)
+            place = seq // ratio
+            place = place % (n_dp // 2) * 2 + place // (n_dp // 2)
+            col = pl.multiple_of(place * down_cols, down_cols)
+            return ref.at[pl.ds(row, high - low), pl.ds(col, down_cols)]
+
+        return view
+
+    gate = [Piece(near_order, gate_weight.shape, gate_view)]
+    up = [Piece(far_order, up_weight.shape, gate_view)]
+    down = [
+        Piece(order, (cuts[i + 1] - cuts[i], down_cols), down_view(i))
+        for i, order in enumerate((near_order, far_order))
+    ]
+
+    def with_core(blocks):
+        return blocks + [swap(v, core[0]) for v in blocks]
+
+    grad_final = (live_mask * cotangent.astype(jnp.float32)).astype(jnp.bfloat16)
+    middle = len(orders[0]) // 2
+    z_first, last = len(zs) // 2, len(zs) + len(ys) - 1
+    mixer = [gather_steps(v, order[:1]) for v, order in zip(mixer, orders)]
+    mixer, small, tokens = tie(mixer, small, tokens)
+    mixer = [gather_steps(v, order[1:middle]) for v, order in zip(mixer, orders)]
+    before = lax.ppermute(
+        tokens[tok_rows - HALO :], "seq", [(i, i + 1) for i in range(n_seq - 1)]
+    )
     small = gather_steps(small[None], small_order)
+    mixer, gate_weight, up_weight = tie(mixer, gate_weight, up_weight)
+    mixer = [gather_steps(v, order[middle:-1]) for v, order in zip(mixer, orders)]
+    gate_up = [
+        gather_steps(v[None], p.steps[:z_first])
+        for v, p in zip((gate_weight, up_weight), (*gate, *up))
+    ]
+    extended = jnp.concatenate([before, tokens], axis=0)
     places = jnp.stack([jnp.int32(masks_at(p, small_order)[1]) for p in range(n_seq)])
     chosen = (own_seq ^ jnp.arange(n_seq))[:, None] == places[None]
     consts = jnp.einsum(
@@ -672,61 +743,13 @@
         small[:, :8, :small_cols],
         preferred_element_type=jnp.float32,
     ).reshape(8, features)
-    mixer = [in_weight[None, :, :in_cut], in_weight[None, :, in_cut:], out_weight[None]]
-    orders = [*in_orders, out_order]
-    before = lax.ppermute(
-        tokens[tok_rows - HALO :], "seq", [(i, i + 1) for i in range(n_seq - 1)]
-    )
-    extended = jnp.concatenate([before, tokens], axis=0)
-    hidden_units = gate_weight.shape[1]
-    gate_rows = gate_weight.shape[0]
-    down_rows, down_cols = down_weight.shape
-    ratio = n_seq // n_dp
-    home = [
-        (e * n_seq + s, (s // ratio) * n_seq + e * ratio + s % ratio)
-        for e in range(n_dp)
-        for s in range(n_seq)
-    ]
-    cuts = [0, -(-down_rows // 32) * 16, down_rows]
-
-    def gate_view(ref, dp, seq):
-        return ref.at[pl.ds(pl.multiple_of(seq * gate_rows, gate_rows), gate_rows)]
-
-    def down_view(cut):
-        low, high = cuts[cut], cuts[cut + 1]
-
-        def view(ref, dp, seq):
-            row = pl.multiple_of((seq % ratio) * down_rows + low, 16)
-            col = pl.multiple_of((seq // ratio) * down_cols, down_cols)
-            return ref.at[pl.ds(row, high - low), pl.ds(col, down_cols)]
-
-        return view
-
-    gate = [Piece(near_order, gate_weight.shape, gate_view)]
-    up = [Piece(far_order, up_weight.shape, gate_view)]
-    down = [
-        Piece(order, (cuts[i + 1] - cuts[i], down_cols), down_view(i))
-        for i, order in enumerate((near_order, far_order))
-    ]
-
-    grad_final = (live_mask * cotangent.astype(jnp.float32)).astype(jnp.bfloat16)
-    middle = len(orders[0]) // 2
-    z_first, last = len(zs) // 2, len(zs) + len(ys) - 1
-    mixer = [gather_steps(v, order[:middle]) for v, order in zip(mixer, orders)]
-    mixer, gate_weight, up_weight = tie(mixer, gate_weight, up_weight)
-    mixer = [gather_steps(v, order[middle:-1]) for v, order in zip(mixer, orders)]
-    gate_up = [
-        gather_steps(v[None], p.steps[:z_first])
-        for v, p in zip((gate_weight, up_weight), (*gate, *up))
-    ]
     mixer, gate_up, consts, extended, down_weight, grad_final = tie(
         mixer, gate_up, consts, extended, down_weight, grad_final
     )
     stacks = [last_step(v, order[-1]) for v, order in zip(mixer, orders)]
     stacks, gate_up, down_weight, grad_final = tie(stacks, gate_up, down_weight, grad_final)
 
-    def in_view(cut):
-        low, high = in_cuts[cut], in_cuts[cut + 1]
+    def in_view(low, high):
 
         def view(ref, dp, seq):
             row = pl.multiple_of(seq * in_rows, in_rows)
@@ -739,9 +762,14 @@
         return tile_of(ref, seq, out_rows, dp, out_cols)
 
     in_pieces = [
-        Piece(order, (in_rows, in_cuts[i + 1] - in_cuts[i]), in_view(i))
+        Piece(order, (in_rows, in_cuts[i + 1] - in_cuts[i]), in_view(in_cuts[i], in_cuts[i + 1]))
         for i, order in enumerate(in_orders)
     ]
+    in_grads = [
+        Piece(order, (in_rows, third), in_view(i * third, (i + 1) * third))
+        for i, order in enumerate(orders)
+    ]
+    out_grads = [Piece(zs + xs + ys + core, out_weight.shape, out_view)]
     out_pieces = [Piece(out_order, out_weight.shape, out_view)]
     in_stacks, out_stacks = stacks[0] + stacks[1], stacks[2]
 
@@ -752,12 +780,6 @@
     )
     forward, gate_up, down_shard, grad_final = tie(forward, gate_up, down_shard, grad_final)
     normed_one, b_part, c_part, x_part, mixed, conv, gated, hidden, normed_two = forward
-
-    def split_rows(v):
-        return [v[i : i + tok_rows] for i in range(0, v.shape[0], tok_rows)]
-
-    def with_core(blocks):
-        return blocks + [swap(v, core[0]) for v in blocks]
 
     wide = (features, hidden_units)
     gate_stacks, up_stacks = [last_step(v, p.steps[-1]) for v, p in zip(gate_up, (*gate, *up))]
@@ -770,17 +792,18 @@
         normed_two, normed_there, gate_stacks, up_stacks, downs, grad_final
     )
     normed_blocks = with_core([normed_two]) + with_core(normed_there)
-    downs = [gather_steps(v, p.steps[z_first:last]) for v, p in zip(downs, down)]
     normed_blocks, downs, gate_stacks, up_stacks, grad_final = tie(
         normed_blocks, downs, gate_stacks, up_stacks, grad_final
     )
+    final_there = dp_gather(grad_final, xs)[1:]
+    final_near = swap(grad_final, core[0])
+    downs = [gather_steps(v, p.steps[z_first:last]) for v, p in zip(downs, down)]
+    activated, slope, silu = feed_up(ids, normed_blocks, gate, gate_stacks, up, up_stacks, wide)
+    activated, downs, grad_final, final_near, final_there = tie(
+        activated, downs, grad_final, final_near, final_there
+    )
+    final_blocks = [grad_final, final_near] + with_core(final_there)
     down_stacks = [v for stack, p in zip(downs, down) for v in last_step(stack, p.steps[-1])]
-    final_there = dp_gather(grad_final, xs)[1:]
-    activated, slope, silu = feed_up(ids, normed_blocks, gate, gate_stacks, up, up_stacks, wide)
-    activated, down_stacks, grad_final, final_there = tie(
-        activated, down_stacks, grad_final, final_there
-    )
-    final_blocks = with_core([grad_final]) + with_core(final_there)
     down_parts = weight_gradient(ids, [activated], final_blocks, down)
     down_parts, down_stacks = tie(down_parts, down_stacks)
 
@@ -790,11 +813,11 @@
     def upper(parts):
         return tuple(v[v.shape[0] // 2 :] for v in parts)
 
-    def one_step(parts, pieces, place):
-        return [scatter_step(v, p.steps[place]) for v, p in zip(parts, pieces)]
-
-    def exchanged(parts, step):
-        return (parts[0], swap(parts[1], step))
+    def sent(parts, pieces, place):
+        return [exchanged(v, p.steps[place]) for v, p in zip(parts, pieces)]
+
+    def fold_all(parts):
+        return [folded(v) for v in parts]
 
     def added(low, high):
         return tuple(
@@ -803,108 +826,153 @@
         )
 
     def core_halves(v):
-        blocks = split_rows(v)
-        near, far = blocks[:2], blocks[2:]
+        near, far = v[:2], v[2:]
         half = len(far) // 2
         return near[0], near[1], far[:half], far[half:]
 
-    down_parts = one_step(down_parts, down, -1)
-    grad_gate, grad_up, back, feed = feed_back(
+    def far_added(keep, come):
+        return [
+            (a.astype(jnp.float32) + b.astype(jnp.float32)).astype(jnp.bfloat16)
+            for a, b in zip(keep, come)
+        ]
+
+    down_parts = sent(down_parts, down, -1)
+    grad_gate, grad_up, *back = feed_back(
         ids, final_blocks, activated, slope, silu, gate, gate_stacks, up, up_stacks, down, down_stacks, wide
     )
+    back, feed = back[:n_dp], back[n_dp:]
     back, feed, grad_gate, grad_up, down_parts = tie(back, feed, grad_gate, grad_up, down_parts)
     near, near_send, far, far_send = core_halves(back)
-    far = dp_scatter(far + far_send, core)
-    far, near, near_send, grad_gate, grad_up, feed = tie(far, near, near_send, grad_gate, grad_up, feed)
-    far = [v.astype(jnp.bfloat16) for v in far]
+    far_come = [swap(v, core[0]) for v in far_send]
+    far, far_come, near, near_send, grad_gate, grad_up, feed, down_parts = tie(
+        far, far_come, near, near_send, grad_gate, grad_up, feed, down_parts
+    )
+    far = far_added(far, far_come)
     half_rows = tok_rows // 2
-    far_low = dp_scatter([None] + [v[:half_rows] for v in far], xs)
+    far_low, far_high = [v[:half_rows] for v in far], [v[half_rows:] for v in far]
+    down_parts = fold_all(down_parts)
+    far_low, far_high, down_parts, near, near_send, grad_gate, grad_up, feed = tie(
+        far_low, far_high, down_parts, near, near_send, grad_gate, grad_up, feed
+    )
+    far_low = dp_scatter([None] + far_low, xs)
     near_more = swap(near_send, core[0])
-    feed_near, feed_send, feed_far, feed_far_send = core_halves(feed)
-    down_parts = one_step(down_parts, down, -2)
+    down_parts = sent(down_parts, down, -2)
     gate_parts = weight_gradient(ids, normed_blocks, [grad_gate], gate)
-    gate_parts, far, far_low, grad_up, near, near_more, down_parts, feed_far, feed_far_send = tie(
-        gate_parts, far, far_low, grad_up, near, near_more, down_parts, feed_far, feed_far_send
-    )
-    far_high = dp_scatter([None] + [v[half_rows:] for v in far], xs)
-    gate_low = exchanged(lower(gate_parts[0]), gate[0].steps[-1])
-    feed_far = [v.astype(jnp.bfloat16) for v in dp_scatter(feed_far + feed_far_send, core)]
+    gate_parts, far_low, far_high, grad_up, near, near_more, down_parts, feed = tie(
+        gate_parts, far_low, far_high, grad_up, near, near_more, down_parts, feed
+    )
+    down_parts = fold_all(down_parts)
+    gate_low, gate_high = lower(gate_parts[0]), upper(gate_parts[0])
+    feed_near, feed_send, feed_far, feed_come = core_halves(feed)
+    down_parts, gate_low, gate_high, feed_far, feed_come, grad_up, far_low, far_high = tie(
+        down_parts, gate_low, gate_high, feed_far, feed_come, grad_up, far_low, far_high
+    )
+    far_high = dp_scatter([None] + far_high, xs)
+    gate_low = exchanged(gate_low, gate[0].steps[-1])
+    feed_come = [swap(v, core[0]) for v in feed_come]
+    down_parts = sent(down_parts, down, -3)
     up_parts = weight_gradient(ids, normed_blocks, [grad_up], up)
-    up_parts, far_low, far_high, gate_low, gate_parts, feed_far, down_parts = tie(
-        up_parts, far_low, far_high, gate_low, gate_parts, feed_far, down_parts
-    )
-
-    gate_high = exchanged(upper(gate_parts[0]), gate[0].steps[-1])
-    up_low = exchanged(lower(up_parts[0]), up[0].steps[-1])
-    feed_low = dp_scatter([None] + [v[:half_rows] for v in feed_far], xs)
-    far = jnp.concatenate(far_low + far_high, axis=0)
+    up_parts, far_low, far_high, gate_low, gate_high, feed_far, feed_come, down_parts = tie(
+        up_parts, far_low, far_high, gate_low, gate_high, feed_far, feed_come, down_parts
+    )
+
+    feed_far = far_added(feed_far, feed_come)
+    feed_low, feed_high = [v[:half_rows] for v in feed_far], [v[half_rows:] for v in feed_far]
+    up_low, up_high = lower(up_parts[0]), upper(up_parts[0])
+    own_down = fold_all(down_parts)
+    for place in range(len(down[0].steps) - 4, -1, -1):
+        own_down = fold_all(sent(own_down, down, place))
+    own_down = jnp.concatenate(own_down, axis=0).astype(jnp.bfloat16)
+    feed_low, feed_high, up_low, up_high, gate_low, gate_high, far_low, far_high, own_down = tie(
+        feed_low, feed_high, up_low, up_high, gate_low, gate_high, far_low, far_high, own_down
+    )
+    gate_high = exchanged(gate_high, gate[0].steps[-1])
+    up_low = exchanged(up_low, up[0].steps[-1])
+    feed_low = dp_scatter([None] + feed_low, xs)
+    own_down = lax.ppermute(own_down, ("dp", "seq"), [(b, a) for a, b in home])
     grad_hidden, grad_c, grad_mixed, first_rows, sums, out_parts = mixer_back(
         ids,
-        near,
-        near_more,
-        far,
-        grad_final,
-        hidden,
-        c_part,
-        conv,
-        gated,
+        [near, near_more, grad_final, hidden, c_part, conv, gated],
+        far_low + far_high,
         mixed,
         consts,
         out_pieces,
         out_stacks,
+        out_grads,
         slot_size,
     )
-    out_parts, grad_mixed, first_rows, gate_low, gate_high, up_low, up_parts, feed_far, feed_low = tie(
-        out_parts, grad_mixed, first_rows, gate_low, gate_high, up_low, up_parts, feed_far, feed_low
+    out_parts, grad_mixed, first_rows, gate_low, gate_high, up_low, up_high, feed_low, feed_high, own_down = tie(
+        out_parts, grad_mixed, first_rows, gate_low, gate_high, up_low, up_high, feed_low, feed_high, own_down
     )
     returned = lax.ppermute(first_rows, "seq", [(i + 1, i) for i in range(n_seq - 1)])
-    up_high = exchanged(upper(up_parts[0]), up[0].steps[-1])
-    feed_high = dp_scatter([None] + [v[half_rows:] for v in feed_far], xs)
-    own_down = [scatter_steps(v, p.steps[:-2]) for v, p in zip(down_parts, down)]
-    own_down = jnp.concatenate(own_down, axis=0).astype(jnp.bfloat16)
+    out_parts = fold_all(sent(out_parts, out_grads, -1))
+    gate_parts = added(gate_low, gate_high)
+    returned, out_parts, up_high, gate_parts, feed_high = tie(
+        returned, out_parts, up_high, gate_parts, feed_high
+    )
+    up_high = exchanged(up_high, up[0].steps[-1])
+    out_parts = sent(out_parts, out_grads, -2)
+    feed_high = dp_scatter([None] + feed_high, xs)
     grad_proj, in_parts = projection_gradient(
-        ids, normed_one, grad_mixed, returned, grad_c, b_part, x_part, in_pieces
-    )
-    in_parts, up_low, up_high, own_down, gate_low, gate_high, grad_proj, out_parts, feed_high = tie(
-        in_parts, up_low, up_high, own_down, gate_low, gate_high, grad_proj, out_parts, feed_high
-    )
-    in_parts = one_step(in_parts, in_pieces, -1)
-    out_parts = one_step(out_parts, out_pieces, -1)
-    in_parts, out_parts, grad_proj, gate_low, gate_high, up_low, up_high = tie(
-        in_parts, out_parts, grad_proj, gate_low, gate_high, up_low, up_high
-    )
-    in_parts = one_step(in_parts, in_pieces, -2)
-    out_parts = one_step(out_parts, out_pieces, -2)
-    gate_parts = scatter_step(added(gate_low, gate_high), gate[0].steps[-2])
-    up_parts = added(up_low, up_high)
+        ids, normed_one, grad_mixed, returned, grad_c, b_part, x_part, in_grads
+    )
+    in_parts, up_low, up_high, gate_parts, grad_proj, out_parts, feed_high = tie(
+        in_parts, up_low, up_high, gate_parts, grad_proj, out_parts, feed_high
+    )
+    up_parts, out_parts = added(up_low, up_high), fold_all(out_parts)
+    in_parts, up_parts, gate_parts, out_parts, grad_proj = tie(
+        in_parts, up_parts, gate_parts, out_parts, grad_proj
+    )
+    in_parts = sent(in_parts, in_grads, -1)
+    out_parts = sent(out_parts, out_grads, -3)
+    gate_parts = exchanged(gate_parts, gate[0].steps[-2])
+    up_parts = exchanged(up_parts, up[0].steps[-2])
     grad_tokens, sums = mixer_first(ids, grad_proj, tokens, grad_hidden, sums, consts, in_pieces, in_stacks)
-    in_parts, sums, out_parts, gate_parts, up_parts, own_down = tie(
-        in_parts, sums, out_parts, gate_parts, up_parts, own_down
-    )
-    in_parts = one_step(in_parts, in_pieces, -3)
-    out_parts = one_step(out_parts, out_pieces, -3)
-    own_gate = scatter_steps(gate_parts, gate[0].steps[:-2])
-    up_parts = scatter_step(up_parts, up[0].steps[-2])
-    sum_steps = zs + ys + xs + core
-    for step in sum_steps[:2]:
+    in_parts, out_parts, sums, gate_parts, up_parts, feed_send = tie(
+        in_parts, out_parts, sums, gate_parts, up_parts, feed_send
+    )
+    sum_steps = core + ys + xs + zs[::-1]
+    for step in sum_steps[:1]:
         sums = sums + swap(sums, step)
-    in_parts, out_parts, own_gate, up_parts, sums, own_down = tie(
-        in_parts, out_parts, own_gate, up_parts, sums, own_down
-    )
-    own_in = [scatter_step(v, p.steps[-4]) for v, p in zip(in_parts, in_pieces)]
-    own_up = scatter_steps(up_parts, up[0].steps[:-2])
-    out_parts = one_step(out_parts, out_pieces, -4)
-    for step in sum_steps[2:4]:
-        sums = sums + swap(sums, step)
-    own_in, out_parts, own_up, sums, own_down = tie(own_in, out_parts, own_up, sums, own_down)
-    own_in = [scatter_steps(v, p.steps[:-4]) for v, p in zip(own_in, in_pieces)]
-    own_in = jnp.concatenate(own_in, axis=1)
-    own_out = scatter_steps(out_parts[0], out_order[:-4])
+    in_parts, out_parts, gate_parts, up_parts = fold_all(in_parts), fold_all(out_parts), folded(gate_parts), folded(up_parts)
+    in_parts, out_parts, gate_parts, up_parts, sums = tie(in_parts, out_parts, gate_parts, up_parts, sums)
+    in_parts = sent(in_parts, in_grads, -2)
+    out_parts = sent(out_parts, out_grads, -4)
+    gate_parts = exchanged(gate_parts, gate[0].steps[-3])
+    sums = (sums, swap(sums, sum_steps[1]))
+    in_parts, out_parts, gate_parts, up_parts, sums, feed_send = tie(
+        in_parts, out_parts, gate_parts, up_parts, sums, feed_send
+    )
+    in_parts, out_parts, sums = fold_all(in_parts), fold_all(out_parts), sums[0] + sums[1]
+    in_parts, out_parts, up_parts, sums = tie(in_parts, out_parts, up_parts, sums)
+    in_parts = sent(in_parts, in_grads, -3)
+    out_parts = sent(out_parts, out_grads, -5)
+    up_parts = exchanged(up_parts, up[0].steps[-3])
+    sums = (sums, swap(sums, sum_steps[2]))
+    in_parts, out_parts, up_parts, sums, feed_send = tie(in_parts, out_parts, up_parts, sums, feed_send)
+    in_parts, sums = fold_all(in_parts), sums[0] + sums[1]
+    in_parts, sums = tie(in_parts, sums)
+    in_parts = sent(in_parts, in_grads, -4)
+    sums = (sums, swap(sums, sum_steps[3]))
+    feed_more = swap(feed_send, core[0])
+    in_parts, sums, feed_more = tie(in_parts, sums, feed_more)
+    sums = sums[0] + sums[1]
     for step in sum_steps[4:]:
         sums = sums + swap(sums, step)
-    own_down = lax.ppermute(own_down, ("dp", "seq"), [(b, a) for a, b in home]).astype(jnp.float32)
+    own_down = own_down.astype(jnp.float32)
+
+    def rest(parts, piece, done):
+        parts = folded(parts)
+        for place in range(len(piece.steps) - done - 1, -1, -1):
+            parts = folded(exchanged(parts, piece.steps[place]))
+        return parts
+
+    own_in = [rest(v, p, 4) for v, p in zip(in_parts, in_grads)]
+    own_in = jnp.concatenate(own_in, axis=1)
+    own_out = rest(out_parts[0], out_grads[0], 5)
+    own_gate = rest(gate_parts, gate[0], 3)
+    own_up = rest(up_parts, up[0], 3)
     own_sums = lax.dynamic_slice(sums, (0, own_seq * small_cols), (8, small_cols))
-    feed_more = swap(feed_send, core[0])
     feed_out = jnp.concatenate(feed_low + feed_high, axis=0).astype(jnp.float32)
     feed_out = feed_out + feed_near.astype(jnp.float32) + feed_more.astype(jnp.float32)
     output = (live_mask * (hidden + feed_out)).astype(jnp.bfloat16)

time: 436 us -> 414 us (0.950)
  waiting for transfers between devices: 159 us -> 150 us
  other arithmetic: 27.5 us -> 19.5 us
    ppermute x78 -> x83, waiting for transfers between devices: 159 us -> 149 us  [swap(): return lax.ppermute(shard, axis, [(i, i ^ bit) for i in range(count)])]
    slice x28 -> x24, local copies, waits for them, and re-layouts: 9.32 us -> 0.93 us  [the longest x22 0.79 us: folded(): total[half:].astype(jnp.bfloat16)]
    unnamed x105 -> x103, local copies, waits for them, and re-layouts: 5.4 us -> 11.1 us
    ppermute x78 -> x83, starting transfers between devices: 80.8 us -> 79.3 us  [swap(): return lax.ppermute(shard, axis, [(i, i ^ bit) for i in range(count)])]
  transfers between devices with their start and end apart: 82 -> 87, of which waited for: 34 -> 37; matrix products, arithmetic and copies ran while one was open for 8% -> 4% of each run, Pallas kernels for 29% -> 34%
where the time goes in v4:
time: 414 us; the launch traced here: 410 us
  waiting for transfers between devices  150 us (36%)
  Pallas kernels  137 us (33%)
  starting transfers between devices  84.7 us (20%)
  other arithmetic  19.5 us (5%)
  local copies, waits for them, and re-layouts  14.5 us (4%)
    ppermute x83, waiting for transfers between devices, swap(): return lax.ppermute(shard, axis, [(i, i ^ bit) for i in range(count)])  149 us
    ppermute x83, starting transfers between devices, swap(): return lax.ppermute(shard, axis, [(i, i ^ bit) for i in range(count)])  79.3 us
    pallas_call x2, Pallas kernels, token_call(): pl.pallas_call(kernel, out_shape=[jax.ShapeDtypeStruct((rows * steps, n),...  51.9 us
    pallas_call x3, Pallas kernels, weight_gradient(): pl.pallas_call(kernel, out_shape=shapes, grid_spec=pltpu.PrefetchScalarGr...  32.8 us
    pallas_call x1, Pallas kernels, mixer_back(): pl.pallas_call(kernel, out_shape=[jax.ShapeDtypeStruct((rows, features),...  14.6 us
    pallas_call x1, Pallas kernels, mixer_forward(): pl.pallas_call(kernel, out_shape=[jax.ShapeDtypeStruct(s, t) for s, t in...  13.9 us
    pallas_call x1, Pallas kernels, projection_gradient(): pl.pallas_call(kernel, out_shape=[jax.ShapeDtypeStruct((rows, 3 * feature...  13.5 us
    unnamed x103, local copies, waits for them, and re-layouts  11.1 us
  transfers between devices with their start and end apart: 87, of which 37 were waited for; matrix products, arithmetic and copies ran while one was open for 4% of the time, Pallas kernels for 34%

profile of v4, /device:TPU:0, one launch (start us, length us, event | category | flops | bytes accessed | tf_op | source)
XLA Modules:
  0.0 409.7 jit_solution(1609853457845180535)
XLA Ops:
  0.7 4.1 %collective-permute-start.2 = (bf16[1,128,256]{2,1,0:T(8,128)(2,1)}, bf16[1,128,256]{2,1,0:T(8,128)(2,1)S(1)}, u32[]{:S(2)}, u32[]{:S(2)}) collective-permute-start(bf16[1,128,256]{2,1,0:T(8,128)(2,1)} %bitcast.51), channel_id=1, source_target_pairs={{0,4},{1,5},{2,6},{3,7},{4,0},{5,1},{6,2},{7,3},{8,12},{9,13},{10,... | collective-permute-start | bytes 196616 | tf_op jit(solution)/shard_map/ppermute | solution.py:43
  25.2 5.1 %collective-permute-done.4 = bf16[2,128,384]{2,1,0:T(8,128)(2,1)S(1)} collective-permute-done((bf16[2,128,384]{2,1,0:T(8,128)(2,1)S(1)}, bf16[2,128,384]{2,1,0:T(8,128)(2,1)S(1)}, u32[]{:S(2)}, u32[]{:S(2)}) %collective-permute-start.4) | collective-permute-done | bytes 196640 | tf_op jit(solution)/shard_map/ppermute | solution.py:43
  44.2 9.5 %collective-permute-done.8 = bf16[4,128,384]{2,1,0:T(8,128)(2,1)S(1)} collective-permute-done((bf16[4,128,384]{2,1,0:T(8,128)(2,1)S(1)}, bf16[4,128,384]{2,1,0:T(8,128)(2,1)S(1)}, u32[]{:S(2)}, u32[]{:S(2)}) %collective-permute-start.8) | collective-permute-done | bytes 393248 | tf_op jit(solution)/shard_map/ppermute | solution.py:43
  55.1 5.6 %collective-permute-done.13 = bf16[1,128,1152]{2,1,0:T(8,128)(2,1)S(1)} collective-permute-done((bf16[1,128,1152]{2,1,0:T(8,128)(2,1)S(1)}, bf16[1,128,1152]{2,1,0:T(8,128)(2,1)S(1)}, u32[]{:S(2)}, u32[]{:S(2)}) %collective-permute-start.13) | collective-permute-done | bytes 294944 | tf_op jit(solution)/shard_map/ppermute | solution.py:43
  60.8 3.9 collective-permute-done.12
  64.7 4.6 %collective-permute-done.11 = bf16[8,128,256]{2,1,0:T(8,128)(2,1)S(1)} collective-permute-done((bf16[8,128,256]{2,1,0:T(8,128)(2,1)S(1)}, bf16[8,128,256]{2,1,0:T(8,128)(2,1)S(1)}, u32[]{:S(2)}, u32[]{:S(2)}) %collective-permute-start.11) | collective-permute-done | bytes 524320 | tf_op jit(solution)/shard_map/ppermute | solution.py:43
  73.5 6.3 %collective-permute-done.20.refs_5_.refs_12_ = bf16[16,128,256]{2,1,0:T(8,128)(2,1)} collective-permute-done((bf16[16,128,256]{2,1,0:T(8,128)(2,1)}, bf16[16,128,256]{2,1,0:T(8,128)(2,1)}, u32[]{:S(2)}, u32[]{:S(2)}) %collective-permute-start.20) | collective-permute-done | bytes 1048608 | tf_op jit(solution)/shard_map/ppermute | solution.py:43
  85.5 13.9 %shard_map.186 = (bf16[512,1024]{1,0:T(8,128)(2,1)}, f32[512,1024]{1,0:T(8,128)}, f32[512,1024]{1,0:T(8,128)}, f32[512,1024]{1,0:T(8,128)}, bf16[528,1024]{1,0:T...) custom-call(s32[2]{0:T(128)} %pad_add_fusion.ids_ref, ...), custom_call_target="tpu_custom_call" | custom-call | flops 68719476736 | bytes 1048576 | tf_op jit(solution)/shard_map/pallas_call | solution.py:409
  99.4 7.6 %collective-permute-done.21 = bf16[2,128,1152]{2,1,0:T(8,128)(2,1)S(1)} collective-permute-done((bf16[2,128,1152]{2,1,0:T(8,128)(2,1)S(1)}, bf16[2,128,1152]{2,1,0:T(8,128)(2,1)S(1)}, u32[]{:S(2)}, u32[]{:S(2)}) %collective-permute-start.21) | collective-permute-done | bytes 589856 | tf_op jit(solution)/shard_map/ppermute | solution.py:43
  112.2 23.6 %collective-permute-done.28 = bf16[1,288,256]{2,1,0:T(8,128)(2,1)S(1)} collective-permute-done((bf16[1,288,256]{2,1,0:T(8,128)(2,1)S(1)}, bf16[1,288,256]{2,1,0:T(8,128)(2,1)S(1)}, u32[]{:S(2)}, u32[]{:S(2)}) %collective-permute-start.28) | collective-permute-done | bytes 147488 | tf_op jit(solution)/shard_map/ppermute | solution.py:43
  146.0 18.2 %shard_map.187 = (bf16[2048,1152]{1,0:T(8,128)(2,1)}, bf16[2048,1152]{1,0:T(8,128)(2,1)}, bf16[2048,1152]{1,0:T(8,128)(2,1)}) custom-call(s32[2]{0:T(128)} %pad_add_fusion.ids_ref, bf16[512,1024]{1,0:T(8,128)(2,1)} %get-tuple-element.416.refs_0_, bf16[512,1024]{1,0:T(8,128)(2,1)} %copy-done.37, bf16[512,1024]{1,0:T(8,128)(2,1)} %copy-done.36, ...), custom_call_target="tpu_custom_call" | custom-call | flops 68719476736 | bytes 1048576 | tf_op jit(solution)/shard_map/pallas_call | solution.py:167
  164.4 4.5 %collective-permute-done.34.refs_3_.refs_2_ = bf16[512,1024]{1,0:T(8,128)(2,1)S(1)} collective-permute-done((bf16[512,1024]{1,0:T(8,128)(2,1)S(1)}, bf16[512,1024]{1,0:T(8,128)(2,1)S(1)}, u32[]{:S(2)}, u32[]{:S(2)}) %collective-permute-start.34) | collective-permute-done | bytes 1048608 | tf_op jit(solution)/shard_map/ppermute | solution.py:43
  172.6 10.3 %shard_map.188 = (bf16[4,288,256]{2,1,0:T(8,128)(2,1)}, bf16[4,288,256]{2,1,0:T(8,128)(2,1)}, bf16[4,288,256]{2,1,0:T(8,128)(2,1)}, bf16[4,288,256]{2,1,0:T(8,128)(2,1)}) custom-call(s32[2]{0:T(128)} %pad_add_fusion.ids_ref, bf16[2048,1152]{1,0:T(8,128)(2,1)} %get-tuple-element.431.refs_0_.refs_4_, ...), custom_call_target="tpu_custom_call" | custom-call | flops 68719476736 | bytes 1048576 | tf_op jit(solution)/shard_map/pallas_call | solution.py:326
  186.8 33.7 %shard_map.189 = (bf16[2048,1152]{1,0:T(8,128)(2,1)}, bf16[2048,1152]{1,0:T(8,128)(2,1)}, bf16[512,1024]{1,0:T(8,128)(2,1)}, bf16[512,1024]{1,0:T(8,128)(2,1)}, ...) custom-call(s32[2]{0:T(128)} %pad_add_fusion.ids_ref, ...), custom_call_target="tpu_custom_call" | custom-call | flops 68719476736 | bytes 1048576 | tf_op jit(solution)/shard_map/pallas_call | solution.py:167
  229.4 11.4 %shard_map.190 = (bf16[4,128,1152]{2,1,0:T(8,128)(2,1)}, bf16[4,128,1152]{2,1,0:T(8,128)(2,1)}) custom-call(s32[2]{0:T(128)} %pad_add_fusion.ids_ref, bf16[512,1024]{1,0:T(8,128)(2,1)} %get-tuple-element.416.refs_0_, bf16[512,1024]{1,0:T(8,128)(2,1)} %copy-done.37, bf16[512,1024]{1,0:T(8,128)(2,1)} %copy-done.36, bf16[512,1024]{1,0:T(8,128)(2,1)} %copy-done.38, ...), custom_call_target="tpu_custom_call" | custom-call | flops 68719476736 | bytes 1048576 | tf_op jit(solution)/shard_map/pallas_call | solution.py:326
  249.8 11.2 %shard_map.191 = (bf16[4,128,1152]{2,1,0:T(8,128)(2,1)}, bf16[4,128,1152]{2,1,0:T(8,128)(2,1)}) custom-call(s32[2]{0:T(128)} %pad_add_fusion.ids_ref, bf16[512,1024]{1,0:T(8,128)(2,1)} %get-tuple-element.416.refs_0_, bf16[512,1024]{1,0:T(8,128)(2,1)} %copy-done.37, bf16[512,1024]{1,0:T(8,128)(2,1)} %copy-done.36, bf16[512,1024]{1,0:T(8,128)(2,1)} %copy-done.38, ...), custom_call_target="tpu_custom_call" | custom-call | flops 68719476736 | bytes 1048576 | tf_op jit(solution)/shard_map/pallas_call | solution.py:326
  266.8 4.0 collective-permute-start.52
  272.3 14.6 %shard_map.192 = (f32[512,1024]{1,0:T(8,128)}, bf16[512,1024]{1,0:T(8,128)(2,1)}, f32[512,1024]{1,0:T(8,128)}, f32[8,1024]{1,0:T(8,128)}, f32[8,1024]{1,0:T(8,12...) custom-call(s32[2]{0:T(128)} %pad_add_fusion.ids_ref, bf16[512,1024]{1,0:T(8,128)(2,1)} %get-tuple-element.502.refs_0_, ...), custom_call_target="tpu_custom_call" | custom-call | flops 68719476736 | bytes 1048576 | tf_op jit(solution)/shard_map/pallas_call | solution.py:499
  288.2 5.4 %collective-permute-done.51 = bf16[2,128,1152]{2,1,0:T(8,128)(2,1)S(1)} collective-permute-done((bf16[2,128,1152]{2,1,0:T(8,128)(2,1)S(1)}, bf16[2,128,1152]{2,1,0:T(8,128)(2,1)S(1)}, u32[]{:S(2)}, u32[]{:S(2)}) %collective-permute-start.51) | collective-permute-done | bytes 589856 | tf_op jit(solution)/shard_map/ppermute | solution.py:43
  301.9 13.5 %shard_map.193 = (bf16[512,3072]{1,0:T(8,128)(2,1)}, bf16[16,128,256]{2,1,0:T(8,128)(2,1)}, bf16[16,128,256]{2,1,0:T(8,128)(2,1)}, bf16[16,128,256]{2,1,0:T(8,12...) custom-call(s32[2]{0:T(128)} %pad_add_fusion.ids_ref, ...), custom_call_target="tpu_custom_call" | custom-call | flops 68719476736 | bytes 1048576 | tf_op jit(solution)/shard_map/pallas_call | solution.py:556
  324.9 10.6 %shard_map.194 = (bf16[512,1024]{1,0:T(8,128)(2,1)}, f32[8,1024]{1,0:T(8,128)}) custom-call(s32[2]{0:T(128)} %pad_add_fusion.ids_ref, bf16[512,3072]{1,0:T(8,128)(2,1)} %get-tuple-element.623.proj_ref, bf16[512,1024]{1,0:T(8,128)(2,1)} %x_ref, f32[512,1024]{1,0:T(8,128)} %get-tuple-element.624.hidden_ref, f32[8,1024]{1,0:T(8,128)} %get-tuple-element.625.sums_ref, ...), custom_call_target="tpu_custom_call" | custom-call | flops 68719476736 | bytes 1048576 | tf_op jit(solution)/shard_map/pallas_call | solution.py:608
  345.5 9.8 %collective-permute-done.71 = f32[8,1024]{1,0:T(8,128)S(1)} collective-permute-done((f32[8,1024]{1,0:T(8,128)S(1)}, f32[8,1024]{1,0:T(8,128)S(1)}, u32[]{:S(2)}, u32[]{:S(2)}) %collective-permute-start.71) | collective-permute-done | bytes 32800 | tf_op jit(solution)/shard_map/ppermute | solution.py:43
  356.2 10.3 %collective-permute-done.69 = bf16[2,128,256]{2,1,0:T(8,128)(2,1)S(1)} collective-permute-done((bf16[2,128,256]{2,1,0:T(8,128)(2,1)S(1)}, bf16[2,128,256]{2,1,0:T(8,128)(2,1)S(1)}, u32[]{:S(2)}, u32[]{:S(2)}) %collective-permute-start.69) | collective-permute-done | bytes 131104 | tf_op jit(solution)/shard_map/ppermute | solution.py:43
  376.4 7.3 %collective-permute-done.73 = bf16[4,128,256]{2,1,0:T(8,128)(2,1)S(1)} collective-permute-done((bf16[4,128,256]{2,1,0:T(8,128)(2,1)S(1)}, bf16[4,128,256]{2,1,0:T(8,128)(2,1)S(1)}, u32[]{:S(2)}, u32[]{:S(2)}) %collective-permute-start.73) | collective-permute-done | bytes 262176 | tf_op jit(solution)/shard_map/ppermute | solution.py:43
  (369 shorter events, 157.6 us)
Async XLA Ops:
  39.0 21.8 %collective-permute-start.13 = (bf16[1,128,1152]{2,1,0:T(8,128)(2,1)S(1)}, bf16[1,128,1152]{2,1,0:T(8,128)(2,1)S(1)}, u32[]{:S(2)}, u32[]{:S(2)}) collective-permute-start(bf16[1,128,1152]{2,1,0:T(8,128)(2,1)S(1)} %bitcast.47), channel_id=1, source_target_pairs={{0,4},{1,5},{2,6},{3,7},{4,0},{5,1},{6,2},{7,3},{8,12},{9,13},{10,... | collective-permute-start | bytes 884744 | tf_op jit(solution)/shard_map/ppermute | solution.py:43
  40.9 23.8 %collective-permute-start.12 = (bf16[1,128,1152]{2,1,0:T(8,128)(2,1)S(1)}, bf16[1,128,1152]{2,1,0:T(8,128)(2,1)S(1)}, u32[]{:S(2)}, u32[]{:S(2)}) collective-permute-start(bf16[1,128,1152]{2,1,0:T(8,128)(2,1)S(1)} %bitcast.49), channel_id=1, source_target_pairs={{0,4},{1,5},{2,6},{3,7},{4,0},{5,1},{6,2},{7,3},{8,12},{9,13},{10,... | collective-permute-start | bytes 884744 | tf_op jit(solution)/shard_map/ppermute | solution.py:43
  42.0 28.4 %collective-permute-start.7 = (bf16[8,128,384]{2,1,0:T(8,128)(2,1)S(1)}, bf16[8,128,384]{2,1,0:T(8,128)(2,1)S(1)}, u32[]{:S(2)}, u32[]{:S(2)}) collective-permute-start(bf16[8,128,384]{2,1,0:T(8,128)(2,1)S(1)} %pad_maximum_fusion.6), channel_id=1, source_target_pairs={{0,1},{1,0},{2,3},{3,2},{4,5},{5,4},{6,7},{7,6},{8,9},{9,8},{10,11... | collective-permute-start | bytes 2359304 | tf_op jit(solution)/shard_map/ppermute | solution.py:43
  43.5 25.9 %collective-permute-start.11 = (bf16[8,128,256]{2,1,0:T(8,128)(2,1)S(1)}, bf16[8,128,256]{2,1,0:T(8,128)(2,1)S(1)}, u32[]{:S(2)}, u32[]{:S(2)}) collective-permute-start(bf16[8,128,256]{2,1,0:T(8,128)(2,1)S(1)} %pad_maximum_fusion.12), channel_id=1, source_target_pairs={{0,2},{1,3},{2,0},{3,1},{4,6},{5,7},{6,4},{7,5},{8,10},{9,11},{10,... | collective-permute-start | bytes 1572872 | tf_op jit(solution)/shard_map/ppermute | solution.py:43
  79.8 27.5 %collective-permute-start.23 = (bf16[576,256]{1,0:T(8,128)(2,1)S(1)}, bf16[576,256]{1,0:T(8,128)(2,1)S(1)}, u32[]{:S(2)}, u32[]{:S(2)}) collective-permute-start(bf16[576,256]{1,0:T(8,128)(2,1)S(1)} %copy-done.48), channel_id=1, source_target_pairs={{0,0},{1,1},{2,8},{3,9},{4,16},{5,17},{6,24},{7,25},{8,4},{9,5},{1... | collective-permute-start | bytes 884744 | tf_op jit(solution)/shard_map/ppermute | solution.py:777
  80.7 26.3 %collective-permute-start.21 = (bf16[2,128,1152]{2,1,0:T(8,128)(2,1)S(1)}, bf16[2,128,1152]{2,1,0:T(8,128)(2,1)S(1)}, u32[]{:S(2)}, u32[]{:S(2)}) collective-permute-start(bf16[2,128,1152]{2,1,0:T(8,128)(2,1)S(1)} %pad_maximum_fusion.8), channel_id=1, source_target_pairs={{0,2},{1,3},{2,0},{3,1},{4,6},{5,7},{6,4},{7,5},{8,10},{9,11},{10,... | collective-permute-start | bytes 1769480 | tf_op jit(solution)/shard_map/ppermute | solution.py:43
  83.8 23.4 %collective-permute-start.22 = (bf16[2,128,1152]{2,1,0:T(8,128)(2,1)S(1)}, bf16[2,128,1152]{2,1,0:T(8,128)(2,1)S(1)}, u32[]{:S(2)}, u32[]{:S(2)}) collective-permute-start(bf16[2,128,1152]{2,1,0:T(8,128)(2,1)S(1)} %pad_maximum_fusion.9), channel_id=1, source_target_pairs={{0,1},{1,0},{2,3},{3,2},{4,5},{5,4},{6,7},{7,6},{8,9},{9,8},{10,11... | collective-permute-start | bytes 1769480 | tf_op jit(solution)/shard_map/ppermute | solution.py:43
  107.3 30.1 %collective-permute-start.25 = (bf16[4,128,1152]{2,1,0:T(8,128)(2,1)S(1)}, bf16[4,128,1152]{2,1,0:T(8,128)(2,1)S(1)}, u32[]{:S(2)}, u32[]{:S(2)}) collective-permute-start(bf16[4,128,1152]{2,1,0:T(8,128)(2,1)S(1)} %pad_maximum_fusion.2.refs_4_.refs_7_), channel_id=1, source_target_pairs={{0,1},{1,0},{2,3},{3,2},{4,5},{5,4},{6,7},{7,6},{8,9},{9,8},{10,11... | collective-permute-start | bytes 3538952 | tf_op jit(solution)/shard_map/ppermute | solution.py:43
  109.0 30.6 %collective-permute-start.26 = (bf16[4,128,1152]{2,1,0:T(8,128)(2,1)S(1)}, bf16[4,128,1152]{2,1,0:T(8,128)(2,1)S(1)}, u32[]{:S(2)}, u32[]{:S(2)}) collective-permute-start(bf16[4,128,1152]{2,1,0:T(8,128)(2,1)S(1)} %pad_maximum_fusion.3.refs_6_.refs_9_), channel_id=1, source_target_pairs={{0,2},{1,3},{2,0},{3,1},{4,6},{5,7},{6,4},{7,5},{8,10},{9,11},{10,... | collective-permute-start | bytes 3538952 | tf_op jit(solution)/shard_map/ppermute | solution.py:43
  109.2 28.2 %collective-permute-start.24 = (bf16[512,1024]{1,0:T(8,128)(2,1)S(1)}, bf16[512,1024]{1,0:T(8,128)(2,1)S(1)}, u32[]{:S(2)}, u32[]{:S(2)}) collective-permute-start(bf16[512,1024]{1,0:T(8,128)(2,1)S(1)} %copy-done.35), channel_id=1, source_target_pairs={{0,16},{8,24},{16,0},{24,8},{1,17},{9,25},{17,1},{25,9},{2,18},{10... | collective-permute-start | bytes 3145736 | tf_op jit(solution)/shard_map/ppermute | solution.py:43
  109.2 26.6 %collective-permute-start.28 = (bf16[1,288,256]{2,1,0:T(8,128)(2,1)S(1)}, bf16[1,288,256]{2,1,0:T(8,128)(2,1)S(1)}, u32[]{:S(2)}, u32[]{:S(2)}) collective-permute-start(bf16[1,288,256]{2,1,0:T(8,128)(2,1)S(1)} %get-tuple-element.756), channel_id=1, source_target_pairs={{0,4},{1,5},{2,6},{3,7},{4,0},{5,1},{6,2},{7,3},{8,12},{9,13},{10,... | collective-permute-start | bytes 442376 | tf_op jit(solution)/shard_map/ppermute | solution.py:43
  109.3 28.1 %collective-permute-start.27 = (bf16[1,288,256]{2,1,0:T(8,128)(2,1)S(1)}, bf16[1,288,256]{2,1,0:T(8,128)(2,1)S(1)}, u32[]{:S(2)}, u32[]{:S(2)}) collective-permute-start(bf16[1,288,256]{2,1,0:T(8,128)(2,1)S(1)} %get-tuple-element.757), channel_id=1, source_target_pairs={{0,4},{1,5},{2,6},{3,7},{4,0},{5,1},{6,2},{7,3},{8,12},{9,13},{10,... | collective-permute-start | bytes 442376 | tf_op jit(solution)/shard_map/ppermute | solution.py:43
  143.7 25.2 %collective-permute-start.34 = (bf16[512,1024]{1,0:T(8,128)(2,1)S(1)}, bf16[512,1024]{1,0:T(8,128)(2,1)S(1)}, u32[]{:S(2)}, u32[]{:S(2)}) collective-permute-start(bf16[512,1024]{1,0:T(8,128)(2,1)S(1)} %copy-done.15), channel_id=1, source_target_pairs={{0,16},{8,24},{16,0},{24,8},{1,17},{9,25},{17,1},{25,9},{2,18},{10... | collective-permute-start | bytes 3145736 | tf_op jit(solution)/shard_map/ppermute | solution.py:43
  143.7 25.2 %collective-permute-start.33 = (bf16[512,1024]{1,0:T(8,128)(2,1)S(1)}, bf16[512,1024]{1,0:T(8,128)(2,1)}, u32[]{:S(2)}, u32[]{:S(2)}) collective-permute-start(bf16[512,1024]{1,0:T(8,128)(2,1)S(1)} %copy-done.15), channel_id=1, source_target_pairs={{0,8},{8,0},{16,24},{24,16},{1,9},{9,1},{17,25},{25,17},{2,10},{10... | collective-permute-start | bytes 3145736 | tf_op jit(solution)/shard_map/ppermute | solution.py:43
  143.9 20.4 %collective-permute-start.31 = (bf16[2,288,256]{2,1,0:T(8,128)(2,1)S(1)}, bf16[2,288,256]{2,1,0:T(8,128)(2,1)S(1)}, u32[]{:S(2)}, u32[]{:S(2)}) collective-permute-start(bf16[2,288,256]{2,1,0:T(8,128)(2,1)S(1)} %pad_maximum_fusion.16), channel_id=1, source_target_pairs={{0,2},{1,3},{2,0},{3,1},{4,6},{5,7},{6,4},{7,5},{8,10},{9,11},{10,... | collective-permute-start | bytes 884744 | tf_op jit(solution)/shard_map/ppermute | solution.py:43
  185.0 35.5 %collective-permute-start.38 = (bf16[4,288,256]{2,1,0:T(8,128)(2,1)}, bf16[4,288,256]{2,1,0:T(8,128)(2,1)S(1)}, u32[]{:S(2)}, u32[]{:S(2)}) collective-permute-start(bf16[4,288,256]{2,1,0:T(8,128)(2,1)} %get-tuple-element.455), channel_id=1, source_target_pairs={{0,1},{1,0},{2,3},{3,2},{4,5},{5,4},{6,7},{7,6},{8,9},{9,8},{10,11... | collective-permute-start | bytes 1769480 | tf_op jit(solution)/shard_map/ppermute | solution.py:43
  186.4 34.2 %collective-permute-start.39 = (bf16[4,288,256]{2,1,0:T(8,128)(2,1)}, bf16[4,288,256]{2,1,0:T(8,128)(2,1)S(1)}, u32[]{:S(2)}, u32[]{:S(2)}) collective-permute-start(bf16[4,288,256]{2,1,0:T(8,128)(2,1)} %get-tuple-element.457), channel_id=1, source_target_pairs={{0,2},{1,3},{2,0},{3,1},{4,6},{5,7},{6,4},{7,5},{8,10},{9,11},{10,... | collective-permute-start | bytes 1769480 | tf_op jit(solution)/shard_map/ppermute | solution.py:43
  266.1 20.8 %collective-permute-start.53 = (bf16[576,256]{1,0:T(8,128)(2,1)S(1)}, bf16[576,256]{1,0:T(8,128)(2,1)S(1)}, u32[]{:S(2)}, u32[]{:S(2)}) collective-permute-start(bf16[576,256]{1,0:T(8,128)(2,1)S(1)} %pad_maximum_fusion.18), channel_id=1, source_target_pairs={{0,0},{1,1},{8,2},{9,3},{16,4},{17,5},{24,6},{25,7},{4,8},{5,9},{1... | collective-permute-start | bytes 884744 | tf_op jit(solution)/shard_map/ppermute | solution.py:892
  266.8 21.4 %collective-permute-start.52 = (bf16[256,1024]{1,0:T(8,128)(2,1)S(1)}, bf16[256,1024]{1,0:T(8,128)(2,1)S(1)}, u32[]{:S(2)}, u32[]{:S(2)}) collective-permute-start(bf16[256,1024]{1,0:T(8,128)(2,1)S(1)} %get-tuple-element.562), channel_id=1, source_target_pairs={{0,16},{8,24},{16,0},{24,8},{1,17},{9,25},{17,1},{25,9},{2,18},{10... | collective-permute-start | bytes 1572872 | tf_op jit(solution)/shard_map/ppermute | solution.py:43
  272.3 21.3 %collective-permute-start.51 = (bf16[2,128,1152]{2,1,0:T(8,128)(2,1)S(1)}, bf16[2,128,1152]{2,1,0:T(8,128)(2,1)S(1)}, u32[]{:S(2)}, u32[]{:S(2)}) collective-permute-start(bf16[2,128,1152]{2,1,0:T(8,128)(2,1)S(1)} %get-tuple-element.559), channel_id=1, source_target_pairs={{0,2},{1,3},{2,0},{3,1},{4,6},{5,7},{6,4},{7,5},{8,10},{9,11},{10,... | collective-permute-start | bytes 1769480 | tf_op jit(solution)/shard_map/ppermute | solution.py:43
  340.7 25.8 %collective-permute-start.66 = (bf16[8,128,256]{2,1,0:T(8,128)(2,1)S(1)}, bf16[8,128,256]{2,1,0:T(8,128)(2,1)S(1)}, u32[]{:S(2)}, u32[]{:S(2)}) collective-permute-start(bf16[8,128,256]{2,1,0:T(8,128)(2,1)S(1)} %get-tuple-element.646), channel_id=1, source_target_pairs={{0,1},{1,0},{2,3},{3,2},{4,5},{5,4},{6,7},{7,6},{8,9},{9,8},{10,11... | collective-permute-start | bytes 1572872 | tf_op jit(solution)/shard_map/ppermute | solution.py:43
  342.4 24.2 %collective-permute-start.67 = (bf16[8,128,256]{2,1,0:T(8,128)(2,1)S(1)}, bf16[8,128,256]{2,1,0:T(8,128)(2,1)S(1)}, u32[]{:S(2)}, u32[]{:S(2)}) collective-permute-start(bf16[8,128,256]{2,1,0:T(8,128)(2,1)S(1)} %get-tuple-element.648), channel_id=1, source_target_pairs={{0,16},{8,24},{16,0},{24,8},{1,17},{9,25},{17,1},{25,9},{2,18},{10... | collective-permute-start | bytes 1572872 | tf_op jit(solution)/shard_map/ppermute | solution.py:43
  344.1 22.4 %collective-permute-start.68 = (bf16[8,128,256]{2,1,0:T(8,128)(2,1)S(1)}, bf16[8,128,256]{2,1,0:T(8,128)(2,1)S(1)}, u32[]{:S(2)}, u32[]{:S(2)}) collective-permute-start(bf16[8,128,256]{2,1,0:T(8,128)(2,1)S(1)} %get-tuple-element.650), channel_id=1, source_target_pairs={{0,2},{1,3},{2,0},{3,1},{4,6},{5,7},{6,4},{7,5},{8,10},{9,11},{10,... | collective-permute-start | bytes 1572872 | tf_op jit(solution)/shard_map/ppermute | solution.py:43
  344.4 22.1 %collective-permute-start.70 = (bf16[1,128,1152]{2,1,0:T(8,128)(2,1)S(1)}, bf16[1,128,1152]{2,1,0:T(8,128)(2,1)S(1)}, u32[]{:S(2)}, u32[]{:S(2)}) collective-permute-start(bf16[1,128,1152]{2,1,0:T(8,128)(2,1)S(1)} %get-tuple-element.654), channel_id=1, source_target_pairs={{0,4},{1,5},{2,6},{3,7},{4,0},{5,1},{6,2},{7,3},{8,12},{9,13},{10,... | collective-permute-start | bytes 884744 | tf_op jit(solution)/shard_map/ppermute | solution.py:43
  (114 other events, 1088.9 us)

commit v5 on v4

--- a/solution.py
+++ b/solution.py
@@ -121,17 +121,18 @@
 
 
 def start_stores(ids_ref, whole, pieces, outs, sem):
+    each = len(outs) // len(pieces)
     for place, piece in enumerate(pieces):
-        half = 2 ** (len(piece.steps) - 1)
-        for first, out in ((0, outs[2 * place]), (half, outs[2 * place + 1])):
-
-            def start(position, carry, first=first, out=out, piece=piece):
+        size = 2 ** len(piece.steps) // each
+        for part in range(each):
+
+            def start(position, carry, first=part * size, out=outs[each * place + part], piece=piece):
                 mask_dp, mask_seq = masks_at(position + first, piece.steps)
                 source = piece.view(whole, ids_ref[0] ^ mask_dp, ids_ref[1] ^ mask_seq)
                 pltpu.make_async_copy(source, out.at[position], sem).start()
                 return carry
 
-            lax.fori_loop(0, half, start, 0)
+            lax.fori_loop(0, size, start, 0)
 
 
 def wait_whole(ref, sem):
@@ -195,8 +196,8 @@
     count = len(normed)
 
     def kernel(ids_ref, *refs):
-        blocks, stacks, refs = refs[:count], refs[count:-8], refs[-8:]
-        act, slope, silu, buffers, block_sems, gate_v, up_v, sems = refs
+        blocks, stacks, refs = refs[:count], refs[count:-9], refs[-9:]
+        act, slope, silu, whole, buffers, block_sems, gate_v, up_v, sems = refs
 
         @pl.when(pl.program_id(0) == 0)
         def _():
@@ -210,6 +211,7 @@
             wait_whole(gate_v, sems.at[0])
             wait_whole(up_v, sems.at[1])
 
+        whole[...] = x
         gate_val = multiply(x, gate_v[...])
         up_val = multiply(x, up_v[...])
         sigmoid = jax.nn.sigmoid(gate_val)
@@ -225,7 +227,7 @@
         normed,
         [],
         [*gate_stacks, *up_stacks],
-        [(n, jnp.bfloat16)] * 3,
+        [(n, jnp.bfloat16)] * 3 + [(shape[0], jnp.bfloat16)],
         [],
         [pltpu.VMEM(shape, jnp.bfloat16)] * 2 + [pltpu.SemaphoreType.DMA((2,))],
     )
@@ -288,24 +290,24 @@
     )
 
 
-def stack_shapes(pieces):
+def stack_shapes(pieces, each=2):
     shapes = []
     for piece in pieces:
-        half = 2 ** (len(piece.steps) - 1)
-        shapes += [jax.ShapeDtypeStruct((half, *piece.block), jnp.bfloat16)] * 2
+        size = 2 ** len(piece.steps) // each
+        shapes += [jax.ShapeDtypeStruct((size, *piece.block), jnp.bfloat16)] * each
     return shapes
 
 
-def paired(parts):
-    return [(parts[i], parts[i + 1]) for i in range(0, len(parts), 2)]
-
-
-def weight_gradient(ids, lefts, rights, pieces):
+def paired(parts, each=2):
+    return [tuple(parts[i : i + each]) for i in range(0, len(parts), each)]
+
+
+def weight_gradient(ids, lefts, rights, pieces, each=2):
     rows, columns = lefts[0].shape[1], rights[0].shape[1]
     step = min(v.shape[0] for v in (*lefts, *rights))
     tile = next((t for t in (512, 384, 256, 128) if rows % t == 0), rows)
     count = rows // tile
-    shapes = stack_shapes(pieces)
+    shapes = stack_shapes(pieces, each)
 
     def kernel(ids_ref, *refs):
         sides, refs = refs[: len(lefts) + len(rights)], refs[len(lefts) + len(rights) :]
@@ -342,7 +344,7 @@
         compiler_params=pltpu.CompilerParams(vmem_limit_bytes=VMEM_BYTES),
         cost_estimate=KERNEL_COST,
     )(ids, *lefts, *rights)
-    return paired(parts)
+    return paired(parts, each)
 
 
 def mixer_forward(ids, extended, consts, in_pieces, in_stacks, out_pieces, out_stacks, slot_size):
@@ -354,8 +356,8 @@
 
     def kernel(ids_ref, ext_ref, const_ref, *refs):
         stacks, refs = refs[: count + len(out_stacks)], refs[count + len(out_stacks) :]
-        normed_one, b_out, c_out, x_out, mixed_out, conv_out, gated_out, hidden_out, normed_two = refs[:9]
-        in_v, out_v, mixed_s, sems = refs[9:]
+        normed_one, b_out, c_out, x_out, mixed_out, gated_out, hidden_out, normed_two = refs[:8]
+        in_v, out_v, mixed_s, sems = refs[8:]
         i = pl.program_id(0)
 
         @pl.when(i == 0)
@@ -376,8 +378,8 @@
 
         b_part = multiply(normed, in_v[:, :features])
         x_part = multiply(normed, in_v[:, 2 * features :])
-        b_out[...] = b_part[HALO:]
-        x_out[...] = x_part[HALO:]
+        b_out[...] = b_part[HALO:].astype(jnp.bfloat16)
+        x_out[...] = x_part[HALO:].astype(jnp.bfloat16)
         mixed = (b_part * x_part).astype(jnp.bfloat16)
         mixed_s[...] = mixed.astype(jnp.float32)
         base = lax.rem(ids_ref[1] * rows, slot_size)
@@ -391,9 +393,8 @@
         conv = sum(
             const_ref[2 + k : 3 + k] * mixed_s[HALO - 2 + k : HALO - 2 + k + tile] for k in range(3)
         )
-        conv_out[...] = conv
         c_part = multiply(normed[HALO:], in_v[:, features : 2 * features])
-        c_out[...] = c_part
+        c_out[...] = c_part.astype(jnp.bfloat16)
         gated = (c_part * conv).astype(jnp.bfloat16)
         gated_out[...] = gated
         hidden = x[HALO:] + multiply(gated, out_v[...])
@@ -402,8 +403,8 @@
         normed_two[...] = (hidden * scale * const_ref[1:2]).astype(jnp.bfloat16)
 
     f32, bf16 = jnp.float32, jnp.bfloat16
-    kinds = [bf16, f32, f32, f32, bf16, f32, bf16, f32, bf16]
-    shapes = [(rows + (HALO if i == 4 else 0), features) for i in range(9)]
+    kinds = [bf16, bf16, bf16, bf16, bf16, bf16, f32, bf16]
+    shapes = [(rows + (HALO if i == 4 else 0), features) for i in range(8)]
     whole = pl.BlockSpec((rows + HALO, features), lambda i, ids: (0, 0))
     part = pl.BlockSpec((tile, features), lambda i, ids: (i, 0))
     return pl.pallas_call(
@@ -414,7 +415,7 @@
             grid=(2,),
             in_specs=[whole, pl.BlockSpec(consts.shape, lambda i, ids: (0, 0))]
             + [pl.BlockSpec(memory_space=pl.ANY)] * (count + len(out_stacks)),
-            out_specs=[whole if i == 4 else part for i in range(9)],
+            out_specs=[whole if i == 4 else part for i in range(8)],
             scratch_shapes=[
                 pltpu.VMEM((features, wide), bf16),
                 pltpu.VMEM((features, features), bf16),
@@ -433,9 +434,9 @@
     shapes = stack_shapes(out_grads)
 
     def kernel(ids_ref, *refs):
-        near_ref, more_ref, final_ref, hidden_ref, c_ref, conv_ref, gated_ref = refs[:7]
-        low_ref, high_ref, mixed_ref, const_ref = refs[7:11]
-        refs = refs[11:]
+        near_ref, more_ref, final_ref, hidden_ref, c_ref, gated_ref = refs[:6]
+        low_ref, high_ref, mixed_ref, const_ref = refs[6:10]
+        refs = refs[10:]
         stacks, refs = refs[: len(out_stacks)], refs[len(out_stacks) :]
         grad_hidden, grad_c, grad_mixed, head, sums = refs[:5]
         outs, (out_v, whole, mixed_s, conv_s, sems) = refs[5:-5], refs[-5:]
@@ -468,11 +469,14 @@
             wait_whole(out_v, sems.at[0])
 
         grad_gated = against(branch, out_v[...])
-        grad_c[...] = (grad_gated * conv_ref[...]).astype(jnp.bfloat16)
-        grad_conv = grad_gated * c_ref[...]
-        conv_s[0:tile] = grad_conv
         at = pl.multiple_of((1 - i) * tile, HALO)
         mixed_s[...] = mixed_ref[pl.ds(at, HALO + tile)].astype(jnp.float32)
+        conv = sum(
+            const_ref[2 + k : 3 + k] * mixed_s[HALO - 2 + k : HALO - 2 + k + tile] for k in range(3)
+        )
+        grad_c[...] = (grad_gated * conv).astype(jnp.bfloat16)
+        grad_conv = grad_gated * c_ref[...].astype(jnp.float32)
+        conv_s[0:tile] = grad_conv
         for k in range(3):
             sums[2 + k : 3 + k] += jnp.sum(
                 grad_conv * mixed_s[HALO - 2 + k : HALO - 2 + k + tile], axis=0, keepdims=True
@@ -504,7 +508,7 @@
         grid_spec=pltpu.PrefetchScalarGridSpec(
             num_scalar_prefetch=1,
             grid=(2,),
-            in_specs=[part] * 7
+            in_specs=[part] * 6
             + [pl.BlockSpec((tile, features), lambda i, ids: (0, 0))] * 2
             + [pl.BlockSpec((rows + HALO, features), lambda i, ids: (0, 0)), once]
             + [pl.BlockSpec(memory_space=pl.ANY)] * len(out_stacks),
@@ -537,9 +541,9 @@
             mixed_s[...] = mixed_ref[...]
             mixed_s[rows - 2 :] += back_ref[0:2]
             grad = mixed_s[...]
-            proj[:, :features] = (grad * x_ref[...]).astype(jnp.bfloat16)
+            proj[:, :features] = (grad * x_ref[...].astype(jnp.float32)).astype(jnp.bfloat16)
             proj[:, features : 2 * features] = c_ref[...]
-            proj[:, 2 * features :] = (grad * b_ref[...]).astype(jnp.bfloat16)
+            proj[:, 2 * features :] = (grad * b_ref[...].astype(jnp.float32)).astype(jnp.bfloat16)
 
         whole[pl.ds(pl.multiple_of(i * tile, tile), tile)] = outer_sum(
             normed_ref[...], proj[...]
@@ -720,7 +724,7 @@
 
     grad_final = (live_mask * cotangent.astype(jnp.float32)).astype(jnp.bfloat16)
     middle = len(orders[0]) // 2
-    z_first, last = len(zs) // 2, len(zs) + len(ys) - 1
+    z_first, last = 1, len(zs) + len(ys) - 1
     mixer = [gather_steps(v, order[:1]) for v, order in zip(mixer, orders)]
     mixer, small, tokens = tie(mixer, small, tokens)
     mixer = [gather_steps(v, order[1:middle]) for v, order in zip(mixer, orders)]
@@ -765,6 +769,19 @@
         Piece(order, (in_rows, in_cuts[i + 1] - in_cuts[i]), in_view(in_cuts[i], in_cuts[i + 1]))
         for i, order in enumerate(in_orders)
     ]
+    half_block = gate_rows // 2
+
+    def half_view(low):
+        def view(ref, dp, seq):
+            row = pl.multiple_of(seq * gate_rows + low, half_block)
+            return ref.at[pl.ds(row, half_block)]
+
+        return view
+
+    feed_grads = [
+        Piece(order, (half_block, hidden_units), half_view(low))
+        for order, low in ((near_order, 0), (far_order, half_block))
+    ]
     in_grads = [
         Piece(order, (in_rows, third), in_view(i * third, (i + 1) * third))
         for i, order in enumerate(orders)
@@ -775,55 +792,48 @@
 
     gate_up = [gather_steps(v, p.steps[z_first:last]) for v, p in zip(gate_up, (*gate, *up))]
     down_shard = lax.ppermute(down_weight, ("dp", "seq"), home)
+    final_there = dp_gather(grad_final, xs)[1:]
+    final_near = swap(grad_final, core[0])
     forward = mixer_forward(
         ids, extended, consts, in_pieces, in_stacks, out_pieces, out_stacks, slot_size
     )
-    forward, gate_up, down_shard, grad_final = tie(forward, gate_up, down_shard, grad_final)
-    normed_one, b_part, c_part, x_part, mixed, conv, gated, hidden, normed_two = forward
+    forward, gate_up, down_shard, grad_final, final_near, final_there = tie(
+        forward, gate_up, down_shard, grad_final, final_near, final_there
+    )
+    normed_one, b_part, c_part, x_part, mixed, gated, hidden, normed_two = forward
 
     wide = (features, hidden_units)
     gate_stacks, up_stacks = [last_step(v, p.steps[-1]) for v, p in zip(gate_up, (*gate, *up))]
-    downs = [
-        gather_steps(down_shard[None, a:b], p.steps[:z_first])
-        for a, b, p in zip(cuts, cuts[1:], down)
-    ]
+    down_stack = gather_steps(down_shard[None], near_order[:z_first])
     normed_there = dp_gather(normed_two, xs)[1:]
-    normed_two, normed_there, gate_stacks, up_stacks, downs, grad_final = tie(
-        normed_two, normed_there, gate_stacks, up_stacks, downs, grad_final
-    )
+    final_blocks = [grad_final, final_near] + with_core(final_there)
+    normed_two, normed_there, gate_stacks, up_stacks, down_stack, final_blocks = tie(
+        normed_two, normed_there, gate_stacks, up_stacks, down_stack, final_blocks
+    )
+    downs = [down_stack[:, a:b] for a, b in zip(cuts, cuts[1:])]
     normed_blocks = with_core([normed_two]) + with_core(normed_there)
-    normed_blocks, downs, gate_stacks, up_stacks, grad_final = tie(
-        normed_blocks, downs, gate_stacks, up_stacks, grad_final
-    )
-    final_there = dp_gather(grad_final, xs)[1:]
-    final_near = swap(grad_final, core[0])
+    normed_blocks, downs, gate_stacks, up_stacks = tie(normed_blocks, downs, gate_stacks, up_stacks)
     downs = [gather_steps(v, p.steps[z_first:last]) for v, p in zip(downs, down)]
-    activated, slope, silu = feed_up(ids, normed_blocks, gate, gate_stacks, up, up_stacks, wide)
-    activated, downs, grad_final, final_near, final_there = tie(
-        activated, downs, grad_final, final_near, final_there
-    )
-    final_blocks = [grad_final, final_near] + with_core(final_there)
+    activated, slope, silu, normed_all = feed_up(ids, normed_blocks, gate, gate_stacks, up, up_stacks, wide)
+    activated, downs = tie(activated, downs)
     down_stacks = [v for stack, p in zip(downs, down) for v in last_step(stack, p.steps[-1])]
     down_parts = weight_gradient(ids, [activated], final_blocks, down)
     down_parts, down_stacks = tie(down_parts, down_stacks)
 
-    def lower(parts):
-        return tuple(v[: v.shape[0] // 2] for v in parts)
-
-    def upper(parts):
-        return tuple(v[v.shape[0] // 2 :] for v in parts)
-
     def sent(parts, pieces, place):
         return [exchanged(v, p.steps[place]) for v, p in zip(parts, pieces)]
 
     def fold_all(parts):
         return [folded(v) for v in parts]
 
-    def added(low, high):
-        return tuple(
-            (v[0].astype(jnp.float32) + v[1].astype(jnp.float32)).astype(jnp.bfloat16)
-            for v in (low, high)
-        )
+    def sent_on(parts, pieces):
+        count = len(pieces[0].steps)
+        for place in range(count - 2, 0, -1):
+            parts = sent(fold_all(parts) if place < count - 2 else parts, pieces, place)
+        return parts
+
+    def joined(parts):
+        return [tuple(jnp.concatenate(v, axis=1) for v in zip(*parts))]
 
     def core_halves(v):
         near, far = v[:2], v[2:]
@@ -856,43 +866,37 @@
     )
     far_low = dp_scatter([None] + far_low, xs)
     near_more = swap(near_send, core[0])
-    down_parts = sent(down_parts, down, -2)
-    gate_parts = weight_gradient(ids, normed_blocks, [grad_gate], gate)
+    down_parts = sent_on(down_parts, down)
+    gate_parts = weight_gradient(ids, [normed_all], [grad_gate], feed_grads)
     gate_parts, far_low, far_high, grad_up, near, near_more, down_parts, feed = tie(
         gate_parts, far_low, far_high, grad_up, near, near_more, down_parts, feed
     )
-    down_parts = fold_all(down_parts)
-    gate_low, gate_high = lower(gate_parts[0]), upper(gate_parts[0])
+    down_parts = joined(fold_all(down_parts))
     feed_near, feed_send, feed_far, feed_come = core_halves(feed)
-    down_parts, gate_low, gate_high, feed_far, feed_come, grad_up, far_low, far_high = tie(
-        down_parts, gate_low, gate_high, feed_far, feed_come, grad_up, far_low, far_high
+    down_parts, gate_parts, feed_far, feed_come, grad_up, far_low, far_high = tie(
+        down_parts, gate_parts, feed_far, feed_come, grad_up, far_low, far_high
     )
     far_high = dp_scatter([None] + far_high, xs)
-    gate_low = exchanged(gate_low, gate[0].steps[-1])
+    gate_parts = sent(gate_parts, feed_grads, -1)
     feed_come = [swap(v, core[0]) for v in feed_come]
-    down_parts = sent(down_parts, down, -3)
-    up_parts = weight_gradient(ids, normed_blocks, [grad_up], up)
-    up_parts, far_low, far_high, gate_low, gate_high, feed_far, feed_come, down_parts = tie(
-        up_parts, far_low, far_high, gate_low, gate_high, feed_far, feed_come, down_parts
+    down_parts = sent(down_parts, down, 0)
+    up_parts = weight_gradient(ids, [normed_all], [grad_up], feed_grads)
+    up_parts, far_low, far_high, gate_parts, feed_far, feed_come, down_parts = tie(
+        up_parts, far_low, far_high, gate_parts, feed_far, feed_come, down_parts
     )
 
     feed_far = far_added(feed_far, feed_come)
     feed_low, feed_high = [v[:half_rows] for v in feed_far], [v[half_rows:] for v in feed_far]
-    up_low, up_high = lower(up_parts[0]), upper(up_parts[0])
-    own_down = fold_all(down_parts)
-    for place in range(len(down[0].steps) - 4, -1, -1):
-        own_down = fold_all(sent(own_down, down, place))
-    own_down = jnp.concatenate(own_down, axis=0).astype(jnp.bfloat16)
-    feed_low, feed_high, up_low, up_high, gate_low, gate_high, far_low, far_high, own_down = tie(
-        feed_low, feed_high, up_low, up_high, gate_low, gate_high, far_low, far_high, own_down
-    )
-    gate_high = exchanged(gate_high, gate[0].steps[-1])
-    up_low = exchanged(up_low, up[0].steps[-1])
+    own_down = folded(down_parts[0]).astype(jnp.bfloat16)
+    feed_low, feed_high, up_parts, gate_parts, far_low, far_high, own_down = tie(
+        feed_low, feed_high, up_parts, gate_parts, far_low, far_high, own_down
+    )
+    up_parts = sent(up_parts, feed_grads, -1)
     feed_low = dp_scatter([None] + feed_low, xs)
     own_down = lax.ppermute(own_down, ("dp", "seq"), [(b, a) for a, b in home])
     grad_hidden, grad_c, grad_mixed, first_rows, sums, out_parts = mixer_back(
         ids,
-        [near, near_more, grad_final, hidden, c_part, conv, gated],
+        [near, near_more, grad_final, hidden, c_part, gated],
         far_low + far_high,
         mixed,
         consts,
@@ -901,32 +905,29 @@
         out_grads,
         slot_size,
     )
-    out_parts, grad_mixed, first_rows, gate_low, gate_high, up_low, up_high, feed_low, feed_high, own_down = tie(
-        out_parts, grad_mixed, first_rows, gate_low, gate_high, up_low, up_high, feed_low, feed_high, own_down
+    out_parts, grad_mixed, first_rows, gate_parts, up_parts, feed_low, feed_high, own_down = tie(
+        out_parts, grad_mixed, first_rows, gate_parts, up_parts, feed_low, feed_high, own_down
     )
     returned = lax.ppermute(first_rows, "seq", [(i + 1, i) for i in range(n_seq - 1)])
     out_parts = fold_all(sent(out_parts, out_grads, -1))
-    gate_parts = added(gate_low, gate_high)
-    returned, out_parts, up_high, gate_parts, feed_high = tie(
-        returned, out_parts, up_high, gate_parts, feed_high
-    )
-    up_high = exchanged(up_high, up[0].steps[-1])
-    out_parts = sent(out_parts, out_grads, -2)
+    gate_parts, up_parts = fold_all(gate_parts), fold_all(up_parts)
+    returned, out_parts, up_parts, gate_parts, feed_high = tie(
+        returned, out_parts, up_parts, gate_parts, feed_high
+    )
+    gate_parts = sent_on(gate_parts, feed_grads)
+    up_parts = sent_on(up_parts, feed_grads)
     feed_high = dp_scatter([None] + feed_high, xs)
     grad_proj, in_parts = projection_gradient(
         ids, normed_one, grad_mixed, returned, grad_c, b_part, x_part, in_grads
     )
-    in_parts, up_low, up_high, gate_parts, grad_proj, out_parts, feed_high = tie(
-        in_parts, up_low, up_high, gate_parts, grad_proj, out_parts, feed_high
-    )
-    up_parts, out_parts = added(up_low, up_high), fold_all(out_parts)
-    in_parts, up_parts, gate_parts, out_parts, grad_proj = tie(
-        in_parts, up_parts, gate_parts, out_parts, grad_proj
-    )
+    in_parts, up_parts, gate_parts, grad_proj, out_parts, feed_high = tie(
+        in_parts, up_parts, gate_parts, grad_proj, out_parts, feed_high
+    )
+    gate_parts = joined(fold_all(gate_parts))
+    in_parts, gate_parts, out_parts, grad_proj = tie(in_parts, gate_parts, out_parts, grad_proj)
     in_parts = sent(in_parts, in_grads, -1)
-    out_parts = sent(out_parts, out_grads, -3)
-    gate_parts = exchanged(gate_parts, gate[0].steps[-2])
-    up_parts = exchanged(up_parts, up[0].steps[-2])
+    out_parts = sent(out_parts, out_grads, -2)
+    gate_parts = sent(gate_parts, feed_grads, 0)
     grad_tokens, sums = mixer_first(ids, grad_proj, tokens, grad_hidden, sums, consts, in_pieces, in_stacks)
     in_parts, out_parts, sums, gate_parts, up_parts, feed_send = tie(
         in_parts, out_parts, sums, gate_parts, up_parts, feed_send
@@ -934,28 +935,26 @@
     sum_steps = core + ys + xs + zs[::-1]
     for step in sum_steps[:1]:
         sums = sums + swap(sums, step)
-    in_parts, out_parts, gate_parts, up_parts = fold_all(in_parts), fold_all(out_parts), folded(gate_parts), folded(up_parts)
-    in_parts, out_parts, gate_parts, up_parts, sums = tie(in_parts, out_parts, gate_parts, up_parts, sums)
+    in_parts, out_parts, up_parts = fold_all(in_parts), fold_all(out_parts), joined(fold_all(up_parts))
+    in_parts, out_parts, up_parts, sums = tie(in_parts, out_parts, up_parts, sums)
     in_parts = sent(in_parts, in_grads, -2)
+    out_parts = sent(out_parts, out_grads, -3)
+    up_parts = sent(up_parts, feed_grads, 0)
+    sums = (sums, swap(sums, sum_steps[1]))
+    in_parts, out_parts, up_parts, sums, feed_send = tie(in_parts, out_parts, up_parts, sums, feed_send)
+    in_parts, out_parts, sums = fold_all(in_parts), fold_all(out_parts), sums[0] + sums[1]
+    in_parts, out_parts, sums = tie(in_parts, out_parts, sums)
+    in_parts = sent(in_parts, in_grads, -3)
     out_parts = sent(out_parts, out_grads, -4)
-    gate_parts = exchanged(gate_parts, gate[0].steps[-3])
-    sums = (sums, swap(sums, sum_steps[1]))
-    in_parts, out_parts, gate_parts, up_parts, sums, feed_send = tie(
-        in_parts, out_parts, gate_parts, up_parts, sums, feed_send
-    )
+    sums = (sums, swap(sums, sum_steps[2]))
+    in_parts, out_parts, sums, feed_send = tie(in_parts, out_parts, sums, feed_send)
     in_parts, out_parts, sums = fold_all(in_parts), fold_all(out_parts), sums[0] + sums[1]
-    in_parts, out_parts, up_parts, sums = tie(in_parts, out_parts, up_parts, sums)
-    in_parts = sent(in_parts, in_grads, -3)
+    in_parts, out_parts, sums = tie(in_parts, out_parts, sums)
+    in_parts = sent(in_parts, in_grads, -4)
     out_parts = sent(out_parts, out_grads, -5)
-    up_parts = exchanged(up_parts, up[0].steps[-3])
-    sums = (sums, swap(sums, sum_steps[2]))
-    in_parts, out_parts, up_parts, sums, feed_send = tie(in_parts, out_parts, up_parts, sums, feed_send)
-    in_parts, sums = fold_all(in_parts), sums[0] + sums[1]
-    in_parts, sums = tie(in_parts, sums)
-    in_parts = sent(in_parts, in_grads, -4)
     sums = (sums, swap(sums, sum_steps[3]))
     feed_more = swap(feed_send, core[0])
-    in_parts, sums, feed_more = tie(in_parts, sums, feed_more)
+    in_parts, out_parts, sums, feed_more, own_down = tie(in_parts, out_parts, sums, feed_more, own_down)
     sums = sums[0] + sums[1]
     for step in sum_steps[4:]:
         sums = sums + swap(sums, step)
@@ -970,8 +969,8 @@
     own_in = [rest(v, p, 4) for v, p in zip(in_parts, in_grads)]
     own_in = jnp.concatenate(own_in, axis=1)
     own_out = rest(out_parts[0], out_grads[0], 5)
-    own_gate = rest(gate_parts, gate[0], 3)
-    own_up = rest(up_parts, up[0], 3)
+    own_gate = folded(gate_parts[0])
+    own_up = folded(up_parts[0])
     own_sums = lax.dynamic_slice(sums, (0, own_seq * small_cols), (8, small_cols))
     feed_out = jnp.concatenate(feed_low + feed_high, axis=0).astype(jnp.float32)
     feed_out = feed_out + feed_near.astype(jnp.float32) + feed_more.astype(jnp.float32)

time: 414 us -> 412 us (level)
  waiting for transfers between devices: 150 us -> 142 us
  starting transfers between devices: 84.7 us -> 90.1 us
    ppermute x83, waiting for transfers between devices: 149 us -> 142 us  [swap(): return lax.ppermute(shard, axis, [(i, i ^ bit) for i in range(count)])]
    ppermute x83, starting transfers between devices: 79.3 us -> 83.5 us  [swap(): return lax.ppermute(shard, axis, [(i, i ^ bit) for i in range(count)])]
    unnamed x103 -> x107, local copies, waits for them, and re-layouts: 11.1 us -> 8.89 us
  transfers between devices with their start and end apart: 87 -> 87, of which waited for: 37 -> 37; matrix products, arithmetic and copies ran while one was open for 4% -> 5% of each run, Pallas kernels for 34% -> 33%
where the time goes in v5:
time: 412 us; the launch traced here: 408 us
  waiting for transfers between devices  142 us (34%)
  Pallas kernels  136 us (33%)
  starting transfers between devices  90.1 us (22%)
  other arithmetic  21.5 us (5%)
  local copies, waits for them, and re-layouts  14.2 us (3%)
    ppermute x83, waiting for transfers between devices, swap(): return lax.ppermute(shard, axis, [(i, i ^ bit) for i in range(count)])  142 us
    ppermute x83, starting transfers between devices, swap(): return lax.ppermute(shard, axis, [(i, i ^ bit) for i in range(count)])  83.5 us
    pallas_call x2, Pallas kernels, token_call(): pl.pallas_call(kernel, out_shape=[jax.ShapeDtypeStruct((rows * steps, n),...  52.2 us
    pallas_call x3, Pallas kernels, weight_gradient(): pl.pallas_call(kernel, out_shape=shapes, grid_spec=pltpu.PrefetchScalarGr...  32.2 us
    pallas_call x1, Pallas kernels, mixer_back(): pl.pallas_call(kernel, out_shape=[jax.ShapeDtypeStruct((rows, features),...  14.7 us
    pallas_call x1, Pallas kernels, mixer_forward(): pl.pallas_call(kernel, out_shape=[jax.ShapeDtypeStruct(s, t) for s, t in...  13.8 us
    pallas_call x1, Pallas kernels, projection_gradient(): pl.pallas_call(kernel, out_shape=[jax.ShapeDtypeStruct((rows, 3 * feature...  12.7 us
    pallas_call x1, Pallas kernels, mixer_first(): pl.pallas_call(kernel, out_shape=[jax.ShapeDtypeStruct((rows, features),...  10.7 us
  transfers between devices with their start and end apart: 87, of which 37 were waited for; matrix products, arithmetic and copies ran while one was open for 5% of the time, Pallas kernels for 33%

profile of v5, /device:TPU:0, one launch (start us, length us, event | category | flops | bytes accessed | tf_op | source)
XLA Modules:
  0.0 407.8 jit_solution(8261337208557066783)
XLA Ops:
  0.7 4.1 %collective-permute-start.2 = (bf16[1,128,256]{2,1,0:T(8,128)(2,1)}, bf16[1,128,256]{2,1,0:T(8,128)(2,1)S(1)}, u32[]{:S(2)}, u32[]{:S(2)}) collective-permute-start(bf16[1,128,256]{2,1,0:T(8,128)(2,1)} %bitcast.48), channel_id=1, source_target_pairs={{0,4},{1,5},{2,6},{3,7},{4,0},{5,1},{6,2},{7,3},{8,12},{9,13},{10,... | collective-permute-start | bytes 196616 | tf_op jit(solution)/shard_map/ppermute | solution.py:43
  25.1 5.1 %collective-permute-done.4 = bf16[2,128,384]{2,1,0:T(8,128)(2,1)S(1)} collective-permute-done((bf16[2,128,384]{2,1,0:T(8,128)(2,1)S(1)}, bf16[2,128,384]{2,1,0:T(8,128)(2,1)S(1)}, u32[]{:S(2)}, u32[]{:S(2)}) %collective-permute-start.4) | collective-permute-done | bytes 196640 | tf_op jit(solution)/shard_map/ppermute | solution.py:43
  44.1 9.6 %collective-permute-done.8 = bf16[4,128,384]{2,1,0:T(8,128)(2,1)S(1)} collective-permute-done((bf16[4,128,384]{2,1,0:T(8,128)(2,1)S(1)}, bf16[4,128,384]{2,1,0:T(8,128)(2,1)S(1)}, u32[]{:S(2)}, u32[]{:S(2)}) %collective-permute-start.8) | collective-permute-done | bytes 393248 | tf_op jit(solution)/shard_map/ppermute | solution.py:43
  55.1 5.5 %collective-permute-done.13 = bf16[1,128,1152]{2,1,0:T(8,128)(2,1)S(1)} collective-permute-done((bf16[1,128,1152]{2,1,0:T(8,128)(2,1)S(1)}, bf16[1,128,1152]{2,1,0:T(8,128)(2,1)S(1)}, u32[]{:S(2)}, u32[]{:S(2)}) %collective-permute-start.13) | collective-permute-done | bytes 294944 | tf_op jit(solution)/shard_map/ppermute | solution.py:43
  60.7 3.9 collective-permute-done.12
  64.6 4.7 %collective-permute-done.11 = bf16[8,128,256]{2,1,0:T(8,128)(2,1)S(1)} collective-permute-done((bf16[8,128,256]{2,1,0:T(8,128)(2,1)S(1)}, bf16[8,128,256]{2,1,0:T(8,128)(2,1)S(1)}, u32[]{:S(2)}, u32[]{:S(2)}) %collective-permute-start.11) | collective-permute-done | bytes 524320 | tf_op jit(solution)/shard_map/ppermute | solution.py:43
  73.4 6.4 %collective-permute-done.20.refs_5_.refs_11_ = bf16[16,128,256]{2,1,0:T(8,128)(2,1)} collective-permute-done((bf16[16,128,256]{2,1,0:T(8,128)(2,1)}, bf16[16,128,256]{2,1,0:T(8,128)(2,1)}, u32[]{:S(2)}, u32[]{:S(2)}) %collective-permute-start.20) | collective-permute-done | bytes 1048608 | tf_op jit(solution)/shard_map/ppermute | solution.py:43
  87.3 13.8 %shard_map.186 = (bf16[512,1024]{1,0:T(8,128)(2,1)}, bf16[512,1024]{1,0:T(8,128)(2,1)}, bf16[512,1024]{1,0:T(8,128)(2,1)}, bf16[512,1024]{1,0:T(8,128)(2,1)}, bf...) custom-call(s32[2]{0:T(128)} %pad_add_fusion.ids_ref, ...), custom_call_target="tpu_custom_call" | custom-call | flops 68719476736 | bytes 1048576 | tf_op jit(solution)/shard_map/pallas_call | solution.py:410
  101.2 7.5 %collective-permute-done.21 = bf16[2,128,1152]{2,1,0:T(8,128)(2,1)S(1)} collective-permute-done((bf16[2,128,1152]{2,1,0:T(8,128)(2,1)S(1)}, bf16[2,128,1152]{2,1,0:T(8,128)(2,1)S(1)}, u32[]{:S(2)}, u32[]{:S(2)}) %collective-permute-start.21) | collective-permute-done | bytes 589856 | tf_op jit(solution)/shard_map/ppermute | solution.py:43
  114.9 30.1 %collective-permute-done.29 = bf16[1,576,256]{2,1,0:T(8,128)(2,1)S(1)} collective-permute-done((bf16[1,576,256]{2,1,0:T(8,128)(2,1)S(1)}, bf16[1,576,256]{2,1,0:T(8,128)(2,1)S(1)}, u32[]{:S(2)}, u32[]{:S(2)}) %collective-permute-start.29) | collective-permute-done | bytes 294944 | tf_op jit(solution)/shard_map/ppermute | solution.py:43
  151.2 18.4 %shard_map.187 = (bf16[2048,1152]{1,0:T(8,128)(2,1)}, bf16[2048,1152]{1,0:T(8,128)(2,1)}, bf16[2048,1152]{1,0:T(8,128)(2,1)}, bf16[2048,1024]{1,0:T(8,128)(2,1)}) custom-call(s32[2]{0:T(128)} %pad_add_fusion.ids_ref, bf16[512,1024]{1,0:T(8,128)(2,1)} %get-tuple-element.421.refs_0_, bf16[512,1024]{1,0:T(8,128)(2,1)} %copy-done.41, ...), custom_call_target="tpu_custom_call" | custom-call | flops 68719476736 | bytes 1048576 | tf_op jit(solution)/shard_map/pallas_call | solution.py:168
  172.7 10.3 %shard_map.188 = (bf16[4,288,256]{2,1,0:T(8,128)(2,1)}, bf16[4,288,256]{2,1,0:T(8,128)(2,1)}, bf16[4,288,256]{2,1,0:T(8,128)(2,1)}, bf16[4,288,256]{2,1,0:T(8,128)(2,1)}) custom-call(s32[2]{0:T(128)} %pad_add_fusion.ids_ref, bf16[2048,1152]{1,0:T(8,128)(2,1)} %get-tuple-element.437.refs_0_.refs_4_, ...), custom_call_target="tpu_custom_call" | custom-call | flops 68719476736 | bytes 1048576 | tf_op jit(solution)/shard_map/pallas_call | solution.py:328
  187.5 33.8 %shard_map.189 = (bf16[2048,1152]{1,0:T(8,128)(2,1)}, bf16[2048,1152]{1,0:T(8,128)(2,1)}, bf16[512,1024]{1,0:T(8,128)(2,1)}, bf16[512,1024]{1,0:T(8,128)(2,1)}, ...) custom-call(s32[2]{0:T(128)} %pad_add_fusion.ids_ref, ...), custom_call_target="tpu_custom_call" | custom-call | flops 68719476736 | bytes 1048576 | tf_op jit(solution)/shard_map/pallas_call | solution.py:168
  232.9 11.1 %shard_map.190 = (bf16[4,64,1152]{2,1,0:T(8,128)(2,1)}, bf16[4,64,1152]{2,1,0:T(8,128)(2,1)}, bf16[4,64,1152]{2,1,0:T(8,128)(2,1)}, bf16[4,64,1152]{2,1,0:T(8,128)(2,1)}) custom-call(s32[2]{0:T(128)} %pad_add_fusion.ids_ref, bf16[2048,1024]{1,0:T(8,128)(2,1)} %get-tuple-element.429.refs_0_, bf16[2048,1152]{1,0:T(8,128)(2,1)} %get-tuple-element.492.refs_1_), custom_call_target="tpu_custom_call" | custom-call | flops 68719476736 | bytes 1048576 | tf_op jit(solution)/shard_map/pallas_call | solution.py:328
  250.2 10.9 %shard_map.191 = (bf16[4,64,1152]{2,1,0:T(8,128)(2,1)}, bf16[4,64,1152]{2,1,0:T(8,128)(2,1)}, bf16[4,64,1152]{2,1,0:T(8,128)(2,1)}, bf16[4,64,1152]{2,1,0:T(8,128)(2,1)}) custom-call(s32[2]{0:T(128)} %pad_add_fusion.ids_ref, bf16[2048,1024]{1,0:T(8,128)(2,1)} %get-tuple-element.429.refs_0_, bf16[2048,1152]{1,0:T(8,128)(2,1)} %get-tuple-element.527.refs_1_), custom_call_target="tpu_custom_call" | custom-call | flops 68719476736 | bytes 1048576 | tf_op jit(solution)/shard_map/pallas_call | solution.py:328
  263.0 6.1 %collective-permute-done.46 = bf16[4,64,1152]{2,1,0:T(8,128)(2,1)S(1)} collective-permute-done((bf16[4,64,1152]{2,1,0:T(8,128)(2,1)S(1)}, bf16[4,64,1152]{2,1,0:T(8,128)(2,1)S(1)}, u32[]{:S(2)}, u32[]{:S(2)}) %collective-permute-start.46) | collective-permute-done | bytes 589856 | tf_op jit(solution)/shard_map/ppermute | solution.py:43
  276.0 14.7 %shard_map.192 = (f32[512,1024]{1,0:T(8,128)}, bf16[512,1024]{1,0:T(8,128)(2,1)}, f32[512,1024]{1,0:T(8,128)}, f32[8,1024]{1,0:T(8,128)}, f32[8,1024]{1,0:T(8,12...) custom-call(s32[2]{0:T(128)} %pad_add_fusion.ids_ref, bf16[512,1024]{1,0:T(8,128)(2,1)} %get-tuple-element.510.refs_0_, ...), custom_call_target="tpu_custom_call" | custom-call | flops 68719476736 | bytes 1048576 | tf_op jit(solution)/shard_map/pallas_call | solution.py:503
  291.5 5.7 %collective-permute-done.50 = bf16[4,64,1152]{2,1,0:T(8,128)(2,1)S(1)} collective-permute-done((bf16[4,64,1152]{2,1,0:T(8,128)(2,1)S(1)}, bf16[4,64,1152]{2,1,0:T(8,128)(2,1)S(1)}, u32[]{:S(2)}, u32[]{:S(2)}) %collective-permute-start.50) | collective-permute-done | bytes 589856 | tf_op jit(solution)/shard_map/ppermute | solution.py:43
  303.3 4.2 %collective-permute-start.55 = (bf16[2,64,1152]{2,1,0:T(8,128)(2,1)S(1)}, bf16[2,64,1152]{2,1,0:T(8,128)(2,1)S(1)}, u32[]{:S(2)}, u32[]{:S(2)}) collective-permute-start(bf16[2,64,1152]{2,1,0:T(8,128)(2,1)S(1)} %get-tuple-element.600), channel_id=1, source_target_pairs={{0,2},{1,3},{2,0},{3,1},{4,6},{5,7},{6,4},{7,5},{8,10},{9,11},{10,... | collective-permute-start | bytes 884744 | tf_op jit(solution)/shard_map/ppermute | solution.py:43
  309.7 12.7 %shard_map.193 = (bf16[512,3072]{1,0:T(8,128)(2,1)}, bf16[16,128,256]{2,1,0:T(8,128)(2,1)}, bf16[16,128,256]{2,1,0:T(8,128)(2,1)}, bf16[16,128,256]{2,1,0:T(8,12...) custom-call(s32[2]{0:T(128)} %pad_add_fusion.ids_ref, ...), custom_call_target="tpu_custom_call" | custom-call | flops 68719476736 | bytes 1048576 | tf_op jit(solution)/shard_map/pallas_call | solution.py:560
  324.6 10.7 %shard_map.194 = (bf16[512,1024]{1,0:T(8,128)(2,1)}, f32[8,1024]{1,0:T(8,128)}) custom-call(s32[2]{0:T(128)} %pad_add_fusion.ids_ref, bf16[512,3072]{1,0:T(8,128)(2,1)} %get-tuple-element.634.proj_ref, bf16[512,1024]{1,0:T(8,128)(2,1)} %x_ref, f32[512,1024]{1,0:T(8,128)} %get-tuple-element.635.hidden_ref, f32[8,1024]{1,0:T(8,128)} %get-tuple-element.636.sums_ref, ...), custom_call_target="tpu_custom_call" | custom-call | flops 68719476736 | bytes 1048576 | tf_op jit(solution)/shard_map/pallas_call | solution.py:612
  348.7 9.3 %collective-permute-done.71 = f32[8,1024]{1,0:T(8,128)S(1)} collective-permute-done((f32[8,1024]{1,0:T(8,128)S(1)}, f32[8,1024]{1,0:T(8,128)S(1)}, u32[]{:S(2)}, u32[]{:S(2)}) %collective-permute-start.71) | collective-permute-done | bytes 32800 | tf_op jit(solution)/shard_map/ppermute | solution.py:43
  359.8 6.2 %collective-permute-done.69 = bf16[4,128,256]{2,1,0:T(8,128)(2,1)S(1)} collective-permute-done((bf16[4,128,256]{2,1,0:T(8,128)(2,1)S(1)}, bf16[4,128,256]{2,1,0:T(8,128)(2,1)S(1)}, u32[]{:S(2)}, u32[]{:S(2)}) %collective-permute-start.69) | collective-permute-done | bytes 262176 | tf_op jit(solution)/shard_map/ppermute | solution.py:43
  391.1 4.0 collective-permute-done.77
  (380 shorter events, 155.9 us)
Async XLA Ops:
  38.9 21.8 %collective-permute-start.13 = (bf16[1,128,1152]{2,1,0:T(8,128)(2,1)S(1)}, bf16[1,128,1152]{2,1,0:T(8,128)(2,1)S(1)}, u32[]{:S(2)}, u32[]{:S(2)}) collective-permute-start(bf16[1,128,1152]{2,1,0:T(8,128)(2,1)S(1)} %bitcast.42), channel_id=1, source_target_pairs={{0,4},{1,5},{2,6},{3,7},{4,0},{5,1},{6,2},{7,3},{8,12},{9,13},{10,... | collective-permute-start | bytes 884744 | tf_op jit(solution)/shard_map/ppermute | solution.py:43
  40.8 23.8 %collective-permute-start.12 = (bf16[1,128,1152]{2,1,0:T(8,128)(2,1)S(1)}, bf16[1,128,1152]{2,1,0:T(8,128)(2,1)S(1)}, u32[]{:S(2)}, u32[]{:S(2)}) collective-permute-start(bf16[1,128,1152]{2,1,0:T(8,128)(2,1)S(1)} %bitcast.44), channel_id=1, source_target_pairs={{0,4},{1,5},{2,6},{3,7},{4,0},{5,1},{6,2},{7,3},{8,12},{9,13},{10,... | collective-permute-start | bytes 884744 | tf_op jit(solution)/shard_map/ppermute | solution.py:43
  41.9 28.5 %collective-permute-start.7 = (bf16[8,128,384]{2,1,0:T(8,128)(2,1)S(1)}, bf16[8,128,384]{2,1,0:T(8,128)(2,1)S(1)}, u32[]{:S(2)}, u32[]{:S(2)}) collective-permute-start(bf16[8,128,384]{2,1,0:T(8,128)(2,1)S(1)} %pad_maximum_fusion.6), channel_id=1, source_target_pairs={{0,1},{1,0},{2,3},{3,2},{4,5},{5,4},{6,7},{7,6},{8,9},{9,8},{10,11... | collective-permute-start | bytes 2359304 | tf_op jit(solution)/shard_map/ppermute | solution.py:43
  43.4 26.0 %collective-permute-start.11 = (bf16[8,128,256]{2,1,0:T(8,128)(2,1)S(1)}, bf16[8,128,256]{2,1,0:T(8,128)(2,1)S(1)}, u32[]{:S(2)}, u32[]{:S(2)}) collective-permute-start(bf16[8,128,256]{2,1,0:T(8,128)(2,1)S(1)} %pad_maximum_fusion.13), channel_id=1, source_target_pairs={{0,2},{1,3},{2,0},{3,1},{4,6},{5,7},{6,4},{7,5},{8,10},{9,11},{10,... | collective-permute-start | bytes 1572872 | tf_op jit(solution)/shard_map/ppermute | solution.py:43
  79.8 30.8 %collective-permute-start.25 = (bf16[512,1024]{1,0:T(8,128)(2,1)}, bf16[512,1024]{1,0:T(8,128)(2,1)S(1)}, u32[]{:S(2)}, u32[]{:S(2)}) collective-permute-start(bf16[512,1024]{1,0:T(8,128)(2,1)} %multiply_convert_fusion.1.refs_1_.refs_0_.refs_2_), channel_id=1, source_target_pairs={{0,16},{8,24},{16,0},{24,8},{1,17},{9,25},{17,1},{25,9},{2,18},{10... | collective-permute-start | bytes 3145736 | tf_op jit(solution)/shard_map/ppermute | solution.py:43
  81.3 29.4 %collective-permute-start.24 = (bf16[512,1024]{1,0:T(8,128)(2,1)}, bf16[512,1024]{1,0:T(8,128)(2,1)S(1)}, u32[]{:S(2)}, u32[]{:S(2)}) collective-permute-start(bf16[512,1024]{1,0:T(8,128)(2,1)} %multiply_convert_fusion.1.refs_1_.refs_0_.refs_2_), channel_id=1, source_target_pairs={{0,8},{8,0},{16,24},{24,16},{1,9},{9,1},{17,25},{25,17},{2,10},{10... | collective-permute-start | bytes 3145736 | tf_op jit(solution)/shard_map/ppermute | solution.py:43
  81.3 27.7 %collective-permute-start.23 = (bf16[576,256]{1,0:T(8,128)(2,1)}, bf16[576,256]{1,0:T(8,128)(2,1)S(1)}, u32[]{:S(2)}, u32[]{:S(2)}) collective-permute-start(bf16[576,256]{1,0:T(8,128)(2,1)} %param.19), channel_id=1, source_target_pairs={{0,0},{1,1},{2,8},{3,9},{4,16},{5,17},{6,24},{7,25},{8,4},{9,5},{1... | collective-permute-start | bytes 884744 | tf_op jit(solution)/shard_map/ppermute | solution.py:794
  83.1 25.6 %collective-permute-start.21 = (bf16[2,128,1152]{2,1,0:T(8,128)(2,1)S(1)}, bf16[2,128,1152]{2,1,0:T(8,128)(2,1)S(1)}, u32[]{:S(2)}, u32[]{:S(2)}) collective-permute-start(bf16[2,128,1152]{2,1,0:T(8,128)(2,1)S(1)} %pad_maximum_fusion.8), channel_id=1, source_target_pairs={{0,2},{1,3},{2,0},{3,1},{4,6},{5,7},{6,4},{7,5},{8,10},{9,11},{10,... | collective-permute-start | bytes 1769480 | tf_op jit(solution)/shard_map/ppermute | solution.py:43
  85.6 23.2 %collective-permute-start.22 = (bf16[2,128,1152]{2,1,0:T(8,128)(2,1)S(1)}, bf16[2,128,1152]{2,1,0:T(8,128)(2,1)S(1)}, u32[]{:S(2)}, u32[]{:S(2)}) collective-permute-start(bf16[2,128,1152]{2,1,0:T(8,128)(2,1)S(1)} %pad_maximum_fusion.9), channel_id=1, source_target_pairs={{0,1},{1,0},{2,3},{3,2},{4,5},{5,4},{6,7},{7,6},{8,9},{9,8},{10,11... | collective-permute-start | bytes 1769480 | tf_op jit(solution)/shard_map/ppermute | solution.py:43
  110.7 34.4 %collective-permute-start.27 = (bf16[4,128,1152]{2,1,0:T(8,128)(2,1)S(1)}, bf16[4,128,1152]{2,1,0:T(8,128)(2,1)S(1)}, u32[]{:S(2)}, u32[]{:S(2)}) collective-permute-start(bf16[4,128,1152]{2,1,0:T(8,128)(2,1)S(1)} %pad_maximum_fusion.2.refs_4_.refs_7_), channel_id=1, source_target_pairs={{0,1},{1,0},{2,3},{3,2},{4,5},{5,4},{6,7},{7,6},{8,9},{9,8},{10,11... | collective-permute-start | bytes 3538952 | tf_op jit(solution)/shard_map/ppermute | solution.py:43
  112.4 33.3 %collective-permute-start.28 = (bf16[4,128,1152]{2,1,0:T(8,128)(2,1)S(1)}, bf16[4,128,1152]{2,1,0:T(8,128)(2,1)S(1)}, u32[]{:S(2)}, u32[]{:S(2)}) collective-permute-start(bf16[4,128,1152]{2,1,0:T(8,128)(2,1)S(1)} %pad_maximum_fusion.3.refs_6_.refs_9_), channel_id=1, source_target_pairs={{0,2},{1,3},{2,0},{3,1},{4,6},{5,7},{6,4},{7,5},{8,10},{9,11},{10,... | collective-permute-start | bytes 3538952 | tf_op jit(solution)/shard_map/ppermute | solution.py:43
  112.4 32.6 %collective-permute-start.26 = (bf16[512,1024]{1,0:T(8,128)(2,1)S(1)}, bf16[512,1024]{1,0:T(8,128)(2,1)S(1)}, u32[]{:S(2)}, u32[]{:S(2)}) collective-permute-start(bf16[512,1024]{1,0:T(8,128)(2,1)S(1)} %copy-done.37), channel_id=1, source_target_pairs={{0,16},{8,24},{16,0},{24,8},{1,17},{9,25},{17,1},{25,9},{2,18},{10... | collective-permute-start | bytes 3145736 | tf_op jit(solution)/shard_map/ppermute | solution.py:43
  114.9 30.2 %collective-permute-start.30 = (bf16[512,1024]{1,0:T(8,128)(2,1)S(1)}, bf16[512,1024]{1,0:T(8,128)(2,1)S(1)}, u32[]{:S(2)}, u32[]{:S(2)}) collective-permute-start(bf16[512,1024]{1,0:T(8,128)(2,1)S(1)} %collective-permute-done.25.refs_3_.refs_2_), channel_id=1, source_target_pairs={{0,8},{8,0},{16,24},{24,16},{1,9},{9,1},{17,25},{25,17},{2,10},{10... | collective-permute-start | bytes 3145736 | tf_op jit(solution)/shard_map/ppermute | solution.py:43
  114.9 30.1 %collective-permute-start.29 = (bf16[1,576,256]{2,1,0:T(8,128)(2,1)S(1)}, bf16[1,576,256]{2,1,0:T(8,128)(2,1)S(1)}, u32[]{:S(2)}, u32[]{:S(2)}) collective-permute-start(bf16[1,576,256]{2,1,0:T(8,128)(2,1)S(1)} %bitcast.46), channel_id=1, source_target_pairs={{0,4},{1,5},{2,6},{3,7},{4,0},{5,1},{6,2},{7,3},{8,12},{9,13},{10,... | collective-permute-start | bytes 884744 | tf_op jit(solution)/shard_map/ppermute | solution.py:43
  149.9 19.8 %collective-permute-start.33 = (bf16[2,288,256]{2,1,0:T(8,128)(2,1)S(1)}, bf16[2,288,256]{2,1,0:T(8,128)(2,1)S(1)}, u32[]{:S(2)}, u32[]{:S(2)}) collective-permute-start(bf16[2,288,256]{2,1,0:T(8,128)(2,1)S(1)} %get-tuple-element.435), channel_id=1, source_target_pairs={{0,2},{1,3},{2,0},{3,1},{4,6},{5,7},{6,4},{7,5},{8,10},{9,11},{10,... | collective-permute-start | bytes 884744 | tf_op jit(solution)/shard_map/ppermute | solution.py:43
  186.4 35.0 %collective-permute-start.37 = (bf16[4,288,256]{2,1,0:T(8,128)(2,1)}, bf16[4,288,256]{2,1,0:T(8,128)(2,1)S(1)}, u32[]{:S(2)}, u32[]{:S(2)}) collective-permute-start(bf16[4,288,256]{2,1,0:T(8,128)(2,1)} %get-tuple-element.461), channel_id=1, source_target_pairs={{0,1},{1,0},{2,3},{3,2},{4,5},{5,4},{6,7},{7,6},{8,9},{9,8},{10,11... | collective-permute-start | bytes 1769480 | tf_op jit(solution)/shard_map/ppermute | solution.py:43
  186.7 34.6 %collective-permute-start.38 = (bf16[4,288,256]{2,1,0:T(8,128)(2,1)}, bf16[4,288,256]{2,1,0:T(8,128)(2,1)S(1)}, u32[]{:S(2)}, u32[]{:S(2)}) collective-permute-start(bf16[4,288,256]{2,1,0:T(8,128)(2,1)} %get-tuple-element.463), channel_id=1, source_target_pairs={{0,2},{1,3},{2,0},{3,1},{4,6},{5,7},{6,4},{7,5},{8,10},{9,11},{10,... | collective-permute-start | bytes 1769480 | tf_op jit(solution)/shard_map/ppermute | solution.py:43
  249.4 19.7 %collective-permute-start.46 = (bf16[4,64,1152]{2,1,0:T(8,128)(2,1)S(1)}, bf16[4,64,1152]{2,1,0:T(8,128)(2,1)S(1)}, u32[]{:S(2)}, u32[]{:S(2)}) collective-permute-start(bf16[4,64,1152]{2,1,0:T(8,128)(2,1)S(1)} %copy-done.44), channel_id=1, source_target_pairs={{0,2},{1,3},{2,0},{3,1},{4,6},{5,7},{6,4},{7,5},{8,10},{9,11},{10,... | collective-permute-start | bytes 1769480 | tf_op jit(solution)/shard_map/ppermute | solution.py:43
  269.7 21.0 %collective-permute-start.52 = (bf16[576,256]{1,0:T(8,128)(2,1)S(1)}, bf16[576,256]{1,0:T(8,128)(2,1)S(1)}, u32[]{:S(2)}, u32[]{:S(2)}) collective-permute-start(bf16[576,256]{1,0:T(8,128)(2,1)S(1)} %fusion), channel_id=1, source_target_pairs={{0,0},{1,1},{8,2},{9,3},{16,4},{17,5},{24,6},{25,7},{4,8},{5,9},{1... | collective-permute-start | bytes 884744 | tf_op jit(solution)/shard_map/ppermute | solution.py:896
  270.5 21.0 %collective-permute-start.51 = (bf16[256,1024]{1,0:T(8,128)(2,1)S(1)}, bf16[256,1024]{1,0:T(8,128)(2,1)S(1)}, u32[]{:S(2)}, u32[]{:S(2)}) collective-permute-start(bf16[256,1024]{1,0:T(8,128)(2,1)S(1)} %get-tuple-element.571), channel_id=1, source_target_pairs={{0,16},{8,24},{16,0},{24,8},{1,17},{9,25},{17,1},{25,9},{2,18},{10... | collective-permute-start | bytes 1572872 | tf_op jit(solution)/shard_map/ppermute | solution.py:43
  274.4 22.8 %collective-permute-start.50 = (bf16[4,64,1152]{2,1,0:T(8,128)(2,1)S(1)}, bf16[4,64,1152]{2,1,0:T(8,128)(2,1)S(1)}, u32[]{:S(2)}, u32[]{:S(2)}) collective-permute-start(bf16[4,64,1152]{2,1,0:T(8,128)(2,1)S(1)} %copy-done.43), channel_id=1, source_target_pairs={{0,2},{1,3},{2,0},{3,1},{4,6},{5,7},{6,4},{7,5},{8,10},{9,11},{10,... | collective-permute-start | bytes 1769480 | tf_op jit(solution)/shard_map/ppermute | solution.py:43
  343.0 23.0 %collective-permute-start.66 = (bf16[8,128,256]{2,1,0:T(8,128)(2,1)S(1)}, bf16[8,128,256]{2,1,0:T(8,128)(2,1)S(1)}, u32[]{:S(2)}, u32[]{:S(2)}) collective-permute-start(bf16[8,128,256]{2,1,0:T(8,128)(2,1)S(1)} %get-tuple-element.659), channel_id=1, source_target_pairs={{0,1},{1,0},{2,3},{3,2},{4,5},{5,4},{6,7},{7,6},{8,9},{9,8},{10,11... | collective-permute-start | bytes 1572872 | tf_op jit(solution)/shard_map/ppermute | solution.py:43
  343.5 22.5 %collective-permute-start.67 = (bf16[8,128,256]{2,1,0:T(8,128)(2,1)S(1)}, bf16[8,128,256]{2,1,0:T(8,128)(2,1)S(1)}, u32[]{:S(2)}, u32[]{:S(2)}) collective-permute-start(bf16[8,128,256]{2,1,0:T(8,128)(2,1)S(1)} %get-tuple-element.661), channel_id=1, source_target_pairs={{0,16},{8,24},{16,0},{24,8},{1,17},{9,25},{17,1},{25,9},{2,18},{10... | collective-permute-start | bytes 1572872 | tf_op jit(solution)/shard_map/ppermute | solution.py:43
  345.1 20.9 %collective-permute-start.68 = (bf16[8,128,256]{2,1,0:T(8,128)(2,1)S(1)}, bf16[8,128,256]{2,1,0:T(8,128)(2,1)S(1)}, u32[]{:S(2)}, u32[]{:S(2)}) collective-permute-start(bf16[8,128,256]{2,1,0:T(8,128)(2,1)S(1)} %get-tuple-element.663), channel_id=1, source_target_pairs={{0,2},{1,3},{2,0},{3,1},{4,6},{5,7},{6,4},{7,5},{8,10},{9,11},{10,... | collective-permute-start | bytes 1572872 | tf_op jit(solution)/shard_map/ppermute | solution.py:43
  (116 other events, 1228.9 us)

commit v6 on v5

--- a/solution.py
+++ b/solution.py
@@ -660,7 +660,7 @@
     zs = [("seq", b) for b in reversed(seq_bits[len(along_y) :])]
     core = [("dp", 1)]
     xs = [("dp", b) for b in reversed(bits_below(n_dp)[1:])]
-    in_orders = [zs + xs + ys + core, ys + zs + xs + core]
+    in_orders = [zs + xs + ys + core, zs[::-1] + ys + xs + core]
     out_order = zs[:1] + xs + ys + zs[1:] + core
     far_order, near_order = zs[:1] + ys + zs[1:], zs + ys
     token_order = xs + core
@@ -784,7 +784,7 @@
     ]
     in_grads = [
         Piece(order, (in_rows, third), in_view(i * third, (i + 1) * third))
-        for i, order in enumerate(orders)
+        for i, order in enumerate((in_orders[0], ys + zs + xs + core, out_order))
     ]
     out_grads = [Piece(zs + xs + ys + core, out_weight.shape, out_view)]
     out_pieces = [Piece(out_order, out_weight.shape, out_view)]
@@ -854,40 +854,39 @@
     back, feed, grad_gate, grad_up, down_parts = tie(back, feed, grad_gate, grad_up, down_parts)
     near, near_send, far, far_send = core_halves(back)
     far_come = [swap(v, core[0]) for v in far_send]
+    down_parts = sent_on(fold_all(down_parts), down)
     far, far_come, near, near_send, grad_gate, grad_up, feed, down_parts = tie(
         far, far_come, near, near_send, grad_gate, grad_up, feed, down_parts
     )
     far = far_added(far, far_come)
     half_rows = tok_rows // 2
     far_low, far_high = [v[:half_rows] for v in far], [v[half_rows:] for v in far]
-    down_parts = fold_all(down_parts)
+    down_parts = joined(fold_all(down_parts))
     far_low, far_high, down_parts, near, near_send, grad_gate, grad_up, feed = tie(
         far_low, far_high, down_parts, near, near_send, grad_gate, grad_up, feed
     )
     far_low = dp_scatter([None] + far_low, xs)
     near_more = swap(near_send, core[0])
-    down_parts = sent_on(down_parts, down)
+    down_parts = sent(down_parts, down, 0)
     gate_parts = weight_gradient(ids, [normed_all], [grad_gate], feed_grads)
     gate_parts, far_low, far_high, grad_up, near, near_more, down_parts, feed = tie(
         gate_parts, far_low, far_high, grad_up, near, near_more, down_parts, feed
     )
-    down_parts = joined(fold_all(down_parts))
+    own_down = folded(down_parts[0]).astype(jnp.bfloat16)
     feed_near, feed_send, feed_far, feed_come = core_halves(feed)
-    down_parts, gate_parts, feed_far, feed_come, grad_up, far_low, far_high = tie(
-        down_parts, gate_parts, feed_far, feed_come, grad_up, far_low, far_high
+    own_down, gate_parts, feed_far, feed_come, grad_up, far_low, far_high = tie(
+        own_down, gate_parts, feed_far, feed_come, grad_up, far_low, far_high
     )
     far_high = dp_scatter([None] + far_high, xs)
     gate_parts = sent(gate_parts, feed_grads, -1)
     feed_come = [swap(v, core[0]) for v in feed_come]
-    down_parts = sent(down_parts, down, 0)
     up_parts = weight_gradient(ids, [normed_all], [grad_up], feed_grads)
-    up_parts, far_low, far_high, gate_parts, feed_far, feed_come, down_parts = tie(
-        up_parts, far_low, far_high, gate_parts, feed_far, feed_come, down_parts
+    up_parts, far_low, far_high, gate_parts, feed_far, feed_come, own_down = tie(
+        up_parts, far_low, far_high, gate_parts, feed_far, feed_come, own_down
     )
 
     feed_far = far_added(feed_far, feed_come)
     feed_low, feed_high = [v[:half_rows] for v in feed_far], [v[half_rows:] for v in feed_far]
-    own_down = folded(down_parts[0]).astype(jnp.bfloat16)
     feed_low, feed_high, up_parts, gate_parts, far_low, far_high, own_down = tie(
         feed_low, feed_high, up_parts, gate_parts, far_low, far_high, own_down
     )
@@ -938,20 +937,19 @@
     in_parts, out_parts, up_parts = fold_all(in_parts), fold_all(out_parts), joined(fold_all(up_parts))
     in_parts, out_parts, up_parts, sums = tie(in_parts, out_parts, up_parts, sums)
     in_parts = sent(in_parts, in_grads, -2)
+    sums = (sums, swap(sums, sum_steps[1]))
+    in_parts, out_parts, up_parts, sums, feed_send = tie(in_parts, out_parts, up_parts, sums, feed_send)
+    in_parts, sums = fold_all(in_parts), sums[0] + sums[1]
+    in_parts, out_parts, up_parts, sums = tie(in_parts, out_parts, up_parts, sums)
+    in_parts = sent(in_parts, in_grads, -3)
     out_parts = sent(out_parts, out_grads, -3)
     up_parts = sent(up_parts, feed_grads, 0)
-    sums = (sums, swap(sums, sum_steps[1]))
+    sums = (sums, swap(sums, sum_steps[2]))
     in_parts, out_parts, up_parts, sums, feed_send = tie(in_parts, out_parts, up_parts, sums, feed_send)
     in_parts, out_parts, sums = fold_all(in_parts), fold_all(out_parts), sums[0] + sums[1]
     in_parts, out_parts, sums = tie(in_parts, out_parts, sums)
-    in_parts = sent(in_parts, in_grads, -3)
+    in_parts = sent(in_parts, in_grads, -4)
     out_parts = sent(out_parts, out_grads, -4)
-    sums = (sums, swap(sums, sum_steps[2]))
-    in_parts, out_parts, sums, feed_send = tie(in_parts, out_parts, sums, feed_send)
-    in_parts, out_parts, sums = fold_all(in_parts), fold_all(out_parts), sums[0] + sums[1]
-    in_parts, out_parts, sums = tie(in_parts, out_parts, sums)
-    in_parts = sent(in_parts, in_grads, -4)
-    out_parts = sent(out_parts, out_grads, -5)
     sums = (sums, swap(sums, sum_steps[3]))
     feed_more = swap(feed_send, core[0])
     in_parts, out_parts, sums, feed_more, own_down = tie(in_parts, out_parts, sums, feed_more, own_down)
@@ -968,7 +966,7 @@
 
     own_in = [rest(v, p, 4) for v, p in zip(in_parts, in_grads)]
     own_in = jnp.concatenate(own_in, axis=1)
-    own_out = rest(out_parts[0], out_grads[0], 5)
+    own_out = rest(out_parts[0], out_grads[0], 4)
     own_gate = folded(gate_parts[0])
     own_up = folded(up_parts[0])
     own_sums = lax.dynamic_slice(sums, (0, own_seq * small_cols), (8, small_cols))

time: 412 us -> 408 us (level)
  waiting for transfers between devices: 142 us -> 136 us
  starting transfers between devices: 90.1 us -> 94.6 us
    ppermute x83, waiting for transfers between devices: 142 us -> 136 us  [swap(): return lax.ppermute(shard, axis, [(i, i ^ bit) for i in range(count)])]
    ppermute x83, starting transfers between devices: 83.5 us -> 88.5 us  [swap(): return lax.ppermute(shard, axis, [(i, i ^ bit) for i in range(count)])]
    unnamed x107 -> x109, local copies, waits for them, and re-layouts: 8.89 us -> 5.98 us
  transfers between devices with their start and end apart: 87 -> 87, of which waited for: 37 -> 41; matrix products, arithmetic and copies ran while one was open for 5% -> 5% of each run, Pallas kernels for 33% -> 34%
where the time goes in v6:
time: 408 us; the launch traced here: 404 us
  Pallas kernels  137 us (34%)
  waiting for transfers between devices  136 us (33%)
  starting transfers between devices  94.6 us (23%)
  other arithmetic  21.2 us (5%)
  local copies, waits for them, and re-layouts  12 us (3%)
    ppermute x83, waiting for transfers between devices, swap(): return lax.ppermute(shard, axis, [(i, i ^ bit) for i in range(count)])  136 us
    ppermute x83, starting transfers between devices, swap(): return lax.ppermute(shard, axis, [(i, i ^ bit) for i in range(count)])  88.5 us
    pallas_call x2, Pallas kernels, token_call(): pl.pallas_call(kernel, out_shape=[jax.ShapeDtypeStruct((rows * steps, n),...  52.4 us
    pallas_call x3, Pallas kernels, weight_gradient(): pl.pallas_call(kernel, out_shape=shapes, grid_spec=pltpu.PrefetchScalarGr...  32.3 us
    pallas_call x1, Pallas kernels, mixer_back(): pl.pallas_call(kernel, out_shape=[jax.ShapeDtypeStruct((rows, features),...  14.7 us
    pallas_call x1, Pallas kernels, mixer_forward(): pl.pallas_call(kernel, out_shape=[jax.ShapeDtypeStruct(s, t) for s, t in...  14 us
    pallas_call x1, Pallas kernels, projection_gradient(): pl.pallas_call(kernel, out_shape=[jax.ShapeDtypeStruct((rows, 3 * feature...  13 us
    pallas_call x1, Pallas kernels, mixer_first(): pl.pallas_call(kernel, out_shape=[jax.ShapeDtypeStruct((rows, features),...  10.7 us
  transfers between devices with their start and end apart: 87, of which 41 were waited for; matrix products, arithmetic and copies ran while one was open for 5% of the time, Pallas kernels for 34%

profile of v6, /device:TPU:0, one launch (start us, length us, event | category | flops | bytes accessed | tf_op | source)
XLA Modules:
  0.0 403.9 jit_solution(6789358337379280341)
XLA Ops:
  0.7 4.1 %collective-permute-start.2 = (bf16[1,128,256]{2,1,0:T(8,128)(2,1)}, bf16[1,128,256]{2,1,0:T(8,128)(2,1)S(1)}, u32[]{:S(2)}, u32[]{:S(2)}) collective-permute-start(bf16[1,128,256]{2,1,0:T(8,128)(2,1)} %bitcast.48), channel_id=1, source_target_pairs={{0,4},{1,5},{2,6},{3,7},{4,0},{5,1},{6,2},{7,3},{8,12},{9,13},{10,... | collective-permute-start | bytes 196616 | tf_op jit(solution)/shard_map/ppermute | solution.py:43
  10.7 3.6 collective-permute-done
  22.2 4.7 %collective-permute-done.3 = bf16[2,128,384]{2,1,0:T(8,128)(2,1)S(1)} collective-permute-done((bf16[2,128,384]{2,1,0:T(8,128)(2,1)S(1)}, bf16[2,128,384]{2,1,0:T(8,128)(2,1)S(1)}, u32[]{:S(2)}, u32[]{:S(2)}) %collective-permute-start.3) | collective-permute-done | bytes 196640 | tf_op jit(solution)/shard_map/ppermute | solution.py:43
  39.1 8.6 %collective-permute-start.13 = (bf16[1,128,1152]{2,1,0:T(8,128)(2,1)S(1)}, bf16[1,128,1152]{2,1,0:T(8,128)(2,1)S(1)}, u32[]{:S(2)}, u32[]{:S(2)}) collective-permute-start(bf16[1,128,1152]{2,1,0:T(8,128)(2,1)S(1)} %bitcast.42), channel_id=1, source_target_pairs={{0,4},{1,5},{2,6},{3,7},{4,0},{5,1},{6,2},{7,3},{8,12},{9,13},{10,... | collective-permute-start | bytes 884744 | tf_op jit(solution)/shard_map/ppermute | solution.py:43
  48.1 5.6 %collective-permute-done.8 = bf16[4,128,384]{2,1,0:T(8,128)(2,1)S(1)} collective-permute-done((bf16[4,128,384]{2,1,0:T(8,128)(2,1)S(1)}, bf16[4,128,384]{2,1,0:T(8,128)(2,1)S(1)}, u32[]{:S(2)}, u32[]{:S(2)}) %collective-permute-start.8) | collective-permute-done | bytes 393248 | tf_op jit(solution)/shard_map/ppermute | solution.py:43
  55.3 4.3 %collective-permute-done.13 = bf16[1,128,1152]{2,1,0:T(8,128)(2,1)S(1)} collective-permute-done((bf16[1,128,1152]{2,1,0:T(8,128)(2,1)S(1)}, bf16[1,128,1152]{2,1,0:T(8,128)(2,1)S(1)}, u32[]{:S(2)}, u32[]{:S(2)}) %collective-permute-start.13) | collective-permute-done | bytes 294944 | tf_op jit(solution)/shard_map/ppermute | solution.py:43
  59.7 3.8 collective-permute-done.12
  70.4 6.4 %collective-permute-done.20.refs_5_.refs_11_ = bf16[16,128,256]{2,1,0:T(8,128)(2,1)} collective-permute-done((bf16[16,128,256]{2,1,0:T(8,128)(2,1)}, bf16[16,128,256]{2,1,0:T(8,128)(2,1)}, u32[]{:S(2)}, u32[]{:S(2)}) %collective-permute-start.20) | collective-permute-done | bytes 1048608 | tf_op jit(solution)/shard_map/ppermute | solution.py:43
  83.1 14.0 %shard_map.186 = (bf16[512,1024]{1,0:T(8,128)(2,1)}, bf16[512,1024]{1,0:T(8,128)(2,1)}, bf16[512,1024]{1,0:T(8,128)(2,1)}, bf16[512,1024]{1,0:T(8,128)(2,1)}, bf...) custom-call(s32[2]{0:T(128)} %pad_add_fusion.ids_ref, ...), custom_call_target="tpu_custom_call" | custom-call | flops 68719476736 | bytes 1048576 | tf_op jit(solution)/shard_map/pallas_call | solution.py:410
  97.1 7.8 %collective-permute-done.21 = bf16[2,128,1152]{2,1,0:T(8,128)(2,1)S(1)} collective-permute-done((bf16[2,128,1152]{2,1,0:T(8,128)(2,1)S(1)}, bf16[2,128,1152]{2,1,0:T(8,128)(2,1)S(1)}, u32[]{:S(2)}, u32[]{:S(2)}) %collective-permute-start.21) | collective-permute-done | bytes 589856 | tf_op jit(solution)/shard_map/ppermute | solution.py:43
  112.8 28.1 %collective-permute-done.29 = bf16[1,576,256]{2,1,0:T(8,128)(2,1)S(1)} collective-permute-done((bf16[1,576,256]{2,1,0:T(8,128)(2,1)S(1)}, bf16[1,576,256]{2,1,0:T(8,128)(2,1)S(1)}, u32[]{:S(2)}, u32[]{:S(2)}) %collective-permute-start.29) | collective-permute-done | bytes 294944 | tf_op jit(solution)/shard_map/ppermute | solution.py:43
  149.0 18.4 %shard_map.187 = (bf16[2048,1152]{1,0:T(8,128)(2,1)}, bf16[2048,1152]{1,0:T(8,128)(2,1)}, bf16[2048,1152]{1,0:T(8,128)(2,1)}, bf16[2048,1024]{1,0:T(8,128)(2,1)}) custom-call(s32[2]{0:T(128)} %pad_add_fusion.ids_ref, bf16[512,1024]{1,0:T(8,128)(2,1)} %get-tuple-element.419.refs_0_, bf16[512,1024]{1,0:T(8,128)(2,1)} %copy-done.44, ...), custom_call_target="tpu_custom_call" | custom-call | flops 68719476736 | bytes 1048576 | tf_op jit(solution)/shard_map/pallas_call | solution.py:168
  170.3 10.3 %shard_map.188 = (bf16[4,288,256]{2,1,0:T(8,128)(2,1)}, bf16[4,288,256]{2,1,0:T(8,128)(2,1)}, bf16[4,288,256]{2,1,0:T(8,128)(2,1)}, bf16[4,288,256]{2,1,0:T(8,128)(2,1)}) custom-call(s32[2]{0:T(128)} %pad_add_fusion.ids_ref, bf16[2048,1152]{1,0:T(8,128)(2,1)} %get-tuple-element.435.refs_0_.refs_4_, ...), custom_call_target="tpu_custom_call" | custom-call | flops 68719476736 | bytes 1048576 | tf_op jit(solution)/shard_map/pallas_call | solution.py:328
  185.5 33.9 %shard_map.189 = (bf16[2048,1152]{1,0:T(8,128)(2,1)}, bf16[2048,1152]{1,0:T(8,128)(2,1)}, bf16[512,1024]{1,0:T(8,128)(2,1)}, bf16[512,1024]{1,0:T(8,128)(2,1)}, ...) custom-call(s32[2]{0:T(128)} %pad_add_fusion.ids_ref, ...), custom_call_target="tpu_custom_call" | custom-call | flops 68719476736 | bytes 1048576 | tf_op jit(solution)/shard_map/pallas_call | solution.py:168
  222.5 6.8 %collective-permute-done.41 = bf16[2,288,256]{2,1,0:T(8,128)(2,1)S(1)} collective-permute-done((bf16[2,288,256]{2,1,0:T(8,128)(2,1)S(1)}, bf16[2,288,256]{2,1,0:T(8,128)(2,1)S(1)}, u32[]{:S(2)}, u32[]{:S(2)}) %collective-permute-start.41) | collective-permute-done | bytes 294944 | tf_op jit(solution)/shard_map/ppermute | solution.py:43
  234.0 11.2 %shard_map.190 = (bf16[4,64,1152]{2,1,0:T(8,128)(2,1)}, bf16[4,64,1152]{2,1,0:T(8,128)(2,1)}, bf16[4,64,1152]{2,1,0:T(8,128)(2,1)}, bf16[4,64,1152]{2,1,0:T(8,128)(2,1)}) custom-call(s32[2]{0:T(128)} %pad_add_fusion.ids_ref, bf16[2048,1024]{1,0:T(8,128)(2,1)} %get-tuple-element.427.refs_0_, bf16[2048,1152]{1,0:T(8,128)(2,1)} %get-tuple-element.490.refs_1_), custom_call_target="tpu_custom_call" | custom-call | flops 68719476736 | bytes 1048576 | tf_op jit(solution)/shard_map/pallas_call | solution.py:328
  248.8 10.9 %shard_map.191 = (bf16[4,64,1152]{2,1,0:T(8,128)(2,1)}, bf16[4,64,1152]{2,1,0:T(8,128)(2,1)}, bf16[4,64,1152]{2,1,0:T(8,128)(2,1)}, bf16[4,64,1152]{2,1,0:T(8,128)(2,1)}) custom-call(s32[2]{0:T(128)} %pad_add_fusion.ids_ref, bf16[2048,1024]{1,0:T(8,128)(2,1)} %get-tuple-element.427.refs_0_, bf16[2048,1152]{1,0:T(8,128)(2,1)} %get-tuple-element.521.refs_1_), custom_call_target="tpu_custom_call" | custom-call | flops 68719476736 | bytes 1048576 | tf_op jit(solution)/shard_map/pallas_call | solution.py:328
  264.3 4.2 %collective-permute-start.51 = (bf16[256,1024]{1,0:T(8,128)(2,1)S(1)}, bf16[256,1024]{1,0:T(8,128)(2,1)S(1)}, u32[]{:S(2)}, u32[]{:S(2)}) collective-permute-start(bf16[256,1024]{1,0:T(8,128)(2,1)S(1)} %get-tuple-element.563), channel_id=1, source_target_pairs={{0,16},{8,24},{16,0},{24,8},{1,17},{9,25},{17,1},{25,9},{2,18},{10... | collective-permute-start | bytes 1572872 | tf_op jit(solution)/shard_map/ppermute | solution.py:43
  270.3 14.7 %shard_map.192 = (f32[512,1024]{1,0:T(8,128)}, bf16[512,1024]{1,0:T(8,128)(2,1)}, f32[512,1024]{1,0:T(8,128)}, f32[8,1024]{1,0:T(8,128)}, f32[8,1024]{1,0:T(8,12...) custom-call(s32[2]{0:T(128)} %pad_add_fusion.ids_ref, bf16[512,1024]{1,0:T(8,128)(2,1)} %get-tuple-element.506.refs_0_, ...), custom_call_target="tpu_custom_call" | custom-call | flops 68719476736 | bytes 1048576 | tf_op jit(solution)/shard_map/pallas_call | solution.py:503
  286.6 5.5 %collective-permute-done.50 = bf16[4,64,1152]{2,1,0:T(8,128)(2,1)S(1)} collective-permute-done((bf16[4,64,1152]{2,1,0:T(8,128)(2,1)S(1)}, bf16[4,64,1152]{2,1,0:T(8,128)(2,1)S(1)}, u32[]{:S(2)}, u32[]{:S(2)}) %collective-permute-start.50) | collective-permute-done | bytes 589856 | tf_op jit(solution)/shard_map/ppermute | solution.py:43
  303.7 13.0 %shard_map.193 = (bf16[512,3072]{1,0:T(8,128)(2,1)}, bf16[16,128,256]{2,1,0:T(8,128)(2,1)}, bf16[16,128,256]{2,1,0:T(8,128)(2,1)}, bf16[16,128,256]{2,1,0:T(8,12...) custom-call(s32[2]{0:T(128)} %pad_add_fusion.ids_ref, ...), custom_call_target="tpu_custom_call" | custom-call | flops 68719476736 | bytes 1048576 | tf_op jit(solution)/shard_map/pallas_call | solution.py:560
  318.8 10.7 %shard_map.194 = (bf16[512,1024]{1,0:T(8,128)(2,1)}, f32[8,1024]{1,0:T(8,128)}) custom-call(s32[2]{0:T(128)} %pad_add_fusion.ids_ref, bf16[512,3072]{1,0:T(8,128)(2,1)} %get-tuple-element.626.proj_ref, bf16[512,1024]{1,0:T(8,128)(2,1)} %x_ref, f32[512,1024]{1,0:T(8,128)} %get-tuple-element.627.hidden_ref, f32[8,1024]{1,0:T(8,128)} %get-tuple-element.628.sums_ref, ...), custom_call_target="tpu_custom_call" | custom-call | flops 68719476736 | bytes 1048576 | tf_op jit(solution)/shard_map/pallas_call | solution.py:612
  341.2 11.3 %collective-permute-done.69 = f32[8,1024]{1,0:T(8,128)S(1)} collective-permute-done((f32[8,1024]{1,0:T(8,128)S(1)}, f32[8,1024]{1,0:T(8,128)S(1)}, u32[]{:S(2)}, u32[]{:S(2)}) %collective-permute-start.69) | collective-permute-done | bytes 32800 | tf_op jit(solution)/shard_map/ppermute | solution.py:43
  361.9 4.8 %collective-permute-done.70 = bf16[4,128,256]{2,1,0:T(8,128)(2,1)} collective-permute-done((bf16[4,128,256]{2,1,0:T(8,128)(2,1)}, bf16[4,128,256]{2,1,0:T(8,128)(2,1)}, u32[]{:S(2)}, u32[]{:S(2)}) %collective-permute-start.70) | collective-permute-done | bytes 262176 | tf_op jit(solution)/shard_map/ppermute | solution.py:43
  (382 shorter events, 154.2 us)
Async XLA Ops:
  30.5 17.3 %collective-permute-start.6 = (bf16[4,128,384]{2,1,0:T(8,128)(2,1)S(1)}, bf16[4,128,384]{2,1,0:T(8,128)(2,1)S(1)}, u32[]{:S(2)}, u32[]{:S(2)}) collective-permute-start(bf16[4,128,384]{2,1,0:T(8,128)(2,1)S(1)} %pad_maximum_fusion.14), channel_id=1, source_target_pairs={{0,16},{8,24},{16,0},{24,8},{1,17},{9,25},{17,1},{25,9},{2,18},{10... | collective-permute-start | bytes 1179656 | tf_op jit(solution)/shard_map/ppermute | solution.py:43
  37.5 16.2 %collective-permute-start.8 = (bf16[4,128,384]{2,1,0:T(8,128)(2,1)S(1)}, bf16[4,128,384]{2,1,0:T(8,128)(2,1)S(1)}, u32[]{:S(2)}, u32[]{:S(2)}) collective-permute-start(bf16[4,128,384]{2,1,0:T(8,128)(2,1)S(1)} %pad_maximum_fusion.15), channel_id=1, source_target_pairs={{0,1},{1,0},{2,3},{3,2},{4,5},{5,4},{6,7},{7,6},{8,9},{9,8},{10,11... | collective-permute-start | bytes 1179656 | tf_op jit(solution)/shard_map/ppermute | solution.py:43
  39.1 20.5 %collective-permute-start.13 = (bf16[1,128,1152]{2,1,0:T(8,128)(2,1)S(1)}, bf16[1,128,1152]{2,1,0:T(8,128)(2,1)S(1)}, u32[]{:S(2)}, u32[]{:S(2)}) collective-permute-start(bf16[1,128,1152]{2,1,0:T(8,128)(2,1)S(1)} %bitcast.42), channel_id=1, source_target_pairs={{0,4},{1,5},{2,6},{3,7},{4,0},{5,1},{6,2},{7,3},{8,12},{9,13},{10,... | collective-permute-start | bytes 884744 | tf_op jit(solution)/shard_map/ppermute | solution.py:43
  47.9 19.5 %collective-permute-start.7 = (bf16[8,128,384]{2,1,0:T(8,128)(2,1)S(1)}, bf16[8,128,384]{2,1,0:T(8,128)(2,1)S(1)}, u32[]{:S(2)}, u32[]{:S(2)}) collective-permute-start(bf16[8,128,384]{2,1,0:T(8,128)(2,1)S(1)} %pad_maximum_fusion.6), channel_id=1, source_target_pairs={{0,1},{1,0},{2,3},{3,2},{4,5},{5,4},{6,7},{7,6},{8,9},{9,8},{10,11... | collective-permute-start | bytes 2359304 | tf_op jit(solution)/shard_map/ppermute | solution.py:43
  48.0 18.3 %collective-permute-start.11 = (bf16[8,128,256]{2,1,0:T(8,128)(2,1)S(1)}, bf16[8,128,256]{2,1,0:T(8,128)(2,1)S(1)}, u32[]{:S(2)}, u32[]{:S(2)}) collective-permute-start(bf16[8,128,256]{2,1,0:T(8,128)(2,1)S(1)} %pad_maximum_fusion.13), channel_id=1, source_target_pairs={{0,2},{1,3},{2,0},{3,1},{4,6},{5,7},{6,4},{7,5},{8,10},{9,11},{10,... | collective-permute-start | bytes 1572872 | tf_op jit(solution)/shard_map/ppermute | solution.py:43
  76.8 29.6 %collective-permute-start.25 = (bf16[512,1024]{1,0:T(8,128)(2,1)}, bf16[512,1024]{1,0:T(8,128)(2,1)S(1)}, u32[]{:S(2)}, u32[]{:S(2)}) collective-permute-start(bf16[512,1024]{1,0:T(8,128)(2,1)} %multiply_convert_fusion.1.refs_1_.refs_0_.refs_2_), channel_id=1, source_target_pairs={{0,16},{8,24},{16,0},{24,8},{1,17},{9,25},{17,1},{25,9},{2,18},{10... | collective-permute-start | bytes 3145736 | tf_op jit(solution)/shard_map/ppermute | solution.py:43
  77.0 29.4 %collective-permute-start.24 = (bf16[512,1024]{1,0:T(8,128)(2,1)}, bf16[512,1024]{1,0:T(8,128)(2,1)S(1)}, u32[]{:S(2)}, u32[]{:S(2)}) collective-permute-start(bf16[512,1024]{1,0:T(8,128)(2,1)} %multiply_convert_fusion.1.refs_1_.refs_0_.refs_2_), channel_id=1, source_target_pairs={{0,8},{8,0},{16,24},{24,16},{1,9},{9,1},{17,25},{25,17},{2,10},{10... | collective-permute-start | bytes 3145736 | tf_op jit(solution)/shard_map/ppermute | solution.py:43
  77.0 28.2 %collective-permute-start.23 = (bf16[576,256]{1,0:T(8,128)(2,1)}, bf16[576,256]{1,0:T(8,128)(2,1)S(1)}, u32[]{:S(2)}, u32[]{:S(2)}) collective-permute-start(bf16[576,256]{1,0:T(8,128)(2,1)} %param.19), channel_id=1, source_target_pairs={{0,0},{1,1},{2,8},{3,9},{4,16},{5,17},{6,24},{7,25},{8,4},{9,5},{1... | collective-permute-start | bytes 884744 | tf_op jit(solution)/shard_map/ppermute | solution.py:794
  78.6 26.3 %collective-permute-start.21 = (bf16[2,128,1152]{2,1,0:T(8,128)(2,1)S(1)}, bf16[2,128,1152]{2,1,0:T(8,128)(2,1)S(1)}, u32[]{:S(2)}, u32[]{:S(2)}) collective-permute-start(bf16[2,128,1152]{2,1,0:T(8,128)(2,1)S(1)} %pad_maximum_fusion.8), channel_id=1, source_target_pairs={{0,2},{1,3},{2,0},{3,1},{4,6},{5,7},{6,4},{7,5},{8,10},{9,11},{10,... | collective-permute-start | bytes 1769480 | tf_op jit(solution)/shard_map/ppermute | solution.py:43
  81.1 23.9 %collective-permute-start.22 = (bf16[2,128,1152]{2,1,0:T(8,128)(2,1)S(1)}, bf16[2,128,1152]{2,1,0:T(8,128)(2,1)S(1)}, u32[]{:S(2)}, u32[]{:S(2)}) collective-permute-start(bf16[2,128,1152]{2,1,0:T(8,128)(2,1)S(1)} %pad_maximum_fusion.9), channel_id=1, source_target_pairs={{0,1},{1,0},{2,3},{3,2},{4,5},{5,4},{6,7},{7,6},{8,9},{9,8},{10,11... | collective-permute-start | bytes 1769480 | tf_op jit(solution)/shard_map/ppermute | solution.py:43
  106.4 34.6 %collective-permute-start.27 = (bf16[4,128,1152]{2,1,0:T(8,128)(2,1)S(1)}, bf16[4,128,1152]{2,1,0:T(8,128)(2,1)S(1)}, u32[]{:S(2)}, u32[]{:S(2)}) collective-permute-start(bf16[4,128,1152]{2,1,0:T(8,128)(2,1)S(1)} %pad_maximum_fusion.2.refs_4_.refs_7_), channel_id=1, source_target_pairs={{0,1},{1,0},{2,3},{3,2},{4,5},{5,4},{6,7},{7,6},{8,9},{9,8},{10,11... | collective-permute-start | bytes 3538952 | tf_op jit(solution)/shard_map/ppermute | solution.py:43
  108.5 33.7 %collective-permute-start.28 = (bf16[4,128,1152]{2,1,0:T(8,128)(2,1)S(1)}, bf16[4,128,1152]{2,1,0:T(8,128)(2,1)S(1)}, u32[]{:S(2)}, u32[]{:S(2)}) collective-permute-start(bf16[4,128,1152]{2,1,0:T(8,128)(2,1)S(1)} %pad_maximum_fusion.3.refs_6_.refs_9_), channel_id=1, source_target_pairs={{0,2},{1,3},{2,0},{3,1},{4,6},{5,7},{6,4},{7,5},{8,10},{9,11},{10,... | collective-permute-start | bytes 3538952 | tf_op jit(solution)/shard_map/ppermute | solution.py:43
  108.5 32.5 %collective-permute-start.26 = (bf16[512,1024]{1,0:T(8,128)(2,1)S(1)}, bf16[512,1024]{1,0:T(8,128)(2,1)S(1)}, u32[]{:S(2)}, u32[]{:S(2)}) collective-permute-start(bf16[512,1024]{1,0:T(8,128)(2,1)S(1)} %copy-done.41), channel_id=1, source_target_pairs={{0,16},{8,24},{16,0},{24,8},{1,17},{9,25},{17,1},{25,9},{2,18},{10... | collective-permute-start | bytes 3145736 | tf_op jit(solution)/shard_map/ppermute | solution.py:43
  111.0 30.0 %collective-permute-start.30 = (bf16[512,1024]{1,0:T(8,128)(2,1)S(1)}, bf16[512,1024]{1,0:T(8,128)(2,1)S(1)}, u32[]{:S(2)}, u32[]{:S(2)}) collective-permute-start(bf16[512,1024]{1,0:T(8,128)(2,1)S(1)} %collective-permute-done.25.refs_3_.refs_2_), channel_id=1, source_target_pairs={{0,8},{8,0},{16,24},{24,16},{1,9},{9,1},{17,25},{25,17},{2,10},{10... | collective-permute-start | bytes 3145736 | tf_op jit(solution)/shard_map/ppermute | solution.py:43
  111.0 30.0 %collective-permute-start.29 = (bf16[1,576,256]{2,1,0:T(8,128)(2,1)S(1)}, bf16[1,576,256]{2,1,0:T(8,128)(2,1)S(1)}, u32[]{:S(2)}, u32[]{:S(2)}) collective-permute-start(bf16[1,576,256]{2,1,0:T(8,128)(2,1)S(1)} %bitcast.46), channel_id=1, source_target_pairs={{0,4},{1,5},{2,6},{3,7},{4,0},{5,1},{6,2},{7,3},{8,12},{9,13},{10,... | collective-permute-start | bytes 884744 | tf_op jit(solution)/shard_map/ppermute | solution.py:43
  146.4 21.0 %collective-permute-start.33 = (bf16[2,288,256]{2,1,0:T(8,128)(2,1)S(1)}, bf16[2,288,256]{2,1,0:T(8,128)(2,1)S(1)}, u32[]{:S(2)}, u32[]{:S(2)}) collective-permute-start(bf16[2,288,256]{2,1,0:T(8,128)(2,1)S(1)} %get-tuple-element.433), channel_id=1, source_target_pairs={{0,2},{1,3},{2,0},{3,1},{4,6},{5,7},{6,4},{7,5},{8,10},{9,11},{10,... | collective-permute-start | bytes 884744 | tf_op jit(solution)/shard_map/ppermute | solution.py:43
  148.6 18.9 %collective-permute-start.34 = (bf16[2,288,256]{2,1,0:T(8,128)(2,1)S(1)}, bf16[2,288,256]{2,1,0:T(8,128)(2,1)S(1)}, u32[]{:S(2)}, u32[]{:S(2)}) collective-permute-start(bf16[2,288,256]{2,1,0:T(8,128)(2,1)S(1)} %get-tuple-element.434), channel_id=1, source_target_pairs={{0,1},{1,0},{2,3},{3,2},{4,5},{5,4},{6,7},{7,6},{8,9},{9,8},{10,11... | collective-permute-start | bytes 884744 | tf_op jit(solution)/shard_map/ppermute | solution.py:43
  183.9 35.6 %collective-permute-start.37 = (bf16[4,288,256]{2,1,0:T(8,128)(2,1)}, bf16[4,288,256]{2,1,0:T(8,128)(2,1)S(1)}, u32[]{:S(2)}, u32[]{:S(2)}) collective-permute-start(bf16[4,288,256]{2,1,0:T(8,128)(2,1)} %get-tuple-element.459), channel_id=1, source_target_pairs={{0,1},{1,0},{2,3},{3,2},{4,5},{5,4},{6,7},{7,6},{8,9},{9,8},{10,11... | collective-permute-start | bytes 1769480 | tf_op jit(solution)/shard_map/ppermute | solution.py:43
  184.2 35.2 %collective-permute-start.38 = (bf16[4,288,256]{2,1,0:T(8,128)(2,1)}, bf16[4,288,256]{2,1,0:T(8,128)(2,1)S(1)}, u32[]{:S(2)}, u32[]{:S(2)}) collective-permute-start(bf16[4,288,256]{2,1,0:T(8,128)(2,1)} %get-tuple-element.461), channel_id=1, source_target_pairs={{0,2},{1,3},{2,0},{3,1},{4,6},{5,7},{6,4},{7,5},{8,10},{9,11},{10,... | collective-permute-start | bytes 1769480 | tf_op jit(solution)/shard_map/ppermute | solution.py:43
  263.5 21.6 %collective-permute-start.52 = (bf16[576,256]{1,0:T(8,128)(2,1)S(1)}, bf16[576,256]{1,0:T(8,128)(2,1)S(1)}, u32[]{:S(2)}, u32[]{:S(2)}) collective-permute-start(bf16[576,256]{1,0:T(8,128)(2,1)S(1)} %fusion), channel_id=1, source_target_pairs={{0,0},{1,1},{8,2},{9,3},{16,4},{17,5},{24,6},{25,7},{4,8},{5,9},{1... | collective-permute-start | bytes 884744 | tf_op jit(solution)/shard_map/ppermute | solution.py:895
  264.3 22.3 %collective-permute-start.51 = (bf16[256,1024]{1,0:T(8,128)(2,1)S(1)}, bf16[256,1024]{1,0:T(8,128)(2,1)S(1)}, u32[]{:S(2)}, u32[]{:S(2)}) collective-permute-start(bf16[256,1024]{1,0:T(8,128)(2,1)S(1)} %get-tuple-element.563), channel_id=1, source_target_pairs={{0,16},{8,24},{16,0},{24,8},{1,17},{9,25},{17,1},{25,9},{2,18},{10... | collective-permute-start | bytes 1572872 | tf_op jit(solution)/shard_map/ppermute | solution.py:43
  268.4 18.1 %collective-permute-start.49 = (bf16[4,64,1152]{2,1,0:T(8,128)(2,1)S(1)}, bf16[4,64,1152]{2,1,0:T(8,128)(2,1)S(1)}, u32[]{:S(2)}, u32[]{:S(2)}) collective-permute-start(bf16[4,64,1152]{2,1,0:T(8,128)(2,1)S(1)} %copy-done.47), channel_id=1, source_target_pairs={{0,1},{1,0},{2,3},{3,2},{4,5},{5,4},{6,7},{7,6},{8,9},{9,8},{10,11... | collective-permute-start | bytes 1769480 | tf_op jit(solution)/shard_map/ppermute | solution.py:43
  270.0 22.1 %collective-permute-start.50 = (bf16[4,64,1152]{2,1,0:T(8,128)(2,1)S(1)}, bf16[4,64,1152]{2,1,0:T(8,128)(2,1)S(1)}, u32[]{:S(2)}, u32[]{:S(2)}) collective-permute-start(bf16[4,64,1152]{2,1,0:T(8,128)(2,1)S(1)} %copy-done.46), channel_id=1, source_target_pairs={{0,2},{1,3},{2,0},{3,1},{4,6},{5,7},{6,4},{7,5},{8,10},{9,11},{10,... | collective-permute-start | bytes 1769480 | tf_op jit(solution)/shard_map/ppermute | solution.py:43
  298.1 18.6 %collective-permute-start.55 = (bf16[2,64,1152]{2,1,0:T(8,128)(2,1)S(1)}, bf16[2,64,1152]{2,1,0:T(8,128)(2,1)S(1)}, u32[]{:S(2)}, u32[]{:S(2)}) collective-permute-start(bf16[2,64,1152]{2,1,0:T(8,128)(2,1)S(1)} %get-tuple-element.592), channel_id=1, source_target_pairs={{0,2},{1,3},{2,0},{3,1},{4,6},{5,7},{6,4},{7,5},{8,10},{9,11},{10,... | collective-permute-start | bytes 884744 | tf_op jit(solution)/shard_map/ppermute | solution.py:43
  (117 other events, 1335.4 us)

commit v7 on v6

--- a/solution.py
+++ b/solution.py
@@ -133,6 +133,27 @@
                 return carry
 
             lax.fori_loop(0, size, start, 0)
+
+
+def start_row_stores(ids_ref, whole, pieces, outs, sem, first, count):
+    each = len(outs) // len(pieces)
+    for step in range(count):
+        seq = first + step
+        mask = seq ^ ids_ref[1]
+        for place, piece in enumerate(pieces):
+            size = 2 ** len(piece.steps) // each
+            position = sum(
+                ((mask >> (bit.bit_length() - 1)) & 1) << at for at, (_, bit) in enumerate(piece.steps)
+            )
+            for part in range(each):
+
+                @pl.when(jnp.logical_and(position >= part * size, position < (part + 1) * size))
+                def _(part=part, position=position, seq=seq, piece=piece, place=place, size=size):
+                    pltpu.make_async_copy(
+                        piece.view(whole, ids_ref[0], seq),
+                        outs[each * place + part].at[position - part * size],
+                        sem,
+                    ).start()
 
 
 def wait_whole(ref, sem):
@@ -176,11 +197,7 @@
             + [pl.BlockSpec((rows, v.shape[1]), lambda i, ids: (i, 0)) for v in tiled]
             + [pl.BlockSpec(memory_space=pl.ANY)] * len(stacks),
             out_specs=[pl.BlockSpec((rows, n), lambda i, ids: (i, 0)) for n, _ in outs]
-            + [
-                pl.BlockSpec((rows, n), lambda i, ids, b=b: (jnp.clip(i - 2 * b, 0, 1), 0))
-                for n, _ in apart
-                for b in range(count)
-            ],
+            + [pl.BlockSpec(memory_space=pl.ANY)] * (len(apart) * count),
             scratch_shapes=[
                 pltpu.VMEM((2, rows, width), jnp.bfloat16),
                 pltpu.SemaphoreType.DMA((2,)),
@@ -240,8 +257,11 @@
     def kernel(ids_ref, *refs):
         blocks, (act_ref, slope_ref, silu_ref) = refs[:count], refs[count : count + 3]
         parts = 2 * count
-        stacks, refs = refs[count + 3 : -8 - parts], refs[-8 - parts :]
-        grad_gate, grad_up, buffers, block_sems, gate_v, up_v, down_v, sems = refs[:2] + refs[2 + parts :]
+        stacks, refs = refs[count + 3 : -10 - parts], refs[-10 - parts :]
+        grad_gate, grad_up, buffers, block_sems, gate_v, up_v, down_v, sems = refs[:2] + refs[2 + parts : -2]
+        tiles, store_sems = refs[-2:]
+        i = pl.program_id(0)
+        slot = i % 2
         norm_parts, out_parts = refs[2 : 2 + count], refs[2 + count : 2 + parts]
 
         @pl.when(pl.program_id(0) == 0)
@@ -263,14 +283,25 @@
         gu = (grad_act * silu_ref[...].astype(jnp.float32)).astype(jnp.bfloat16)
         grad_gate[...] = gg
         grad_up[...] = gu
-        out = multiply(act_ref[...], down_v[...]).astype(jnp.bfloat16)
-        grad_norm = (against(gg, gate_v[...]) + against(gu, up_v[...])).astype(jnp.bfloat16)
+        @pl.when(i >= 2)
+        def _():
+            wait_whole(tiles.at[slot], store_sems.at[slot])
+
+        tiles[slot, 0] = multiply(act_ref[...], down_v[...]).astype(jnp.bfloat16)
+        tiles[slot, 1] = (against(gg, gate_v[...]) + against(gu, up_v[...])).astype(jnp.bfloat16)
+        rows = tiles.shape[2]
         for place in range(count):
 
-            @pl.when(pl.program_id(0) // 2 == place)
+            @pl.when(i // 2 == place)
             def _(place=place):
-                norm_parts[place][...] = grad_norm
-                out_parts[place][...] = out
+                at = pl.ds(pl.multiple_of(slot * rows, rows), rows)
+                for kind, target in ((0, out_parts[place]), (1, norm_parts[place])):
+                    pltpu.make_async_copy(tiles.at[slot, kind], target.at[at], store_sems.at[slot]).start()
+
+        @pl.when(i == 2 * count - 1)
+        def _():
+            wait_whole(tiles.at[0], store_sems.at[0])
+            wait_whole(tiles.at[1], store_sems.at[1])
 
     features, n = shape
     return token_call(
@@ -286,6 +317,8 @@
             pltpu.VMEM(shape, jnp.bfloat16),
             pltpu.VMEM((n, features), jnp.bfloat16),
             pltpu.SemaphoreType.DMA((3,)),
+            pltpu.VMEM((2, 2, final[0].shape[0] // 2, features), jnp.bfloat16),
+            pltpu.SemaphoreType.DMA((2,)),
         ],
     )
 
@@ -302,7 +335,7 @@
     return [tuple(parts[i : i + each]) for i in range(0, len(parts), each)]
 
 
-def weight_gradient(ids, lefts, rights, pieces, each=2):
+def weight_gradient(ids, lefts, rights, pieces, each=2, by_rows=False):
     rows, columns = lefts[0].shape[1], rights[0].shape[1]
     step = min(v.shape[0] for v in (*lefts, *rights))
     tile = next((t for t in (512, 384, 256, 128) if rows % t == 0), rows)
@@ -320,9 +353,14 @@
         total = sum(outer_sum(a, b) for a, b in zip(left_rows, right_rows))
         whole[pl.ds(pl.multiple_of(i * tile, tile), tile)] = total.astype(jnp.bfloat16)
 
+        if by_rows:
+            seqs = 2 ** len(pieces[0].steps) // count
+            start_row_stores(ids_ref, whole, pieces, outs, sems.at[0], i * seqs, seqs)
+
         @pl.when(i == count - 1)
         def _():
-            start_stores(ids_ref, whole, pieces, outs, sems.at[0])
+            if not by_rows:
+                start_stores(ids_ref, whole, pieces, outs, sems.at[0])
             wait_whole(whole, sems.at[0])
 
     parts = pl.pallas_call(
@@ -868,7 +906,7 @@
     far_low = dp_scatter([None] + far_low, xs)
     near_more = swap(near_send, core[0])
     down_parts = sent(down_parts, down, 0)
-    gate_parts = weight_gradient(ids, [normed_all], [grad_gate], feed_grads)
+    gate_parts = weight_gradient(ids, [normed_all], [grad_gate], feed_grads, by_rows=True)
     gate_parts, far_low, far_high, grad_up, near, near_more, down_parts, feed = tie(
         gate_parts, far_low, far_high, grad_up, near, near_more, down_parts, feed
     )
@@ -880,7 +918,7 @@
     far_high = dp_scatter([None] + far_high, xs)
     gate_parts = sent(gate_parts, feed_grads, -1)
     feed_come = [swap(v, core[0]) for v in feed_come]
-    up_parts = weight_gradient(ids, [normed_all], [grad_up], feed_grads)
+    up_parts = weight_gradient(ids, [normed_all], [grad_up], feed_grads, by_rows=True)
     up_parts, far_low, far_high, gate_parts, feed_far, feed_come, own_down = tie(
         up_parts, far_low, far_high, gate_parts, feed_far, feed_come, own_down
     )

time: 408 us -> 407 us (level)
  no operation moved by 1% of the time
where the time goes in v7:
time: 407 us; the launch traced here: 404 us
  waiting for transfers between devices  136 us (33%)
  Pallas kernels  136 us (33%)
  starting transfers between devices  94.9 us (23%)
  other arithmetic  21.2 us (5%)
  local copies, waits for them, and re-layouts  12 us (3%)
    ppermute x83, waiting for transfers between devices, swap(): return lax.ppermute(shard, axis, [(i, i ^ bit) for i in range(count)])  136 us
    ppermute x83, starting transfers between devices, swap(): return lax.ppermute(shard, axis, [(i, i ^ bit) for i in range(count)])  88.6 us
    pallas_call x2, Pallas kernels, token_call(): pl.pallas_call(kernel, out_shape=[jax.ShapeDtypeStruct((rows * steps, n),...  51.9 us
    pallas_call x3, Pallas kernels, weight_gradient(): pl.pallas_call(kernel, out_shape=shapes, grid_spec=pltpu.PrefetchScalarGr...  31.6 us
    pallas_call x1, Pallas kernels, mixer_back(): pl.pallas_call(kernel, out_shape=[jax.ShapeDtypeStruct((rows, features),...  14.7 us
    pallas_call x1, Pallas kernels, mixer_forward(): pl.pallas_call(kernel, out_shape=[jax.ShapeDtypeStruct(s, t) for s, t in...  13.8 us
    pallas_call x1, Pallas kernels, projection_gradient(): pl.pallas_call(kernel, out_shape=[jax.ShapeDtypeStruct((rows, 3 * feature...  13 us
    pallas_call x1, Pallas kernels, mixer_first(): pl.pallas_call(kernel, out_shape=[jax.ShapeDtypeStruct((rows, features),...  10.7 us
  transfers between devices with their start and end apart: 87, of which 41 were waited for; matrix products, arithmetic and copies ran while one was open for 5% of the time, Pallas kernels for 34%

profile of v7, /device:TPU:0, one launch (start us, length us, event | category | flops | bytes accessed | tf_op | source)
XLA Modules:
  0.0 403.5 jit_solution(10051801311746423784)
XLA Ops:
  0.7 4.1 %collective-permute-start.2 = (bf16[1,128,256]{2,1,0:T(8,128)(2,1)}, bf16[1,128,256]{2,1,0:T(8,128)(2,1)S(1)}, u32[]{:S(2)}, u32[]{:S(2)}) collective-permute-start(bf16[1,128,256]{2,1,0:T(8,128)(2,1)} %bitcast.48), channel_id=1, source_target_pairs={{0,4},{1,5},{2,6},{3,7},{4,0},{5,1},{6,2},{7,3},{8,12},{9,13},{10,... | collective-permute-start | bytes 196616 | tf_op jit(solution)/shard_map/ppermute | solution.py:43
  10.7 3.6 collective-permute-done
  22.2 4.7 %collective-permute-done.3 = bf16[2,128,384]{2,1,0:T(8,128)(2,1)S(1)} collective-permute-done((bf16[2,128,384]{2,1,0:T(8,128)(2,1)S(1)}, bf16[2,128,384]{2,1,0:T(8,128)(2,1)S(1)}, u32[]{:S(2)}, u32[]{:S(2)}) %collective-permute-start.3) | collective-permute-done | bytes 196640 | tf_op jit(solution)/shard_map/ppermute | solution.py:43
  39.1 8.6 %collective-permute-start.13 = (bf16[1,128,1152]{2,1,0:T(8,128)(2,1)S(1)}, bf16[1,128,1152]{2,1,0:T(8,128)(2,1)S(1)}, u32[]{:S(2)}, u32[]{:S(2)}) collective-permute-start(bf16[1,128,1152]{2,1,0:T(8,128)(2,1)S(1)} %bitcast.42), channel_id=1, source_target_pairs={{0,4},{1,5},{2,6},{3,7},{4,0},{5,1},{6,2},{7,3},{8,12},{9,13},{10,... | collective-permute-start | bytes 884744 | tf_op jit(solution)/shard_map/ppermute | solution.py:43
  48.1 5.6 %collective-permute-done.8 = bf16[4,128,384]{2,1,0:T(8,128)(2,1)S(1)} collective-permute-done((bf16[4,128,384]{2,1,0:T(8,128)(2,1)S(1)}, bf16[4,128,384]{2,1,0:T(8,128)(2,1)S(1)}, u32[]{:S(2)}, u32[]{:S(2)}) %collective-permute-start.8) | collective-permute-done | bytes 393248 | tf_op jit(solution)/shard_map/ppermute | solution.py:43
  55.3 4.3 %collective-permute-done.13 = bf16[1,128,1152]{2,1,0:T(8,128)(2,1)S(1)} collective-permute-done((bf16[1,128,1152]{2,1,0:T(8,128)(2,1)S(1)}, bf16[1,128,1152]{2,1,0:T(8,128)(2,1)S(1)}, u32[]{:S(2)}, u32[]{:S(2)}) %collective-permute-start.13) | collective-permute-done | bytes 294944 | tf_op jit(solution)/shard_map/ppermute | solution.py:43
  59.7 3.8 collective-permute-done.12
  70.4 6.4 %collective-permute-done.20.refs_5_.refs_11_ = bf16[16,128,256]{2,1,0:T(8,128)(2,1)} collective-permute-done((bf16[16,128,256]{2,1,0:T(8,128)(2,1)}, bf16[16,128,256]{2,1,0:T(8,128)(2,1)}, u32[]{:S(2)}, u32[]{:S(2)}) %collective-permute-start.20) | collective-permute-done | bytes 1048608 | tf_op jit(solution)/shard_map/ppermute | solution.py:43
  83.2 13.8 %shard_map.186 = (bf16[512,1024]{1,0:T(8,128)(2,1)}, bf16[512,1024]{1,0:T(8,128)(2,1)}, bf16[512,1024]{1,0:T(8,128)(2,1)}, bf16[512,1024]{1,0:T(8,128)(2,1)}, bf...) custom-call(s32[2]{0:T(128)} %pad_add_fusion.ids_ref, ...), custom_call_target="tpu_custom_call" | custom-call | flops 68719476736 | bytes 1048576 | tf_op jit(solution)/shard_map/pallas_call | solution.py:448
  97.1 7.8 %collective-permute-done.21 = bf16[2,128,1152]{2,1,0:T(8,128)(2,1)S(1)} collective-permute-done((bf16[2,128,1152]{2,1,0:T(8,128)(2,1)S(1)}, bf16[2,128,1152]{2,1,0:T(8,128)(2,1)S(1)}, u32[]{:S(2)}, u32[]{:S(2)}) %collective-permute-start.21) | collective-permute-done | bytes 589856 | tf_op jit(solution)/shard_map/ppermute | solution.py:43
  112.8 28.1 %collective-permute-done.29 = bf16[1,576,256]{2,1,0:T(8,128)(2,1)S(1)} collective-permute-done((bf16[1,576,256]{2,1,0:T(8,128)(2,1)S(1)}, bf16[1,576,256]{2,1,0:T(8,128)(2,1)S(1)}, u32[]{:S(2)}, u32[]{:S(2)}) %collective-permute-start.29) | collective-permute-done | bytes 294944 | tf_op jit(solution)/shard_map/ppermute | solution.py:43
  149.0 18.4 %shard_map.187 = (bf16[2048,1152]{1,0:T(8,128)(2,1)}, bf16[2048,1152]{1,0:T(8,128)(2,1)}, bf16[2048,1152]{1,0:T(8,128)(2,1)}, bf16[2048,1024]{1,0:T(8,128)(2,1)}) custom-call(s32[2]{0:T(128)} %pad_add_fusion.ids_ref, bf16[512,1024]{1,0:T(8,128)(2,1)} %get-tuple-element.419.refs_0_, bf16[512,1024]{1,0:T(8,128)(2,1)} %copy-done.44, ...), custom_call_target="tpu_custom_call" | custom-call | flops 68719476736 | bytes 1048576 | tf_op jit(solution)/shard_map/pallas_call | solution.py:189
  170.3 10.3 %shard_map.188 = (bf16[4,288,256]{2,1,0:T(8,128)(2,1)}, bf16[4,288,256]{2,1,0:T(8,128)(2,1)}, bf16[4,288,256]{2,1,0:T(8,128)(2,1)}, bf16[4,288,256]{2,1,0:T(8,128)(2,1)}) custom-call(s32[2]{0:T(128)} %pad_add_fusion.ids_ref, bf16[2048,1152]{1,0:T(8,128)(2,1)} %get-tuple-element.435.refs_0_.refs_4_, ...), custom_call_target="tpu_custom_call" | custom-call | flops 68719476736 | bytes 1048576 | tf_op jit(solution)/shard_map/pallas_call | solution.py:366
  185.5 33.4 %shard_map.189 = (bf16[2048,1152]{1,0:T(8,128)(2,1)}, bf16[2048,1152]{1,0:T(8,128)(2,1)}, bf16[512,1024]{1,0:T(8,128)(2,1)}, bf16[512,1024]{1,0:T(8,128)(2,1)}, ...) custom-call(s32[2]{0:T(128)} %pad_add_fusion.ids_ref, ...), custom_call_target="tpu_custom_call" | custom-call | flops 68719476736 | bytes 1048576 | tf_op jit(solution)/shard_map/pallas_call | solution.py:189
  222.0 6.8 %collective-permute-done.41 = bf16[2,288,256]{2,1,0:T(8,128)(2,1)S(1)} collective-permute-done((bf16[2,288,256]{2,1,0:T(8,128)(2,1)S(1)}, bf16[2,288,256]{2,1,0:T(8,128)(2,1)S(1)}, u32[]{:S(2)}, u32[]{:S(2)}) %collective-permute-start.41) | collective-permute-done | bytes 294944 | tf_op jit(solution)/shard_map/ppermute | solution.py:43
  233.5 10.8 %shard_map.190 = (bf16[4,64,1152]{2,1,0:T(8,128)(2,1)}, bf16[4,64,1152]{2,1,0:T(8,128)(2,1)}, bf16[4,64,1152]{2,1,0:T(8,128)(2,1)}, bf16[4,64,1152]{2,1,0:T(8,128)(2,1)}) custom-call(s32[2]{0:T(128)} %pad_add_fusion.ids_ref, bf16[2048,1024]{1,0:T(8,128)(2,1)} %get-tuple-element.427.refs_0_, bf16[2048,1152]{1,0:T(8,128)(2,1)} %get-tuple-element.490.refs_1_), custom_call_target="tpu_custom_call" | custom-call | flops 68719476736 | bytes 1048576 | tf_op jit(solution)/shard_map/pallas_call | solution.py:366
  248.3 10.5 %shard_map.191 = (bf16[4,64,1152]{2,1,0:T(8,128)(2,1)}, bf16[4,64,1152]{2,1,0:T(8,128)(2,1)}, bf16[4,64,1152]{2,1,0:T(8,128)(2,1)}, bf16[4,64,1152]{2,1,0:T(8,128)(2,1)}) custom-call(s32[2]{0:T(128)} %pad_add_fusion.ids_ref, bf16[2048,1024]{1,0:T(8,128)(2,1)} %get-tuple-element.427.refs_0_, bf16[2048,1152]{1,0:T(8,128)(2,1)} %get-tuple-element.521.refs_1_), custom_call_target="tpu_custom_call" | custom-call | flops 68719476736 | bytes 1048576 | tf_op jit(solution)/shard_map/pallas_call | solution.py:366
  263.8 4.2 %collective-permute-start.51 = (bf16[256,1024]{1,0:T(8,128)(2,1)S(1)}, bf16[256,1024]{1,0:T(8,128)(2,1)S(1)}, u32[]{:S(2)}, u32[]{:S(2)}) collective-permute-start(bf16[256,1024]{1,0:T(8,128)(2,1)S(1)} %get-tuple-element.563), channel_id=1, source_target_pairs={{0,16},{8,24},{16,0},{24,8},{1,17},{9,25},{17,1},{25,9},{2,18},{10... | collective-permute-start | bytes 1572872 | tf_op jit(solution)/shard_map/ppermute | solution.py:43
  269.8 14.7 %shard_map.192 = (f32[512,1024]{1,0:T(8,128)}, bf16[512,1024]{1,0:T(8,128)(2,1)}, f32[512,1024]{1,0:T(8,128)}, f32[8,1024]{1,0:T(8,128)}, f32[8,1024]{1,0:T(8,12...) custom-call(s32[2]{0:T(128)} %pad_add_fusion.ids_ref, bf16[512,1024]{1,0:T(8,128)(2,1)} %get-tuple-element.506.refs_0_, ...), custom_call_target="tpu_custom_call" | custom-call | flops 68719476736 | bytes 1048576 | tf_op jit(solution)/shard_map/pallas_call | solution.py:541
  286.1 5.6 %collective-permute-done.50 = bf16[4,64,1152]{2,1,0:T(8,128)(2,1)S(1)} collective-permute-done((bf16[4,64,1152]{2,1,0:T(8,128)(2,1)S(1)}, bf16[4,64,1152]{2,1,0:T(8,128)(2,1)S(1)}, u32[]{:S(2)}, u32[]{:S(2)}) %collective-permute-start.50) | collective-permute-done | bytes 589856 | tf_op jit(solution)/shard_map/ppermute | solution.py:43
  303.4 13.0 %shard_map.193 = (bf16[512,3072]{1,0:T(8,128)(2,1)}, bf16[16,128,256]{2,1,0:T(8,128)(2,1)}, bf16[16,128,256]{2,1,0:T(8,128)(2,1)}, bf16[16,128,256]{2,1,0:T(8,12...) custom-call(s32[2]{0:T(128)} %pad_add_fusion.ids_ref, ...), custom_call_target="tpu_custom_call" | custom-call | flops 68719476736 | bytes 1048576 | tf_op jit(solution)/shard_map/pallas_call | solution.py:598
  318.4 10.7 %shard_map.194 = (bf16[512,1024]{1,0:T(8,128)(2,1)}, f32[8,1024]{1,0:T(8,128)}) custom-call(s32[2]{0:T(128)} %pad_add_fusion.ids_ref, bf16[512,3072]{1,0:T(8,128)(2,1)} %get-tuple-element.626.proj_ref, bf16[512,1024]{1,0:T(8,128)(2,1)} %x_ref, f32[512,1024]{1,0:T(8,128)} %get-tuple-element.627.hidden_ref, f32[8,1024]{1,0:T(8,128)} %get-tuple-element.628.sums_ref, ...), custom_call_target="tpu_custom_call" | custom-call | flops 68719476736 | bytes 1048576 | tf_op jit(solution)/shard_map/pallas_call | solution.py:650
  340.9 11.3 %collective-permute-done.69 = f32[8,1024]{1,0:T(8,128)S(1)} collective-permute-done((f32[8,1024]{1,0:T(8,128)S(1)}, f32[8,1024]{1,0:T(8,128)S(1)}, u32[]{:S(2)}, u32[]{:S(2)}) %collective-permute-start.69) | collective-permute-done | bytes 32800 | tf_op jit(solution)/shard_map/ppermute | solution.py:43
  361.6 4.8 %collective-permute-done.70 = bf16[4,128,256]{2,1,0:T(8,128)(2,1)} collective-permute-done((bf16[4,128,256]{2,1,0:T(8,128)(2,1)}, bf16[4,128,256]{2,1,0:T(8,128)(2,1)}, u32[]{:S(2)}, u32[]{:S(2)}) %collective-permute-start.70) | collective-permute-done | bytes 262176 | tf_op jit(solution)/shard_map/ppermute | solution.py:43
  (382 shorter events, 155.1 us)
Async XLA Ops:
  30.5 17.3 %collective-permute-start.6 = (bf16[4,128,384]{2,1,0:T(8,128)(2,1)S(1)}, bf16[4,128,384]{2,1,0:T(8,128)(2,1)S(1)}, u32[]{:S(2)}, u32[]{:S(2)}) collective-permute-start(bf16[4,128,384]{2,1,0:T(8,128)(2,1)S(1)} %pad_maximum_fusion.14), channel_id=1, source_target_pairs={{0,16},{8,24},{16,0},{24,8},{1,17},{9,25},{17,1},{25,9},{2,18},{10... | collective-permute-start | bytes 1179656 | tf_op jit(solution)/shard_map/ppermute | solution.py:43
  37.5 16.2 %collective-permute-start.8 = (bf16[4,128,384]{2,1,0:T(8,128)(2,1)S(1)}, bf16[4,128,384]{2,1,0:T(8,128)(2,1)S(1)}, u32[]{:S(2)}, u32[]{:S(2)}) collective-permute-start(bf16[4,128,384]{2,1,0:T(8,128)(2,1)S(1)} %pad_maximum_fusion.15), channel_id=1, source_target_pairs={{0,1},{1,0},{2,3},{3,2},{4,5},{5,4},{6,7},{7,6},{8,9},{9,8},{10,11... | collective-permute-start | bytes 1179656 | tf_op jit(solution)/shard_map/ppermute | solution.py:43
  39.1 20.5 %collective-permute-start.13 = (bf16[1,128,1152]{2,1,0:T(8,128)(2,1)S(1)}, bf16[1,128,1152]{2,1,0:T(8,128)(2,1)S(1)}, u32[]{:S(2)}, u32[]{:S(2)}) collective-permute-start(bf16[1,128,1152]{2,1,0:T(8,128)(2,1)S(1)} %bitcast.42), channel_id=1, source_target_pairs={{0,4},{1,5},{2,6},{3,7},{4,0},{5,1},{6,2},{7,3},{8,12},{9,13},{10,... | collective-permute-start | bytes 884744 | tf_op jit(solution)/shard_map/ppermute | solution.py:43
  47.9 19.5 %collective-permute-start.7 = (bf16[8,128,384]{2,1,0:T(8,128)(2,1)S(1)}, bf16[8,128,384]{2,1,0:T(8,128)(2,1)S(1)}, u32[]{:S(2)}, u32[]{:S(2)}) collective-permute-start(bf16[8,128,384]{2,1,0:T(8,128)(2,1)S(1)} %pad_maximum_fusion.6), channel_id=1, source_target_pairs={{0,1},{1,0},{2,3},{3,2},{4,5},{5,4},{6,7},{7,6},{8,9},{9,8},{10,11... | collective-permute-start | bytes 2359304 | tf_op jit(solution)/shard_map/ppermute | solution.py:43
  48.0 18.3 %collective-permute-start.11 = (bf16[8,128,256]{2,1,0:T(8,128)(2,1)S(1)}, bf16[8,128,256]{2,1,0:T(8,128)(2,1)S(1)}, u32[]{:S(2)}, u32[]{:S(2)}) collective-permute-start(bf16[8,128,256]{2,1,0:T(8,128)(2,1)S(1)} %pad_maximum_fusion.13), channel_id=1, source_target_pairs={{0,2},{1,3},{2,0},{3,1},{4,6},{5,7},{6,4},{7,5},{8,10},{9,11},{10,... | collective-permute-start | bytes 1572872 | tf_op jit(solution)/shard_map/ppermute | solution.py:43
  76.8 29.6 %collective-permute-start.25 = (bf16[512,1024]{1,0:T(8,128)(2,1)}, bf16[512,1024]{1,0:T(8,128)(2,1)S(1)}, u32[]{:S(2)}, u32[]{:S(2)}) collective-permute-start(bf16[512,1024]{1,0:T(8,128)(2,1)} %multiply_convert_fusion.1.refs_1_.refs_0_.refs_2_), channel_id=1, source_target_pairs={{0,16},{8,24},{16,0},{24,8},{1,17},{9,25},{17,1},{25,9},{2,18},{10... | collective-permute-start | bytes 3145736 | tf_op jit(solution)/shard_map/ppermute | solution.py:43
  77.0 29.4 %collective-permute-start.24 = (bf16[512,1024]{1,0:T(8,128)(2,1)}, bf16[512,1024]{1,0:T(8,128)(2,1)S(1)}, u32[]{:S(2)}, u32[]{:S(2)}) collective-permute-start(bf16[512,1024]{1,0:T(8,128)(2,1)} %multiply_convert_fusion.1.refs_1_.refs_0_.refs_2_), channel_id=1, source_target_pairs={{0,8},{8,0},{16,24},{24,16},{1,9},{9,1},{17,25},{25,17},{2,10},{10... | collective-permute-start | bytes 3145736 | tf_op jit(solution)/shard_map/ppermute | solution.py:43
  77.0 28.2 %collective-permute-start.23 = (bf16[576,256]{1,0:T(8,128)(2,1)}, bf16[576,256]{1,0:T(8,128)(2,1)S(1)}, u32[]{:S(2)}, u32[]{:S(2)}) collective-permute-start(bf16[576,256]{1,0:T(8,128)(2,1)} %param.19), channel_id=1, source_target_pairs={{0,0},{1,1},{2,8},{3,9},{4,16},{5,17},{6,24},{7,25},{8,4},{9,5},{1... | collective-permute-start | bytes 884744 | tf_op jit(solution)/shard_map/ppermute | solution.py:832
  78.8 26.1 %collective-permute-start.21 = (bf16[2,128,1152]{2,1,0:T(8,128)(2,1)S(1)}, bf16[2,128,1152]{2,1,0:T(8,128)(2,1)S(1)}, u32[]{:S(2)}, u32[]{:S(2)}) collective-permute-start(bf16[2,128,1152]{2,1,0:T(8,128)(2,1)S(1)} %pad_maximum_fusion.8), channel_id=1, source_target_pairs={{0,2},{1,3},{2,0},{3,1},{4,6},{5,7},{6,4},{7,5},{8,10},{9,11},{10,... | collective-permute-start | bytes 1769480 | tf_op jit(solution)/shard_map/ppermute | solution.py:43
  81.3 23.8 %collective-permute-start.22 = (bf16[2,128,1152]{2,1,0:T(8,128)(2,1)S(1)}, bf16[2,128,1152]{2,1,0:T(8,128)(2,1)S(1)}, u32[]{:S(2)}, u32[]{:S(2)}) collective-permute-start(bf16[2,128,1152]{2,1,0:T(8,128)(2,1)S(1)} %pad_maximum_fusion.9), channel_id=1, source_target_pairs={{0,1},{1,0},{2,3},{3,2},{4,5},{5,4},{6,7},{7,6},{8,9},{9,8},{10,11... | collective-permute-start | bytes 1769480 | tf_op jit(solution)/shard_map/ppermute | solution.py:43
  106.4 34.6 %collective-permute-start.27 = (bf16[4,128,1152]{2,1,0:T(8,128)(2,1)S(1)}, bf16[4,128,1152]{2,1,0:T(8,128)(2,1)S(1)}, u32[]{:S(2)}, u32[]{:S(2)}) collective-permute-start(bf16[4,128,1152]{2,1,0:T(8,128)(2,1)S(1)} %pad_maximum_fusion.2.refs_4_.refs_7_), channel_id=1, source_target_pairs={{0,1},{1,0},{2,3},{3,2},{4,5},{5,4},{6,7},{7,6},{8,9},{9,8},{10,11... | collective-permute-start | bytes 3538952 | tf_op jit(solution)/shard_map/ppermute | solution.py:43
  108.5 33.7 %collective-permute-start.28 = (bf16[4,128,1152]{2,1,0:T(8,128)(2,1)S(1)}, bf16[4,128,1152]{2,1,0:T(8,128)(2,1)S(1)}, u32[]{:S(2)}, u32[]{:S(2)}) collective-permute-start(bf16[4,128,1152]{2,1,0:T(8,128)(2,1)S(1)} %pad_maximum_fusion.3.refs_6_.refs_9_), channel_id=1, source_target_pairs={{0,2},{1,3},{2,0},{3,1},{4,6},{5,7},{6,4},{7,5},{8,10},{9,11},{10,... | collective-permute-start | bytes 3538952 | tf_op jit(solution)/shard_map/ppermute | solution.py:43
  108.5 32.5 %collective-permute-start.26 = (bf16[512,1024]{1,0:T(8,128)(2,1)S(1)}, bf16[512,1024]{1,0:T(8,128)(2,1)S(1)}, u32[]{:S(2)}, u32[]{:S(2)}) collective-permute-start(bf16[512,1024]{1,0:T(8,128)(2,1)S(1)} %copy-done.41), channel_id=1, source_target_pairs={{0,16},{8,24},{16,0},{24,8},{1,17},{9,25},{17,1},{25,9},{2,18},{10... | collective-permute-start | bytes 3145736 | tf_op jit(solution)/shard_map/ppermute | solution.py:43
  111.0 30.0 %collective-permute-start.30 = (bf16[512,1024]{1,0:T(8,128)(2,1)S(1)}, bf16[512,1024]{1,0:T(8,128)(2,1)S(1)}, u32[]{:S(2)}, u32[]{:S(2)}) collective-permute-start(bf16[512,1024]{1,0:T(8,128)(2,1)S(1)} %collective-permute-done.25.refs_3_.refs_2_), channel_id=1, source_target_pairs={{0,8},{8,0},{16,24},{24,16},{1,9},{9,1},{17,25},{25,17},{2,10},{10... | collective-permute-start | bytes 3145736 | tf_op jit(solution)/shard_map/ppermute | solution.py:43
  111.0 30.0 %collective-permute-start.29 = (bf16[1,576,256]{2,1,0:T(8,128)(2,1)S(1)}, bf16[1,576,256]{2,1,0:T(8,128)(2,1)S(1)}, u32[]{:S(2)}, u32[]{:S(2)}) collective-permute-start(bf16[1,576,256]{2,1,0:T(8,128)(2,1)S(1)} %bitcast.46), channel_id=1, source_target_pairs={{0,4},{1,5},{2,6},{3,7},{4,0},{5,1},{6,2},{7,3},{8,12},{9,13},{10,... | collective-permute-start | bytes 884744 | tf_op jit(solution)/shard_map/ppermute | solution.py:43
  146.4 21.0 %collective-permute-start.33 = (bf16[2,288,256]{2,1,0:T(8,128)(2,1)S(1)}, bf16[2,288,256]{2,1,0:T(8,128)(2,1)S(1)}, u32[]{:S(2)}, u32[]{:S(2)}) collective-permute-start(bf16[2,288,256]{2,1,0:T(8,128)(2,1)S(1)} %get-tuple-element.433), channel_id=1, source_target_pairs={{0,2},{1,3},{2,0},{3,1},{4,6},{5,7},{6,4},{7,5},{8,10},{9,11},{10,... | collective-permute-start | bytes 884744 | tf_op jit(solution)/shard_map/ppermute | solution.py:43
  148.6 18.9 %collective-permute-start.34 = (bf16[2,288,256]{2,1,0:T(8,128)(2,1)S(1)}, bf16[2,288,256]{2,1,0:T(8,128)(2,1)S(1)}, u32[]{:S(2)}, u32[]{:S(2)}) collective-permute-start(bf16[2,288,256]{2,1,0:T(8,128)(2,1)S(1)} %get-tuple-element.434), channel_id=1, source_target_pairs={{0,1},{1,0},{2,3},{3,2},{4,5},{5,4},{6,7},{7,6},{8,9},{9,8},{10,11... | collective-permute-start | bytes 884744 | tf_op jit(solution)/shard_map/ppermute | solution.py:43
  183.9 35.1 %collective-permute-start.37 = (bf16[4,288,256]{2,1,0:T(8,128)(2,1)}, bf16[4,288,256]{2,1,0:T(8,128)(2,1)S(1)}, u32[]{:S(2)}, u32[]{:S(2)}) collective-permute-start(bf16[4,288,256]{2,1,0:T(8,128)(2,1)} %get-tuple-element.459), channel_id=1, source_target_pairs={{0,1},{1,0},{2,3},{3,2},{4,5},{5,4},{6,7},{7,6},{8,9},{9,8},{10,11... | collective-permute-start | bytes 1769480 | tf_op jit(solution)/shard_map/ppermute | solution.py:43
  184.2 34.7 %collective-permute-start.38 = (bf16[4,288,256]{2,1,0:T(8,128)(2,1)}, bf16[4,288,256]{2,1,0:T(8,128)(2,1)S(1)}, u32[]{:S(2)}, u32[]{:S(2)}) collective-permute-start(bf16[4,288,256]{2,1,0:T(8,128)(2,1)} %get-tuple-element.461), channel_id=1, source_target_pairs={{0,2},{1,3},{2,0},{3,1},{4,6},{5,7},{6,4},{7,5},{8,10},{9,11},{10,... | collective-permute-start | bytes 1769480 | tf_op jit(solution)/shard_map/ppermute | solution.py:43
  262.9 21.6 %collective-permute-start.52 = (bf16[576,256]{1,0:T(8,128)(2,1)S(1)}, bf16[576,256]{1,0:T(8,128)(2,1)S(1)}, u32[]{:S(2)}, u32[]{:S(2)}) collective-permute-start(bf16[576,256]{1,0:T(8,128)(2,1)S(1)} %fusion), channel_id=1, source_target_pairs={{0,0},{1,1},{8,2},{9,3},{16,4},{17,5},{24,6},{25,7},{4,8},{5,9},{1... | collective-permute-start | bytes 884744 | tf_op jit(solution)/shard_map/ppermute | solution.py:933
  263.8 22.3 %collective-permute-start.51 = (bf16[256,1024]{1,0:T(8,128)(2,1)S(1)}, bf16[256,1024]{1,0:T(8,128)(2,1)S(1)}, u32[]{:S(2)}, u32[]{:S(2)}) collective-permute-start(bf16[256,1024]{1,0:T(8,128)(2,1)S(1)} %get-tuple-element.563), channel_id=1, source_target_pairs={{0,16},{8,24},{16,0},{24,8},{1,17},{9,25},{17,1},{25,9},{2,18},{10... | collective-permute-start | bytes 1572872 | tf_op jit(solution)/shard_map/ppermute | solution.py:43
  267.9 18.1 %collective-permute-start.49 = (bf16[4,64,1152]{2,1,0:T(8,128)(2,1)S(1)}, bf16[4,64,1152]{2,1,0:T(8,128)(2,1)S(1)}, u32[]{:S(2)}, u32[]{:S(2)}) collective-permute-start(bf16[4,64,1152]{2,1,0:T(8,128)(2,1)S(1)} %copy-done.47), channel_id=1, source_target_pairs={{0,1},{1,0},{2,3},{3,2},{4,5},{5,4},{6,7},{7,6},{8,9},{9,8},{10,11... | collective-permute-start | bytes 1769480 | tf_op jit(solution)/shard_map/ppermute | solution.py:43
  269.5 22.3 %collective-permute-start.50 = (bf16[4,64,1152]{2,1,0:T(8,128)(2,1)S(1)}, bf16[4,64,1152]{2,1,0:T(8,128)(2,1)S(1)}, u32[]{:S(2)}, u32[]{:S(2)}) collective-permute-start(bf16[4,64,1152]{2,1,0:T(8,128)(2,1)S(1)} %copy-done.46), channel_id=1, source_target_pairs={{0,2},{1,3},{2,0},{3,1},{4,6},{5,7},{6,4},{7,5},{8,10},{9,11},{10,... | collective-permute-start | bytes 1769480 | tf_op jit(solution)/shard_map/ppermute | solution.py:43
  297.7 18.6 %collective-permute-start.55 = (bf16[2,64,1152]{2,1,0:T(8,128)(2,1)S(1)}, bf16[2,64,1152]{2,1,0:T(8,128)(2,1)S(1)}, u32[]{:S(2)}, u32[]{:S(2)}) collective-permute-start(bf16[2,64,1152]{2,1,0:T(8,128)(2,1)S(1)} %get-tuple-element.592), channel_id=1, source_target_pairs={{0,2},{1,3},{2,0},{3,1},{4,6},{5,7},{6,4},{7,5},{8,10},{9,11},{10,... | collective-permute-start | bytes 884744 | tf_op jit(solution)/shard_map/ppermute | solution.py:43
  (117 other events, 1334.4 us)

commit v8 on v7

--- a/solution.py
+++ b/solution.py
@@ -969,7 +969,7 @@
     in_parts, out_parts, sums, gate_parts, up_parts, feed_send = tie(
         in_parts, out_parts, sums, gate_parts, up_parts, feed_send
     )
-    sum_steps = core + ys + xs + zs[::-1]
+    sum_steps = core + xs + ys + zs[::-1]
     for step in sum_steps[:1]:
         sums = sums + swap(sums, step)
     in_parts, out_parts, up_parts = fold_all(in_parts), fold_all(out_parts), joined(fold_all(up_parts))

time: 407 us -> 408 us (level)
  transfers between devices with their start and end apart: 87 -> 87, of which waited for: 41 -> 40; matrix products, arithmetic and copies ran while one was open for 5% -> 5% of each run, Pallas kernels for 34% -> 34%
where the time goes in v8:
time: 408 us; the launch traced here: 404 us
  waiting for transfers between devices  138 us (34%)
  Pallas kernels  136 us (33%)
  starting transfers between devices  93.7 us (23%)
  other arithmetic  21.2 us (5%)
  local copies, waits for them, and re-layouts  12 us (3%)
    ppermute x83, waiting for transfers between devices, swap(): return lax.ppermute(shard, axis, [(i, i ^ bit) for i in range(count)])  138 us
    ppermute x83, starting transfers between devices, swap(): return lax.ppermute(shard, axis, [(i, i ^ bit) for i in range(count)])  87.5 us
    pallas_call x2, Pallas kernels, token_call(): pl.pallas_call(kernel, out_shape=[jax.ShapeDtypeStruct((rows * steps, n),...  51.9 us
    pallas_call x3, Pallas kernels, weight_gradient(): pl.pallas_call(kernel, out_shape=shapes, grid_spec=pltpu.PrefetchScalarGr...  31.6 us
    pallas_call x1, Pallas kernels, mixer_back(): pl.pallas_call(kernel, out_shape=[jax.ShapeDtypeStruct((rows, features),...  14.7 us
    pallas_call x1, Pallas kernels, mixer_forward(): pl.pallas_call(kernel, out_shape=[jax.ShapeDtypeStruct(s, t) for s, t in...  13.8 us
    pallas_call x1, Pallas kernels, projection_gradient(): pl.pallas_call(kernel, out_shape=[jax.ShapeDtypeStruct((rows, 3 * feature...  13 us
    pallas_call x1, Pallas kernels, mixer_first(): pl.pallas_call(kernel, out_shape=[jax.ShapeDtypeStruct((rows, features),...  10.7 us
  transfers between devices with their start and end apart: 87, of which 40 were waited for; matrix products, arithmetic and copies ran while one was open for 5% of the time, Pallas kernels for 34%

profile of v8, /device:TPU:0, one launch (start us, length us, event | category | flops | bytes accessed | tf_op | source)
XLA Modules:
  0.0 403.7 jit_solution(1554763720961451748)
XLA Ops:
  0.7 4.1 %collective-permute-start.2 = (bf16[1,128,256]{2,1,0:T(8,128)(2,1)}, bf16[1,128,256]{2,1,0:T(8,128)(2,1)S(1)}, u32[]{:S(2)}, u32[]{:S(2)}) collective-permute-start(bf16[1,128,256]{2,1,0:T(8,128)(2,1)} %bitcast.48), channel_id=1, source_target_pairs={{0,4},{1,5},{2,6},{3,7},{4,0},{5,1},{6,2},{7,3},{8,12},{9,13},{10,... | collective-permute-start | bytes 196616 | tf_op jit(solution)/shard_map/ppermute | solution.py:43
  10.7 3.6 collective-permute-done
  22.2 4.7 %collective-permute-done.3 = bf16[2,128,384]{2,1,0:T(8,128)(2,1)S(1)} collective-permute-done((bf16[2,128,384]{2,1,0:T(8,128)(2,1)S(1)}, bf16[2,128,384]{2,1,0:T(8,128)(2,1)S(1)}, u32[]{:S(2)}, u32[]{:S(2)}) %collective-permute-start.3) | collective-permute-done | bytes 196640 | tf_op jit(solution)/shard_map/ppermute | solution.py:43
  39.1 8.6 %collective-permute-start.13 = (bf16[1,128,1152]{2,1,0:T(8,128)(2,1)S(1)}, bf16[1,128,1152]{2,1,0:T(8,128)(2,1)S(1)}, u32[]{:S(2)}, u32[]{:S(2)}) collective-permute-start(bf16[1,128,1152]{2,1,0:T(8,128)(2,1)S(1)} %bitcast.42), channel_id=1, source_target_pairs={{0,4},{1,5},{2,6},{3,7},{4,0},{5,1},{6,2},{7,3},{8,12},{9,13},{10,... | collective-permute-start | bytes 884744 | tf_op jit(solution)/shard_map/ppermute | solution.py:43
  48.1 5.6 %collective-permute-done.8 = bf16[4,128,384]{2,1,0:T(8,128)(2,1)S(1)} collective-permute-done((bf16[4,128,384]{2,1,0:T(8,128)(2,1)S(1)}, bf16[4,128,384]{2,1,0:T(8,128)(2,1)S(1)}, u32[]{:S(2)}, u32[]{:S(2)}) %collective-permute-start.8) | collective-permute-done | bytes 393248 | tf_op jit(solution)/shard_map/ppermute | solution.py:43
  55.3 4.3 %collective-permute-done.13 = bf16[1,128,1152]{2,1,0:T(8,128)(2,1)S(1)} collective-permute-done((bf16[1,128,1152]{2,1,0:T(8,128)(2,1)S(1)}, bf16[1,128,1152]{2,1,0:T(8,128)(2,1)S(1)}, u32[]{:S(2)}, u32[]{:S(2)}) %collective-permute-start.13) | collective-permute-done | bytes 294944 | tf_op jit(solution)/shard_map/ppermute | solution.py:43
  59.7 3.8 collective-permute-done.12
  70.4 6.4 %collective-permute-done.20.refs_5_.refs_11_ = bf16[16,128,256]{2,1,0:T(8,128)(2,1)} collective-permute-done((bf16[16,128,256]{2,1,0:T(8,128)(2,1)}, bf16[16,128,256]{2,1,0:T(8,128)(2,1)}, u32[]{:S(2)}, u32[]{:S(2)}) %collective-permute-start.20) | collective-permute-done | bytes 1048608 | tf_op jit(solution)/shard_map/ppermute | solution.py:43
  83.2 13.8 %shard_map.186 = (bf16[512,1024]{1,0:T(8,128)(2,1)}, bf16[512,1024]{1,0:T(8,128)(2,1)}, bf16[512,1024]{1,0:T(8,128)(2,1)}, bf16[512,1024]{1,0:T(8,128)(2,1)}, bf...) custom-call(s32[2]{0:T(128)} %pad_add_fusion.ids_ref, ...), custom_call_target="tpu_custom_call" | custom-call | flops 68719476736 | bytes 1048576 | tf_op jit(solution)/shard_map/pallas_call | solution.py:448
  97.1 7.8 %collective-permute-done.21 = bf16[2,128,1152]{2,1,0:T(8,128)(2,1)S(1)} collective-permute-done((bf16[2,128,1152]{2,1,0:T(8,128)(2,1)S(1)}, bf16[2,128,1152]{2,1,0:T(8,128)(2,1)S(1)}, u32[]{:S(2)}, u32[]{:S(2)}) %collective-permute-start.21) | collective-permute-done | bytes 589856 | tf_op jit(solution)/shard_map/ppermute | solution.py:43
  112.8 28.1 %collective-permute-done.29 = bf16[1,576,256]{2,1,0:T(8,128)(2,1)S(1)} collective-permute-done((bf16[1,576,256]{2,1,0:T(8,128)(2,1)S(1)}, bf16[1,576,256]{2,1,0:T(8,128)(2,1)S(1)}, u32[]{:S(2)}, u32[]{:S(2)}) %collective-permute-start.29) | collective-permute-done | bytes 294944 | tf_op jit(solution)/shard_map/ppermute | solution.py:43
  149.0 18.4 %shard_map.187 = (bf16[2048,1152]{1,0:T(8,128)(2,1)}, bf16[2048,1152]{1,0:T(8,128)(2,1)}, bf16[2048,1152]{1,0:T(8,128)(2,1)}, bf16[2048,1024]{1,0:T(8,128)(2,1)}) custom-call(s32[2]{0:T(128)} %pad_add_fusion.ids_ref, bf16[512,1024]{1,0:T(8,128)(2,1)} %get-tuple-element.419.refs_0_, bf16[512,1024]{1,0:T(8,128)(2,1)} %copy-done.44, ...), custom_call_target="tpu_custom_call" | custom-call | flops 68719476736 | bytes 1048576 | tf_op jit(solution)/shard_map/pallas_call | solution.py:189
  170.3 10.3 %shard_map.188 = (bf16[4,288,256]{2,1,0:T(8,128)(2,1)}, bf16[4,288,256]{2,1,0:T(8,128)(2,1)}, bf16[4,288,256]{2,1,0:T(8,128)(2,1)}, bf16[4,288,256]{2,1,0:T(8,128)(2,1)}) custom-call(s32[2]{0:T(128)} %pad_add_fusion.ids_ref, bf16[2048,1152]{1,0:T(8,128)(2,1)} %get-tuple-element.435.refs_0_.refs_4_, ...), custom_call_target="tpu_custom_call" | custom-call | flops 68719476736 | bytes 1048576 | tf_op jit(solution)/shard_map/pallas_call | solution.py:366
  185.5 33.4 %shard_map.189 = (bf16[2048,1152]{1,0:T(8,128)(2,1)}, bf16[2048,1152]{1,0:T(8,128)(2,1)}, bf16[512,1024]{1,0:T(8,128)(2,1)}, bf16[512,1024]{1,0:T(8,128)(2,1)}, ...) custom-call(s32[2]{0:T(128)} %pad_add_fusion.ids_ref, ...), custom_call_target="tpu_custom_call" | custom-call | flops 68719476736 | bytes 1048576 | tf_op jit(solution)/shard_map/pallas_call | solution.py:189
  222.0 6.8 %collective-permute-done.41 = bf16[2,288,256]{2,1,0:T(8,128)(2,1)S(1)} collective-permute-done((bf16[2,288,256]{2,1,0:T(8,128)(2,1)S(1)}, bf16[2,288,256]{2,1,0:T(8,128)(2,1)S(1)}, u32[]{:S(2)}, u32[]{:S(2)}) %collective-permute-start.41) | collective-permute-done | bytes 294944 | tf_op jit(solution)/shard_map/ppermute | solution.py:43
  233.5 10.8 %shard_map.190 = (bf16[4,64,1152]{2,1,0:T(8,128)(2,1)}, bf16[4,64,1152]{2,1,0:T(8,128)(2,1)}, bf16[4,64,1152]{2,1,0:T(8,128)(2,1)}, bf16[4,64,1152]{2,1,0:T(8,128)(2,1)}) custom-call(s32[2]{0:T(128)} %pad_add_fusion.ids_ref, bf16[2048,1024]{1,0:T(8,128)(2,1)} %get-tuple-element.427.refs_0_, bf16[2048,1152]{1,0:T(8,128)(2,1)} %get-tuple-element.490.refs_1_), custom_call_target="tpu_custom_call" | custom-call | flops 68719476736 | bytes 1048576 | tf_op jit(solution)/shard_map/pallas_call | solution.py:366
  248.3 10.5 %shard_map.191 = (bf16[4,64,1152]{2,1,0:T(8,128)(2,1)}, bf16[4,64,1152]{2,1,0:T(8,128)(2,1)}, bf16[4,64,1152]{2,1,0:T(8,128)(2,1)}, bf16[4,64,1152]{2,1,0:T(8,128)(2,1)}) custom-call(s32[2]{0:T(128)} %pad_add_fusion.ids_ref, bf16[2048,1024]{1,0:T(8,128)(2,1)} %get-tuple-element.427.refs_0_, bf16[2048,1152]{1,0:T(8,128)(2,1)} %get-tuple-element.521.refs_1_), custom_call_target="tpu_custom_call" | custom-call | flops 68719476736 | bytes 1048576 | tf_op jit(solution)/shard_map/pallas_call | solution.py:366
  263.8 4.2 %collective-permute-start.51 = (bf16[256,1024]{1,0:T(8,128)(2,1)S(1)}, bf16[256,1024]{1,0:T(8,128)(2,1)S(1)}, u32[]{:S(2)}, u32[]{:S(2)}) collective-permute-start(bf16[256,1024]{1,0:T(8,128)(2,1)S(1)} %get-tuple-element.563), channel_id=1, source_target_pairs={{0,16},{8,24},{16,0},{24,8},{1,17},{9,25},{17,1},{25,9},{2,18},{10... | collective-permute-start | bytes 1572872 | tf_op jit(solution)/shard_map/ppermute | solution.py:43
  269.8 14.7 %shard_map.192 = (f32[512,1024]{1,0:T(8,128)}, bf16[512,1024]{1,0:T(8,128)(2,1)}, f32[512,1024]{1,0:T(8,128)}, f32[8,1024]{1,0:T(8,128)}, f32[8,1024]{1,0:T(8,12...) custom-call(s32[2]{0:T(128)} %pad_add_fusion.ids_ref, bf16[512,1024]{1,0:T(8,128)(2,1)} %get-tuple-element.506.refs_0_, ...), custom_call_target="tpu_custom_call" | custom-call | flops 68719476736 | bytes 1048576 | tf_op jit(solution)/shard_map/pallas_call | solution.py:541
  286.1 5.6 %collective-permute-done.50 = bf16[4,64,1152]{2,1,0:T(8,128)(2,1)S(1)} collective-permute-done((bf16[4,64,1152]{2,1,0:T(8,128)(2,1)S(1)}, bf16[4,64,1152]{2,1,0:T(8,128)(2,1)S(1)}, u32[]{:S(2)}, u32[]{:S(2)}) %collective-permute-start.50) | collective-permute-done | bytes 589856 | tf_op jit(solution)/shard_map/ppermute | solution.py:43
  303.4 13.0 %shard_map.193 = (bf16[512,3072]{1,0:T(8,128)(2,1)}, bf16[16,128,256]{2,1,0:T(8,128)(2,1)}, bf16[16,128,256]{2,1,0:T(8,128)(2,1)}, bf16[16,128,256]{2,1,0:T(8,12...) custom-call(s32[2]{0:T(128)} %pad_add_fusion.ids_ref, ...), custom_call_target="tpu_custom_call" | custom-call | flops 68719476736 | bytes 1048576 | tf_op jit(solution)/shard_map/pallas_call | solution.py:598
  318.4 10.7 %shard_map.194 = (bf16[512,1024]{1,0:T(8,128)(2,1)}, f32[8,1024]{1,0:T(8,128)}) custom-call(s32[2]{0:T(128)} %pad_add_fusion.ids_ref, bf16[512,3072]{1,0:T(8,128)(2,1)} %get-tuple-element.626.proj_ref, bf16[512,1024]{1,0:T(8,128)(2,1)} %x_ref, f32[512,1024]{1,0:T(8,128)} %get-tuple-element.627.hidden_ref, f32[8,1024]{1,0:T(8,128)} %get-tuple-element.628.sums_ref, ...), custom_call_target="tpu_custom_call" | custom-call | flops 68719476736 | bytes 1048576 | tf_op jit(solution)/shard_map/pallas_call | solution.py:650
  339.9 12.7 %collective-permute-done.69 = f32[8,1024]{1,0:T(8,128)S(1)} collective-permute-done((f32[8,1024]{1,0:T(8,128)S(1)}, f32[8,1024]{1,0:T(8,128)S(1)}, u32[]{:S(2)}, u32[]{:S(2)}) %collective-permute-start.69) | collective-permute-done | bytes 32800 | tf_op jit(solution)/shard_map/ppermute | solution.py:43
  362.3 4.9 %collective-permute-done.70 = bf16[4,128,256]{2,1,0:T(8,128)(2,1)} collective-permute-done((bf16[4,128,256]{2,1,0:T(8,128)(2,1)}, bf16[4,128,256]{2,1,0:T(8,128)(2,1)}, u32[]{:S(2)}, u32[]{:S(2)}) %collective-permute-start.70) | collective-permute-done | bytes 262176 | tf_op jit(solution)/shard_map/ppermute | solution.py:43
  (382 shorter events, 153.7 us)
Async XLA Ops:
  30.5 17.3 %collective-permute-start.6 = (bf16[4,128,384]{2,1,0:T(8,128)(2,1)S(1)}, bf16[4,128,384]{2,1,0:T(8,128)(2,1)S(1)}, u32[]{:S(2)}, u32[]{:S(2)}) collective-permute-start(bf16[4,128,384]{2,1,0:T(8,128)(2,1)S(1)} %pad_maximum_fusion.14), channel_id=1, source_target_pairs={{0,16},{8,24},{16,0},{24,8},{1,17},{9,25},{17,1},{25,9},{2,18},{10... | collective-permute-start | bytes 1179656 | tf_op jit(solution)/shard_map/ppermute | solution.py:43
  37.5 16.2 %collective-permute-start.8 = (bf16[4,128,384]{2,1,0:T(8,128)(2,1)S(1)}, bf16[4,128,384]{2,1,0:T(8,128)(2,1)S(1)}, u32[]{:S(2)}, u32[]{:S(2)}) collective-permute-start(bf16[4,128,384]{2,1,0:T(8,128)(2,1)S(1)} %pad_maximum_fusion.15), channel_id=1, source_target_pairs={{0,1},{1,0},{2,3},{3,2},{4,5},{5,4},{6,7},{7,6},{8,9},{9,8},{10,11... | collective-permute-start | bytes 1179656 | tf_op jit(solution)/shard_map/ppermute | solution.py:43
  39.1 20.5 %collective-permute-start.13 = (bf16[1,128,1152]{2,1,0:T(8,128)(2,1)S(1)}, bf16[1,128,1152]{2,1,0:T(8,128)(2,1)S(1)}, u32[]{:S(2)}, u32[]{:S(2)}) collective-permute-start(bf16[1,128,1152]{2,1,0:T(8,128)(2,1)S(1)} %bitcast.42), channel_id=1, source_target_pairs={{0,4},{1,5},{2,6},{3,7},{4,0},{5,1},{6,2},{7,3},{8,12},{9,13},{10,... | collective-permute-start | bytes 884744 | tf_op jit(solution)/shard_map/ppermute | solution.py:43
  47.9 19.5 %collective-permute-start.7 = (bf16[8,128,384]{2,1,0:T(8,128)(2,1)S(1)}, bf16[8,128,384]{2,1,0:T(8,128)(2,1)S(1)}, u32[]{:S(2)}, u32[]{:S(2)}) collective-permute-start(bf16[8,128,384]{2,1,0:T(8,128)(2,1)S(1)} %pad_maximum_fusion.6), channel_id=1, source_target_pairs={{0,1},{1,0},{2,3},{3,2},{4,5},{5,4},{6,7},{7,6},{8,9},{9,8},{10,11... | collective-permute-start | bytes 2359304 | tf_op jit(solution)/shard_map/ppermute | solution.py:43
  48.0 18.3 %collective-permute-start.11 = (bf16[8,128,256]{2,1,0:T(8,128)(2,1)S(1)}, bf16[8,128,256]{2,1,0:T(8,128)(2,1)S(1)}, u32[]{:S(2)}, u32[]{:S(2)}) collective-permute-start(bf16[8,128,256]{2,1,0:T(8,128)(2,1)S(1)} %pad_maximum_fusion.13), channel_id=1, source_target_pairs={{0,2},{1,3},{2,0},{3,1},{4,6},{5,7},{6,4},{7,5},{8,10},{9,11},{10,... | collective-permute-start | bytes 1572872 | tf_op jit(solution)/shard_map/ppermute | solution.py:43
  76.8 29.6 %collective-permute-start.25 = (bf16[512,1024]{1,0:T(8,128)(2,1)}, bf16[512,1024]{1,0:T(8,128)(2,1)S(1)}, u32[]{:S(2)}, u32[]{:S(2)}) collective-permute-start(bf16[512,1024]{1,0:T(8,128)(2,1)} %multiply_convert_fusion.1.refs_1_.refs_0_.refs_2_), channel_id=1, source_target_pairs={{0,16},{8,24},{16,0},{24,8},{1,17},{9,25},{17,1},{25,9},{2,18},{10... | collective-permute-start | bytes 3145736 | tf_op jit(solution)/shard_map/ppermute | solution.py:43
  77.0 29.4 %collective-permute-start.24 = (bf16[512,1024]{1,0:T(8,128)(2,1)}, bf16[512,1024]{1,0:T(8,128)(2,1)S(1)}, u32[]{:S(2)}, u32[]{:S(2)}) collective-permute-start(bf16[512,1024]{1,0:T(8,128)(2,1)} %multiply_convert_fusion.1.refs_1_.refs_0_.refs_2_), channel_id=1, source_target_pairs={{0,8},{8,0},{16,24},{24,16},{1,9},{9,1},{17,25},{25,17},{2,10},{10... | collective-permute-start | bytes 3145736 | tf_op jit(solution)/shard_map/ppermute | solution.py:43
  77.0 28.2 %collective-permute-start.23 = (bf16[576,256]{1,0:T(8,128)(2,1)}, bf16[576,256]{1,0:T(8,128)(2,1)S(1)}, u32[]{:S(2)}, u32[]{:S(2)}) collective-permute-start(bf16[576,256]{1,0:T(8,128)(2,1)} %param.19), channel_id=1, source_target_pairs={{0,0},{1,1},{2,8},{3,9},{4,16},{5,17},{6,24},{7,25},{8,4},{9,5},{1... | collective-permute-start | bytes 884744 | tf_op jit(solution)/shard_map/ppermute | solution.py:832
  78.8 26.1 %collective-permute-start.21 = (bf16[2,128,1152]{2,1,0:T(8,128)(2,1)S(1)}, bf16[2,128,1152]{2,1,0:T(8,128)(2,1)S(1)}, u32[]{:S(2)}, u32[]{:S(2)}) collective-permute-start(bf16[2,128,1152]{2,1,0:T(8,128)(2,1)S(1)} %pad_maximum_fusion.8), channel_id=1, source_target_pairs={{0,2},{1,3},{2,0},{3,1},{4,6},{5,7},{6,4},{7,5},{8,10},{9,11},{10,... | collective-permute-start | bytes 1769480 | tf_op jit(solution)/shard_map/ppermute | solution.py:43
  81.3 23.8 %collective-permute-start.22 = (bf16[2,128,1152]{2,1,0:T(8,128)(2,1)S(1)}, bf16[2,128,1152]{2,1,0:T(8,128)(2,1)S(1)}, u32[]{:S(2)}, u32[]{:S(2)}) collective-permute-start(bf16[2,128,1152]{2,1,0:T(8,128)(2,1)S(1)} %pad_maximum_fusion.9), channel_id=1, source_target_pairs={{0,1},{1,0},{2,3},{3,2},{4,5},{5,4},{6,7},{7,6},{8,9},{9,8},{10,11... | collective-permute-start | bytes 1769480 | tf_op jit(solution)/shard_map/ppermute | solution.py:43
  106.4 34.6 %collective-permute-start.27 = (bf16[4,128,1152]{2,1,0:T(8,128)(2,1)S(1)}, bf16[4,128,1152]{2,1,0:T(8,128)(2,1)S(1)}, u32[]{:S(2)}, u32[]{:S(2)}) collective-permute-start(bf16[4,128,1152]{2,1,0:T(8,128)(2,1)S(1)} %pad_maximum_fusion.2.refs_4_.refs_7_), channel_id=1, source_target_pairs={{0,1},{1,0},{2,3},{3,2},{4,5},{5,4},{6,7},{7,6},{8,9},{9,8},{10,11... | collective-permute-start | bytes 3538952 | tf_op jit(solution)/shard_map/ppermute | solution.py:43
  108.5 33.7 %collective-permute-start.28 = (bf16[4,128,1152]{2,1,0:T(8,128)(2,1)S(1)}, bf16[4,128,1152]{2,1,0:T(8,128)(2,1)S(1)}, u32[]{:S(2)}, u32[]{:S(2)}) collective-permute-start(bf16[4,128,1152]{2,1,0:T(8,128)(2,1)S(1)} %pad_maximum_fusion.3.refs_6_.refs_9_), channel_id=1, source_target_pairs={{0,2},{1,3},{2,0},{3,1},{4,6},{5,7},{6,4},{7,5},{8,10},{9,11},{10,... | collective-permute-start | bytes 3538952 | tf_op jit(solution)/shard_map/ppermute | solution.py:43
  108.5 32.5 %collective-permute-start.26 = (bf16[512,1024]{1,0:T(8,128)(2,1)S(1)}, bf16[512,1024]{1,0:T(8,128)(2,1)S(1)}, u32[]{:S(2)}, u32[]{:S(2)}) collective-permute-start(bf16[512,1024]{1,0:T(8,128)(2,1)S(1)} %copy-done.41), channel_id=1, source_target_pairs={{0,16},{8,24},{16,0},{24,8},{1,17},{9,25},{17,1},{25,9},{2,18},{10... | collective-permute-start | bytes 3145736 | tf_op jit(solution)/shard_map/ppermute | solution.py:43
  111.0 30.0 %collective-permute-start.30 = (bf16[512,1024]{1,0:T(8,128)(2,1)S(1)}, bf16[512,1024]{1,0:T(8,128)(2,1)S(1)}, u32[]{:S(2)}, u32[]{:S(2)}) collective-permute-start(bf16[512,1024]{1,0:T(8,128)(2,1)S(1)} %collective-permute-done.25.refs_3_.refs_2_), channel_id=1, source_target_pairs={{0,8},{8,0},{16,24},{24,16},{1,9},{9,1},{17,25},{25,17},{2,10},{10... | collective-permute-start | bytes 3145736 | tf_op jit(solution)/shard_map/ppermute | solution.py:43
  111.0 30.0 %collective-permute-start.29 = (bf16[1,576,256]{2,1,0:T(8,128)(2,1)S(1)}, bf16[1,576,256]{2,1,0:T(8,128)(2,1)S(1)}, u32[]{:S(2)}, u32[]{:S(2)}) collective-permute-start(bf16[1,576,256]{2,1,0:T(8,128)(2,1)S(1)} %bitcast.46), channel_id=1, source_target_pairs={{0,4},{1,5},{2,6},{3,7},{4,0},{5,1},{6,2},{7,3},{8,12},{9,13},{10,... | collective-permute-start | bytes 884744 | tf_op jit(solution)/shard_map/ppermute | solution.py:43
  146.4 21.0 %collective-permute-start.33 = (bf16[2,288,256]{2,1,0:T(8,128)(2,1)S(1)}, bf16[2,288,256]{2,1,0:T(8,128)(2,1)S(1)}, u32[]{:S(2)}, u32[]{:S(2)}) collective-permute-start(bf16[2,288,256]{2,1,0:T(8,128)(2,1)S(1)} %get-tuple-element.433), channel_id=1, source_target_pairs={{0,2},{1,3},{2,0},{3,1},{4,6},{5,7},{6,4},{7,5},{8,10},{9,11},{10,... | collective-permute-start | bytes 884744 | tf_op jit(solution)/shard_map/ppermute | solution.py:43
  148.6 18.9 %collective-permute-start.34 = (bf16[2,288,256]{2,1,0:T(8,128)(2,1)S(1)}, bf16[2,288,256]{2,1,0:T(8,128)(2,1)S(1)}, u32[]{:S(2)}, u32[]{:S(2)}) collective-permute-start(bf16[2,288,256]{2,1,0:T(8,128)(2,1)S(1)} %get-tuple-element.434), channel_id=1, source_target_pairs={{0,1},{1,0},{2,3},{3,2},{4,5},{5,4},{6,7},{7,6},{8,9},{9,8},{10,11... | collective-permute-start | bytes 884744 | tf_op jit(solution)/shard_map/ppermute | solution.py:43
  183.9 35.1 %collective-permute-start.37 = (bf16[4,288,256]{2,1,0:T(8,128)(2,1)}, bf16[4,288,256]{2,1,0:T(8,128)(2,1)S(1)}, u32[]{:S(2)}, u32[]{:S(2)}) collective-permute-start(bf16[4,288,256]{2,1,0:T(8,128)(2,1)} %get-tuple-element.459), channel_id=1, source_target_pairs={{0,1},{1,0},{2,3},{3,2},{4,5},{5,4},{6,7},{7,6},{8,9},{9,8},{10,11... | collective-permute-start | bytes 1769480 | tf_op jit(solution)/shard_map/ppermute | solution.py:43
  184.2 34.7 %collective-permute-start.38 = (bf16[4,288,256]{2,1,0:T(8,128)(2,1)}, bf16[4,288,256]{2,1,0:T(8,128)(2,1)S(1)}, u32[]{:S(2)}, u32[]{:S(2)}) collective-permute-start(bf16[4,288,256]{2,1,0:T(8,128)(2,1)} %get-tuple-element.461), channel_id=1, source_target_pairs={{0,2},{1,3},{2,0},{3,1},{4,6},{5,7},{6,4},{7,5},{8,10},{9,11},{10,... | collective-permute-start | bytes 1769480 | tf_op jit(solution)/shard_map/ppermute | solution.py:43
  262.9 21.6 %collective-permute-start.52 = (bf16[576,256]{1,0:T(8,128)(2,1)S(1)}, bf16[576,256]{1,0:T(8,128)(2,1)S(1)}, u32[]{:S(2)}, u32[]{:S(2)}) collective-permute-start(bf16[576,256]{1,0:T(8,128)(2,1)S(1)} %fusion), channel_id=1, source_target_pairs={{0,0},{1,1},{8,2},{9,3},{16,4},{17,5},{24,6},{25,7},{4,8},{5,9},{1... | collective-permute-start | bytes 884744 | tf_op jit(solution)/shard_map/ppermute | solution.py:933
  263.8 22.3 %collective-permute-start.51 = (bf16[256,1024]{1,0:T(8,128)(2,1)S(1)}, bf16[256,1024]{1,0:T(8,128)(2,1)S(1)}, u32[]{:S(2)}, u32[]{:S(2)}) collective-permute-start(bf16[256,1024]{1,0:T(8,128)(2,1)S(1)} %get-tuple-element.563), channel_id=1, source_target_pairs={{0,16},{8,24},{16,0},{24,8},{1,17},{9,25},{17,1},{25,9},{2,18},{10... | collective-permute-start | bytes 1572872 | tf_op jit(solution)/shard_map/ppermute | solution.py:43
  267.9 18.1 %collective-permute-start.49 = (bf16[4,64,1152]{2,1,0:T(8,128)(2,1)S(1)}, bf16[4,64,1152]{2,1,0:T(8,128)(2,1)S(1)}, u32[]{:S(2)}, u32[]{:S(2)}) collective-permute-start(bf16[4,64,1152]{2,1,0:T(8,128)(2,1)S(1)} %copy-done.47), channel_id=1, source_target_pairs={{0,1},{1,0},{2,3},{3,2},{4,5},{5,4},{6,7},{7,6},{8,9},{9,8},{10,11... | collective-permute-start | bytes 1769480 | tf_op jit(solution)/shard_map/ppermute | solution.py:43
  269.5 22.3 %collective-permute-start.50 = (bf16[4,64,1152]{2,1,0:T(8,128)(2,1)S(1)}, bf16[4,64,1152]{2,1,0:T(8,128)(2,1)S(1)}, u32[]{:S(2)}, u32[]{:S(2)}) collective-permute-start(bf16[4,64,1152]{2,1,0:T(8,128)(2,1)S(1)} %copy-done.46), channel_id=1, source_target_pairs={{0,2},{1,3},{2,0},{3,1},{4,6},{5,7},{6,4},{7,5},{8,10},{9,11},{10,... | collective-permute-start | bytes 1769480 | tf_op jit(solution)/shard_map/ppermute | solution.py:43
  297.7 18.6 %collective-permute-start.55 = (bf16[2,64,1152]{2,1,0:T(8,128)(2,1)S(1)}, bf16[2,64,1152]{2,1,0:T(8,128)(2,1)S(1)}, u32[]{:S(2)}, u32[]{:S(2)}) collective-permute-start(bf16[2,64,1152]{2,1,0:T(8,128)(2,1)S(1)} %get-tuple-element.592), channel_id=1, source_target_pairs={{0,2},{1,3},{2,0},{3,1},{4,6},{5,7},{6,4},{7,5},{8,10},{9,11},{10,... | collective-permute-start | bytes 884744 | tf_op jit(solution)/shard_map/ppermute | solution.py:43
  (117 other events, 1338.1 us)
